TPU v7x, 32 devices: a whole 2x2x4 slice. The times are simulated.
32 devices in a mesh: groups: 2 (over x), seq: 16 (over z, y, core).
Axes of the slice: x: 2, y: 2, z: 4, core: 2. Of those that a mesh axis runs over, the one named last changes fastest.
Arguments:
- first_inputs: float32 [288, 32768], P(None, ('groups', 'seq')), parts along dimension 1, may hold values from -6 to 6
- second_inputs: float32 [288, 32768], P(None, ('groups', 'seq')), parts along dimension 1, may hold values from -6 to 6
- out_grad: float32 [288, 32768], P(None, ('groups', 'seq')), parts along dimension 1, may hold values from -6 to 6
- weight_in: float32 [2, 288, 384], replicated, may hold values from -0.375 to 0.375
- bias_in: float32 [2, 384], replicated, may hold values from -4 to 4
- weight_out: float32 [2, 384, 288], replicated, may hold values from -0.3125 to 0.3125
- distances: int32 [2, 18], replicated, may hold values from 0 to 8192, as said below
Outputs:
- input_grad: float32 [288, 32768], P(None, ('groups', 'seq')), parts along dimension 1
- weight_in_grad: float32 [4, 288, 384], P('groups'), parts along dimension 0
- bias_in_grad: float32 [4, 384], P('groups'), parts along dimension 0
- weight_out_grad: float32 [4, 384, 288], P('groups'), parts along dimension 0
There are 2 independent parts, one for each index of `groups`. A program takes and returns all parts, laid end to end along the dimension named above; an argument that names none is the same for every part. Nothing has to cross between parts.
Inputs may be any that keep to these rules, and one draw needn't show every extreme that they name: `distances`: every entry is 0 or a power of two. In each layer no more than 3 tracks share a distance; 3 tracks have distance 16384 // 2 and one track has distance 1024 // 2.
All inputs are finite; a program needn't handle non-finite values.
Results may differ from a plain program's by a relative error of at most 0.0001.
Values sent between devices are 32-bit elements; how exact they have to be, the bound alone decides.
No kernel may reach another device: no remote copies, remote signals or barrier semaphores. Data moves between devices by JAX's collectives and lax.ppermute only.
A program may use at most 64 MiB of HBM per device.

v0:
```python
import math

import jax
import jax.numpy as jnp
from jax import lax
from jax.sharding import PartitionSpec as P

TRACKS = 18
TW = 16


root_half = 0.7071067811865476
inv_root_two_pi = 0.3989422804014327


def from_behind(value, axis, steps):
    count = lax.axis_size(axis)
    pairs = [(source, (source + steps) % count) for source in range(count)]
    return lax.ppermute(value, axis, pairs)


def rotate_back(grad, shifts):
    positions = grad.shape[1]
    tracks = grad.reshape(TRACKS, TW, positions)
    devices = lax.axis_size("seq")
    doublings = devices.bit_length() - 1
    device_hops = shifts // positions
    inside = shifts % positions
    moved_all = tracks
    for doubling in range(doublings):
        arrived = from_behind(moved_all, "seq", -(1 << doubling))
        taken_now = device_hops // (1 << doubling) % 2 == 1
        moved_all = jnp.where(taken_now[:, None, None], arrived, moved_all)
    rim_width = positions // 2
    spill_over = from_behind(moved_all[:, :, :rim_width], "seq", -1)
    joined = jnp.concatenate([moved_all, spill_over], axis=2)

    def one_track(track_data, offset_now):
        return lax.dynamic_slice_in_dim(track_data, offset_now, positions, axis=1)

    rolled = jax.vmap(one_track)(joined, inside)
    return rolled.reshape(TRACKS * TW, positions)


def layer_backward(saved, grad_out, weight_a, bias_a, weight_b, shifts, factor):
    highest = lax.Precision.HIGHEST
    preact = jnp.einsum("dh,dp->hp", weight_a, saved, precision=highest) + bias_a[:, None]
    normal_cdf = 0.5 * (1.0 + lax.erf(preact * root_half))
    hidden_act = preact * normal_cdf
    slope = normal_cdf + preact * jnp.exp(-0.5 * preact * preact) * inv_root_two_pi
    grad_mid = rotate_back(grad_out, shifts)
    grad_hidden = jnp.dot(weight_b, grad_mid, precision=highest) * slope
    grad_in = grad_mid + jnp.dot(weight_a, grad_hidden, precision=highest)
    weight_a_term = jnp.einsum("dp,hp->dh", saved, grad_hidden, precision=highest) * factor
    bias_a_term = jnp.sum(grad_hidden, axis=1) * factor
    weight_b_term = jnp.einsum("hp,dp->hd", hidden_act, grad_mid, precision=highest) * factor
    summed = lax.psum((weight_a_term, bias_a_term, weight_b_term), "seq")
    return (grad_in, summed[0], summed[1], summed[2])


def body(first_inputs, second_inputs, out_grad, weight_in, bias_in, weight_out, distances):
    factor = 1.0 / math.sqrt(first_inputs.shape[1] * lax.axis_size("seq"))
    saved_list = [first_inputs, second_inputs]
    grad_now = out_grad
    results_a = [None, None]
    results_b = [None, None]
    results_c = [None, None]
    for layer_index in [1, 0]:
        grad_now, grad_a, grad_b, grad_c = layer_backward(
            saved_list[layer_index],
            grad_now,
            weight_in[layer_index],
            bias_in[layer_index],
            weight_out[layer_index],
            distances[layer_index],
            factor,
        )
        results_a[layer_index] = grad_a
        results_b[layer_index] = grad_b
        results_c[layer_index] = grad_c
    return (grad_now, jnp.stack(results_a), jnp.stack(results_b), jnp.stack(results_c))


def solution(mesh):
    in_specs = (
        P(None, ("groups", "seq")),
        P(None, ("groups", "seq")),
        P(None, ("groups", "seq")),
        P(),
        P(),
        P(),
        P(),
    )
    out_specs = (
        P(None, ("groups", "seq")),
        P("groups", None, None),
        P("groups", None),
        P("groups", None, None),
    )
    return jax.shard_map(body, mesh=mesh, in_specs=in_specs, out_specs=out_specs, check_vma=False)
```

profile of v0, /device:TPU:0, one launch (start us, length us, event | category | flops | bytes accessed | tf_op | source)
XLA Modules:
  0.0 519.9 jit_solution(17968029905615327220)
XLA Ops:
  7.2 5.5 %collective-permute-start = (f32[18,16,1024]{2,1,0:T(8,128)}, f32[18,16,1024]{2,1,0:T(8,128)S(1)}, u32[]{:S(2)}, u32[]{:S(2)}) collective-permute-start(f32[18,16,1024]{2,1,0:T(8,128)} %bitcast.102), channel_id=1, source_target_pairs={{0,15},{1,0},{2,1},{3,2},{4,3},{5,4},{6,5},{7,6},{8,7},{9,8},{10,9... | collective-permute-start | bytes 3538952 | tf_op jit(solution)/shard_map/ppermute | solution.py:19
  13.5 13.2 %collective-permute-done = f32[18,16,1024]{2,1,0:T(8,128)S(1)} collective-permute-done((f32[18,16,1024]{2,1,0:T(8,128)}, f32[18,16,1024]{2,1,0:T(8,128)S(1)}, u32[]{:S(2)}, u32[]{:S(2)}) %collective-permute-start) | collective-permute-done | bytes 1179680 | tf_op jit(solution)/shard_map/ppermute | solution.py:19
  28.9 25.6 %collective-permute-done.1 = f32[18,16,1024]{2,1,0:T(8,128)S(1)} collective-permute-done((f32[18,16,1024]{2,1,0:T(8,128)S(1)}, f32[18,16,1024]{2,1,0:T(8,128)S(1)}, u32[]{:S(2)}, u32[]{:S(2)}) %collective-permute-start.1) | collective-permute-done | bytes 1179680 | tf_op jit(solution)/shard_map/ppermute | solution.py:19
  55.5 28.0 %collective-permute-done.2 = f32[18,16,1024]{2,1,0:T(8,128)S(1)} collective-permute-done((f32[18,16,1024]{2,1,0:T(8,128)S(1)}, f32[18,16,1024]{2,1,0:T(8,128)S(1)}, u32[]{:S(2)}, u32[]{:S(2)}) %collective-permute-start.2) | collective-permute-done | bytes 1179680 | tf_op jit(solution)/shard_map/ppermute | solution.py:19
  84.8 52.8 %collective-permute-done.3 = f32[18,16,1024]{2,1,0:T(8,128)S(1)} collective-permute-done((f32[18,16,1024]{2,1,0:T(8,128)S(1)}, f32[18,16,1024]{2,1,0:T(8,128)S(1)}, u32[]{:S(2)}, u32[]{:S(2)}) %collective-permute-start.3) | collective-permute-done | bytes 1179680 | tf_op jit(solution)/shard_map/ppermute | solution.py:19
  139.9 4.3 convolution_add_fusion.1
  144.2 3.3 collective-permute-done.4
  147.5 2.5 pad_maximum_fusion
  150.1 51.5 %while.2 = (s32[]{:T(128)}, f32[18,16,1536]{2,1,0:T(8,128)}, s32[18,3]{0,1:T(4,128)S(1)}, f32[18,16,1024]{2,1,0:T(8,128)S(1)}, s32[]{:T(128)}) while((s32[]{:T(128)}, f32[18,16,1536]{2,1,0:T(8,128)}, s32[18,3]{0,1:T(4,128)S(1)}, f32[18,16,1024]{2,1,0:T(8,128)S(1)}, s32[]{:T(128)}) %tuple.50), condition=%wide.while_cond, body=%wide.while_body.sunk | while | flops 2 | bytes 131197 | solution.py:39
  150.7 2.3 dynamic-slice_dynamic-update-slice_fusion.4
  153.6 2.3 dynamic-slice_dynamic-update-slice_fusion.4
  159.3 2.3 dynamic-slice_dynamic-update-slice_fusion.4
  162.1 2.3 dynamic-slice_dynamic-update-slice_fusion.4
  165.0 2.3 dynamic-slice_dynamic-update-slice_fusion.4
  167.9 2.3 dynamic-slice_dynamic-update-slice_fusion.4
  170.7 2.3 dynamic-slice_dynamic-update-slice_fusion.4
  173.6 2.3 dynamic-slice_dynamic-update-slice_fusion.4
  176.4 2.3 dynamic-slice_dynamic-update-slice_fusion.4
  179.3 2.3 dynamic-slice_dynamic-update-slice_fusion.4
  182.2 2.3 dynamic-slice_dynamic-update-slice_fusion.4
  187.9 2.3 dynamic-slice_dynamic-update-slice_fusion.4
  190.8 2.3 dynamic-slice_dynamic-update-slice_fusion.4
  193.6 2.3 dynamic-slice_dynamic-update-slice_fusion.4
  196.5 2.3 dynamic-slice_dynamic-update-slice_fusion.4
  199.4 2.3 dynamic-slice_dynamic-update-slice_fusion.4
  201.6 5.3 %fusion.60 = (f32[384]{0:T(512)S(1)}, f32[384,1024]{0,1:T(8,128)S(1)}) fusion(f32[384,1024]{0,1:T(8,128)} %convolution_add_fusion.1, f32[288,1024]{1,0:T(8,128)S(1)} %bitcast.97, f32[2,384,288]{1,2,0:T(8,128)} %param.12), kind=kOutput, calls=%fused_computation.147 | convolution fusion | flops 1362886272 | bytes 4769280 | tf_op jit(solution)/shard_map/dot_general | solution.py:52
  209.1 4.7 collective-permute-start.5
  213.7 13.7 %collective-permute-done.5 = f32[18,16,1024]{2,1,0:T(8,128)S(1)} collective-permute-done((f32[18,16,1024]{2,1,0:T(8,128)S(1)}, f32[18,16,1024]{2,1,0:T(8,128)S(1)}, u32[]{:S(2)}, u32[]{:S(2)}) %collective-permute-start.5) | collective-permute-done | bytes 1179680 | tf_op jit(solution)/shard_map/ppermute | solution.py:19
  227.7 26.4 %collective-permute-done.6 = f32[18,16,1024]{2,1,0:T(8,128)S(1)} collective-permute-done((f32[18,16,1024]{2,1,0:T(8,128)S(1)}, f32[18,16,1024]{2,1,0:T(8,128)S(1)}, u32[]{:S(2)}, u32[]{:S(2)}) %collective-permute-start.6) | collective-permute-done | bytes 1179680 | tf_op jit(solution)/shard_map/ppermute | solution.py:19
  254.3 28.0 %collective-permute-done.7 = f32[18,16,1024]{2,1,0:T(8,128)S(1)} collective-permute-done((f32[18,16,1024]{2,1,0:T(8,128)S(1)}, f32[18,16,1024]{2,1,0:T(8,128)S(1)}, u32[]{:S(2)}, u32[]{:S(2)}) %collective-permute-start.7) | collective-permute-done | bytes 1179680 | tf_op jit(solution)/shard_map/ppermute | solution.py:19
  282.5 53.3 %collective-permute-done.8 = f32[18,16,1024]{2,1,0:T(8,128)S(1)} collective-permute-done((f32[18,16,1024]{2,1,0:T(8,128)S(1)}, f32[18,16,1024]{2,1,0:T(8,128)S(1)}, u32[]{:S(2)}, u32[]{:S(2)}) %collective-permute-start.8) | collective-permute-done | bytes 1179680 | tf_op jit(solution)/shard_map/ppermute | solution.py:19
  337.9 4.3 convolution_add_fusion
  342.2 2.9 fusion.28
  345.1 3.2 fusion.25
  349.7 51.7 %while.3 = (s32[]{:T(128)}, f32[18,16,1536]{2,1,0:T(8,128)}, s32[18,3]{0,1:T(4,128)S(1)}, f32[18,16,1024]{2,1,0:T(8,128)S(1)}, s32[]{:T(128)}) while((s32[]{:T(128)}, f32[18,16,1536]{2,1,0:T(8,128)}, s32[18,3]{0,1:T(4,128)S(1)}, f32[18,16,1024]{2,1,0:T(8,128)S(1)}, s32[]{:T(128)}) %tuple.53), condition=%wide.while_cond.1, body=%wide.while_body.1.sunk | while | flops 2 | bytes 131197 | solution.py:39
  350.6 2.3 dynamic-slice_dynamic-update-slice_fusion.5
  353.4 2.3 dynamic-slice_dynamic-update-slice_fusion.5
  359.2 2.3 dynamic-slice_dynamic-update-slice_fusion.5
  362.0 2.3 dynamic-slice_dynamic-update-slice_fusion.5
  364.9 2.3 dynamic-slice_dynamic-update-slice_fusion.5
  367.7 2.3 dynamic-slice_dynamic-update-slice_fusion.5
  370.6 2.3 dynamic-slice_dynamic-update-slice_fusion.5
  401.5 4.7 fusion.19
  406.2 3.7 fusion.61
  411.1 2.9 fusion.29
  414.1 31.7 %all-reduce.2 = (f32[1,384]{1,0:T(1,128)S(1)}, f32[1,384]{1,0:T(1,128)S(1)}) all-reduce(f32[1,384]{1,0:T(1,128)S(1)} %stack.31, f32[1,384]{1,0:T(1,128)S(1)} %stack.30), channel_id=1, replica_groups=mesh['groups'=2,'seq'=16] {'seq'}, use_global_device_ids=true, to_apply=%region_5.6 | all-reduce | flops 768 | bytes 6144 | tf_op jit(solution)/shard_map/psum | solution.py:57
  446.3 4.5 fusion.15
  450.9 59.0 %all-reduce.6.cloned.1.call-done = (f32[1,288,384]{2,1,0:T(8,128)}, f32[1,288,384]{2,1,0:T(8,128)}, f32[1,384,288]{1,2,0:T(8,128)}, f32[1,384,288]{1,2,0:T(8,128)}) async-done(((f32[1,288,384]{2,1,0:T(8,128)}, f32[1,288,384]{2,1,0:T(8,128)}, f32[1,384,288]{1,2,0:T(8,128)}, f32[1,384,288]{1,2,0:T(8,128)}), (f32[1,288,384]{2,1,0:T(8,128)}, f32[1,288,384]{2,1,0:T(8,128)}, f32[1,384,288]{1,2,0:T(8,128)}, ...) | async-done | bytes 1769488 | tf_op jit(solution)/shard_map/psum | solution.py:57
  (150 shorter events, 69.8 us)
Async XLA Ops:
  7.2 132.7 %copy-start = (f32[288,1024]{1,0:T(8,128)S(1)}, f32[288,1024]{1,0:T(8,128)}, u32[]{:S(2)}) copy-start(f32[288,1024]{1,0:T(8,128)} %param.8) | copy-start | bytes 3538948
  7.2 502.7 %all-reduce.6.cloned.1.call-start = ((), (), s32[]{:S(2)}) async-start(), calls=%async_computation | async-start | bytes 3538944 | tf_op jit(solution)/shard_map/psum | solution.py:57
  7.2 19.5 %collective-permute-start = (f32[18,16,1024]{2,1,0:T(8,128)}, f32[18,16,1024]{2,1,0:T(8,128)S(1)}, u32[]{:S(2)}, u32[]{:S(2)}) collective-permute-start(f32[18,16,1024]{2,1,0:T(8,128)} %bitcast.102), channel_id=1, source_target_pairs={{0,15},{1,0},{2,1},{3,2},{4,3},{5,4},{6,5},{7,6},{8,7},{9,8},{10,9... | collective-permute-start | bytes 3538952 | tf_op jit(solution)/shard_map/ppermute | solution.py:19
  28.3 26.2 %collective-permute-start.1 = (f32[18,16,1024]{2,1,0:T(8,128)S(1)}, f32[18,16,1024]{2,1,0:T(8,128)S(1)}, u32[]{:S(2)}, u32[]{:S(2)}) collective-permute-start(f32[18,16,1024]{2,1,0:T(8,128)S(1)} %broadcast_select_fusion), channel_id=1, source_target_pairs={{0,14},{1,15},{2,0},{3,1},{4,2},{5,3},{6,4},{7,5},{8,6},{9,7},{10,... | collective-permute-start | bytes 3538952 | tf_op jit(solution)/shard_map/ppermute | solution.py:19
  54.7 28.8 %collective-permute-start.2 = (f32[18,16,1024]{2,1,0:T(8,128)S(1)}, f32[18,16,1024]{2,1,0:T(8,128)S(1)}, u32[]{:S(2)}, u32[]{:S(2)}) collective-permute-start(f32[18,16,1024]{2,1,0:T(8,128)S(1)} %broadcast_select_fusion.1), channel_id=1, source_target_pairs={{0,12},{1,13},{2,14},{3,15},{4,0},{5,1},{6,2},{7,3},{8,4},{9,5},{1... | collective-permute-start | bytes 3538952 | tf_op jit(solution)/shard_map/ppermute | solution.py:19
  83.7 53.9 %collective-permute-start.3 = (f32[18,16,1024]{2,1,0:T(8,128)S(1)}, f32[18,16,1024]{2,1,0:T(8,128)S(1)}, u32[]{:S(2)}, u32[]{:S(2)}) collective-permute-start(f32[18,16,1024]{2,1,0:T(8,128)S(1)} %broadcast_select_fusion.2), channel_id=1, source_target_pairs={{0,8},{1,9},{2,10},{3,11},{4,12},{5,13},{6,14},{7,15},{8,0},{9,1},... | collective-permute-start | bytes 3538952 | tf_op jit(solution)/shard_map/ppermute | solution.py:19
  137.8 2.0 copy-start.10
  137.8 2.0 copy-start.11
  137.8 2.0 copy-start.5
  138.7 8.8 %collective-permute-start.4 = (f32[18,16,512]{2,1,0:T(8,128)}, f32[18,16,512]{2,1,0:T(8,128)}, u32[]{:S(2)}, u32[]{:S(2)}) collective-permute-start(f32[18,16,512]{2,1,0:T(8,128)} %slice.68), channel_id=1, source_target_pairs={{0,15},{1,0},{2,1},{3,2},{4,3},{5,4},{6,5},{7,6},{8,7},{9,8},{10,9... | collective-permute-start | bytes 1769480 | tf_op jit(solution)/shard_map/ppermute | solution.py:19
  209.1 18.4 %collective-permute-start.5 = (f32[18,16,1024]{2,1,0:T(8,128)S(1)}, f32[18,16,1024]{2,1,0:T(8,128)S(1)}, u32[]{:S(2)}, u32[]{:S(2)}) collective-permute-start(f32[18,16,1024]{2,1,0:T(8,128)S(1)} %bitcast.100), channel_id=1, source_target_pairs={{0,15},{1,0},{2,1},{3,2},{4,3},{5,4},{6,5},{7,6},{8,7},{9,8},{10,9... | collective-permute-start | bytes 3538952 | tf_op jit(solution)/shard_map/ppermute | solution.py:19
  227.6 26.4 %collective-permute-start.6 = (f32[18,16,1024]{2,1,0:T(8,128)S(1)}, f32[18,16,1024]{2,1,0:T(8,128)S(1)}, u32[]{:S(2)}, u32[]{:S(2)}) collective-permute-start(f32[18,16,1024]{2,1,0:T(8,128)S(1)} %broadcast_select_fusion.4), channel_id=1, source_target_pairs={{0,14},{1,15},{2,0},{3,1},{4,2},{5,3},{6,4},{7,5},{8,6},{9,7},{10,... | collective-permute-start | bytes 3538952 | tf_op jit(solution)/shard_map/ppermute | solution.py:19
  254.2 28.0 %collective-permute-start.7 = (f32[18,16,1024]{2,1,0:T(8,128)S(1)}, f32[18,16,1024]{2,1,0:T(8,128)S(1)}, u32[]{:S(2)}, u32[]{:S(2)}) collective-permute-start(f32[18,16,1024]{2,1,0:T(8,128)S(1)} %broadcast_select_fusion.5), channel_id=1, source_target_pairs={{0,12},{1,13},{2,14},{3,15},{4,0},{5,1},{6,2},{7,3},{8,4},{9,5},{1... | collective-permute-start | bytes 3538952 | tf_op jit(solution)/shard_map/ppermute | solution.py:19
  282.4 53.4 %collective-permute-start.8 = (f32[18,16,1024]{2,1,0:T(8,128)S(1)}, f32[18,16,1024]{2,1,0:T(8,128)S(1)}, u32[]{:S(2)}, u32[]{:S(2)}) collective-permute-start(f32[18,16,1024]{2,1,0:T(8,128)S(1)} %broadcast_select_fusion.6), channel_id=1, source_target_pairs={{0,8},{1,9},{2,10},{3,11},{4,12},{5,13},{6,14},{7,15},{8,0},{9,1},... | collective-permute-start | bytes 3538952 | tf_op jit(solution)/shard_map/ppermute | solution.py:19
  335.8 2.0 copy-start.6
  336.0 1.9 copy-start.4
  336.1 12.2 %collective-permute-start.9 = (f32[18,16,512]{2,1,0:T(8,128)S(1)}, f32[18,16,512]{2,1,0:T(8,128)S(1)}, u32[]{:S(2)}, u32[]{:S(2)}) collective-permute-start(f32[18,16,512]{2,1,0:T(8,128)S(1)} %slice.69), channel_id=1, source_target_pairs={{0,15},{1,0},{2,1},{3,2},{4,3},{5,4},{6,5},{7,6},{8,7},{9,8},{10,9... | collective-permute-start | bytes 1769480 | tf_op jit(solution)/shard_map/ppermute | solution.py:19
  342.2 2.9 copy-start.2
  401.5 4.8 copy-start.3
  401.5 4.8 copy-start.12
  410.0 1.1 copy-start.1
  414.0 32.3 %copy-start.7 = (f32[2,288,384]{2,1,0:T(8,128)S(1)}, f32[2,288,384]{2,1,0:T(8,128)}, u32[]{:S(2)}) copy-start(f32[2,288,384]{2,1,0:T(8,128)} %param.10) | copy-start | bytes 2654212
  509.9 2.2 copy-start.8
  509.9 2.2 copy-start.9
Sparse Core Ops, SparseCore 0:
  414.1 95.7 all-reduce.5
where the time goes:
time: 522 us; the launch traced here: 520 us
  waiting for transfers between devices  303 us (58%)
  local copies, waits for them, and re-layouts  105 us (20%)
  matrix products  37.9 us (7%)
  blocking collectives  31.7 us (6%)
  starting transfers between devices  15.8 us (3%)
  between operations  14.3 us (3%)
  other arithmetic  11.2 us (2%)
    ppermute x10, waiting for transfers between devices, from_behind(): return lax.ppermute(value, axis, pairs)  244 us
    gather x108, local copies, waits for them, and re-layouts  103 us
    psum x1, waiting for transfers between devices, layer_backward(): summed = lax.psum((weight_a_term, bias_a_term, weight_b_term), 'seq')  59 us
    psum x1, blocking collectives, layer_backward(): summed = lax.psum((weight_a_term, bias_a_term, weight_b_term), 'seq')  31.7 us
    ppermute x10, starting transfers between devices, from_behind(): return lax.ppermute(value, axis, pairs)  15.7 us
  transfers between devices with their start and end apart: 11, of which 10 were waited for; matrix products, arithmetic and copies ran while one was open for 4% of the time, Pallas kernels for 0%

commit v1 on v0

v1 whole, which is shorter than its diff:
```python
import math

import jax
import jax.numpy as jnp
from jax import lax
from jax.experimental import pallas as pl
from jax.experimental.pallas import tpu as pltpu
from jax.sharding import PartitionSpec as P

TRACKS = 18
TW = 16
MOST = 3
D = TRACKS * TW
HID = 384
INNER = TRACKS - MOST
LANES = 128
MIB = 1 << 20

ROOT_HALF = 0.7071067811865476
INV_ROOT_TWO_PI = 0.3989422804014327

f32, bf16, i32 = jnp.float32, jnp.bfloat16, jnp.int32
VM = pl.BlockSpec(memory_space=pltpu.VMEM)
SM = pl.BlockSpec(memory_space=pltpu.SMEM)


def params(mib):
    return pltpu.CompilerParams(vmem_limit_bytes=mib * MIB)


def near_slots(pos):
    slots, offset = [], 0
    for slot in range(INNER):
        width = max(LANES, pos >> (slot // MOST))
        slots.append((offset, width))
        offset += width
    return slots, offset


def halves(value):
    high = value.astype(bf16)
    return high, (value - high.astype(f32)).astype(bf16)


def put_triple(ref, value, rows, cols, order):
    pair = halves(value)
    for place, which in enumerate(order):
        ref[place * rows:(place + 1) * rows, cols] = pair[which]


def fill_tables(dist, tab, layer, hops, pos):
    d = [dist[layer, t] for t in range(TRACKS)]
    key = [d[t] * 32 + (31 - t) for t in range(TRACKS)]
    rank = [jnp.int32(0)] * TRACKS
    for t in range(TRACKS):
        for u in range(t + 1, TRACKS):
            above = (key[u] > key[t]).astype(i32)
            rank[t] = rank[t] + above
            rank[u] = rank[u] + (1 - above)
    for t in range(TRACKS):
        tab[layer, rank[t]] = jnp.int32(t)
    for k in range(hops):
        first = jnp.int32(0)
        for t in range(TRACKS):
            first = first + (d[t] > (pos << k)).astype(i32)
        tab[layer, TRACKS + k] = first


def track_at(tab, layer, k, slot):
    place = tab[layer, TRACKS + k] + slot
    return place, tab[layer, jnp.minimum(place, TRACKS - 1)]


def rows_of(track):
    return pl.ds(pl.multiple_of(track * TW, TW), TW)


def pack(src, tab, layer, far, near, hops, pos):
    for k in range(1, hops):
        for slot in range(MOST):
            _, t = track_at(tab, layer, k, slot)
            far[k - 1][slot * TW:(slot + 1) * TW, :] = src[rows_of(t), :]
    for slot, (offset, width) in enumerate(near_slots(pos)[0]):
        _, t = track_at(tab, layer, 0, slot)
        near[:, offset:offset + width] = src[rows_of(t), :width]


def unpack(src, dist, tab, layer, far, near, out, join, hops, pos):
    for k in range(1, hops):
        for slot in range(MOST):
            place, t = track_at(tab, layer, k, slot)

            @pl.when((place < TRACKS) & (dist[layer, t] == (pos << k)))
            def _(k=k, slot=slot, t=t):
                out[rows_of(t), :] = far[k - 1][slot * TW:(slot + 1) * TW, :]

    for slot, (offset, width) in enumerate(near_slots(pos)[0]):
        place, t = track_at(tab, layer, 0, slot)

        @pl.when(place < TRACKS)
        def _(slot=slot, t=t, offset=offset, width=width):
            shift = dist[layer, t]
            join[:, :pos] = src[rows_of(t), :]
            join[:, pos:pos + width] = near[:, offset:offset + width]
            base = pl.multiple_of(shift // LANES * LANES, LANES)
            rest = shift % LANES
            window = join[:, pl.ds(base, pos + LANES)]
            turned = pltpu.roll(window, jnp.where(rest == 0, 0, pos + LANES - rest), 1)
            out[rows_of(t), :] = turned[:, :pos]


def pack_kernel(hops, pos, dist, src, tab, near, *far):
    for layer in (1, 0):
        fill_tables(dist, tab, layer, hops, pos)
    pack(src, tab, 1, far, near, hops, pos)


def act_kernel(pos, x, w_in, bias, w_out, x2, h2, slope, wi3, wo3, xs):
    step = 256
    wt = jnp.transpose(w_in[...], (1, 0))
    wt_hi, wt_lo = halves(wt)
    wt3 = jnp.concatenate([wt_hi, wt_hi, wt_lo], axis=1)
    w_hi, w_lo = halves(w_in[...])
    wi3[...] = jnp.concatenate([w_hi, w_hi, w_lo], axis=1)
    w_hi, w_lo = halves(w_out[...])
    wo3[...] = jnp.concatenate([w_hi, w_hi, w_lo], axis=1)
    for start in range(0, pos, step):
        cols = slice(start, start + step)
        x_hi, x_lo = halves(x[:, cols])
        x2[0:D, cols] = x_hi
        x2[D:D + 16, cols] = jnp.ones((16, step), bf16)
        x2[D + 16:2 * D + 16, cols] = x_lo
        x2[2 * D + 16:2 * D + 32, cols] = jnp.zeros((16, step), bf16)
        xs[0:D, :] = x_hi
        xs[D:2 * D, :] = x_lo
        xs[2 * D:3 * D, :] = x_hi
        pre = jnp.dot(wt3, xs[...], preferred_element_type=f32) + bias[...]
        cdf = 0.5 * (1.0 + lax.erf(pre * ROOT_HALF))
        put_triple(h2, pre * cdf, HID, cols, (0, 1))
        slope[:, cols] = cdf + pre * jnp.exp(-0.5 * pre * pre) * INV_ROOT_TWO_PI


def hidden(pos, wo3, slope, gm, gm3, gh3):
    step = 512
    for start in range(0, pos, step):
        cols = slice(start, start + step)
        put_triple(gm3, gm[:, cols], D, cols, (0, 1, 0))
        gh = jnp.dot(wo3[...], gm3[:, cols], preferred_element_type=f32) * slope[:, cols]
        put_triple(gh3, gh, HID, cols, (0, 1, 0))


def inward(pos, wi3, gm, gh3, out):
    step = 512
    for start in range(0, pos, step):
        cols = slice(start, start + step)
        out[:, cols] = gm[:, cols] + jnp.dot(wi3[...], gh3[:, cols], preferred_element_type=f32)


def weight_terms(factor, x2, gh3, h2, gm3, terms):
    def nt(a, b):
        return lax.dot_general(a, b, (((1,), (1,)), ((), ())), preferred_element_type=f32)

    d1 = D + 16
    first = nt(x2[0:d1, :], gh3[0:HID, :]) + nt(x2[0:d1, :], gh3[HID:2 * HID, :]) + nt(x2[d1:2 * d1, :], gh3[0:HID, :])
    first = first[0:D + 8] * factor
    second = nt(gm3[0:D, :], h2[0:HID, :]) + nt(gm3[0:D, :], h2[HID:2 * HID, :]) + nt(gm3[D:2 * D, :], h2[0:HID, :])
    second = second * factor
    used = 0
    for part in (first, second):
        rows = part.shape[0]
        for j in range(HID // LANES):
            terms[used:used + rows, :] = part[:, j * LANES:(j + 1) * LANES]
            used += rows
    terms[used:, :] = jnp.zeros((terms.shape[0] - used, LANES), f32)


def upper_kernel(hops, pos, dist, tab, src, near_in, *refs):
    far_in, refs = refs[:hops - 1], refs[hops - 1:]
    wo3, wi3, slope, grad, near, *refs = refs
    far, refs = refs[:hops - 1], refs[hops - 1:]
    gm3, gh3, gm, join = refs
    unpack(src, dist, tab, 1, far_in, near_in, gm, join, hops, pos)
    hidden(pos, wo3, slope, gm, gm3, gh3)
    inward(pos, wi3, gm, gh3, grad)
    pack(grad, tab, 0, far, near, hops, pos)


def terms_kernel(factor, x2, gh3, h2, gm3, terms):
    weight_terms(factor, x2, gh3, h2, gm3, terms)


def lower_kernel(hops, pos, factor, dist, tab, src, near_in, *refs):
    far_in, refs = refs[:hops - 1], refs[hops - 1:]
    wo3, slope, x2, h2, gm, gh3, terms, gm3, join = refs
    unpack(src, dist, tab, 0, far_in, near_in, gm, join, hops, pos)
    hidden(pos, wo3, slope, gm, gm3, gh3)
    weight_terms(factor, x2, gh3, h2, gm3, terms)


def input_kernel(pos, wi3, gm, gh3, out):
    inward(pos, wi3, gm, gh3, out)


def finish_kernel(sum0, sum1, w_in_grad, bias_grad, w_out_grad):
    blocks = HID // LANES
    rows = D + 8
    for layer, total in enumerate((sum0, sum1)):
        for j in range(blocks):
            lanes = slice(j * LANES, (j + 1) * LANES)
            w_in_grad[layer, :, lanes] = total[j * rows:j * rows + D, :]
            bias_grad[layer:layer + 1, lanes] = total[j * rows + D:j * rows + D + 1, :]
            start = blocks * rows + j * D
            w_out_grad[layer, lanes, :] = jnp.transpose(total[start:start + D, :], (1, 0))


def from_ahead(value, steps):
    count = lax.axis_size("seq")
    return lax.ppermute(value, "seq", [(s, (s - steps) % count) for s in range(count)])


def exchange(value, mask):
    count = lax.axis_size("seq")
    return lax.ppermute(value, "seq", [(s, s ^ mask) for s in range(count)])


def total_over_seq(x):
    index = lax.axis_index("seq")
    count = lax.axis_size("seq")
    masks = [1 << b for b in range(count.bit_length() - 1)]
    for mask in masks:
        half = x.shape[0] // 2
        bit = (index // mask) % 2
        keep = lax.dynamic_slice_in_dim(x, bit * half, half, 0)
        send = lax.dynamic_slice_in_dim(x, (1 - bit) * half, half, 0)
        x = keep + exchange(send, mask)
    for mask in masks[::-1]:
        bit = (index // mask) % 2
        other = exchange(x, mask)
        x = jnp.concatenate([jnp.where(bit == 0, x, other), jnp.where(bit == 0, other, x)], 0)
    return x


def shape(*dims, dtype=f32):
    return jax.ShapeDtypeStruct(dims, dtype)


def body(first_inputs, second_inputs, out_grad, weight_in, bias_in, weight_out, distances):
    pos = first_inputs.shape[1]
    count = lax.axis_size("seq")
    hops = count.bit_length() - 1
    factor = 1.0 / math.sqrt(pos * count)
    near_width = near_slots(pos)[1]
    saved = [first_inputs, second_inputs]
    far_shapes = [shape(MOST * TW, pos)] * (hops - 1)
    near_shape = shape(TW, near_width)
    rows = 3 * (D + 8) + 3 * D
    rows = -(-rows // (8 * count)) * 8 * count
    far_hops = [1 << k for k in range(1, hops)]

    def travel(near, far):
        moved = [from_ahead(f, h) for f, h in zip(far[::-1], far_hops[::-1])][::-1]
        return from_ahead(near, 1), moved

    tab, near, *far = pl.pallas_call(
        lambda *refs: pack_kernel(hops, pos, *refs),
        out_shape=[shape(2, 32, dtype=i32), near_shape] + far_shapes,
        in_specs=[SM, VM],
        out_specs=[SM, VM] + [VM] * (hops - 1),
        compiler_params=params(16),
        name="pack",
    )(distances, out_grad)
    near, far = travel(near, far)

    acts = []
    for layer in (1, 0):
        acts.append(pl.pallas_call(
            lambda *refs: act_kernel(pos, *refs),
            out_shape=[
                shape(2 * D + 32, pos, dtype=bf16),
                shape(2 * HID, pos, dtype=bf16),
                shape(HID, pos),
                shape(D, 3 * HID, dtype=bf16),
                shape(HID, 3 * D, dtype=bf16),
            ],
            in_specs=[VM] * 4,
            out_specs=[VM] * 5,
            scratch_shapes=[pltpu.VMEM((3 * D, 256), bf16)],
            compiler_params=params(24),
            name="act",
        )(saved[layer], weight_in[layer], bias_in[layer][:, None], weight_out[layer]))
    (x2_1, h2_1, slope_1, wi3_1, wo3_1), (x2_0, h2_0, slope_0, wi3_0, wo3_0) = acts

    grad_1, near, *rest = pl.pallas_call(
        lambda *refs: upper_kernel(hops, pos, *refs),
        out_shape=[shape(D, pos), near_shape] + far_shapes + [shape(3 * D, pos, dtype=bf16), shape(3 * HID, pos, dtype=bf16)],
        in_specs=[SM, SM] + [VM] * (hops + 4),
        out_specs=[VM] * (hops + 3),
        scratch_shapes=[pltpu.VMEM((D, pos), f32), pltpu.VMEM((TW, 2 * pos + LANES), f32)],
        compiler_params=params(32),
        name="upper",
    )(distances, tab, out_grad, near, *far, wo3_1, wi3_1, slope_1)
    far, (gm3_1, gh3_1) = rest[:hops - 1], rest[hops - 1:]
    near, far = travel(near, far)

    terms_1 = pl.pallas_call(
        lambda *refs: terms_kernel(factor, *refs),
        out_shape=shape(rows, LANES),
        in_specs=[VM] * 4,
        out_specs=VM,
        compiler_params=params(24),
        name="terms",
    )(x2_1, gh3_1, h2_1, gm3_1)
    sum_1 = total_over_seq(terms_1)

    gm_0, gh3_0, terms_0 = pl.pallas_call(
        lambda *refs: lower_kernel(hops, pos, factor, *refs),
        out_shape=[shape(D, pos), shape(3 * HID, pos, dtype=bf16), shape(rows, LANES)],
        in_specs=[SM, SM] + [VM] * (hops + 5),
        out_specs=[VM] * 3,
        scratch_shapes=[pltpu.VMEM((3 * D, pos), bf16), pltpu.VMEM((TW, 2 * pos + LANES), f32)],
        compiler_params=params(32),
        name="lower",
    )(distances, tab, grad_1, near, *far, wo3_0, slope_0, x2_0, h2_0)
    sum_0 = total_over_seq(terms_0)

    input_grad = pl.pallas_call(
        lambda *refs: input_kernel(pos, *refs),
        out_shape=shape(D, pos),
        in_specs=[VM] * 3,
        out_specs=VM,
        compiler_params=params(24),
        name="inward",
    )(wi3_0, gm_0, gh3_0)

    grads = pl.pallas_call(
        finish_kernel,
        out_shape=[shape(2, D, HID), shape(2, HID), shape(2, HID, D)],
        in_specs=[VM] * 2,
        out_specs=[VM] * 3,
        compiler_params=params(24),
        name="finish",
    )(sum_0, sum_1)
    return (input_grad, *grads)


def solution(mesh):
    whole = P(None, ("groups", "seq"))
    in_specs = (whole, whole, whole, P(), P(), P(), P())
    out_specs = (whole, P("groups", None, None), P("groups", None), P("groups", None, None))
    return jax.shard_map(body, mesh=mesh, in_specs=in_specs, out_specs=out_specs, check_vma=False)
```

time: 522 us -> 139 us (0.27)
  waiting for transfers between devices: 303 us -> 49.8 us
  local copies, waits for them, and re-layouts: 105 us -> 25.9 us
  matrix products: 37.9 us -> 0 us
  blocking collectives: 31.7 us -> 0 us
  Pallas kernels: 0 us -> 21.3 us
  between operations: 14.3 us -> 1.07 us
  starting transfers between devices: 15.8 us -> 28.8 us
    ppermute x10 -> x24, waiting for transfers between devices: 244 us -> 49.8 us  [the longest x16 27.6 us: exchange(): return lax.ppermute(value, 'seq', [(s, s ^ mask) for s in range(count)])]
    gather x108 -> x0, local copies, waits for them, and re-layouts: 103 us -> none
    psum x1 -> x0, waiting for transfers between devices: 59 us -> none  [layer_backward(): summed = lax.psum((weight_a_term, bias_a_term, weight_b_term), 'seq')]
    dot_general x10 -> x0, matrix products: 37.9 us -> none  [the longest x2 9 us: layer_backward(): grad_hidden = jnp.dot(weight_b, grad_mid, precision=highest) * slope]
    psum x1 -> x0, blocking collectives: 31.7 us -> none  [layer_backward(): summed = lax.psum((weight_a_term, bias_a_term, weight_b_term), 'seq')]
    pallas_call x0 -> x8, Pallas kernels: none -> 21.3 us  [the longest x1 5.01 us: body(): pl.pallas_call(lambda *refs: lower_kernel(hops, pos, factor, *refs), out_...]
    unnamed x29 -> x73, local copies, waits for them, and re-layouts: 1.46 us -> 18.2 us
    ppermute x10 -> x24, starting transfers between devices: 15.7 us -> 28.8 us  [the longest x16 16.2 us: exchange(): return lax.ppermute(value, 'seq', [(s, s ^ mask) for s in range(count)])]
  transfers between devices with their start and end apart: 11 -> 24, of which waited for: 10 -> 16; matrix products, arithmetic and copies ran while one was open for 4% -> 13% of each run, Pallas kernels for 0% -> 8%
where the time goes in v1:
time: 139 us; the launch traced here: 138 us
  waiting for transfers between devices  49.8 us (36%)
  starting transfers between devices  28.8 us (21%)
  local copies, waits for them, and re-layouts  25.9 us (19%)
  Pallas kernels  21.3 us (15%)
  other arithmetic  11.2 us (8%)
    ppermute x16, waiting for transfers between devices, exchange(): return lax.ppermute(value, 'seq', [(s, s ^ mask) for s in range(count)])  27.6 us
    ppermute x8, waiting for transfers between devices, from_ahead(): lax.ppermute(value, 'seq', [(s, (s - steps) % count) for s in range(count)])  22.2 us
    unnamed x73, local copies, waits for them, and re-layouts  18.2 us
    ppermute x16, starting transfers between devices, exchange(): return lax.ppermute(value, 'seq', [(s, s ^ mask) for s in range(count)])  16.2 us
    ppermute x8, starting transfers between devices, from_ahead(): lax.ppermute(value, 'seq', [(s, (s - steps) % count) for s in range(count)])  12.5 us
    add x8, other arithmetic, total_over_seq(): x = keep + exchange(send, mask)  7.03 us
    dynamic_slice x8, local copies, waits for them, and re-layouts, total_over_seq(): send = lax.dynamic_slice_in_dim(x, (1 - bit) * half, half, 0)  5.27 us
    pallas_call x1, Pallas kernels, body(): pl.pallas_call(lambda *refs: lower_kernel(hops, pos, factor, *refs), out_...  5.01 us
  transfers between devices with their start and end apart: 24, of which 16 were waited for; matrix products, arithmetic and copies ran while one was open for 13% of the time, Pallas kernels for 8%

profile of v1, /device:TPU:0, one launch (start us, length us, event | category | flops | bytes accessed | tf_op | source)
XLA Modules:
  0.0 138.0 jit_solution(7454380570137660956)
XLA Ops:
  0.6 1.3 copy-done
  2.6 2.4 %pack.1 = (s32[2,32]{1,0:T(2,128)S(1)}, f32[16,6144]{1,0:T(8,128)}, f32[48,1024]{1,0:T(8,128)}, f32[48,1024]{1,0:T(8,128)}, f32[48,1024]{1,0:T(8,128)}) custom-call(s32[2,18]{1,0:T(2,128)S(1)} %copy-done.17, f32[288,1024]{1,0:T(8,128)S(1)} %copy-done), custom_call_target="tpu_custom_call" | custom-call | tf_op jit(solution)/shard_map/pack/pallas_call | solution.py:264
  5.0 5.5 %collective-permute-start = (f32[16,6144]{1,0:T(8,128)}, f32[16,6144]{1,0:T(8,128)S(1)}, u32[]{:S(2)}, u32[]{:S(2)}) collective-permute-start(f32[16,6144]{1,0:T(8,128)} %get-tuple-element.34), channel_id=1, source_target_pairs={{0,15},{1,0},{2,1},{3,2},{4,3},{5,4},{6,5},{7,6},{8,7},{9,8},{10,9... | collective-permute-start | bytes 1179656 | tf_op jit(solution)/shard_map/ppermute | solution.py:218
  12.8 1.3 slice_bitcast_fusion
  14.2 1.9 %act.3 = (bf16[608,1024]{1,0:T(8,128)(2,1)S(1)}, bf16[768,1024]{1,0:T(8,128)(2,1)S(1)}, f32[384,1024]{1,0:T(8,128)S(1)}, bf16[288,1152]{1,0:T(8,128)(2,1)S(1)}, bf16[384,864]{1,0:T(8,128)(2,1)S(1)}) custom-call(f32[288,1024]{1,0:T(8,128)S(1)} %copy-done.2, f32[288,384]{1,0:T(8,128)S(1)} %get-tuple-element.74.refs_1_, f32[384,1]{1,0:T(8,128)S(1)} %copy.17.refs_2_, ...), custom_call_target="tpu_custom_call" | custom-call | tf_op jit(solution)/shard_map/act/pallas_call | solution.py:276
  16.1 8.4 %collective-permute-done.1.refs_4_ = f32[48,1024]{1,0:T(8,128)S(1)} collective-permute-done((f32[48,1024]{1,0:T(8,128)}, f32[48,1024]{1,0:T(8,128)S(1)}, u32[]{:S(2)}, u32[]{:S(2)}) %collective-permute-start.1) | collective-permute-done | bytes 196640 | tf_op jit(solution)/shard_map/ppermute | solution.py:218
  24.5 2.2 %collective-permute-done.2.refs_5_ = f32[48,1024]{1,0:T(8,128)S(1)} collective-permute-done((f32[48,1024]{1,0:T(8,128)}, f32[48,1024]{1,0:T(8,128)S(1)}, u32[]{:S(2)}, u32[]{:S(2)}) %collective-permute-start.2) | collective-permute-done | bytes 196640 | tf_op jit(solution)/shard_map/ppermute | solution.py:218
  26.7 6.1 %collective-permute-done.3.refs_6_ = f32[48,1024]{1,0:T(8,128)S(1)} collective-permute-done((f32[48,1024]{1,0:T(8,128)}, f32[48,1024]{1,0:T(8,128)S(1)}, u32[]{:S(2)}, u32[]{:S(2)}) %collective-permute-start.3) | collective-permute-done | bytes 196640 | tf_op jit(solution)/shard_map/ppermute | solution.py:218
  32.8 4.9 %upper.1 = (f32[288,1024]{1,0:T(8,128)S(1)}, f32[16,6144]{1,0:T(8,128)}, f32[48,1024]{1,0:T(8,128)}, f32[48,1024]{1,0:T(8,128)S(1)}, f32[48,1024]{1,0:T(8,128)S(...) custom-call(s32[2,18]{1,0:T(2,128)S(1)} %copy-done.18, s32[2,32]{1,0:T(2,128)S(1)} %get-tuple-element.33.refs_1_, ...), custom_call_target="tpu_custom_call" | custom-call | tf_op jit(solution)/shard_map/upper/pallas_call | solution.py:293
  37.7 2.0 %terms.1 = f32[1792,128]{1,0:T(8,128)S(1)} custom-call(bf16[608,1024]{1,0:T(8,128)(2,1)S(1)} %get-tuple-element.53.refs_0_, bf16[1152,1024]{1,0:T(8,128)(2,1)S(1)} %get-tuple-element.54.refs_1_, bf16[768,1024]{1,0:T(8,128)(2,1)S(1)} %get-tuple-element.55.refs_2_, bf16[864,1024]{1,0:T(8,128)(2,1)S(1)} %get-tuple-element.56.refs_3_), custom_call_target="tpu_custom_call" | custom-call | tf_op jit(solution)/shard_map/terms/pallas_call | solution.py:305
  40.6 6.0 %collective-permute-start.5 = (f32[48,1024]{1,0:T(8,128)}, f32[48,1024]{1,0:T(8,128)S(1)}, u32[]{:S(2)}, u32[]{:S(2)}) collective-permute-start(f32[48,1024]{1,0:T(8,128)} %get-tuple-element.43), channel_id=1, source_target_pairs={{0,14},{1,15},{2,0},{3,1},{4,2},{5,3},{6,4},{7,5},{8,6},{9,7},{10,... | collective-permute-start | bytes 589832 | tf_op jit(solution)/shard_map/ppermute | solution.py:218
  46.6 1.2 dynamic-slice_add_fusion
  49.8 1.2 copy.19
  51.2 1.9 %act.2 = (bf16[608,1024]{1,0:T(8,128)(2,1)S(1)}, bf16[768,1024]{1,0:T(8,128)(2,1)S(1)}, f32[384,1024]{1,0:T(8,128)S(1)}, bf16[288,1152]{1,0:T(8,128)(2,1)S(1)}, bf16[384,864]{1,0:T(8,128)(2,1)S(1)}) custom-call(f32[288,1024]{1,0:T(8,128)S(1)} %copy-done.3, f32[288,384]{1,0:T(8,128)S(1)} %get-tuple-element.75.refs_1_, f32[384,1]{1,0:T(8,128)S(1)} %copy.15.refs_2_, ...), custom_call_target="tpu_custom_call" | custom-call | tf_op jit(solution)/shard_map/act/pallas_call | solution.py:276
  55.2 3.9 %collective-permute-done.6.refs_5_ = f32[48,1024]{1,0:T(8,128)S(1)} collective-permute-done((f32[48,1024]{1,0:T(8,128)}, f32[48,1024]{1,0:T(8,128)S(1)}, u32[]{:S(2)}, u32[]{:S(2)}) %collective-permute-start.6) | collective-permute-done | bytes 196640 | tf_op jit(solution)/shard_map/ppermute | solution.py:218
  59.7 1.0 collective-permute-done.7.refs_6_
  62.2 1.3 copy-done.5
  63.5 1.0 copy-done.10
  64.4 0.9 copy-done.12
  65.4 0.9 copy-done.14
  66.3 0.9 copy-done.16
  67.2 5.0 %lower.1 = (f32[288,1024]{1,0:T(8,128)S(1)}, bf16[1152,1024]{1,0:T(8,128)(2,1)S(1)}, f32[1792,128]{1,0:T(8,128)S(1)}) custom-call(s32[2,18]{1,0:T(2,128)S(1)} %copy-done.18, s32[2,32]{1,0:T(2,128)S(1)} %get-tuple-element.33.refs_1_, f32[288,1024]{1,0:T(8,128)S(1)} %copy-done.5, f32[16,6144]{1,0:T(8,128)S(1)} %copy-done.10, f32[48,1024]{1,0:T(8,128)S(1)} %copy-done.12, ...), custom_call_target="tpu_custom_call" | custom-call | tf_op jit(solution)/shard_map/lower/pallas_call | solution.py:315
  74.0 1.0 dynamic-slice_add_fusion.2
  76.3 3.6 %collective-permute-start.18 = (f32[224,128]{1,0:T(8,128)}, f32[224,128]{1,0:T(8,128)}, u32[]{:S(2)}, u32[]{:S(2)}) collective-permute-start(f32[224,128]{1,0:T(8,128)} %constant_dynamic-slice_fusion.1), channel_id=1, source_target_pairs={{0,4},{1,5},{2,6},{3,7},{4,0},{5,1},{6,2},{7,3},{8,12},{9,13},{10,... | collective-permute-start | bytes 344072 | tf_op jit(solution)/shard_map/ppermute | solution.py:223
  79.9 4.1 %collective-permute-done.18 = f32[224,128]{1,0:T(8,128)} collective-permute-done((f32[224,128]{1,0:T(8,128)}, f32[224,128]{1,0:T(8,128)}, u32[]{:S(2)}, u32[]{:S(2)}) %collective-permute-start.18) | collective-permute-done | bytes 114720 | tf_op jit(solution)/shard_map/ppermute | solution.py:223
  84.0 1.0 dynamic-slice_add_fusion.4
  86.2 3.3 %collective-permute-start.19 = (f32[112,128]{1,0:T(8,128)}, f32[112,128]{1,0:T(8,128)}, u32[]{:S(2)}, u32[]{:S(2)}) collective-permute-start(f32[112,128]{1,0:T(8,128)} %constant_dynamic-slice_fusion), channel_id=1, source_target_pairs={{0,8},{1,9},{2,10},{3,11},{4,12},{5,13},{6,14},{7,15},{8,0},{9,1},... | collective-permute-start | bytes 172040 | tf_op jit(solution)/shard_map/ppermute | solution.py:223
  89.5 2.0 %dynamic-slice_add_fusion.1 = f32[896,128]{1,0:T(8,128)} fusion(f32[896,128]{1,0:T(8,128)} %collective-permute-done.8, f32[1792,128]{1,0:T(8,128)} %copy-done.6, s32[]{:T(128)S(6)} %select_n.189), kind=kLoop, calls=%fused_computation.5 | loop fusion | flops 114688 | bytes 1376260 | tf_op jit(solution)/shard_map/add | solution.py:235
  91.5 1.6 %constant_dynamic-slice_fusion.6 = f32[448,128]{1,0:T(8,128)} fusion(f32[896,128]{1,0:T(8,128)} %dynamic-slice_add_fusion.1, s32[]{:T(128)S(6)} %select_n.192), kind=kLoop, calls=%fused_computation.40 | loop fusion | bytes 458756 | tf_op jit(solution)/shard_map/dynamic_slice | solution.py:234
  94.1 1.7 %collective-permute-start.20 = (f32[112,128]{1,0:T(8,128)S(1)}, f32[112,128]{1,0:T(8,128)S(1)}, u32[]{:S(2)}, u32[]{:S(2)}) collective-permute-start(f32[112,128]{1,0:T(8,128)S(1)} %dynamic-slice_add_fusion.6), channel_id=1, source_target_pairs={{0,8},{1,9},{2,10},{3,11},{4,12},{5,13},{6,14},{7,15},{8,0},{9,1},... | collective-permute-start | bytes 172040 | tf_op jit(solution)/shard_map/ppermute | solution.py:223
  95.8 4.8 %collective-permute-done.9 = f32[448,128]{1,0:T(8,128)} collective-permute-done((f32[448,128]{1,0:T(8,128)}, f32[448,128]{1,0:T(8,128)}, u32[]{:S(2)}, u32[]{:S(2)}) %collective-permute-start.9) | collective-permute-done | bytes 229408 | tf_op jit(solution)/shard_map/ppermute | solution.py:223
  100.6 1.1 dynamic-slice_add_fusion.3
  101.7 1.6 %collective-permute-start.10 = (f32[224,128]{1,0:T(8,128)S(1)}, f32[224,128]{1,0:T(8,128)S(1)}, u32[]{:S(2)}, u32[]{:S(2)}) collective-permute-start(f32[224,128]{1,0:T(8,128)S(1)} %constant_dynamic-slice_fusion.5), channel_id=1, source_target_pairs={{0,4},{1,5},{2,6},{3,7},{4,0},{5,1},{6,2},{7,3},{8,12},{9,13},{10,... | collective-permute-start | bytes 344072 | tf_op jit(solution)/shard_map/ppermute | solution.py:223
  103.3 3.2 %collective-permute-done.10 = f32[224,128]{1,0:T(8,128)S(1)} collective-permute-done((f32[224,128]{1,0:T(8,128)S(1)}, f32[224,128]{1,0:T(8,128)S(1)}, u32[]{:S(2)}, u32[]{:S(2)}) %collective-permute-start.10) | collective-permute-done | bytes 114720 | tf_op jit(solution)/shard_map/ppermute | solution.py:223
  107.0 2.0 %collective-permute-start.21 = (f32[224,128]{1,0:T(8,128)S(1)}, f32[224,128]{1,0:T(8,128)S(1)}, u32[]{:S(2)}, u32[]{:S(2)}) collective-permute-start(f32[224,128]{1,0:T(8,128)S(1)} %pad_maximum_fusion.7), channel_id=1, source_target_pairs={{0,4},{1,5},{2,6},{3,7},{4,0},{5,1},{6,2},{7,3},{8,12},{9,13},{10,... | collective-permute-start | bytes 344072 | tf_op jit(solution)/shard_map/ppermute | solution.py:223
  109.0 2.9 %collective-permute-done.11 = f32[112,128]{1,0:T(8,128)S(1)} collective-permute-done((f32[112,128]{1,0:T(8,128)S(1)}, f32[112,128]{1,0:T(8,128)S(1)}, u32[]{:S(2)}, u32[]{:S(2)}) %collective-permute-start.11) | collective-permute-done | bytes 57376 | tf_op jit(solution)/shard_map/ppermute | solution.py:223
  112.1 0.9 collective-permute-done.21
  113.1 3.9 %collective-permute-done.12 = f32[112,128]{1,0:T(8,128)S(1)} collective-permute-done((f32[112,128]{1,0:T(8,128)S(1)}, f32[112,128]{1,0:T(8,128)S(1)}, u32[]{:S(2)}, u32[]{:S(2)}) %collective-permute-start.12) | collective-permute-done | bytes 57376 | tf_op jit(solution)/shard_map/ppermute | solution.py:223
  117.0 2.5 %collective-permute-start.13 = (f32[224,128]{1,0:T(8,128)S(1)}, f32[224,128]{1,0:T(8,128)S(1)}, u32[]{:S(2)}, u32[]{:S(2)}) collective-permute-start(f32[224,128]{1,0:T(8,128)S(1)} %pad_maximum_fusion.6), channel_id=1, source_target_pairs={{0,4},{1,5},{2,6},{3,7},{4,0},{5,1},{6,2},{7,3},{8,12},{9,13},{10,... | collective-permute-start | bytes 344072 | tf_op jit(solution)/shard_map/ppermute | solution.py:223
  119.7 2.6 %collective-permute-done.13 = f32[224,128]{1,0:T(8,128)S(1)} collective-permute-done((f32[224,128]{1,0:T(8,128)S(1)}, f32[224,128]{1,0:T(8,128)S(1)}, u32[]{:S(2)}, u32[]{:S(2)}) %collective-permute-start.13) | collective-permute-done | bytes 114720 | tf_op jit(solution)/shard_map/ppermute | solution.py:223
  122.5 3.2 %collective-permute-done.22 = f32[448,128]{1,0:T(8,128)S(1)} collective-permute-done((f32[448,128]{1,0:T(8,128)S(1)}, f32[448,128]{1,0:T(8,128)S(1)}, u32[]{:S(2)}, u32[]{:S(2)}) %collective-permute-start.22) | collective-permute-done | bytes 229408 | tf_op jit(solution)/shard_map/ppermute | solution.py:223
  126.6 1.9 %collective-permute-done.14 = f32[448,128]{1,0:T(8,128)S(1)} collective-permute-done((f32[448,128]{1,0:T(8,128)S(1)}, f32[448,128]{1,0:T(8,128)S(1)}, u32[]{:S(2)}, u32[]{:S(2)}) %collective-permute-start.14) | collective-permute-done | bytes 229408 | tf_op jit(solution)/shard_map/ppermute | solution.py:223
  130.1 1.1 copy-done.8
  131.2 1.9 %inward.1 = f32[288,1024]{1,0:T(8,128)} custom-call(bf16[288,1152]{1,0:T(8,128)(2,1)S(1)} %copy-done.8, f32[288,1024]{1,0:T(8,128)S(1)} %get-tuple-element.50.refs_1_, bf16[1152,1024]{1,0:T(8,128)(2,1)S(1)} %get-tuple-element.51.refs_2_), custom_call_target="tpu_custom_call" | custom-call | tf_op jit(solution)/shard_map/inward/pallas_call | solution.py:326
  133.1 1.1 broadcast_select_fusion.1
  134.3 1.1 broadcast_select_fusion.3
  135.5 1.3 finish.1
  136.8 1.3 copy.18
  (117 shorter events, 19.2 us)
Async XLA Ops:
  0.6 1.3 copy-start
  2.6 9.0 %copy-start.32 = (f32[2,384,288]{1,2,0:T(8,128)S(1)}, f32[2,384,288]{1,2,0:T(8,128)}, u32[]{:S(2)}) copy-start(f32[2,384,288]{1,2,0:T(8,128)} %param.12) | copy-start | bytes 2654212
  5.0 27.8 %collective-permute-start = (f32[16,6144]{1,0:T(8,128)}, f32[16,6144]{1,0:T(8,128)S(1)}, u32[]{:S(2)}, u32[]{:S(2)}) collective-permute-start(f32[16,6144]{1,0:T(8,128)} %get-tuple-element.34), channel_id=1, source_target_pairs={{0,15},{1,0},{2,1},{3,2},{4,3},{5,4},{6,5},{7,6},{8,7},{9,8},{10,9... | collective-permute-start | bytes 1179656 | tf_op jit(solution)/shard_map/ppermute | solution.py:218
  10.5 14.0 %collective-permute-start.1 = (f32[48,1024]{1,0:T(8,128)}, f32[48,1024]{1,0:T(8,128)S(1)}, u32[]{:S(2)}, u32[]{:S(2)}) collective-permute-start(f32[48,1024]{1,0:T(8,128)} %get-tuple-element.35), channel_id=1, source_target_pairs={{0,14},{1,15},{2,0},{3,1},{4,2},{5,3},{6,4},{7,5},{8,6},{9,7},{10,... | collective-permute-start | bytes 589832 | tf_op jit(solution)/shard_map/ppermute | solution.py:218
  11.1 15.6 %collective-permute-start.2 = (f32[48,1024]{1,0:T(8,128)}, f32[48,1024]{1,0:T(8,128)S(1)}, u32[]{:S(2)}, u32[]{:S(2)}) collective-permute-start(f32[48,1024]{1,0:T(8,128)} %get-tuple-element.36), channel_id=1, source_target_pairs={{0,12},{1,13},{2,14},{3,15},{4,0},{5,1},{6,2},{7,3},{8,4},{9,5},{1... | collective-permute-start | bytes 589832 | tf_op jit(solution)/shard_map/ppermute | solution.py:218
  11.6 21.2 %collective-permute-start.3 = (f32[48,1024]{1,0:T(8,128)}, f32[48,1024]{1,0:T(8,128)S(1)}, u32[]{:S(2)}, u32[]{:S(2)}) collective-permute-start(f32[48,1024]{1,0:T(8,128)} %get-tuple-element.37), channel_id=1, source_target_pairs={{0,8},{1,9},{2,10},{3,11},{4,12},{5,13},{6,14},{7,15},{8,0},{9,1},... | collective-permute-start | bytes 589832 | tf_op jit(solution)/shard_map/ppermute | solution.py:218
  11.6 1.1 copy-start.34
  12.7 1.5 %copy-start.2 = (f32[288,1024]{1,0:T(8,128)S(1)}, f32[288,1024]{1,0:T(8,128)}, u32[]{:S(2)}) copy-start(f32[288,1024]{1,0:T(8,128)} %refs_0_.7) | copy-start | bytes 3538948
  14.1 18.6 %copy-start.1 = (f32[288,1024]{1,0:T(8,128)S(1)}, f32[288,1024]{1,0:T(8,128)}, u32[]{:S(2)}) copy-start(f32[288,1024]{1,0:T(8,128)} %refs_2_.1) | copy-start | bytes 3538948
  14.2 18.6 %copy-start.18 = (s32[2,18]{1,0:T(2,128)S(1)}, s32[2,18]{1,0:T(2,128)}, u32[]{:S(2)}) copy-start(s32[2,18]{1,0:T(2,128)} %refs_0_.9) | copy-start | bytes 436
  37.7 2.1 %copy-start.4 = (f32[288,1024]{1,0:T(8,128)}, f32[288,1024]{1,0:T(8,128)S(1)}, u32[]{:S(2)}) copy-start(f32[288,1024]{1,0:T(8,128)S(1)} %get-tuple-element.41.refs_2_) | copy-start | bytes 3538948
  37.7 2.1 %copy-start.19 = (f32[48,1024]{1,0:T(8,128)}, f32[48,1024]{1,0:T(8,128)S(1)}, u32[]{:S(2)}) copy-start(f32[48,1024]{1,0:T(8,128)S(1)} %get-tuple-element.45) | copy-start | bytes 589828
  37.7 2.1 %copy-start.20 = (f32[48,1024]{1,0:T(8,128)}, f32[48,1024]{1,0:T(8,128)S(1)}, u32[]{:S(2)}) copy-start(f32[48,1024]{1,0:T(8,128)S(1)} %get-tuple-element.44) | copy-start | bytes 589828
  40.6 6.0 %collective-permute-start.16 = (f32[896,128]{1,0:T(8,128)}, f32[896,128]{1,0:T(8,128)}, u32[]{:S(2)}, u32[]{:S(2)}) collective-permute-start(f32[896,128]{1,0:T(8,128)} %constant_dynamic-slice_fusion.3), channel_id=1, source_target_pairs={{0,1},{1,0},{2,3},{3,2},{4,5},{5,4},{6,7},{7,6},{8,9},{9,8},{10,11... | collective-permute-start | bytes 1376264 | tf_op jit(solution)/shard_map/ppermute | solution.py:223
  40.6 20.9 %collective-permute-start.4 = (f32[16,6144]{1,0:T(8,128)}, f32[16,6144]{1,0:T(8,128)S(1)}, u32[]{:S(2)}, u32[]{:S(2)}) collective-permute-start(f32[16,6144]{1,0:T(8,128)} %get-tuple-element.42), channel_id=1, source_target_pairs={{0,15},{1,0},{2,1},{3,2},{4,3},{5,4},{6,5},{7,6},{8,7},{9,8},{10,9... | collective-permute-start | bytes 1179656 | tf_op jit(solution)/shard_map/ppermute | solution.py:218
  40.6 13.9 %collective-permute-start.5 = (f32[48,1024]{1,0:T(8,128)}, f32[48,1024]{1,0:T(8,128)S(1)}, u32[]{:S(2)}, u32[]{:S(2)}) collective-permute-start(f32[48,1024]{1,0:T(8,128)} %get-tuple-element.43), channel_id=1, source_target_pairs={{0,14},{1,15},{2,0},{3,1},{4,2},{5,3},{6,4},{7,5},{8,6},{9,7},{10,... | collective-permute-start | bytes 589832 | tf_op jit(solution)/shard_map/ppermute | solution.py:218
  46.5 12.5 %collective-permute-start.6 = (f32[48,1024]{1,0:T(8,128)}, f32[48,1024]{1,0:T(8,128)S(1)}, u32[]{:S(2)}, u32[]{:S(2)}) collective-permute-start(f32[48,1024]{1,0:T(8,128)} %copy-done.20), channel_id=1, source_target_pairs={{0,12},{1,13},{2,14},{3,15},{4,0},{5,1},{6,2},{7,3},{8,4},{9,5},{1... | collective-permute-start | bytes 589832 | tf_op jit(solution)/shard_map/ppermute | solution.py:218
  46.5 4.7 %copy-start.3 = (f32[288,1024]{1,0:T(8,128)S(1)}, f32[288,1024]{1,0:T(8,128)}, u32[]{:S(2)}) copy-start(f32[288,1024]{1,0:T(8,128)} %refs_0_.5) | copy-start | bytes 3538948
  46.5 14.2 %collective-permute-start.7 = (f32[48,1024]{1,0:T(8,128)}, f32[48,1024]{1,0:T(8,128)S(1)}, u32[]{:S(2)}, u32[]{:S(2)}) collective-permute-start(f32[48,1024]{1,0:T(8,128)} %copy-done.19), channel_id=1, source_target_pairs={{0,8},{1,9},{2,10},{3,11},{4,12},{5,13},{6,14},{7,15},{8,0},{9,1},... | collective-permute-start | bytes 589832 | tf_op jit(solution)/shard_map/ppermute | solution.py:218
  49.2 24.7 %collective-permute-start.17 = (f32[448,128]{1,0:T(8,128)}, f32[448,128]{1,0:T(8,128)}, u32[]{:S(2)}, u32[]{:S(2)}) collective-permute-start(f32[448,128]{1,0:T(8,128)} %constant_dynamic-slice_fusion.2), channel_id=1, source_target_pairs={{0,2},{1,3},{2,0},{3,1},{4,6},{5,7},{6,4},{7,5},{8,10},{9,11},{10,... | collective-permute-start | bytes 688136 | tf_op jit(solution)/shard_map/ppermute | solution.py:223
  62.2 1.3 copy-start.5
  63.4 1.0 copy-start.10
  64.4 0.9 copy-start.12
  65.4 0.9 copy-start.14
  66.3 0.9 copy-start.16
  67.2 6.8 %copy-start.30 = (f32[896,128]{1,0:T(8,128)S(1)}, f32[896,128]{1,0:T(8,128)}, u32[]{:S(2)}) copy-start(f32[896,128]{1,0:T(8,128)} %copy-done.29) | copy-start | bytes 1376260
  74.0 15.5 %collective-permute-start.8 = (f32[896,128]{1,0:T(8,128)}, f32[896,128]{1,0:T(8,128)}, u32[]{:S(2)}, u32[]{:S(2)}) collective-permute-start(f32[896,128]{1,0:T(8,128)} %constant_dynamic-slice_fusion.7), channel_id=1, source_target_pairs={{0,1},{1,0},{2,3},{3,2},{4,5},{5,4},{6,7},{7,6},{8,9},{9,8},{10,11... | collective-permute-start | bytes 1376264 | tf_op jit(solution)/shard_map/ppermute | solution.py:223
  76.3 7.7 %collective-permute-start.18 = (f32[224,128]{1,0:T(8,128)}, f32[224,128]{1,0:T(8,128)}, u32[]{:S(2)}, u32[]{:S(2)}) collective-permute-start(f32[224,128]{1,0:T(8,128)} %constant_dynamic-slice_fusion.1), channel_id=1, source_target_pairs={{0,4},{1,5},{2,6},{3,7},{4,0},{5,1},{6,2},{7,3},{8,12},{9,13},{10,... | collective-permute-start | bytes 344072 | tf_op jit(solution)/shard_map/ppermute | solution.py:223
  86.2 7.0 %collective-permute-start.19 = (f32[112,128]{1,0:T(8,128)}, f32[112,128]{1,0:T(8,128)}, u32[]{:S(2)}, u32[]{:S(2)}) collective-permute-start(f32[112,128]{1,0:T(8,128)} %constant_dynamic-slice_fusion), channel_id=1, source_target_pairs={{0,8},{1,9},{2,10},{3,11},{4,12},{5,13},{6,14},{7,15},{8,0},{9,1},... | collective-permute-start | bytes 172040 | tf_op jit(solution)/shard_map/ppermute | solution.py:223
  93.1 7.5 %collective-permute-start.9 = (f32[448,128]{1,0:T(8,128)}, f32[448,128]{1,0:T(8,128)}, u32[]{:S(2)}, u32[]{:S(2)}) collective-permute-start(f32[448,128]{1,0:T(8,128)} %constant_dynamic-slice_fusion.6), channel_id=1, source_target_pairs={{0,2},{1,3},{2,0},{3,1},{4,6},{5,7},{6,4},{7,5},{8,10},{9,11},{10,... | collective-permute-start | bytes 688136 | tf_op jit(solution)/shard_map/ppermute | solution.py:223
  94.1 9.2 %collective-permute-start.20 = (f32[112,128]{1,0:T(8,128)S(1)}, f32[112,128]{1,0:T(8,128)S(1)}, u32[]{:S(2)}, u32[]{:S(2)}) collective-permute-start(f32[112,128]{1,0:T(8,128)S(1)} %dynamic-slice_add_fusion.6), channel_id=1, source_target_pairs={{0,8},{1,9},{2,10},{3,11},{4,12},{5,13},{6,14},{7,15},{8,0},{9,1},... | collective-permute-start | bytes 172040 | tf_op jit(solution)/shard_map/ppermute | solution.py:223
  101.7 4.9 %collective-permute-start.10 = (f32[224,128]{1,0:T(8,128)S(1)}, f32[224,128]{1,0:T(8,128)S(1)}, u32[]{:S(2)}, u32[]{:S(2)}) collective-permute-start(f32[224,128]{1,0:T(8,128)S(1)} %constant_dynamic-slice_fusion.5), channel_id=1, source_target_pairs={{0,4},{1,5},{2,6},{3,7},{4,0},{5,1},{6,2},{7,3},{8,12},{9,13},{10,... | collective-permute-start | bytes 344072 | tf_op jit(solution)/shard_map/ppermute | solution.py:223
  106.6 5.3 %collective-permute-start.11 = (f32[112,128]{1,0:T(8,128)S(1)}, f32[112,128]{1,0:T(8,128)S(1)}, u32[]{:S(2)}, u32[]{:S(2)}) collective-permute-start(f32[112,128]{1,0:T(8,128)S(1)} %constant_dynamic-slice_fusion.4), channel_id=1, source_target_pairs={{0,8},{1,9},{2,10},{3,11},{4,12},{5,13},{6,14},{7,15},{8,0},{9,1},... | collective-permute-start | bytes 172040 | tf_op jit(solution)/shard_map/ppermute | solution.py:223
  107.0 6.1 %collective-permute-start.21 = (f32[224,128]{1,0:T(8,128)S(1)}, f32[224,128]{1,0:T(8,128)S(1)}, u32[]{:S(2)}, u32[]{:S(2)}) collective-permute-start(f32[224,128]{1,0:T(8,128)S(1)} %pad_maximum_fusion.7), channel_id=1, source_target_pairs={{0,4},{1,5},{2,6},{3,7},{4,0},{5,1},{6,2},{7,3},{8,12},{9,13},{10,... | collective-permute-start | bytes 344072 | tf_op jit(solution)/shard_map/ppermute | solution.py:223
  111.9 5.1 %collective-permute-start.12 = (f32[112,128]{1,0:T(8,128)S(1)}, f32[112,128]{1,0:T(8,128)S(1)}, u32[]{:S(2)}, u32[]{:S(2)}) collective-permute-start(f32[112,128]{1,0:T(8,128)S(1)} %dynamic-slice_add_fusion.7), channel_id=1, source_target_pairs={{0,8},{1,9},{2,10},{3,11},{4,12},{5,13},{6,14},{7,15},{8,0},{9,1},... | collective-permute-start | bytes 172040 | tf_op jit(solution)/shard_map/ppermute | solution.py:223
  117.0 5.3 %collective-permute-start.13 = (f32[224,128]{1,0:T(8,128)S(1)}, f32[224,128]{1,0:T(8,128)S(1)}, u32[]{:S(2)}, u32[]{:S(2)}) collective-permute-start(f32[224,128]{1,0:T(8,128)S(1)} %pad_maximum_fusion.6), channel_id=1, source_target_pairs={{0,4},{1,5},{2,6},{3,7},{4,0},{5,1},{6,2},{7,3},{8,12},{9,13},{10,... | collective-permute-start | bytes 344072 | tf_op jit(solution)/shard_map/ppermute | solution.py:223
  119.5 6.1 %collective-permute-start.22 = (f32[448,128]{1,0:T(8,128)S(1)}, f32[448,128]{1,0:T(8,128)S(1)}, u32[]{:S(2)}, u32[]{:S(2)}) collective-permute-start(f32[448,128]{1,0:T(8,128)S(1)} %pad_maximum_fusion.5), channel_id=1, source_target_pairs={{0,2},{1,3},{2,0},{3,1},{4,6},{5,7},{6,4},{7,5},{8,10},{9,11},{10,... | collective-permute-start | bytes 688136 | tf_op jit(solution)/shard_map/ppermute | solution.py:223
  122.3 6.1 %collective-permute-start.14 = (f32[448,128]{1,0:T(8,128)S(1)}, f32[448,128]{1,0:T(8,128)S(1)}, u32[]{:S(2)}, u32[]{:S(2)}) collective-permute-start(f32[448,128]{1,0:T(8,128)S(1)} %pad_maximum_fusion.4), channel_id=1, source_target_pairs={{0,2},{1,3},{2,0},{3,1},{4,6},{5,7},{6,4},{7,5},{8,10},{9,11},{10,... | collective-permute-start | bytes 688136 | tf_op jit(solution)/shard_map/ppermute | solution.py:223
  125.7 4.3 %copy-start.21 = (f32[448,128]{1,0:T(8,128)}, f32[448,128]{1,0:T(8,128)S(1)}, u32[]{:S(2)}) copy-start(f32[448,128]{1,0:T(8,128)S(1)} %get-tuple-element.76) | copy-start | bytes 688132
  125.7 4.3 %copy-start.23 = (f32[448,128]{1,0:T(8,128)}, f32[448,128]{1,0:T(8,128)S(1)}, u32[]{:S(2)}) copy-start(f32[448,128]{1,0:T(8,128)S(1)} %get-tuple-element.77) | copy-start | bytes 688132
  126.6 6.5 %collective-permute-start.23 = (f32[896,128]{1,0:T(8,128)}, f32[896,128]{1,0:T(8,128)}, u32[]{:S(2)}, u32[]{:S(2)}) collective-permute-start(f32[896,128]{1,0:T(8,128)} %pad_maximum_fusion.3), channel_id=1, source_target_pairs={{0,1},{1,0},{2,3},{3,2},{4,5},{5,4},{6,7},{7,6},{8,9},{9,8},{10,11... | collective-permute-start | bytes 1376264 | tf_op jit(solution)/shard_map/ppermute | solution.py:223
  128.5 1.5 %copy-start.27 = (f32[448,128]{1,0:T(8,128)}, f32[448,128]{1,0:T(8,128)S(1)}, u32[]{:S(2)}) copy-start(f32[448,128]{1,0:T(8,128)S(1)} %get-tuple-element.79) | copy-start | bytes 688132
  130.0 4.3 %collective-permute-start.15 = (f32[896,128]{1,0:T(8,128)}, f32[896,128]{1,0:T(8,128)}, u32[]{:S(2)}, u32[]{:S(2)}) collective-permute-start(f32[896,128]{1,0:T(8,128)} %pad_maximum_fusion.2), channel_id=1, source_target_pairs={{0,1},{1,0},{2,3},{3,2},{4,5},{5,4},{6,7},{7,6},{8,9},{9,8},{10,11... | collective-permute-start | bytes 1376264 | tf_op jit(solution)/shard_map/ppermute | solution.py:223
  130.1 1.1 copy-start.8
  131.2 2.0 %copy-start.22 = (f32[448,128]{1,0:T(8,128)S(1)}, f32[448,128]{1,0:T(8,128)}, u32[]{:S(2)}) copy-start(f32[448,128]{1,0:T(8,128)} %copy-done.21) | copy-start | bytes 688132
  131.2 2.0 %copy-start.24 = (f32[448,128]{1,0:T(8,128)S(1)}, f32[448,128]{1,0:T(8,128)}, u32[]{:S(2)}) copy-start(f32[448,128]{1,0:T(8,128)} %copy-done.23) | copy-start | bytes 688132
  133.1 1.2 copy-start.26
  133.1 1.2 copy-start.28
  (11 other events, 8.1 us)

commit v2 on v1

v2 whole, which is shorter than its diff:
```python
import math

import jax
import jax.numpy as jnp
from jax import lax
from jax.experimental import pallas as pl
from jax.experimental.pallas import tpu as pltpu
from jax.sharding import PartitionSpec as P

TRACKS = 18
TW = 16
MOST = 3
D = TRACKS * TW
HID = 384
INNER = TRACKS - MOST
LANES = 128
MIB = 1 << 20

ROOT_HALF = 0.7071067811865476
INV_ROOT_TWO_PI = 0.3989422804014327

f32, bf16, i32 = jnp.float32, jnp.bfloat16, jnp.int32
VM = pl.BlockSpec(memory_space=pltpu.VMEM)
SM = pl.BlockSpec(memory_space=pltpu.SMEM)
HB = pl.BlockSpec(memory_space=pltpu.HBM)


def kernel_options(name, mib, cost_us):
    return dict(
        name=name,
        compiler_params=pltpu.CompilerParams(vmem_limit_bytes=mib * MIB),
        cost_estimate=pl.CostEstimate(flops=int(cost_us * 1e9), bytes_accessed=int(cost_us * 3e6), transcendentals=0),
    )


def near_slots(pos):
    slots, offset = [], 0
    for slot in range(INNER):
        width = max(LANES, pos >> (slot // MOST))
        slots.append((offset, width))
        offset += width
    return slots, offset


def halves(value):
    high = value.astype(bf16)
    return high, (value - high.astype(f32)).astype(bf16)


def put_triple(ref, value, rows, cols, order):
    pair = halves(value)
    for place, which in enumerate(order):
        ref[place * rows:(place + 1) * rows, cols] = pair[which]


def fill_tables(dist, tab, layer, hops, pos):
    d = [dist[layer, t] for t in range(TRACKS)]
    key = [d[t] * 32 + (31 - t) for t in range(TRACKS)]
    rank = [jnp.int32(0)] * TRACKS
    for t in range(TRACKS):
        for u in range(t + 1, TRACKS):
            above = (key[u] > key[t]).astype(i32)
            rank[t] = rank[t] + above
            rank[u] = rank[u] + (1 - above)
    for t in range(TRACKS):
        tab[rank[t]] = jnp.int32(t)
    for k in range(hops):
        first = jnp.int32(0)
        for t in range(TRACKS):
            first = first + (d[t] > (pos << k)).astype(i32)
        tab[TRACKS + k] = first


def track_at(tab, k, slot):
    place = tab[TRACKS + k] + slot
    return place, tab[jnp.minimum(place, TRACKS - 1)]


def rows_of(track):
    return pl.ds(pl.multiple_of(track * TW, TW), TW)


class Copies:
    def __init__(self, sems):
        self.sems, self.used = sems, 0

    def start(self, src, dst):
        copy = pltpu.make_async_copy(src, dst, self.sems.at[self.used])
        self.used += 1
        copy.start()
        return copy


def pack(copies, src, tab, far, near, hops, pos):
    started = []
    for k in range(hops - 1, 0, -1):
        for slot in range(MOST):
            _, t = track_at(tab, k, slot)
            started.append(copies.start(src.at[rows_of(t), :], far[k - 1].at[slot * TW:(slot + 1) * TW, :]))
    for slot, (offset, width) in enumerate(near_slots(pos)[0]):
        _, t = track_at(tab, 0, slot)
        started.append(copies.start(src.at[rows_of(t), 0:width], near.at[:, offset:offset + width]))
    return started


def unpack(src, dist, tab, layer, far, near, out, join, hops, pos):
    for k in range(1, hops):
        for slot in range(MOST):
            place, t = track_at(tab, k, slot)

            @pl.when((place < TRACKS) & (dist[layer, t] == (pos << k)))
            def _(k=k, slot=slot, t=t):
                out[rows_of(t), :] = far[k - 1][slot * TW:(slot + 1) * TW, :]

    for slot, (offset, width) in enumerate(near_slots(pos)[0]):
        place, t = track_at(tab, 0, slot)

        @pl.when(place < TRACKS)
        def _(slot=slot, t=t, offset=offset, width=width):
            shift = dist[layer, t]
            join[slot, :, :pos] = src[rows_of(t), :]
            join[slot, :, pos:pos + width] = near[:, offset:offset + width]
            base = pl.multiple_of(shift // LANES * LANES, LANES)
            rest = shift % LANES
            window = join[slot, :, pl.ds(base, pos + LANES)]
            turned = pltpu.roll(window, jnp.where(rest == 0, 0, pos + LANES - rest), 1)
            out[rows_of(t), :] = turned[:, :pos]


def pack_kernel(hops, pos, dist, src, tab, near, *refs):
    far, sems = refs[:-1], refs[-1]
    fill_tables(dist, tab, 1, hops, pos)
    for copy in pack(Copies(sems), src, tab, far, near, hops, pos):
        copy.wait()


def act_kernel(hops, pos, dist, *refs):
    ins, tab, outs, xs = refs[:8], refs[8], refs[9:19], refs[19]
    fill_tables(dist, tab, 0, hops, pos)
    for layer in range(2):
        act(pos, *ins[4 * layer:4 * layer + 4], *outs[5 * layer:5 * layer + 5], xs)


def act(pos, x, w_in, bias, w_out_t, x2, h2, slope, wi3, wo3, xs):
    step = 256
    wt = jnp.transpose(w_in[...], (1, 0))
    wt_hi, wt_lo = halves(wt)
    wt3 = jnp.concatenate([wt_hi, wt_hi, wt_lo], axis=1)
    w_hi, w_lo = halves(w_in[...])
    wi3[...] = jnp.concatenate([w_hi, w_hi, w_lo], axis=1)
    w_hi, w_lo = halves(jnp.transpose(w_out_t[...], (1, 0)))
    wo3[...] = jnp.concatenate([w_hi, w_hi, w_lo], axis=1)
    for start in range(0, pos, step):
        cols = slice(start, start + step)
        x_hi, x_lo = halves(x[:, cols])
        x2[0:D, cols] = x_hi
        x2[D:D + 16, cols] = jnp.ones((16, step), bf16)
        x2[D + 16:2 * D + 16, cols] = x_lo
        x2[2 * D + 16:2 * D + 32, cols] = jnp.zeros((16, step), bf16)
        xs[0:D, :] = x_hi
        xs[D:2 * D, :] = x_lo
        xs[2 * D:3 * D, :] = x_hi
        pre = jnp.dot(wt3, xs[...], preferred_element_type=f32) + bias[...]
        cdf = 0.5 * (1.0 + lax.erf(pre * ROOT_HALF))
        put_triple(h2, pre * cdf, HID, cols, (0, 1))
        slope[:, cols] = cdf + pre * jnp.exp(-0.5 * pre * pre) * INV_ROOT_TWO_PI


def hidden(pos, wo3, slope, gm, gm3, gh3):
    step = 512
    for start in range(0, pos, step):
        cols = slice(start, start + step)
        put_triple(gm3, gm[:, cols], D, cols, (0, 1, 0))
        gh = jnp.dot(wo3[...], gm3[:, cols], preferred_element_type=f32) * slope[:, cols]
        put_triple(gh3, gh, HID, cols, (0, 1, 0))


def inward(pos, wi3, gm, gh3, out):
    step = 512
    for start in range(0, pos, step):
        cols = slice(start, start + step)
        out[:, cols] = gm[:, cols] + jnp.dot(wi3[...], gh3[:, cols], preferred_element_type=f32)


def weight_terms(factor, odd, x2, gh, h2, gm, keep, send):
    def nt(a, b):
        return lax.dot_general(a, b, (((1,), (1,)), ((), ())), preferred_element_type=f32)

    d1 = D + 16
    first = nt(x2[0:d1, :], gh[0:HID, :]) + nt(x2[0:d1, :], gh[HID:2 * HID, :]) + nt(x2[d1:2 * d1, :], gh[0:HID, :])
    second = nt(gm[0:D, :], h2[0:HID, :]) + nt(gm[0:D, :], h2[HID:2 * HID, :]) + nt(gm[D:2 * D, :], h2[0:HID, :])
    first, second = first[0:D + 8] * factor, second * factor

    def put(part, out):
        rows, used = part.shape[0], 0
        for j in range(HID // LANES):
            out[used:used + rows, :] = part[:, j * LANES:(j + 1) * LANES]
            used += rows
        out[used:, :] = jnp.zeros((out.shape[0] - used, LANES), f32)

    @pl.when(odd == 0)
    def _():
        put(first, keep)
        put(second, send)

    @pl.when(odd == 1)
    def _():
        put(second, keep)
        put(first, send)


def upper_kernel(hops, pos, dist, tab1, tab0, src_h, wo3_h, wi3_h, slope_h, near_in, *refs):
    far_in, refs = refs[:hops - 1], refs[hops - 1:]
    near, refs = refs[0], refs[1:]
    far, refs = refs[:hops - 1], refs[hops - 1:]
    grad_h, gm_h, gh_h, src, wo3, wi3, slope, gm3, gh3, gm, grad, join, sems = refs
    copies = Copies(sems)
    loads = [copies.start(*pair) for pair in ((src_h, src), (wo3_h, wo3), (slope_h, slope), (wi3_h, wi3))]
    loads[0].wait()
    unpack(src, dist, tab1, 1, far_in, near_in, gm, join, hops, pos)
    loads[1].wait()
    loads[2].wait()
    hidden(pos, wo3, slope, gm, gm3, gh3)
    stores = [copies.start(gm3.at[0:2 * D, :], gm_h), copies.start(gh3.at[0:2 * HID, :], gh_h)]
    loads[3].wait()
    inward(pos, wi3, gm, gh3, grad)
    stores = pack(copies, grad, tab0, far, near, hops, pos) + stores
    stores.append(copies.start(grad, grad_h))
    for copy in stores:
        copy.wait()


def terms_kernel(factor, odd, *refs):
    held_ins, (keep, send), scratch, sems = refs[:4], refs[4:6], refs[6:10], refs[10]
    copies = Copies(sems)
    for copy in [copies.start(*pair) for pair in zip(held_ins, scratch)]:
        copy.wait()
    weight_terms(factor, odd[0], *scratch, keep, send)


def lower_kernel(hops, pos, factor, odd, dist, tab0, src_h, wo3_h, slope_h, x2_h, h2_h, near_in, *refs):
    far_in, refs = refs[:hops - 1], refs[hops - 1:]
    keep, send, gm_h, gh_h, src, wo3, slope, x2, h2, gm3, gh3, gm, join, sems = refs
    copies = Copies(sems)
    loads = [copies.start(*pair) for pair in ((src_h, src), (wo3_h, wo3), (slope_h, slope), (x2_h, x2), (h2_h, h2))]
    loads[0].wait()
    unpack(src, dist, tab0, 0, far_in, near_in, gm, join, hops, pos)
    stores = [copies.start(gm, gm_h)]
    loads[1].wait()
    loads[2].wait()
    hidden(pos, wo3, slope, gm, gm3, gh3)
    stores.append(copies.start(gh3, gh_h))
    loads[3].wait()
    loads[4].wait()
    weight_terms(factor, odd[0], x2, gh3, h2, gm3, keep, send)
    for copy in stores:
        copy.wait()


def input_kernel(pos, *refs):
    held_ins, out, scratch, sems = refs[:3], refs[3], refs[4:7], refs[7]
    copies = Copies(sems)
    for copy in [copies.start(*pair) for pair in zip(held_ins, scratch)]:
        copy.wait()
    inward(pos, *scratch, out)


def finish_kernel(odd, *refs):
    sums, (w_in_grad, bias_grad, w_out_t_grad) = refs[:4], refs[4:]
    rows = D + 8

    def put(layer, first, second):
        for j in range(HID // LANES):
            lanes = slice(j * LANES, (j + 1) * LANES)
            w_in_grad[layer, :, lanes] = first[j * rows:j * rows + D, :]
            bias_grad[layer:layer + 1, lanes] = first[j * rows + D:j * rows + D + 1, :]
            w_out_t_grad[layer, :, lanes] = second[j * D:(j + 1) * D, :]

    for layer in range(2):
        mine, other = sums[2 * layer], sums[2 * layer + 1]

        @pl.when(odd[0] == 0)
        def _(layer=layer, mine=mine, other=other):
            put(layer, mine, other)

        @pl.when(odd[0] == 1)
        def _(layer=layer, mine=mine, other=other):
            put(layer, other, mine)


def from_ahead(value, steps):
    count = lax.axis_size("seq")
    return lax.ppermute(value, "seq", [(s, (s - steps) % count) for s in range(count)])


def exchange(value, mask):
    count = lax.axis_size("seq")
    return lax.ppermute(value, "seq", [(s, s ^ mask) for s in range(count)])


def fold(x, mask, send=None):
    half = x.shape[0] // 2
    bit = (lax.axis_index("seq") & mask) != 0
    low, high = x[:half], x[half:]
    return jnp.where(bit, high, low) + exchange(jnp.where(bit, low, high), mask)


def spread(x, mask):
    bit = (lax.axis_index("seq") & mask) != 0
    other = exchange(x, mask)
    return jnp.concatenate([jnp.where(bit, other, x), jnp.where(bit, x, other)], 0)


def shape(*dims, dtype=f32):
    return jax.ShapeDtypeStruct(dims, dtype)


def stay(*values):
    return [pltpu.with_memory_space_constraint(v, pltpu.HBM) for v in values]


def held(*dims, dtype=f32):
    return pltpu.HBM(dims, dtype)


def body(first_inputs, second_inputs, out_grad, weight_in, bias_in, weight_out, distances):
    pos = first_inputs.shape[1]
    count = lax.axis_size("seq")
    hops = count.bit_length() - 1
    factor = 1.0 / math.sqrt(pos * count)
    near_width = near_slots(pos)[1]
    far_shapes = [shape(MOST * TW, pos)] * (hops - 1)
    near_shape = shape(TW, near_width)
    half = -(-3 * (D + 8) // (8 * count)) * 8 * count
    masks = [1 << b for b in range(1, hops)]
    far_hops = [1 << k for k in range(1, hops)]
    odd = (lax.axis_index("seq") & 1).astype(i32).reshape(1)
    copy_sems = pltpu.SemaphoreType.DMA((MOST * hops + INNER + 16,))

    def travel(near, far):
        moved = [from_ahead(f, h) for f, h in zip(far[::-1], far_hops[::-1])][::-1]
        return from_ahead(near, 1), moved

    tab_1, near, *far = pl.pallas_call(
        lambda *refs: pack_kernel(hops, pos, *refs),
        out_shape=[shape(32, dtype=i32), near_shape] + far_shapes,
        in_specs=[SM, HB],
        out_specs=[SM] + [HB] * hops,
        scratch_shapes=[copy_sems],
        **kernel_options("pack", 4, 2),
    )(distances, *stay(out_grad))
    near, far = travel(near, far)

    w_out_t = jnp.transpose(weight_out, (0, 2, 1))
    saved = [first_inputs, second_inputs]
    act_ins = []
    for layer in range(2):
        act_ins += [saved[layer], weight_in[layer], bias_in[layer][:, None], w_out_t[layer]]
    act_shapes = [
        held(2 * D + 32, pos, dtype=bf16),
        held(2 * HID, pos, dtype=bf16),
        held(HID, pos),
        held(D, 3 * HID, dtype=bf16),
        held(HID, 3 * D, dtype=bf16),
    ]
    tab_0, *acts = pl.pallas_call(
        lambda *refs: act_kernel(hops, pos, *refs),
        out_shape=[shape(32, dtype=i32)] + act_shapes * 2,
        in_specs=[SM] + [VM] * 8,
        out_specs=[SM] + [VM] * 10,
        scratch_shapes=[pltpu.VMEM((3 * D, 256), bf16)],
        **kernel_options("act", 28, 5),
    )(distances, *act_ins)
    x2_0, h2_0, slope_0, wi3_0, wo3_0, x2_1, h2_1, slope_1, wi3_1, wo3_1 = acts

    x2_s = pltpu.VMEM((2 * D + 32, pos), bf16)
    h2_s = pltpu.VMEM((2 * HID, pos), bf16)
    slope_s = pltpu.VMEM((HID, pos), f32)
    wi3_s = pltpu.VMEM((D, 3 * HID), bf16)
    wo3_s = pltpu.VMEM((HID, 3 * D), bf16)
    gm3_s = pltpu.VMEM((3 * D, pos), bf16)
    gh3_s = pltpu.VMEM((3 * HID, pos), bf16)
    whole_s = pltpu.VMEM((D, pos), f32)
    join_s = pltpu.VMEM((INNER, TW, 2 * pos + LANES), f32)

    near, *rest = pl.pallas_call(
        lambda *refs: upper_kernel(hops, pos, *refs),
        out_shape=[near_shape] + far_shapes + [held(D, pos), held(2 * D, pos, dtype=bf16), held(2 * HID, pos, dtype=bf16)],
        in_specs=[SM] * 3 + [HB] * 4 + [VM] * hops,
        out_specs=[HB] * (hops + 3),
        scratch_shapes=[whole_s, wo3_s, wi3_s, slope_s, gm3_s, gh3_s, whole_s, whole_s, join_s, copy_sems],
        **kernel_options("upper", 24, 5),
    )(distances, tab_1, tab_0, *stay(out_grad, wo3_1, wi3_1, slope_1), near, *far)
    far, (grad_1, gm2_1, gh2_1) = rest[:hops - 1], rest[hops - 1:]
    near, far = travel(near, far)

    keep_1, send_1 = pl.pallas_call(
        lambda *refs: terms_kernel(factor, *refs),
        out_shape=[shape(half, LANES)] * 2,
        in_specs=[SM] + [HB] * 4,
        out_specs=[VM] * 2,
        scratch_shapes=[x2_s, pltpu.VMEM((2 * HID, pos), bf16), h2_s, pltpu.VMEM((2 * D, pos), bf16), copy_sems],
        **kernel_options("terms", 16, 0.001),
    )(odd, *stay(x2_1, gh2_1, h2_1, gm2_1))
    send_1, near, far = lax.optimization_barrier((send_1, near, far))
    sum_1 = keep_1 + exchange(send_1, 1)

    keep, send, gm_0, gh3_0 = pl.pallas_call(
        lambda *refs: lower_kernel(hops, pos, factor, *refs),
        out_shape=[shape(half, LANES)] * 2 + [held(D, pos), held(3 * HID, pos, dtype=bf16)],
        in_specs=[SM] * 3 + [HB] * 5 + [VM] * hops,
        out_specs=[VM] * 2 + [HB] * 2,
        scratch_shapes=[whole_s, wo3_s, slope_s, x2_s, h2_s, gm3_s, gh3_s, whole_s, join_s, copy_sems],
        **kernel_options("lower", 24, 5),
    )(odd, distances, tab_0, *stay(grad_1, wo3_0, slope_0, x2_0, h2_0), near, *far)

    sum_0 = keep + exchange(send, 1)
    sum_0, gm_0 = lax.optimization_barrier((sum_0, gm_0))

    input_grad = pl.pallas_call(
        lambda *refs: input_kernel(pos, *refs),
        out_shape=shape(D, pos),
        in_specs=[HB] * 3,
        out_specs=VM,
        scratch_shapes=[wi3_s, whole_s, gh3_s, copy_sems],
        **kernel_options("inward", 12, 3),
    )(*stay(wi3_0, gm_0, gh3_0))

    for number, mask in enumerate(masks):
        sum_1 = fold(sum_1, mask)
        if number == 1:
            sum_0, input_grad = lax.optimization_barrier((sum_0, input_grad))
        sum_0 = fold(sum_0, mask)
    for mask in masks[::-1]:
        sum_1 = spread(sum_1, mask)
        sum_0 = spread(sum_0, mask)
    other_1 = exchange(sum_1, 1)
    other_0 = exchange(sum_0, 1)

    w_in_grad, bias_grad, w_out_t_grad = pl.pallas_call(
        finish_kernel,
        out_shape=[shape(2, D, HID), shape(2, HID), shape(2, D, HID)],
        in_specs=[SM] + [VM] * 4,
        out_specs=[VM] * 3,
        **kernel_options("finish", 12, 1),
    )(odd, sum_0, other_0, sum_1, other_1)
    return input_grad, w_in_grad, bias_grad, jnp.transpose(w_out_t_grad, (0, 2, 1))


def solution(mesh):
    whole = P(None, ("groups", "seq"))
    in_specs = (whole, whole, whole, P(), P(), P(), P())
    out_specs = (whole, P("groups", None, None), P("groups", None), P("groups", None, None))
    return jax.shard_map(body, mesh=mesh, in_specs=in_specs, out_specs=out_specs, check_vma=False)
```

time: 139 us -> 115 us (0.83)
  local copies, waits for them, and re-layouts: 25.9 us -> 2.83 us
  waiting for transfers between devices: 49.8 us -> 32.3 us
  Pallas kernels: 21.3 us -> 37.1 us
  starting transfers between devices: 28.8 us -> 39.9 us
  other arithmetic: 11.2 us -> 1.63 us
    unnamed x73 -> x12, local copies, waits for them, and re-layouts: 18.2 us -> 1.14 us
    ppermute x16, waiting for transfers between devices: 27.6 us -> 12 us  [exchange(): return lax.ppermute(value, 'seq', [(s, s ^ mask) for s in range(count)])]
    ppermute x16, starting transfers between devices: 16.2 us -> 27.8 us  [exchange(): return lax.ppermute(value, 'seq', [(s, s ^ mask) for s in range(count)])]
    pallas_call x4 -> x3, Pallas kernels: 10.6 us -> 20.9 us  [the longest x1 8.04 us: body(): pl.pallas_call(lambda *refs: upper_kernel(hops, pos, *refs), out_shape=[n...]
    add x8, other arithmetic: 7.03 us -> 1.29 us  [the longest x1 1.08 us: body(): sum_1 = keep_1 + exchange(send_1, 1)]
    dynamic_slice x8 -> x0, local copies, waits for them, and re-layouts: 5.27 us -> none  [total_over_seq(): send = lax.dynamic_slice_in_dim(x, (1 - bit) * half, half, 0)]
    pallas_call x1, Pallas kernels: 1.94 us -> 4.56 us  [body(): pl.pallas_call(lambda *refs: input_kernel(pos, *refs), out_shape=shape(D,...]
    pallas_call x1, Pallas kernels: 5.01 us -> 7.22 us  [body(): pl.pallas_call(lambda *refs: lower_kernel(hops, pos, factor, *refs), out_...]
  transfers between devices with their start and end apart: 24 -> 24, of which waited for: 16 -> 16; matrix products, arithmetic and copies ran while one was open for 13% -> 3% of each run, Pallas kernels for 8% -> 21%
where the time goes in v2:
time: 115 us
  starting transfers between devices  39.9 us (35%)
  Pallas kernels  37.1 us (32%)
  waiting for transfers between devices  32.3 us (28%)
  local copies, waits for them, and re-layouts  2.83 us (2%)
  other arithmetic  1.63 us (1%)
    ppermute x16, starting transfers between devices, exchange(): return lax.ppermute(value, 'seq', [(s, s ^ mask) for s in range(count)])  27.8 us
    ppermute x8, waiting for transfers between devices, from_ahead(): lax.ppermute(value, 'seq', [(s, (s - steps) % count) for s in range(count)])  20.3 us
    ppermute x8, starting transfers between devices, from_ahead(): lax.ppermute(value, 'seq', [(s, (s - steps) % count) for s in range(count)])  12.1 us
    ppermute x16, waiting for transfers between devices, exchange(): return lax.ppermute(value, 'seq', [(s, s ^ mask) for s in range(count)])  12 us
    pallas_call x1, Pallas kernels, body(): pl.pallas_call(lambda *refs: upper_kernel(hops, pos, *refs), out_shape=[n...  8.04 us
    pallas_call x1, Pallas kernels, body(): pl.pallas_call(lambda *refs: act_kernel(hops, pos, *refs), out_shape=[sha...  7.74 us
    pallas_call x1, Pallas kernels, body(): pl.pallas_call(lambda *refs: lower_kernel(hops, pos, factor, *refs), out_...  7.22 us
    pallas_call x1, Pallas kernels, body(): pl.pallas_call(lambda *refs: terms_kernel(factor, *refs), out_shape=[shap...  5.08 us
  transfers between devices with their start and end apart: 24, of which 16 were waited for; matrix products, arithmetic and copies ran while one was open for 3% of the time, Pallas kernels for 21%

profile of v2, /device:TPU:0, one launch (start us, length us, event | category | flops | bytes accessed | tf_op | source)
XLA Modules:
  0.0 114.7 jit_solution(1595531663697661633)
XLA Ops:
  0.6 0.7 copy-done.2
  1.3 3.1 %pack.1 = (s32[32]{0:T(128)S(1)}, f32[16,6144]{1,0:T(8,128)S(1)}, f32[48,1024]{1,0:T(8,128)S(1)}, f32[48,1024]{1,0:T(8,128)S(1)}, f32[48,1024]{1,0:T(8,128)S(1)}) custom-call(s32[2,18]{1,0:T(2,128)S(1)} %copy-done.2, f32[288,1024]{1,0:T(8,128)} %refs_3_.1), custom_call_target="tpu_custom_call" | custom-call | flops 2000000000 | bytes 6000000 | tf_op jit(solution)/shard_map/pack/pallas_call | solution.py:344
  4.4 5.5 %collective-permute-start = (f32[16,6144]{1,0:T(8,128)S(1)}, f32[16,6144]{1,0:T(8,128)S(1)}, u32[]{:S(2)}, u32[]{:S(2)}) collective-permute-start(f32[16,6144]{1,0:T(8,128)S(1)} %get-tuple-element.50), channel_id=1, source_target_pairs={{0,15},{1,0},{2,1},{3,2},{4,3},{5,4},{6,5},{7,6},{8,7},{9,8},{10,9... | collective-permute-start | bytes 1179656 | tf_op jit(solution)/shard_map/ppermute | solution.py:293
  9.9 0.6 collective-permute-start.1
  10.6 0.4 collective-permute-start.2
  11.0 0.1 copy.11.refs_3_
  11.2 0.1 copy.12.refs_7_
  11.4 1.4 %slice_bitcast_fusion = (f32[288,384]{1,0:T(8,128)S(1)}, f32[288,384]{1,0:T(8,128)S(1)}, f32[288,384]{1,0:T(8,128)S(1)}, f32[288,384]{1,0:T(8,128)S(1)}) fusion(f32[2,288,384]{2,1,0:T(8,128)S(1)} %bitcast.15, f32[2,288,384]{2,1,0:T(8,128)} %param.10), kind=kLoop, calls=%fused_computation.2 | loop fusion | bytes 3538944 | tf_op jit(solution)/shard_map/squeeze | solution.py:358
  12.8 0.1 copy-done
  12.9 0.4 copy-done.1
  13.2 7.7 %act.1 = (s32[32]{0:T(128)S(1)}, bf16[608,1024]{1,0:T(8,128)(2,1)}, bf16[768,1024]{1,0:T(8,128)(2,1)}, f32[384,1024]{1,0:T(8,128)}, bf16[288,1152]{1,0:T(8,128)(...) custom-call(s32[2,18]{1,0:T(2,128)S(1)} %copy-done.3, ...), custom_call_target="tpu_custom_call" | custom-call | flops 5000000000 | bytes 15000000 | tf_op jit(solution)/shard_map/act/pallas_call | solution.py:366
  21.0 2.6 %collective-permute-done.1.refs_8_ = f32[48,1024]{1,0:T(8,128)S(1)} collective-permute-done((f32[48,1024]{1,0:T(8,128)S(1)}, f32[48,1024]{1,0:T(8,128)S(1)}, u32[]{:S(2)}, u32[]{:S(2)}) %collective-permute-start.1) | collective-permute-done | bytes 196640 | tf_op jit(solution)/shard_map/ppermute | solution.py:293
  23.6 2.2 %collective-permute-done.2.refs_9_ = f32[48,1024]{1,0:T(8,128)S(1)} collective-permute-done((f32[48,1024]{1,0:T(8,128)S(1)}, f32[48,1024]{1,0:T(8,128)S(1)}, u32[]{:S(2)}, u32[]{:S(2)}) %collective-permute-start.2) | collective-permute-done | bytes 196640 | tf_op jit(solution)/shard_map/ppermute | solution.py:293
  25.8 6.2 %collective-permute-done.3.refs_10_ = f32[48,1024]{1,0:T(8,128)S(1)} collective-permute-done((f32[48,1024]{1,0:T(8,128)S(1)}, f32[48,1024]{1,0:T(8,128)S(1)}, u32[]{:S(2)}, u32[]{:S(2)}) %collective-permute-start.3) | collective-permute-done | bytes 196640 | tf_op jit(solution)/shard_map/ppermute | solution.py:293
  32.0 8.0 %upper.1 = (f32[16,6144]{1,0:T(8,128)S(1)}, f32[48,1024]{1,0:T(8,128)S(1)}, f32[48,1024]{1,0:T(8,128)S(1)}, f32[48,1024]{1,0:T(8,128)S(1)}, f32[288,1024]{1,0:T(...) custom-call(s32[2,18]{1,0:T(2,128)S(1)} %copy-done.3, s32[32]{0:T(128)S(1)} %get-tuple-element.46.refs_1_, ...), custom_call_target="tpu_custom_call" | custom-call | flops 5000000000 | bytes 15000000 | tf_op jit(solution)/shard_map/upper/pallas_call | solution.py:386
  40.1 5.5 %collective-permute-start.5 = (f32[48,1024]{1,0:T(8,128)S(1)}, f32[48,1024]{1,0:T(8,128)S(1)}, u32[]{:S(2)}, u32[]{:S(2)}) collective-permute-start(f32[48,1024]{1,0:T(8,128)S(1)} %get-tuple-element.65), channel_id=1, source_target_pairs={{0,14},{1,15},{2,0},{3,1},{4,2},{5,3},{6,4},{7,5},{8,6},{9,7},{10,... | collective-permute-start | bytes 589832 | tf_op jit(solution)/shard_map/ppermute | solution.py:293
  45.6 5.1 %terms.1 = (f32[896,128]{1,0:T(8,128)S(1)}, f32[896,128]{1,0:T(8,128)S(1)}) custom-call(s32[1]{0:T(128)} %bitcast.refs_0_.odd, bf16[608,1024]{1,0:T(8,128)(2,1)} %get-tuple-element.59.refs_1_, bf16[768,1024]{1,0:T(8,128)(2,1)} %get-tuple-element.60.refs_2_, bf16[768,1024]{1,0:T(8,128)(2,1)} %get-tuple-element.61.refs_3_, ...), custom_call_target="tpu_custom_call" | custom-call | flops 1000000 | bytes 3000 | tf_op jit(solution)/shard_map/terms/pallas_call | solution.py:397
  50.7 3.0 %collective-permute-done.5.refs_9_ = f32[48,1024]{1,0:T(8,128)S(1)} collective-permute-done((f32[48,1024]{1,0:T(8,128)S(1)}, f32[48,1024]{1,0:T(8,128)S(1)}, u32[]{:S(2)}, u32[]{:S(2)}) %collective-permute-start.5) | collective-permute-done | bytes 196640 | tf_op jit(solution)/shard_map/ppermute | solution.py:293
  53.7 4.4 %collective-permute-done.6.refs_10_ = f32[48,1024]{1,0:T(8,128)S(1)} collective-permute-done((f32[48,1024]{1,0:T(8,128)S(1)}, f32[48,1024]{1,0:T(8,128)S(1)}, u32[]{:S(2)}, u32[]{:S(2)}) %collective-permute-start.6) | collective-permute-done | bytes 196640 | tf_op jit(solution)/shard_map/ppermute | solution.py:293
  58.1 1.9 %collective-permute-done.7.refs_11_ = f32[48,1024]{1,0:T(8,128)S(1)} collective-permute-done((f32[48,1024]{1,0:T(8,128)S(1)}, f32[48,1024]{1,0:T(8,128)S(1)}, u32[]{:S(2)}, u32[]{:S(2)}) %collective-permute-start.7) | collective-permute-done | bytes 196640 | tf_op jit(solution)/shard_map/ppermute | solution.py:293
  60.0 7.2 %lower.1 = (f32[896,128]{1,0:T(8,128)S(1)}, f32[896,128]{1,0:T(8,128)S(1)}, f32[288,1024]{1,0:T(8,128)}, bf16[1152,1024]{1,0:T(8,128)(2,1)}) custom-call(s32[1]{0:T(128)} %bitcast.refs_0_.odd, s32[2,18]{1,0:T(2,128)S(1)} %copy-done.3, s32[32]{0:T(128)S(1)} %get-tuple-element.45.refs_2_, f32[288,1024]{1,0:T(8,128)} %get-tuple-element.54.refs_3_, ...), custom_call_target="tpu_custom_call" | custom-call | flops 5000000000 | bytes 15000000 | tf_op jit(solution)/shard_map/lower/pallas_call | solution.py:408
  67.2 0.6 collective-permute-start.8
  67.8 1.1 add.28
  68.9 0.1 collective-permute-start.17
  69.0 0.2 collective-permute-done.8
  69.3 1.8 %collective-permute-start.9 = (f32[448,128]{1,0:T(8,128)S(1)}, f32[448,128]{1,0:T(8,128)S(1)}, u32[]{:S(2)}, u32[]{:S(2)}) collective-permute-start(f32[448,128]{1,0:T(8,128)S(1)} %slice_select_fusion.1), channel_id=1, source_target_pairs={{0,2},{1,3},{2,0},{3,1},{4,6},{5,7},{6,4},{7,5},{8,10},{9,11},{10,... | collective-permute-start | bytes 688136 | tf_op jit(solution)/shard_map/ppermute | solution.py:298
  71.1 4.6 %inward.1 = f32[288,1024]{1,0:T(8,128)} custom-call(bf16[288,1152]{1,0:T(8,128)(2,1)} %get-tuple-element.76.refs_0_, f32[288,1024]{1,0:T(8,128)} %get-tuple-element.77.refs_1_, bf16[1152,1024]{1,0:T(8,128)(2,1)} %get-tuple-element.78.refs_2_), custom_call_target="tpu_custom_call" | custom-call | flops 3000000000 | bytes 9000000 | tf_op jit(solution)/shard_map/inward/pallas_call | solution.py:420
  75.7 1.7 %collective-permute-done.17 = f32[448,128]{1,0:T(8,128)S(1)} collective-permute-done((f32[448,128]{1,0:T(8,128)S(1)}, f32[448,128]{1,0:T(8,128)S(1)}, u32[]{:S(2)}, u32[]{:S(2)}) %collective-permute-start.17) | collective-permute-done | bytes 229408 | tf_op jit(solution)/shard_map/ppermute | solution.py:298
  77.5 3.6 %collective-permute-start.18 = (f32[224,128]{1,0:T(8,128)S(1)}, f32[224,128]{1,0:T(8,128)S(1)}, u32[]{:S(2)}, u32[]{:S(2)}) collective-permute-start(f32[224,128]{1,0:T(8,128)S(1)} %slice_select_fusion.2), channel_id=1, source_target_pairs={{0,4},{1,5},{2,6},{3,7},{4,0},{5,1},{6,2},{7,3},{8,12},{9,13},{10,... | collective-permute-start | bytes 344072 | tf_op jit(solution)/shard_map/ppermute | solution.py:298
  81.1 0.3 collective-permute-done.9
  81.5 3.6 %collective-permute-start.10 = (f32[224,128]{1,0:T(8,128)S(1)}, f32[224,128]{1,0:T(8,128)S(1)}, u32[]{:S(2)}, u32[]{:S(2)}) collective-permute-start(f32[224,128]{1,0:T(8,128)S(1)} %slice_select_fusion.3), channel_id=1, source_target_pairs={{0,4},{1,5},{2,6},{3,7},{4,0},{5,1},{6,2},{7,3},{8,12},{9,13},{10,... | collective-permute-start | bytes 344072 | tf_op jit(solution)/shard_map/ppermute | solution.py:298
  85.1 3.4 %collective-permute-start.19 = (f32[112,128]{1,0:T(8,128)S(1)}, f32[112,128]{1,0:T(8,128)S(1)}, u32[]{:S(2)}, u32[]{:S(2)}) collective-permute-start(f32[112,128]{1,0:T(8,128)S(1)} %slice_select_fusion.4), channel_id=1, source_target_pairs={{0,8},{1,9},{2,10},{3,11},{4,12},{5,13},{6,14},{7,15},{8,0},{9,1},... | collective-permute-start | bytes 172040 | tf_op jit(solution)/shard_map/ppermute | solution.py:298
  88.6 3.1 %collective-permute-start.11 = (f32[112,128]{1,0:T(8,128)S(1)}, f32[112,128]{1,0:T(8,128)S(1)}, u32[]{:S(2)}, u32[]{:S(2)}) collective-permute-start(f32[112,128]{1,0:T(8,128)S(1)} %slice_select_fusion.5), channel_id=1, source_target_pairs={{0,8},{1,9},{2,10},{3,11},{4,12},{5,13},{6,14},{7,15},{8,0},{9,1},... | collective-permute-start | bytes 172040 | tf_op jit(solution)/shard_map/ppermute | solution.py:298
  91.7 2.5 %collective-permute-start.20 = (f32[112,128]{1,0:T(8,128)S(1)}, f32[112,128]{1,0:T(8,128)S(1)}, u32[]{:S(2)}, u32[]{:S(2)}) collective-permute-start(f32[112,128]{1,0:T(8,128)S(1)} %select_add_fusion.4), channel_id=1, source_target_pairs={{0,8},{1,9},{2,10},{3,11},{4,12},{5,13},{6,14},{7,15},{8,0},{9,1},... | collective-permute-start | bytes 172040 | tf_op jit(solution)/shard_map/ppermute | solution.py:298
  94.3 2.6 %collective-permute-start.12 = (f32[112,128]{1,0:T(8,128)S(1)}, f32[112,128]{1,0:T(8,128)S(1)}, u32[]{:S(2)}, u32[]{:S(2)}) collective-permute-start(f32[112,128]{1,0:T(8,128)S(1)} %select_add_fusion.5), channel_id=1, source_target_pairs={{0,8},{1,9},{2,10},{3,11},{4,12},{5,13},{6,14},{7,15},{8,0},{9,1},... | collective-permute-start | bytes 172040 | tf_op jit(solution)/shard_map/ppermute | solution.py:298
  96.9 1.0 collective-permute-done.20
  97.9 1.1 collective-permute-start.21
  99.0 0.4 collective-permute-done.12
  99.5 1.7 %collective-permute-start.13 = (f32[224,128]{1,0:T(8,128)S(1)}, f32[224,128]{1,0:T(8,128)S(1)}, u32[]{:S(2)}, u32[]{:S(2)}) collective-permute-start(f32[224,128]{1,0:T(8,128)S(1)} %pad_maximum_fusion.4), channel_id=1, source_target_pairs={{0,4},{1,5},{2,6},{3,7},{4,0},{5,1},{6,2},{7,3},{8,12},{9,13},{10,... | collective-permute-start | bytes 344072 | tf_op jit(solution)/shard_map/ppermute | solution.py:298
  101.2 1.6 %collective-permute-done.21 = f32[224,128]{1,0:T(8,128)S(1)} collective-permute-done((f32[224,128]{1,0:T(8,128)S(1)}, f32[224,128]{1,0:T(8,128)S(1)}, u32[]{:S(2)}, u32[]{:S(2)}) %collective-permute-start.21) | collective-permute-done | bytes 114720 | tf_op jit(solution)/shard_map/ppermute | solution.py:298
  102.8 1.3 %collective-permute-start.22 = (f32[448,128]{1,0:T(8,128)S(1)}, f32[448,128]{1,0:T(8,128)S(1)}, u32[]{:S(2)}, u32[]{:S(2)}) collective-permute-start(f32[448,128]{1,0:T(8,128)S(1)} %pad_maximum_fusion.3), channel_id=1, source_target_pairs={{0,2},{1,3},{2,0},{3,1},{4,6},{5,7},{6,4},{7,5},{8,10},{9,11},{10,... | collective-permute-start | bytes 688136 | tf_op jit(solution)/shard_map/ppermute | solution.py:298
  104.1 0.2 collective-permute-done.13
  104.4 2.0 %collective-permute-start.14 = (f32[448,128]{1,0:T(8,128)S(1)}, f32[448,128]{1,0:T(8,128)S(1)}, u32[]{:S(2)}, u32[]{:S(2)}) collective-permute-start(f32[448,128]{1,0:T(8,128)S(1)} %pad_maximum_fusion.2), channel_id=1, source_target_pairs={{0,2},{1,3},{2,0},{3,1},{4,6},{5,7},{6,4},{7,5},{8,10},{9,11},{10,... | collective-permute-start | bytes 688136 | tf_op jit(solution)/shard_map/ppermute | solution.py:298
  106.4 2.5 %collective-permute-done.22 = f32[448,128]{1,0:T(8,128)S(1)} collective-permute-done((f32[448,128]{1,0:T(8,128)S(1)}, f32[448,128]{1,0:T(8,128)S(1)}, u32[]{:S(2)}, u32[]{:S(2)}) %collective-permute-start.22) | collective-permute-done | bytes 229408 | tf_op jit(solution)/shard_map/ppermute | solution.py:298
  109.1 2.3 %collective-permute-done.14 = f32[448,128]{1,0:T(8,128)S(1)} collective-permute-done((f32[448,128]{1,0:T(8,128)S(1)}, f32[448,128]{1,0:T(8,128)S(1)}, u32[]{:S(2)}, u32[]{:S(2)}) %collective-permute-start.14) | collective-permute-done | bytes 229408 | tf_op jit(solution)/shard_map/ppermute | solution.py:298
  111.4 0.1 collective-permute-start.15
  111.5 1.8 %collective-permute-done.15.refs_1_ = f32[896,128]{1,0:T(8,128)S(1)} collective-permute-done((f32[896,128]{1,0:T(8,128)S(1)}, f32[896,128]{1,0:T(8,128)S(1)}, u32[]{:S(2)}, u32[]{:S(2)}) %collective-permute-start.15) | collective-permute-done | bytes 458784 | tf_op jit(solution)/shard_map/ppermute | solution.py:298
  113.3 1.3 %finish.1 = (f32[2,288,384]{2,1,0:T(8,128)}, f32[2,384]{1,0:T(2,128)}, f32[2,288,384]{2,1,0:T(8,128)}) custom-call(s32[1]{0:T(128)} %bitcast.refs_0_.odd, f32[896,128]{1,0:T(8,128)S(1)} %pad_maximum_fusion.refs_0_, f32[896,128]{1,0:T(8,128)S(1)} %collective-permute-done.15.refs_1_, f32[896,128]{1,0:T(8,128)S(1)} %pad_maximum_fusion.1.refs_2_, ...), custom_call_target="tpu_custom_call" | custom-call | flops 1000000000 | bytes 3000000 | tf_op jit(solution)/shard_map/finish/pallas_call | solution.py:440
  (49 shorter events, 0.7 us)
Async XLA Ops:
  0.6 0.7 copy-start.2
  1.3 9.7 %copy-start.5 = (f32[2,384]{1,0:T(2,128)S(1)}, f32[2,384]{1,0:T(2,128)}, u32[]{:S(2)}) copy-start(f32[2,384]{1,0:T(2,128)} %param.11) | copy-start | bytes 9220
  1.3 10.0 %copy-start.4 = (f32[2,384,288]{1,2,0:T(8,128)S(1)}, f32[2,384,288]{1,2,0:T(8,128)}, u32[]{:S(2)}) copy-start(f32[2,384,288]{1,2,0:T(8,128)} %param.12) | copy-start | bytes 2654212
  4.4 27.5 %collective-permute-start = (f32[16,6144]{1,0:T(8,128)S(1)}, f32[16,6144]{1,0:T(8,128)S(1)}, u32[]{:S(2)}, u32[]{:S(2)}) collective-permute-start(f32[16,6144]{1,0:T(8,128)S(1)} %get-tuple-element.50), channel_id=1, source_target_pairs={{0,15},{1,0},{2,1},{3,2},{4,3},{5,4},{6,5},{7,6},{8,7},{9,8},{10,9... | collective-permute-start | bytes 1179656 | tf_op jit(solution)/shard_map/ppermute | solution.py:293
  9.9 13.7 %collective-permute-start.1 = (f32[48,1024]{1,0:T(8,128)S(1)}, f32[48,1024]{1,0:T(8,128)S(1)}, u32[]{:S(2)}, u32[]{:S(2)}) collective-permute-start(f32[48,1024]{1,0:T(8,128)S(1)} %get-tuple-element.51), channel_id=1, source_target_pairs={{0,14},{1,15},{2,0},{3,1},{4,2},{5,3},{6,4},{7,5},{8,6},{9,7},{10,... | collective-permute-start | bytes 589832 | tf_op jit(solution)/shard_map/ppermute | solution.py:293
  10.6 15.2 %collective-permute-start.2 = (f32[48,1024]{1,0:T(8,128)S(1)}, f32[48,1024]{1,0:T(8,128)S(1)}, u32[]{:S(2)}, u32[]{:S(2)}) collective-permute-start(f32[48,1024]{1,0:T(8,128)S(1)} %get-tuple-element.52), channel_id=1, source_target_pairs={{0,12},{1,13},{2,14},{3,15},{4,0},{5,1},{6,2},{7,3},{8,4},{9,5},{1... | collective-permute-start | bytes 589832 | tf_op jit(solution)/shard_map/ppermute | solution.py:293
  11.0 21.0 %collective-permute-start.3 = (f32[48,1024]{1,0:T(8,128)S(1)}, f32[48,1024]{1,0:T(8,128)S(1)}, u32[]{:S(2)}, u32[]{:S(2)}) collective-permute-start(f32[48,1024]{1,0:T(8,128)S(1)} %get-tuple-element.53), channel_id=1, source_target_pairs={{0,8},{1,9},{2,10},{3,11},{4,12},{5,13},{6,14},{7,15},{8,0},{9,1},... | collective-permute-start | bytes 589832 | tf_op jit(solution)/shard_map/ppermute | solution.py:293
  11.3 1.5 %copy-start = (f32[288,1024]{1,0:T(8,128)S(1)}, f32[288,1024]{1,0:T(8,128)}, u32[]{:S(2)}) copy-start(f32[288,1024]{1,0:T(8,128)} %refs_1_.3) | copy-start | bytes 3538948
  11.3 1.9 %copy-start.1 = (f32[288,1024]{1,0:T(8,128)S(1)}, f32[288,1024]{1,0:T(8,128)}, u32[]{:S(2)}) copy-start(f32[288,1024]{1,0:T(8,128)} %refs_5_.1) | copy-start | bytes 3538948
  11.4 1.9 %copy-start.3 = (s32[2,18]{1,0:T(2,128)S(1)}, s32[2,18]{1,0:T(2,128)}, u32[]{:S(2)}) copy-start(s32[2,18]{1,0:T(2,128)} %refs_1_.5) | copy-start | bytes 436
  40.0 19.9 %collective-permute-start.4 = (f32[16,6144]{1,0:T(8,128)S(1)}, f32[16,6144]{1,0:T(8,128)S(1)}, u32[]{:S(2)}, u32[]{:S(2)}) collective-permute-start(f32[16,6144]{1,0:T(8,128)S(1)} %get-tuple-element.64), channel_id=1, source_target_pairs={{0,15},{1,0},{2,1},{3,2},{4,3},{5,4},{6,5},{7,6},{8,7},{9,8},{10,9... | collective-permute-start | bytes 1179656 | tf_op jit(solution)/shard_map/ppermute | solution.py:293
  40.1 13.6 %collective-permute-start.5 = (f32[48,1024]{1,0:T(8,128)S(1)}, f32[48,1024]{1,0:T(8,128)S(1)}, u32[]{:S(2)}, u32[]{:S(2)}) collective-permute-start(f32[48,1024]{1,0:T(8,128)S(1)} %get-tuple-element.65), channel_id=1, source_target_pairs={{0,14},{1,15},{2,0},{3,1},{4,2},{5,3},{6,4},{7,5},{8,6},{9,7},{10,... | collective-permute-start | bytes 589832 | tf_op jit(solution)/shard_map/ppermute | solution.py:293
  45.6 12.5 %collective-permute-start.6 = (f32[48,1024]{1,0:T(8,128)S(1)}, f32[48,1024]{1,0:T(8,128)S(1)}, u32[]{:S(2)}, u32[]{:S(2)}) collective-permute-start(f32[48,1024]{1,0:T(8,128)S(1)} %get-tuple-element.66), channel_id=1, source_target_pairs={{0,12},{1,13},{2,14},{3,15},{4,0},{5,1},{6,2},{7,3},{8,4},{9,5},{1... | collective-permute-start | bytes 589832 | tf_op jit(solution)/shard_map/ppermute | solution.py:293
  45.6 14.4 %collective-permute-start.7 = (f32[48,1024]{1,0:T(8,128)S(1)}, f32[48,1024]{1,0:T(8,128)S(1)}, u32[]{:S(2)}, u32[]{:S(2)}) collective-permute-start(f32[48,1024]{1,0:T(8,128)S(1)} %get-tuple-element.67), channel_id=1, source_target_pairs={{0,8},{1,9},{2,10},{3,11},{4,12},{5,13},{6,14},{7,15},{8,0},{9,1},... | collective-permute-start | bytes 589832 | tf_op jit(solution)/shard_map/ppermute | solution.py:293
  60.0 7.8 %collective-permute-start.16 = (f32[896,128]{1,0:T(8,128)S(1)}, f32[896,128]{1,0:T(8,128)}, u32[]{:S(2)}, u32[]{:S(2)}) collective-permute-start(f32[896,128]{1,0:T(8,128)S(1)} %get-tuple-element.82), channel_id=1, source_target_pairs={{0,1},{1,0},{2,3},{3,2},{4,5},{5,4},{6,7},{7,6},{8,9},{9,8},{10,11... | collective-permute-start | bytes 1376264 | tf_op jit(solution)/shard_map/ppermute | solution.py:298
  67.2 2.0 %collective-permute-start.8 = (f32[896,128]{1,0:T(8,128)S(1)}, f32[896,128]{1,0:T(8,128)S(1)}, u32[]{:S(2)}, u32[]{:S(2)}) collective-permute-start(f32[896,128]{1,0:T(8,128)S(1)} %get-tuple-element.73), channel_id=1, source_target_pairs={{0,1},{1,0},{2,3},{3,2},{4,5},{5,4},{6,7},{7,6},{8,9},{9,8},{10,11... | collective-permute-start | bytes 1376264 | tf_op jit(solution)/shard_map/ppermute | solution.py:298
  68.9 8.5 %collective-permute-start.17 = (f32[448,128]{1,0:T(8,128)S(1)}, f32[448,128]{1,0:T(8,128)S(1)}, u32[]{:S(2)}, u32[]{:S(2)}) collective-permute-start(f32[448,128]{1,0:T(8,128)S(1)} %slice_select_fusion), channel_id=1, source_target_pairs={{0,2},{1,3},{2,0},{3,1},{4,6},{5,7},{6,4},{7,5},{8,10},{9,11},{10,... | collective-permute-start | bytes 688136 | tf_op jit(solution)/shard_map/ppermute | solution.py:298
  69.3 12.1 %collective-permute-start.9 = (f32[448,128]{1,0:T(8,128)S(1)}, f32[448,128]{1,0:T(8,128)S(1)}, u32[]{:S(2)}, u32[]{:S(2)}) collective-permute-start(f32[448,128]{1,0:T(8,128)S(1)} %slice_select_fusion.1), channel_id=1, source_target_pairs={{0,2},{1,3},{2,0},{3,1},{4,6},{5,7},{6,4},{7,5},{8,10},{9,11},{10,... | collective-permute-start | bytes 688136 | tf_op jit(solution)/shard_map/ppermute | solution.py:298
  77.5 7.6 %collective-permute-start.18 = (f32[224,128]{1,0:T(8,128)S(1)}, f32[224,128]{1,0:T(8,128)S(1)}, u32[]{:S(2)}, u32[]{:S(2)}) collective-permute-start(f32[224,128]{1,0:T(8,128)S(1)} %slice_select_fusion.2), channel_id=1, source_target_pairs={{0,4},{1,5},{2,6},{3,7},{4,0},{5,1},{6,2},{7,3},{8,12},{9,13},{10,... | collective-permute-start | bytes 344072 | tf_op jit(solution)/shard_map/ppermute | solution.py:298
  81.5 7.1 %collective-permute-start.10 = (f32[224,128]{1,0:T(8,128)S(1)}, f32[224,128]{1,0:T(8,128)S(1)}, u32[]{:S(2)}, u32[]{:S(2)}) collective-permute-start(f32[224,128]{1,0:T(8,128)S(1)} %slice_select_fusion.3), channel_id=1, source_target_pairs={{0,4},{1,5},{2,6},{3,7},{4,0},{5,1},{6,2},{7,3},{8,12},{9,13},{10,... | collective-permute-start | bytes 344072 | tf_op jit(solution)/shard_map/ppermute | solution.py:298
  85.1 6.6 %collective-permute-start.19 = (f32[112,128]{1,0:T(8,128)S(1)}, f32[112,128]{1,0:T(8,128)S(1)}, u32[]{:S(2)}, u32[]{:S(2)}) collective-permute-start(f32[112,128]{1,0:T(8,128)S(1)} %slice_select_fusion.4), channel_id=1, source_target_pairs={{0,8},{1,9},{2,10},{3,11},{4,12},{5,13},{6,14},{7,15},{8,0},{9,1},... | collective-permute-start | bytes 172040 | tf_op jit(solution)/shard_map/ppermute | solution.py:298
  88.6 5.6 %collective-permute-start.11 = (f32[112,128]{1,0:T(8,128)S(1)}, f32[112,128]{1,0:T(8,128)S(1)}, u32[]{:S(2)}, u32[]{:S(2)}) collective-permute-start(f32[112,128]{1,0:T(8,128)S(1)} %slice_select_fusion.5), channel_id=1, source_target_pairs={{0,8},{1,9},{2,10},{3,11},{4,12},{5,13},{6,14},{7,15},{8,0},{9,1},... | collective-permute-start | bytes 172040 | tf_op jit(solution)/shard_map/ppermute | solution.py:298
  91.7 6.2 %collective-permute-start.20 = (f32[112,128]{1,0:T(8,128)S(1)}, f32[112,128]{1,0:T(8,128)S(1)}, u32[]{:S(2)}, u32[]{:S(2)}) collective-permute-start(f32[112,128]{1,0:T(8,128)S(1)} %select_add_fusion.4), channel_id=1, source_target_pairs={{0,8},{1,9},{2,10},{3,11},{4,12},{5,13},{6,14},{7,15},{8,0},{9,1},... | collective-permute-start | bytes 172040 | tf_op jit(solution)/shard_map/ppermute | solution.py:298
  94.3 5.2 %collective-permute-start.12 = (f32[112,128]{1,0:T(8,128)S(1)}, f32[112,128]{1,0:T(8,128)S(1)}, u32[]{:S(2)}, u32[]{:S(2)}) collective-permute-start(f32[112,128]{1,0:T(8,128)S(1)} %select_add_fusion.5), channel_id=1, source_target_pairs={{0,8},{1,9},{2,10},{3,11},{4,12},{5,13},{6,14},{7,15},{8,0},{9,1},... | collective-permute-start | bytes 172040 | tf_op jit(solution)/shard_map/ppermute | solution.py:298
  97.9 4.9 %collective-permute-start.21 = (f32[224,128]{1,0:T(8,128)S(1)}, f32[224,128]{1,0:T(8,128)S(1)}, u32[]{:S(2)}, u32[]{:S(2)}) collective-permute-start(f32[224,128]{1,0:T(8,128)S(1)} %pad_maximum_fusion.5), channel_id=1, source_target_pairs={{0,4},{1,5},{2,6},{3,7},{4,0},{5,1},{6,2},{7,3},{8,12},{9,13},{10,... | collective-permute-start | bytes 344072 | tf_op jit(solution)/shard_map/ppermute | solution.py:298
  99.5 4.9 %collective-permute-start.13 = (f32[224,128]{1,0:T(8,128)S(1)}, f32[224,128]{1,0:T(8,128)S(1)}, u32[]{:S(2)}, u32[]{:S(2)}) collective-permute-start(f32[224,128]{1,0:T(8,128)S(1)} %pad_maximum_fusion.4), channel_id=1, source_target_pairs={{0,4},{1,5},{2,6},{3,7},{4,0},{5,1},{6,2},{7,3},{8,12},{9,13},{10,... | collective-permute-start | bytes 344072 | tf_op jit(solution)/shard_map/ppermute | solution.py:298
  102.8 6.1 %collective-permute-start.22 = (f32[448,128]{1,0:T(8,128)S(1)}, f32[448,128]{1,0:T(8,128)S(1)}, u32[]{:S(2)}, u32[]{:S(2)}) collective-permute-start(f32[448,128]{1,0:T(8,128)S(1)} %pad_maximum_fusion.3), channel_id=1, source_target_pairs={{0,2},{1,3},{2,0},{3,1},{4,6},{5,7},{6,4},{7,5},{8,10},{9,11},{10,... | collective-permute-start | bytes 688136 | tf_op jit(solution)/shard_map/ppermute | solution.py:298
  104.4 7.0 %collective-permute-start.14 = (f32[448,128]{1,0:T(8,128)S(1)}, f32[448,128]{1,0:T(8,128)S(1)}, u32[]{:S(2)}, u32[]{:S(2)}) collective-permute-start(f32[448,128]{1,0:T(8,128)S(1)} %pad_maximum_fusion.2), channel_id=1, source_target_pairs={{0,2},{1,3},{2,0},{3,1},{4,6},{5,7},{6,4},{7,5},{8,10},{9,11},{10,... | collective-permute-start | bytes 688136 | tf_op jit(solution)/shard_map/ppermute | solution.py:298
  109.0 2.5 %collective-permute-start.23 = (f32[896,128]{1,0:T(8,128)S(1)}, f32[896,128]{1,0:T(8,128)S(1)}, u32[]{:S(2)}, u32[]{:S(2)}) collective-permute-start(f32[896,128]{1,0:T(8,128)S(1)} %pad_maximum_fusion.1.refs_2_), channel_id=1, source_target_pairs={{0,1},{1,0},{2,3},{3,2},{4,5},{5,4},{6,7},{7,6},{8,9},{9,8},{10,11... | collective-permute-start | bytes 1376264 | tf_op jit(solution)/shard_map/ppermute | solution.py:298
  111.4 1.9 %collective-permute-start.15 = (f32[896,128]{1,0:T(8,128)S(1)}, f32[896,128]{1,0:T(8,128)S(1)}, u32[]{:S(2)}, u32[]{:S(2)}) collective-permute-start(f32[896,128]{1,0:T(8,128)S(1)} %pad_maximum_fusion.refs_0_), channel_id=1, source_target_pairs={{0,1},{1,0},{2,3},{3,2},{4,5},{5,4},{6,7},{7,6},{8,9},{9,8},{10,11... | collective-permute-start | bytes 1376264 | tf_op jit(solution)/shard_map/ppermute | solution.py:298

commit v3 on v2

--- a/solution.py
+++ b/solution.py
@@ -80,27 +80,14 @@
     return pl.ds(pl.multiple_of(track * TW, TW), TW)
 
 
-class Copies:
-    def __init__(self, sems):
-        self.sems, self.used = sems, 0
-
-    def start(self, src, dst):
-        copy = pltpu.make_async_copy(src, dst, self.sems.at[self.used])
-        self.used += 1
-        copy.start()
-        return copy
-
-
-def pack(copies, src, tab, far, near, hops, pos):
-    started = []
+def pack(src, tab, far, near, hops, pos):
     for k in range(hops - 1, 0, -1):
         for slot in range(MOST):
             _, t = track_at(tab, k, slot)
-            started.append(copies.start(src.at[rows_of(t), :], far[k - 1].at[slot * TW:(slot + 1) * TW, :]))
+            far[k - 1][slot * TW:(slot + 1) * TW, :] = src[rows_of(t), :]
     for slot, (offset, width) in enumerate(near_slots(pos)[0]):
         _, t = track_at(tab, 0, slot)
-        started.append(copies.start(src.at[rows_of(t), 0:width], near.at[:, offset:offset + width]))
-    return started
+        near[:, offset:offset + width] = src[rows_of(t), 0:width]
 
 
 def unpack(src, dist, tab, layer, far, near, out, join, hops, pos):
@@ -127,11 +114,13 @@
             out[rows_of(t), :] = turned[:, :pos]
 
 
-def pack_kernel(hops, pos, dist, src, tab, near, *refs):
-    far, sems = refs[:-1], refs[-1]
+def pack_kernel(hops, pos, dist, src_h, tab, near, *refs):
+    far, (src, sem) = refs[:-2], refs[-2:]
+    load = pltpu.make_async_copy(src_h, src, sem)
+    load.start()
     fill_tables(dist, tab, 1, hops, pos)
-    for copy in pack(Copies(sems), src, tab, far, near, hops, pos):
-        copy.wait()
+    load.wait()
+    pack(src, tab, far, near, hops, pos)
 
 
 def act_kernel(hops, pos, dist, *refs):
@@ -209,60 +198,60 @@
         put(first, send)
 
 
-def upper_kernel(hops, pos, dist, tab1, tab0, src_h, wo3_h, wi3_h, slope_h, near_in, *refs):
+def fetch(sems, refs, count):
+    loads = [pltpu.make_async_copy(refs[n], refs[count + n], sems.at[n]) for n in range(count)]
+    for load in loads:
+        load.start()
+    for load in loads:
+        load.wait()
+    return refs[count:2 * count]
+
+
+def upper_kernel(hops, pos, dist, tab1, tab0, src, wo3, wi3, slope, near_in, *refs):
     far_in, refs = refs[:hops - 1], refs[hops - 1:]
     near, refs = refs[0], refs[1:]
     far, refs = refs[:hops - 1], refs[hops - 1:]
-    grad_h, gm_h, gh_h, src, wo3, wi3, slope, gm3, gh3, gm, grad, join, sems = refs
-    copies = Copies(sems)
-    loads = [copies.start(*pair) for pair in ((src_h, src), (wo3_h, wo3), (slope_h, slope), (wi3_h, wi3))]
-    loads[0].wait()
+    grad_h, gm_h, gh_h, grad, gm3, gh3, gm, join, sems = refs
     unpack(src, dist, tab1, 1, far_in, near_in, gm, join, hops, pos)
-    loads[1].wait()
-    loads[2].wait()
     hidden(pos, wo3, slope, gm, gm3, gh3)
-    stores = [copies.start(gm3.at[0:2 * D, :], gm_h), copies.start(gh3.at[0:2 * HID, :], gh_h)]
-    loads[3].wait()
+    stores = [
+        pltpu.make_async_copy(gm3.at[0:2 * D, :], gm_h, sems.at[0]),
+        pltpu.make_async_copy(gh3.at[0:2 * HID, :], gh_h, sems.at[1]),
+        pltpu.make_async_copy(grad, grad_h, sems.at[2]),
+    ]
+    stores[0].start()
+    stores[1].start()
     inward(pos, wi3, gm, gh3, grad)
-    stores = pack(copies, grad, tab0, far, near, hops, pos) + stores
-    stores.append(copies.start(grad, grad_h))
-    for copy in stores:
-        copy.wait()
-
-
-def terms_kernel(factor, odd, *refs):
-    held_ins, (keep, send), scratch, sems = refs[:4], refs[4:6], refs[6:10], refs[10]
-    copies = Copies(sems)
-    for copy in [copies.start(*pair) for pair in zip(held_ins, scratch)]:
-        copy.wait()
-    weight_terms(factor, odd[0], *scratch, keep, send)
-
-
-def lower_kernel(hops, pos, factor, odd, dist, tab0, src_h, wo3_h, slope_h, x2_h, h2_h, near_in, *refs):
+    stores[2].start()
+    pack(grad, tab0, far, near, hops, pos)
+    for store in stores:
+        store.wait()
+
+
+def terms_kernel(factor, odd, x2_h, gh_h, h2_h, gm_h, keep, send, x2, gh, h2, gm, sems):
+    fetch(sems, (x2_h, gh_h, h2_h, gm_h, x2, gh, h2, gm), 4)
+    weight_terms(factor, odd[0], x2, gh, h2, gm, keep, send)
+
+
+def lower_kernel(hops, pos, factor, odd, dist, tab0, wo3_h, src, slope, x2, h2, near_in, *refs):
     far_in, refs = refs[:hops - 1], refs[hops - 1:]
-    keep, send, gm_h, gh_h, src, wo3, slope, x2, h2, gm3, gh3, gm, join, sems = refs
-    copies = Copies(sems)
-    loads = [copies.start(*pair) for pair in ((src_h, src), (wo3_h, wo3), (slope_h, slope), (x2_h, x2), (h2_h, h2))]
-    loads[0].wait()
+    keep, send, gm_h, gh_h, gm, gh3, gm3, join, wo3, sems = refs
+    load = pltpu.make_async_copy(wo3_h, wo3, sems.at[2])
+    load.start()
     unpack(src, dist, tab0, 0, far_in, near_in, gm, join, hops, pos)
-    stores = [copies.start(gm, gm_h)]
-    loads[1].wait()
-    loads[2].wait()
+    stores = [pltpu.make_async_copy(gm, gm_h, sems.at[0]), pltpu.make_async_copy(gh3, gh_h, sems.at[1])]
+    stores[0].start()
+    load.wait()
     hidden(pos, wo3, slope, gm, gm3, gh3)
-    stores.append(copies.start(gh3, gh_h))
-    loads[3].wait()
-    loads[4].wait()
+    stores[1].start()
     weight_terms(factor, odd[0], x2, gh3, h2, gm3, keep, send)
-    for copy in stores:
-        copy.wait()
-
-
-def input_kernel(pos, *refs):
-    held_ins, out, scratch, sems = refs[:3], refs[3], refs[4:7], refs[7]
-    copies = Copies(sems)
-    for copy in [copies.start(*pair) for pair in zip(held_ins, scratch)]:
-        copy.wait()
-    inward(pos, *scratch, out)
+    for store in stores:
+        store.wait()
+
+
+def input_kernel(pos, wi3_h, gm_h, gh_h, out, wi3, gm, gh3, sems):
+    fetch(sems, (wi3_h, gm_h, gh_h, wi3, gm, gh3), 3)
+    inward(pos, wi3, gm, gh3, out)
 
 
 def finish_kernel(odd, *refs):
@@ -315,12 +304,16 @@
     return jax.ShapeDtypeStruct(dims, dtype)
 
 
-def stay(*values):
-    return [pltpu.with_memory_space_constraint(v, pltpu.HBM) for v in values]
+def stay(*values, where=pltpu.VMEM):
+    return [pltpu.with_memory_space_constraint(v, where) for v in values]
+
+
+def stored(*dims, dtype=f32):
+    return pltpu.HBM(dims, dtype)
 
 
 def held(*dims, dtype=f32):
-    return pltpu.HBM(dims, dtype)
+    return pltpu.VMEM(dims, dtype)
 
 
 def body(first_inputs, second_inputs, out_grad, weight_in, bias_in, weight_out, distances):
@@ -335,20 +328,23 @@
     masks = [1 << b for b in range(1, hops)]
     far_hops = [1 << k for k in range(1, hops)]
     odd = (lax.axis_index("seq") & 1).astype(i32).reshape(1)
-    copy_sems = pltpu.SemaphoreType.DMA((MOST * hops + INNER + 16,))
 
     def travel(near, far):
         moved = [from_ahead(f, h) for f, h in zip(far[::-1], far_hops[::-1])][::-1]
         return from_ahead(near, 1), moved
 
+    whole_s = pltpu.VMEM((D, pos), f32)
+    gm3_s = pltpu.VMEM((3 * D, pos), bf16)
+    join_s = pltpu.VMEM((INNER, TW, 2 * pos + LANES), f32)
+    distances, out_grad_h = [pltpu.with_memory_space_constraint(v, pltpu.HBM) for v in (distances, out_grad)]
     tab_1, near, *far = pl.pallas_call(
         lambda *refs: pack_kernel(hops, pos, *refs),
         out_shape=[shape(32, dtype=i32), near_shape] + far_shapes,
         in_specs=[SM, HB],
-        out_specs=[SM] + [HB] * hops,
-        scratch_shapes=[copy_sems],
-        **kernel_options("pack", 4, 2),
-    )(distances, *stay(out_grad))
+        out_specs=[SM] + [VM] * hops,
+        scratch_shapes=[whole_s, pltpu.SemaphoreType.DMA],
+        **kernel_options("pack", 3, 2),
+    )(distances, out_grad_h)
     near, far = travel(near, far)
 
     w_out_t = jnp.transpose(weight_out, (0, 2, 1))
@@ -356,41 +352,38 @@
     act_ins = []
     for layer in range(2):
         act_ins += [saved[layer], weight_in[layer], bias_in[layer][:, None], w_out_t[layer]]
-    act_shapes = [
-        held(2 * D + 32, pos, dtype=bf16),
-        held(2 * HID, pos, dtype=bf16),
-        held(HID, pos),
-        held(D, 3 * HID, dtype=bf16),
-        held(HID, 3 * D, dtype=bf16),
-    ]
+    def act_shapes(of):
+        return [
+            stored(2 * D + 32, pos, dtype=bf16),
+            stored(2 * HID, pos, dtype=bf16),
+            of(HID, pos),
+            of(D, 3 * HID, dtype=bf16),
+            of(HID, 3 * D, dtype=bf16),
+        ]
+
     tab_0, *acts = pl.pallas_call(
         lambda *refs: act_kernel(hops, pos, *refs),
-        out_shape=[shape(32, dtype=i32)] + act_shapes * 2,
+        out_shape=[shape(32, dtype=i32)] + act_shapes(stored) + act_shapes(held),
         in_specs=[SM] + [VM] * 8,
         out_specs=[SM] + [VM] * 10,
         scratch_shapes=[pltpu.VMEM((3 * D, 256), bf16)],
-        **kernel_options("act", 28, 5),
+        **kernel_options("act", 24, 5),
     )(distances, *act_ins)
     x2_0, h2_0, slope_0, wi3_0, wo3_0, x2_1, h2_1, slope_1, wi3_1, wo3_1 = acts
 
     x2_s = pltpu.VMEM((2 * D + 32, pos), bf16)
     h2_s = pltpu.VMEM((2 * HID, pos), bf16)
-    slope_s = pltpu.VMEM((HID, pos), f32)
-    wi3_s = pltpu.VMEM((D, 3 * HID), bf16)
-    wo3_s = pltpu.VMEM((HID, 3 * D), bf16)
-    gm3_s = pltpu.VMEM((3 * D, pos), bf16)
+    gm2_s = pltpu.VMEM((2 * D, pos), bf16)
     gh3_s = pltpu.VMEM((3 * HID, pos), bf16)
-    whole_s = pltpu.VMEM((D, pos), f32)
-    join_s = pltpu.VMEM((INNER, TW, 2 * pos + LANES), f32)
-
+    sems_s = pltpu.SemaphoreType.DMA((4,))
     near, *rest = pl.pallas_call(
         lambda *refs: upper_kernel(hops, pos, *refs),
-        out_shape=[near_shape] + far_shapes + [held(D, pos), held(2 * D, pos, dtype=bf16), held(2 * HID, pos, dtype=bf16)],
-        in_specs=[SM] * 3 + [HB] * 4 + [VM] * hops,
-        out_specs=[HB] * (hops + 3),
-        scratch_shapes=[whole_s, wo3_s, wi3_s, slope_s, gm3_s, gh3_s, whole_s, whole_s, join_s, copy_sems],
-        **kernel_options("upper", 24, 5),
-    )(distances, tab_1, tab_0, *stay(out_grad, wo3_1, wi3_1, slope_1), near, *far)
+        out_shape=[near_shape] + far_shapes + [stored(D, pos), stored(2 * D, pos, dtype=bf16), stored(2 * HID, pos, dtype=bf16)],
+        in_specs=[SM] * 3 + [VM] * (hops + 4),
+        out_specs=[VM] * hops + [HB] * 3,
+        scratch_shapes=[whole_s, gm3_s, gh3_s, whole_s, join_s, sems_s],
+        **kernel_options("upper", 14, 5),
+    )(distances, tab_1, tab_0, out_grad, *stay(wo3_1, wi3_1, slope_1), near, *far)
     far, (grad_1, gm2_1, gh2_1) = rest[:hops - 1], rest[hops - 1:]
     near, far = travel(near, far)
 
@@ -399,21 +392,20 @@
         out_shape=[shape(half, LANES)] * 2,
         in_specs=[SM] + [HB] * 4,
         out_specs=[VM] * 2,
-        scratch_shapes=[x2_s, pltpu.VMEM((2 * HID, pos), bf16), h2_s, pltpu.VMEM((2 * D, pos), bf16), copy_sems],
-        **kernel_options("terms", 16, 0.001),
-    )(odd, *stay(x2_1, gh2_1, h2_1, gm2_1))
+        scratch_shapes=[x2_s, h2_s, h2_s, gm2_s, sems_s],
+        **kernel_options("terms", 14, 0.001),
+    )(odd, *stay(x2_1, gh2_1, h2_1, gm2_1, where=pltpu.HBM))
     send_1, near, far = lax.optimization_barrier((send_1, near, far))
     sum_1 = keep_1 + exchange(send_1, 1)
 
     keep, send, gm_0, gh3_0 = pl.pallas_call(
         lambda *refs: lower_kernel(hops, pos, factor, *refs),
-        out_shape=[shape(half, LANES)] * 2 + [held(D, pos), held(3 * HID, pos, dtype=bf16)],
-        in_specs=[SM] * 3 + [HB] * 5 + [VM] * hops,
+        out_shape=[shape(half, LANES)] * 2 + [stored(D, pos), stored(3 * HID, pos, dtype=bf16)],
+        in_specs=[SM] * 3 + [HB] + [VM] * (hops + 4),
         out_specs=[VM] * 2 + [HB] * 2,
-        scratch_shapes=[whole_s, wo3_s, slope_s, x2_s, h2_s, gm3_s, gh3_s, whole_s, join_s, copy_sems],
-        **kernel_options("lower", 24, 5),
-    )(odd, distances, tab_0, *stay(grad_1, wo3_0, slope_0, x2_0, h2_0), near, *far)
-
+        scratch_shapes=[whole_s, gh3_s, gm3_s, join_s, pltpu.VMEM((HID, 3 * D), bf16), sems_s],
+        **kernel_options("lower", 16, 5),
+    )(odd, distances, tab_0, *stay(wo3_0, where=pltpu.HBM), grad_1, slope_0, x2_0, h2_0, near, *far)
     sum_0 = keep + exchange(send, 1)
     sum_0, gm_0 = lax.optimization_barrier((sum_0, gm_0))
 
@@ -422,10 +414,9 @@
         out_shape=shape(D, pos),
         in_specs=[HB] * 3,
         out_specs=VM,
-        scratch_shapes=[wi3_s, whole_s, gh3_s, copy_sems],
+        scratch_shapes=[pltpu.VMEM((D, 3 * HID), bf16), whole_s, gh3_s, sems_s],
         **kernel_options("inward", 12, 3),
-    )(*stay(wi3_0, gm_0, gh3_0))
-
+    )(*stay(wi3_0, gm_0, gh3_0, where=pltpu.HBM))
     for number, mask in enumerate(masks):
         sum_1 = fold(sum_1, mask)
         if number == 1:
@@ -442,7 +433,7 @@
         out_shape=[shape(2, D, HID), shape(2, HID), shape(2, D, HID)],
         in_specs=[SM] + [VM] * 4,
         out_specs=[VM] * 3,
-        **kernel_options("finish", 12, 1),
+        **kernel_options("finish", 4, 1),
     )(odd, sum_0, other_0, sum_1, other_1)
     return input_grad, w_in_grad, bias_grad, jnp.transpose(w_out_t_grad, (0, 2, 1))
 

time: 115 us -> 111 us (0.965)
  Pallas kernels: 37.1 us -> 32.7 us
    pallas_call x1, Pallas kernels: 8.04 us -> 6.12 us  [body(): pl.pallas_call(lambda *refs: upper_kernel(hops, pos, *refs), out_shape=[n...]
  transfers between devices with their start and end apart: 24 -> 24, of which waited for: 16 -> 16; matrix products, arithmetic and copies ran while one was open for 3% -> 3% of each run, Pallas kernels for 21% -> 20%
where the time goes in v3:
time: 111 us
  starting transfers between devices  39.9 us (36%)
  waiting for transfers between devices  33.2 us (30%)
  Pallas kernels  32.7 us (29%)
  local copies, waits for them, and re-layouts  2.19 us (2%)
  other arithmetic  1.59 us (1%)
    ppermute x16, starting transfers between devices, exchange(): return lax.ppermute(value, 'seq', [(s, s ^ mask) for s in range(count)])  27.8 us
    ppermute x8, waiting for transfers between devices, from_ahead(): lax.ppermute(value, 'seq', [(s, (s - steps) % count) for s in range(count)])  20.9 us
    ppermute x16, waiting for transfers between devices, exchange(): return lax.ppermute(value, 'seq', [(s, s ^ mask) for s in range(count)])  12.3 us
    ppermute x8, starting transfers between devices, from_ahead(): lax.ppermute(value, 'seq', [(s, (s - steps) % count) for s in range(count)])  12.1 us
    pallas_call x1, Pallas kernels, body(): pl.pallas_call(lambda *refs: act_kernel(hops, pos, *refs), out_shape=[sha...  7.25 us
    pallas_call x1, Pallas kernels, body(): pl.pallas_call(lambda *refs: lower_kernel(hops, pos, factor, *refs), out_...  6.21 us
    pallas_call x1, Pallas kernels, body(): pl.pallas_call(lambda *refs: upper_kernel(hops, pos, *refs), out_shape=[n...  6.12 us
    pallas_call x1, Pallas kernels, body(): pl.pallas_call(lambda *refs: terms_kernel(factor, *refs), out_shape=[shap...  4.89 us
  transfers between devices with their start and end apart: 24, of which 16 were waited for; matrix products, arithmetic and copies ran while one was open for 3% of the time, Pallas kernels for 20%

profile of v3, /device:TPU:0, one launch (start us, length us, event | category | flops | bytes accessed | tf_op | source)
XLA Modules:
  0.0 110.6 jit_solution(6159952551397246969)
XLA Ops:
  0.7 2.7 %pack.1 = (s32[32]{0:T(128)S(1)}, f32[16,6144]{1,0:T(8,128)S(1)}, f32[48,1024]{1,0:T(8,128)S(1)}, f32[48,1024]{1,0:T(8,128)S(1)}, f32[48,1024]{1,0:T(8,128)S(1)}) custom-call(s32[2,18]{1,0:T(2,128)} %refs_1_.5, f32[288,1024]{1,0:T(8,128)} %refs_3_.1), custom_call_target="tpu_custom_call" | custom-call | flops 2000000000 | bytes 6000000 | tf_op jit(solution)/shard_map/pack/pallas_call | solution.py:340
  3.4 5.5 %collective-permute-start = (f32[16,6144]{1,0:T(8,128)S(1)}, f32[16,6144]{1,0:T(8,128)S(1)}, u32[]{:S(2)}, u32[]{:S(2)}) collective-permute-start(f32[16,6144]{1,0:T(8,128)S(1)} %get-tuple-element.51), channel_id=1, source_target_pairs={{0,15},{1,0},{2,1},{3,2},{4,3},{5,4},{6,5},{7,6},{8,7},{9,8},{10,9... | collective-permute-start | bytes 1179656 | tf_op jit(solution)/shard_map/ppermute | solution.py:282
  8.8 0.6 collective-permute-start.1
  9.5 0.4 collective-permute-start.2
  9.9 0.1 copy.11.refs_3_
  10.1 0.1 copy.12.refs_7_
  10.3 1.5 %slice_bitcast_fusion = (f32[288,384]{1,0:T(8,128)S(1)}, f32[288,384]{1,0:T(8,128)S(1)}, f32[288,384]{1,0:T(8,128)S(1)}, f32[288,384]{1,0:T(8,128)S(1)}) fusion(f32[2,288,384]{2,1,0:T(8,128)S(1)} %bitcast.15, f32[2,288,384]{2,1,0:T(8,128)} %param.10), kind=kLoop, calls=%fused_computation.2 | loop fusion | bytes 3538944 | tf_op jit(solution)/shard_map/squeeze | solution.py:354
  11.8 0.4 copy-done.1
  12.1 7.2 %act.1 = (s32[32]{0:T(128)S(1)}, bf16[608,1024]{1,0:T(8,128)(2,1)}, bf16[768,1024]{1,0:T(8,128)(2,1)}, f32[384,1024]{1,0:T(8,128)}, bf16[288,1152]{1,0:T(8,128)(...) custom-call(s32[2,18]{1,0:T(2,128)} %refs_1_.5, ...), custom_call_target="tpu_custom_call" | custom-call | flops 5000000000 | bytes 15000000 | tf_op jit(solution)/shard_map/act/pallas_call | solution.py:364
  19.4 3.1 %collective-permute-done.1.refs_8_ = f32[48,1024]{1,0:T(8,128)S(1)} collective-permute-done((f32[48,1024]{1,0:T(8,128)S(1)}, f32[48,1024]{1,0:T(8,128)S(1)}, u32[]{:S(2)}, u32[]{:S(2)}) %collective-permute-start.1) | collective-permute-done | bytes 196640 | tf_op jit(solution)/shard_map/ppermute | solution.py:282
  22.5 2.2 %collective-permute-done.2.refs_9_ = f32[48,1024]{1,0:T(8,128)S(1)} collective-permute-done((f32[48,1024]{1,0:T(8,128)S(1)}, f32[48,1024]{1,0:T(8,128)S(1)}, u32[]{:S(2)}, u32[]{:S(2)}) %collective-permute-start.2) | collective-permute-done | bytes 196640 | tf_op jit(solution)/shard_map/ppermute | solution.py:282
  24.7 6.2 %collective-permute-done.3.refs_10_ = f32[48,1024]{1,0:T(8,128)S(1)} collective-permute-done((f32[48,1024]{1,0:T(8,128)S(1)}, f32[48,1024]{1,0:T(8,128)S(1)}, u32[]{:S(2)}, u32[]{:S(2)}) %collective-permute-start.3) | collective-permute-done | bytes 196640 | tf_op jit(solution)/shard_map/ppermute | solution.py:282
  30.9 6.1 %upper.1 = (f32[16,6144]{1,0:T(8,128)S(1)}, f32[48,1024]{1,0:T(8,128)S(1)}, f32[48,1024]{1,0:T(8,128)S(1)}, f32[48,1024]{1,0:T(8,128)S(1)}, f32[288,1024]{1,0:T(...) custom-call(s32[2,18]{1,0:T(2,128)} %refs_1_.5, s32[32]{0:T(128)S(1)} %get-tuple-element.47.refs_1_, ...), custom_call_target="tpu_custom_call" | custom-call | flops 5000000000 | bytes 15000000 | tf_op jit(solution)/shard_map/upper/pallas_call | solution.py:379
  37.0 0.1 collective-permute-start.4
  37.1 5.5 %collective-permute-start.5 = (f32[48,1024]{1,0:T(8,128)S(1)}, f32[48,1024]{1,0:T(8,128)S(1)}, u32[]{:S(2)}, u32[]{:S(2)}) collective-permute-start(f32[48,1024]{1,0:T(8,128)S(1)} %get-tuple-element.65), channel_id=1, source_target_pairs={{0,14},{1,15},{2,0},{3,1},{4,2},{5,3},{6,4},{7,5},{8,6},{9,7},{10,... | collective-permute-start | bytes 589832 | tf_op jit(solution)/shard_map/ppermute | solution.py:282
  42.6 4.9 %terms.1 = (f32[896,128]{1,0:T(8,128)S(1)}, f32[896,128]{1,0:T(8,128)S(1)}) custom-call(s32[1]{0:T(128)} %bitcast.refs_0_.odd, bf16[608,1024]{1,0:T(8,128)(2,1)} %get-tuple-element.59.refs_1_, bf16[768,1024]{1,0:T(8,128)(2,1)} %get-tuple-element.60.refs_2_, bf16[768,1024]{1,0:T(8,128)(2,1)} %get-tuple-element.61.refs_3_, ...), custom_call_target="tpu_custom_call" | custom-call | flops 1000000 | bytes 3000 | tf_op jit(solution)/shard_map/terms/pallas_call | solution.py:390
  47.5 3.2 %collective-permute-done.5.refs_9_ = f32[48,1024]{1,0:T(8,128)S(1)} collective-permute-done((f32[48,1024]{1,0:T(8,128)S(1)}, f32[48,1024]{1,0:T(8,128)S(1)}, u32[]{:S(2)}, u32[]{:S(2)}) %collective-permute-start.5) | collective-permute-done | bytes 196640 | tf_op jit(solution)/shard_map/ppermute | solution.py:282
  50.7 4.5 %collective-permute-done.6.refs_10_ = f32[48,1024]{1,0:T(8,128)S(1)} collective-permute-done((f32[48,1024]{1,0:T(8,128)S(1)}, f32[48,1024]{1,0:T(8,128)S(1)}, u32[]{:S(2)}, u32[]{:S(2)}) %collective-permute-start.6) | collective-permute-done | bytes 196640 | tf_op jit(solution)/shard_map/ppermute | solution.py:282
  55.2 1.8 %collective-permute-done.7.refs_11_ = f32[48,1024]{1,0:T(8,128)S(1)} collective-permute-done((f32[48,1024]{1,0:T(8,128)S(1)}, f32[48,1024]{1,0:T(8,128)S(1)}, u32[]{:S(2)}, u32[]{:S(2)}) %collective-permute-start.7) | collective-permute-done | bytes 196640 | tf_op jit(solution)/shard_map/ppermute | solution.py:282
  57.0 6.2 %lower.1 = (f32[896,128]{1,0:T(8,128)S(1)}, f32[896,128]{1,0:T(8,128)S(1)}, f32[288,1024]{1,0:T(8,128)}, bf16[1152,1024]{1,0:T(8,128)(2,1)}) custom-call(s32[1]{0:T(128)} %bitcast.refs_0_.odd, s32[2,18]{1,0:T(2,128)} %refs_1_.5, s32[32]{0:T(128)S(1)} %get-tuple-element.45.refs_2_, bf16[384,864]{1,0:T(8,128)(2,1)} %get-tuple-element.46.refs_3_, ...), custom_call_target="tpu_custom_call" | custom-call | flops 5000000000 | bytes 15000000 | tf_op jit(solution)/shard_map/lower/pallas_call | solution.py:401
  63.2 0.6 collective-permute-start.8
  63.8 1.1 add.28
  64.9 0.1 collective-permute-start.17
  64.9 0.3 collective-permute-done.8
  65.3 1.8 %collective-permute-start.9 = (f32[448,128]{1,0:T(8,128)S(1)}, f32[448,128]{1,0:T(8,128)S(1)}, u32[]{:S(2)}, u32[]{:S(2)}) collective-permute-start(f32[448,128]{1,0:T(8,128)S(1)} %slice_select_fusion.1), channel_id=1, source_target_pairs={{0,2},{1,3},{2,0},{3,1},{4,6},{5,7},{6,4},{7,5},{8,10},{9,11},{10,... | collective-permute-start | bytes 688136 | tf_op jit(solution)/shard_map/ppermute | solution.py:287
  67.1 4.2 %inward.1 = f32[288,1024]{1,0:T(8,128)} custom-call(bf16[288,1152]{1,0:T(8,128)(2,1)} %get-tuple-element.76.refs_0_, f32[288,1024]{1,0:T(8,128)} %get-tuple-element.77.refs_1_, bf16[1152,1024]{1,0:T(8,128)(2,1)} %get-tuple-element.78.refs_2_), custom_call_target="tpu_custom_call" | custom-call | flops 3000000000 | bytes 9000000 | tf_op jit(solution)/shard_map/inward/pallas_call | solution.py:412
  71.3 2.1 %collective-permute-done.17 = f32[448,128]{1,0:T(8,128)S(1)} collective-permute-done((f32[448,128]{1,0:T(8,128)S(1)}, f32[448,128]{1,0:T(8,128)S(1)}, u32[]{:S(2)}, u32[]{:S(2)}) %collective-permute-start.17) | collective-permute-done | bytes 229408 | tf_op jit(solution)/shard_map/ppermute | solution.py:287
  73.4 3.6 %collective-permute-start.18 = (f32[224,128]{1,0:T(8,128)S(1)}, f32[224,128]{1,0:T(8,128)S(1)}, u32[]{:S(2)}, u32[]{:S(2)}) collective-permute-start(f32[224,128]{1,0:T(8,128)S(1)} %slice_select_fusion.2), channel_id=1, source_target_pairs={{0,4},{1,5},{2,6},{3,7},{4,0},{5,1},{6,2},{7,3},{8,12},{9,13},{10,... | collective-permute-start | bytes 344072 | tf_op jit(solution)/shard_map/ppermute | solution.py:287
  77.1 0.3 collective-permute-done.9
  77.4 3.6 %collective-permute-start.10 = (f32[224,128]{1,0:T(8,128)S(1)}, f32[224,128]{1,0:T(8,128)S(1)}, u32[]{:S(2)}, u32[]{:S(2)}) collective-permute-start(f32[224,128]{1,0:T(8,128)S(1)} %slice_select_fusion.3), channel_id=1, source_target_pairs={{0,4},{1,5},{2,6},{3,7},{4,0},{5,1},{6,2},{7,3},{8,12},{9,13},{10,... | collective-permute-start | bytes 344072 | tf_op jit(solution)/shard_map/ppermute | solution.py:287
  81.1 3.4 %collective-permute-start.19 = (f32[112,128]{1,0:T(8,128)S(1)}, f32[112,128]{1,0:T(8,128)S(1)}, u32[]{:S(2)}, u32[]{:S(2)}) collective-permute-start(f32[112,128]{1,0:T(8,128)S(1)} %slice_select_fusion.4), channel_id=1, source_target_pairs={{0,8},{1,9},{2,10},{3,11},{4,12},{5,13},{6,14},{7,15},{8,0},{9,1},... | collective-permute-start | bytes 172040 | tf_op jit(solution)/shard_map/ppermute | solution.py:287
  84.6 3.1 %collective-permute-start.11 = (f32[112,128]{1,0:T(8,128)S(1)}, f32[112,128]{1,0:T(8,128)S(1)}, u32[]{:S(2)}, u32[]{:S(2)}) collective-permute-start(f32[112,128]{1,0:T(8,128)S(1)} %slice_select_fusion.5), channel_id=1, source_target_pairs={{0,8},{1,9},{2,10},{3,11},{4,12},{5,13},{6,14},{7,15},{8,0},{9,1},... | collective-permute-start | bytes 172040 | tf_op jit(solution)/shard_map/ppermute | solution.py:287
  87.7 2.5 %collective-permute-start.20 = (f32[112,128]{1,0:T(8,128)S(1)}, f32[112,128]{1,0:T(8,128)S(1)}, u32[]{:S(2)}, u32[]{:S(2)}) collective-permute-start(f32[112,128]{1,0:T(8,128)S(1)} %select_add_fusion.4), channel_id=1, source_target_pairs={{0,8},{1,9},{2,10},{3,11},{4,12},{5,13},{6,14},{7,15},{8,0},{9,1},... | collective-permute-start | bytes 172040 | tf_op jit(solution)/shard_map/ppermute | solution.py:287
  90.2 2.6 %collective-permute-start.12 = (f32[112,128]{1,0:T(8,128)S(1)}, f32[112,128]{1,0:T(8,128)S(1)}, u32[]{:S(2)}, u32[]{:S(2)}) collective-permute-start(f32[112,128]{1,0:T(8,128)S(1)} %select_add_fusion.5), channel_id=1, source_target_pairs={{0,8},{1,9},{2,10},{3,11},{4,12},{5,13},{6,14},{7,15},{8,0},{9,1},... | collective-permute-start | bytes 172040 | tf_op jit(solution)/shard_map/ppermute | solution.py:287
  92.9 1.0 collective-permute-done.20
  93.9 1.1 %collective-permute-start.21 = (f32[224,128]{1,0:T(8,128)S(1)}, f32[224,128]{1,0:T(8,128)S(1)}, u32[]{:S(2)}, u32[]{:S(2)}) collective-permute-start(f32[224,128]{1,0:T(8,128)S(1)} %pad_maximum_fusion.5), channel_id=1, source_target_pairs={{0,4},{1,5},{2,6},{3,7},{4,0},{5,1},{6,2},{7,3},{8,12},{9,13},{10,... | collective-permute-start | bytes 344072 | tf_op jit(solution)/shard_map/ppermute | solution.py:287
  95.0 0.4 collective-permute-done.12
  95.4 1.7 %collective-permute-start.13 = (f32[224,128]{1,0:T(8,128)S(1)}, f32[224,128]{1,0:T(8,128)S(1)}, u32[]{:S(2)}, u32[]{:S(2)}) collective-permute-start(f32[224,128]{1,0:T(8,128)S(1)} %pad_maximum_fusion.4), channel_id=1, source_target_pairs={{0,4},{1,5},{2,6},{3,7},{4,0},{5,1},{6,2},{7,3},{8,12},{9,13},{10,... | collective-permute-start | bytes 344072 | tf_op jit(solution)/shard_map/ppermute | solution.py:287
  97.2 1.6 %collective-permute-done.21 = f32[224,128]{1,0:T(8,128)S(1)} collective-permute-done((f32[224,128]{1,0:T(8,128)S(1)}, f32[224,128]{1,0:T(8,128)S(1)}, u32[]{:S(2)}, u32[]{:S(2)}) %collective-permute-start.21) | collective-permute-done | bytes 114720 | tf_op jit(solution)/shard_map/ppermute | solution.py:287
  98.8 1.3 %collective-permute-start.22 = (f32[448,128]{1,0:T(8,128)S(1)}, f32[448,128]{1,0:T(8,128)S(1)}, u32[]{:S(2)}, u32[]{:S(2)}) collective-permute-start(f32[448,128]{1,0:T(8,128)S(1)} %pad_maximum_fusion.3), channel_id=1, source_target_pairs={{0,2},{1,3},{2,0},{3,1},{4,6},{5,7},{6,4},{7,5},{8,10},{9,11},{10,... | collective-permute-start | bytes 688136 | tf_op jit(solution)/shard_map/ppermute | solution.py:287
  100.1 0.2 collective-permute-done.13
  100.3 2.0 %collective-permute-start.14 = (f32[448,128]{1,0:T(8,128)S(1)}, f32[448,128]{1,0:T(8,128)S(1)}, u32[]{:S(2)}, u32[]{:S(2)}) collective-permute-start(f32[448,128]{1,0:T(8,128)S(1)} %pad_maximum_fusion.2), channel_id=1, source_target_pairs={{0,2},{1,3},{2,0},{3,1},{4,6},{5,7},{6,4},{7,5},{8,10},{9,11},{10,... | collective-permute-start | bytes 688136 | tf_op jit(solution)/shard_map/ppermute | solution.py:287
  102.4 2.5 %collective-permute-done.22 = f32[448,128]{1,0:T(8,128)S(1)} collective-permute-done((f32[448,128]{1,0:T(8,128)S(1)}, f32[448,128]{1,0:T(8,128)S(1)}, u32[]{:S(2)}, u32[]{:S(2)}) %collective-permute-start.22) | collective-permute-done | bytes 229408 | tf_op jit(solution)/shard_map/ppermute | solution.py:287
  105.0 0.1 collective-permute-start.23
  105.0 2.3 %collective-permute-done.14 = f32[448,128]{1,0:T(8,128)S(1)} collective-permute-done((f32[448,128]{1,0:T(8,128)S(1)}, f32[448,128]{1,0:T(8,128)S(1)}, u32[]{:S(2)}, u32[]{:S(2)}) %collective-permute-start.14) | collective-permute-done | bytes 229408 | tf_op jit(solution)/shard_map/ppermute | solution.py:287
  107.4 0.1 collective-permute-start.15
  107.5 1.8 %collective-permute-done.15.refs_1_ = f32[896,128]{1,0:T(8,128)S(1)} collective-permute-done((f32[896,128]{1,0:T(8,128)S(1)}, f32[896,128]{1,0:T(8,128)S(1)}, u32[]{:S(2)}, u32[]{:S(2)}) %collective-permute-start.15) | collective-permute-done | bytes 458784 | tf_op jit(solution)/shard_map/ppermute | solution.py:287
  109.3 1.3 %finish.1 = (f32[2,288,384]{2,1,0:T(8,128)}, f32[2,384]{1,0:T(2,128)}, f32[2,288,384]{2,1,0:T(8,128)}) custom-call(s32[1]{0:T(128)} %bitcast.refs_0_.odd, f32[896,128]{1,0:T(8,128)S(1)} %pad_maximum_fusion.refs_0_, f32[896,128]{1,0:T(8,128)S(1)} %collective-permute-done.15.refs_1_, f32[896,128]{1,0:T(8,128)S(1)} %pad_maximum_fusion.1.refs_2_, ...), custom_call_target="tpu_custom_call" | custom-call | flops 1000000000 | bytes 3000000 | tf_op jit(solution)/shard_map/finish/pallas_call | solution.py:431
  (55 shorter events, 0.6 us)
Async XLA Ops:
  0.6 9.3 %copy-start.8 = (f32[2,384]{1,0:T(2,128)S(1)}, f32[2,384]{1,0:T(2,128)}, u32[]{:S(2)}) copy-start(f32[2,384]{1,0:T(2,128)} %param.11) | copy-start | bytes 9220
  0.6 9.6 %copy-start.7 = (f32[2,384,288]{1,2,0:T(8,128)S(1)}, f32[2,384,288]{1,2,0:T(8,128)}, u32[]{:S(2)}) copy-start(f32[2,384,288]{1,2,0:T(8,128)} %param.12) | copy-start | bytes 2654212
  3.4 27.5 %collective-permute-start = (f32[16,6144]{1,0:T(8,128)S(1)}, f32[16,6144]{1,0:T(8,128)S(1)}, u32[]{:S(2)}, u32[]{:S(2)}) collective-permute-start(f32[16,6144]{1,0:T(8,128)S(1)} %get-tuple-element.51), channel_id=1, source_target_pairs={{0,15},{1,0},{2,1},{3,2},{4,3},{5,4},{6,5},{7,6},{8,7},{9,8},{10,9... | collective-permute-start | bytes 1179656 | tf_op jit(solution)/shard_map/ppermute | solution.py:282
  8.8 13.7 %collective-permute-start.1 = (f32[48,1024]{1,0:T(8,128)S(1)}, f32[48,1024]{1,0:T(8,128)S(1)}, u32[]{:S(2)}, u32[]{:S(2)}) collective-permute-start(f32[48,1024]{1,0:T(8,128)S(1)} %get-tuple-element.52), channel_id=1, source_target_pairs={{0,14},{1,15},{2,0},{3,1},{4,2},{5,3},{6,4},{7,5},{8,6},{9,7},{10,... | collective-permute-start | bytes 589832 | tf_op jit(solution)/shard_map/ppermute | solution.py:282
  9.5 15.2 %collective-permute-start.2 = (f32[48,1024]{1,0:T(8,128)S(1)}, f32[48,1024]{1,0:T(8,128)S(1)}, u32[]{:S(2)}, u32[]{:S(2)}) collective-permute-start(f32[48,1024]{1,0:T(8,128)S(1)} %get-tuple-element.53), channel_id=1, source_target_pairs={{0,12},{1,13},{2,14},{3,15},{4,0},{5,1},{6,2},{7,3},{8,4},{9,5},{1... | collective-permute-start | bytes 589832 | tf_op jit(solution)/shard_map/ppermute | solution.py:282
  9.9 21.0 %collective-permute-start.3 = (f32[48,1024]{1,0:T(8,128)S(1)}, f32[48,1024]{1,0:T(8,128)S(1)}, u32[]{:S(2)}, u32[]{:S(2)}) collective-permute-start(f32[48,1024]{1,0:T(8,128)S(1)} %get-tuple-element.54), channel_id=1, source_target_pairs={{0,8},{1,9},{2,10},{3,11},{4,12},{5,13},{6,14},{7,15},{8,0},{9,1},... | collective-permute-start | bytes 589832 | tf_op jit(solution)/shard_map/ppermute | solution.py:282
  10.2 1.5 %copy-start = (f32[288,1024]{1,0:T(8,128)S(1)}, f32[288,1024]{1,0:T(8,128)}, u32[]{:S(2)}) copy-start(f32[288,1024]{1,0:T(8,128)} %refs_1_.3) | copy-start | bytes 3538948
  10.3 1.9 %copy-start.1 = (f32[288,1024]{1,0:T(8,128)S(1)}, f32[288,1024]{1,0:T(8,128)}, u32[]{:S(2)}) copy-start(f32[288,1024]{1,0:T(8,128)} %refs_5_.1) | copy-start | bytes 3538948
  12.1 18.8 %copy-start.2 = (f32[288,1024]{1,0:T(8,128)S(1)}, f32[288,1024]{1,0:T(8,128)}, u32[]{:S(2)}) copy-start(f32[288,1024]{1,0:T(8,128)} %refs_3_.1) | copy-start | bytes 3538948
  37.0 19.9 %collective-permute-start.4 = (f32[16,6144]{1,0:T(8,128)S(1)}, f32[16,6144]{1,0:T(8,128)S(1)}, u32[]{:S(2)}, u32[]{:S(2)}) collective-permute-start(f32[16,6144]{1,0:T(8,128)S(1)} %get-tuple-element.64), channel_id=1, source_target_pairs={{0,15},{1,0},{2,1},{3,2},{4,3},{5,4},{6,5},{7,6},{8,7},{9,8},{10,9... | collective-permute-start | bytes 1179656 | tf_op jit(solution)/shard_map/ppermute | solution.py:282
  37.1 13.6 %collective-permute-start.5 = (f32[48,1024]{1,0:T(8,128)S(1)}, f32[48,1024]{1,0:T(8,128)S(1)}, u32[]{:S(2)}, u32[]{:S(2)}) collective-permute-start(f32[48,1024]{1,0:T(8,128)S(1)} %get-tuple-element.65), channel_id=1, source_target_pairs={{0,14},{1,15},{2,0},{3,1},{4,2},{5,3},{6,4},{7,5},{8,6},{9,7},{10,... | collective-permute-start | bytes 589832 | tf_op jit(solution)/shard_map/ppermute | solution.py:282
  42.6 12.6 %collective-permute-start.6 = (f32[48,1024]{1,0:T(8,128)S(1)}, f32[48,1024]{1,0:T(8,128)S(1)}, u32[]{:S(2)}, u32[]{:S(2)}) collective-permute-start(f32[48,1024]{1,0:T(8,128)S(1)} %get-tuple-element.66), channel_id=1, source_target_pairs={{0,12},{1,13},{2,14},{3,15},{4,0},{5,1},{6,2},{7,3},{8,4},{9,5},{1... | collective-permute-start | bytes 589832 | tf_op jit(solution)/shard_map/ppermute | solution.py:282
  42.6 14.4 %collective-permute-start.7 = (f32[48,1024]{1,0:T(8,128)S(1)}, f32[48,1024]{1,0:T(8,128)S(1)}, u32[]{:S(2)}, u32[]{:S(2)}) collective-permute-start(f32[48,1024]{1,0:T(8,128)S(1)} %get-tuple-element.67), channel_id=1, source_target_pairs={{0,8},{1,9},{2,10},{3,11},{4,12},{5,13},{6,14},{7,15},{8,0},{9,1},... | collective-permute-start | bytes 589832 | tf_op jit(solution)/shard_map/ppermute | solution.py:282
  42.6 14.4 %copy-start.3 = (bf16[768,1024]{1,0:T(8,128)(2,1)S(1)}, bf16[768,1024]{1,0:T(8,128)(2,1)}, u32[]{:S(2)}) copy-start(bf16[768,1024]{1,0:T(8,128)(2,1)} %get-tuple-element.58.refs_7_) | copy-start | bytes 4718596
  42.6 14.4 %copy-start.4 = (f32[384,1024]{1,0:T(8,128)S(1)}, f32[384,1024]{1,0:T(8,128)}, u32[]{:S(2)}) copy-start(f32[384,1024]{1,0:T(8,128)} %get-tuple-element.56.refs_5_) | copy-start | bytes 4718596
  42.6 14.4 %copy-start.5 = (bf16[608,1024]{1,0:T(8,128)(2,1)S(1)}, bf16[608,1024]{1,0:T(8,128)(2,1)}, u32[]{:S(2)}) copy-start(bf16[608,1024]{1,0:T(8,128)(2,1)} %get-tuple-element.57.refs_6_) | copy-start | bytes 3735556
  42.6 14.4 %copy-start.6 = (f32[288,1024]{1,0:T(8,128)S(1)}, f32[288,1024]{1,0:T(8,128)}, u32[]{:S(2)}) copy-start(f32[288,1024]{1,0:T(8,128)} %get-tuple-element.55.refs_4_) | copy-start | bytes 3538948
  56.9 6.8 %collective-permute-start.16 = (f32[896,128]{1,0:T(8,128)S(1)}, f32[896,128]{1,0:T(8,128)}, u32[]{:S(2)}, u32[]{:S(2)}) collective-permute-start(f32[896,128]{1,0:T(8,128)S(1)} %get-tuple-element.82), channel_id=1, source_target_pairs={{0,1},{1,0},{2,3},{3,2},{4,5},{5,4},{6,7},{7,6},{8,9},{9,8},{10,11... | collective-permute-start | bytes 1376264 | tf_op jit(solution)/shard_map/ppermute | solution.py:287
  63.2 2.0 %collective-permute-start.8 = (f32[896,128]{1,0:T(8,128)S(1)}, f32[896,128]{1,0:T(8,128)S(1)}, u32[]{:S(2)}, u32[]{:S(2)}) collective-permute-start(f32[896,128]{1,0:T(8,128)S(1)} %get-tuple-element.73), channel_id=1, source_target_pairs={{0,1},{1,0},{2,3},{3,2},{4,5},{5,4},{6,7},{7,6},{8,9},{9,8},{10,11... | collective-permute-start | bytes 1376264 | tf_op jit(solution)/shard_map/ppermute | solution.py:287
  64.9 8.5 %collective-permute-start.17 = (f32[448,128]{1,0:T(8,128)S(1)}, f32[448,128]{1,0:T(8,128)S(1)}, u32[]{:S(2)}, u32[]{:S(2)}) collective-permute-start(f32[448,128]{1,0:T(8,128)S(1)} %slice_select_fusion), channel_id=1, source_target_pairs={{0,2},{1,3},{2,0},{3,1},{4,6},{5,7},{6,4},{7,5},{8,10},{9,11},{10,... | collective-permute-start | bytes 688136 | tf_op jit(solution)/shard_map/ppermute | solution.py:287
  65.3 12.1 %collective-permute-start.9 = (f32[448,128]{1,0:T(8,128)S(1)}, f32[448,128]{1,0:T(8,128)S(1)}, u32[]{:S(2)}, u32[]{:S(2)}) collective-permute-start(f32[448,128]{1,0:T(8,128)S(1)} %slice_select_fusion.1), channel_id=1, source_target_pairs={{0,2},{1,3},{2,0},{3,1},{4,6},{5,7},{6,4},{7,5},{8,10},{9,11},{10,... | collective-permute-start | bytes 688136 | tf_op jit(solution)/shard_map/ppermute | solution.py:287
  73.4 7.6 %collective-permute-start.18 = (f32[224,128]{1,0:T(8,128)S(1)}, f32[224,128]{1,0:T(8,128)S(1)}, u32[]{:S(2)}, u32[]{:S(2)}) collective-permute-start(f32[224,128]{1,0:T(8,128)S(1)} %slice_select_fusion.2), channel_id=1, source_target_pairs={{0,4},{1,5},{2,6},{3,7},{4,0},{5,1},{6,2},{7,3},{8,12},{9,13},{10,... | collective-permute-start | bytes 344072 | tf_op jit(solution)/shard_map/ppermute | solution.py:287
  77.4 7.1 %collective-permute-start.10 = (f32[224,128]{1,0:T(8,128)S(1)}, f32[224,128]{1,0:T(8,128)S(1)}, u32[]{:S(2)}, u32[]{:S(2)}) collective-permute-start(f32[224,128]{1,0:T(8,128)S(1)} %slice_select_fusion.3), channel_id=1, source_target_pairs={{0,4},{1,5},{2,6},{3,7},{4,0},{5,1},{6,2},{7,3},{8,12},{9,13},{10,... | collective-permute-start | bytes 344072 | tf_op jit(solution)/shard_map/ppermute | solution.py:287
  81.1 6.6 %collective-permute-start.19 = (f32[112,128]{1,0:T(8,128)S(1)}, f32[112,128]{1,0:T(8,128)S(1)}, u32[]{:S(2)}, u32[]{:S(2)}) collective-permute-start(f32[112,128]{1,0:T(8,128)S(1)} %slice_select_fusion.4), channel_id=1, source_target_pairs={{0,8},{1,9},{2,10},{3,11},{4,12},{5,13},{6,14},{7,15},{8,0},{9,1},... | collective-permute-start | bytes 172040 | tf_op jit(solution)/shard_map/ppermute | solution.py:287
  84.6 5.6 %collective-permute-start.11 = (f32[112,128]{1,0:T(8,128)S(1)}, f32[112,128]{1,0:T(8,128)S(1)}, u32[]{:S(2)}, u32[]{:S(2)}) collective-permute-start(f32[112,128]{1,0:T(8,128)S(1)} %slice_select_fusion.5), channel_id=1, source_target_pairs={{0,8},{1,9},{2,10},{3,11},{4,12},{5,13},{6,14},{7,15},{8,0},{9,1},... | collective-permute-start | bytes 172040 | tf_op jit(solution)/shard_map/ppermute | solution.py:287
  87.7 6.2 %collective-permute-start.20 = (f32[112,128]{1,0:T(8,128)S(1)}, f32[112,128]{1,0:T(8,128)S(1)}, u32[]{:S(2)}, u32[]{:S(2)}) collective-permute-start(f32[112,128]{1,0:T(8,128)S(1)} %select_add_fusion.4), channel_id=1, source_target_pairs={{0,8},{1,9},{2,10},{3,11},{4,12},{5,13},{6,14},{7,15},{8,0},{9,1},... | collective-permute-start | bytes 172040 | tf_op jit(solution)/shard_map/ppermute | solution.py:287
  90.2 5.2 %collective-permute-start.12 = (f32[112,128]{1,0:T(8,128)S(1)}, f32[112,128]{1,0:T(8,128)S(1)}, u32[]{:S(2)}, u32[]{:S(2)}) collective-permute-start(f32[112,128]{1,0:T(8,128)S(1)} %select_add_fusion.5), channel_id=1, source_target_pairs={{0,8},{1,9},{2,10},{3,11},{4,12},{5,13},{6,14},{7,15},{8,0},{9,1},... | collective-permute-start | bytes 172040 | tf_op jit(solution)/shard_map/ppermute | solution.py:287
  93.9 4.9 %collective-permute-start.21 = (f32[224,128]{1,0:T(8,128)S(1)}, f32[224,128]{1,0:T(8,128)S(1)}, u32[]{:S(2)}, u32[]{:S(2)}) collective-permute-start(f32[224,128]{1,0:T(8,128)S(1)} %pad_maximum_fusion.5), channel_id=1, source_target_pairs={{0,4},{1,5},{2,6},{3,7},{4,0},{5,1},{6,2},{7,3},{8,12},{9,13},{10,... | collective-permute-start | bytes 344072 | tf_op jit(solution)/shard_map/ppermute | solution.py:287
  95.4 4.9 %collective-permute-start.13 = (f32[224,128]{1,0:T(8,128)S(1)}, f32[224,128]{1,0:T(8,128)S(1)}, u32[]{:S(2)}, u32[]{:S(2)}) collective-permute-start(f32[224,128]{1,0:T(8,128)S(1)} %pad_maximum_fusion.4), channel_id=1, source_target_pairs={{0,4},{1,5},{2,6},{3,7},{4,0},{5,1},{6,2},{7,3},{8,12},{9,13},{10,... | collective-permute-start | bytes 344072 | tf_op jit(solution)/shard_map/ppermute | solution.py:287
  98.8 6.1 %collective-permute-start.22 = (f32[448,128]{1,0:T(8,128)S(1)}, f32[448,128]{1,0:T(8,128)S(1)}, u32[]{:S(2)}, u32[]{:S(2)}) collective-permute-start(f32[448,128]{1,0:T(8,128)S(1)} %pad_maximum_fusion.3), channel_id=1, source_target_pairs={{0,2},{1,3},{2,0},{3,1},{4,6},{5,7},{6,4},{7,5},{8,10},{9,11},{10,... | collective-permute-start | bytes 688136 | tf_op jit(solution)/shard_map/ppermute | solution.py:287
  100.3 7.0 %collective-permute-start.14 = (f32[448,128]{1,0:T(8,128)S(1)}, f32[448,128]{1,0:T(8,128)S(1)}, u32[]{:S(2)}, u32[]{:S(2)}) collective-permute-start(f32[448,128]{1,0:T(8,128)S(1)} %pad_maximum_fusion.2), channel_id=1, source_target_pairs={{0,2},{1,3},{2,0},{3,1},{4,6},{5,7},{6,4},{7,5},{8,10},{9,11},{10,... | collective-permute-start | bytes 688136 | tf_op jit(solution)/shard_map/ppermute | solution.py:287
  105.0 2.5 %collective-permute-start.23 = (f32[896,128]{1,0:T(8,128)S(1)}, f32[896,128]{1,0:T(8,128)S(1)}, u32[]{:S(2)}, u32[]{:S(2)}) collective-permute-start(f32[896,128]{1,0:T(8,128)S(1)} %pad_maximum_fusion.1.refs_2_), channel_id=1, source_target_pairs={{0,1},{1,0},{2,3},{3,2},{4,5},{5,4},{6,7},{7,6},{8,9},{9,8},{10,11... | collective-permute-start | bytes 1376264 | tf_op jit(solution)/shard_map/ppermute | solution.py:287
  107.4 1.9 %collective-permute-start.15 = (f32[896,128]{1,0:T(8,128)S(1)}, f32[896,128]{1,0:T(8,128)S(1)}, u32[]{:S(2)}, u32[]{:S(2)}) collective-permute-start(f32[896,128]{1,0:T(8,128)S(1)} %pad_maximum_fusion.refs_0_), channel_id=1, source_target_pairs={{0,1},{1,0},{2,3},{3,2},{4,5},{5,4},{6,7},{7,6},{8,9},{9,8},{10,11... | collective-permute-start | bytes 1376264 | tf_op jit(solution)/shard_map/ppermute | solution.py:287

commit v4 on v3

--- a/solution.py
+++ b/solution.py
@@ -90,7 +90,7 @@
         near[:, offset:offset + width] = src[rows_of(t), 0:width]
 
 
-def unpack(src, dist, tab, layer, far, near, out, join, hops, pos):
+def unpack_far(dist, tab, layer, far, out, hops, pos):
     for k in range(1, hops):
         for slot in range(MOST):
             place, t = track_at(tab, k, slot)
@@ -99,17 +99,19 @@
             def _(k=k, slot=slot, t=t):
                 out[rows_of(t), :] = far[k - 1][slot * TW:(slot + 1) * TW, :]
 
+
+def unpack_near(src, dist, tab, layer, near, out, join, pos):
     for slot, (offset, width) in enumerate(near_slots(pos)[0]):
         place, t = track_at(tab, 0, slot)
 
         @pl.when(place < TRACKS)
         def _(slot=slot, t=t, offset=offset, width=width):
             shift = dist[layer, t]
-            join[slot, :, :pos] = src[rows_of(t), :]
-            join[slot, :, pos:pos + width] = near[:, offset:offset + width]
+            join[slot % 4, :, :pos] = src[rows_of(t), :]
+            join[slot % 4, :, pos:pos + width] = near[:, offset:offset + width]
             base = pl.multiple_of(shift // LANES * LANES, LANES)
             rest = shift % LANES
-            window = join[slot, :, pl.ds(base, pos + LANES)]
+            window = join[slot % 4, :, pl.ds(base, pos + LANES)]
             turned = pltpu.roll(window, jnp.where(rest == 0, 0, pos + LANES - rest), 1)
             out[rows_of(t), :] = turned[:, :pos]
 
@@ -198,59 +200,59 @@
         put(first, send)
 
 
-def fetch(sems, refs, count):
-    loads = [pltpu.make_async_copy(refs[n], refs[count + n], sems.at[n]) for n in range(count)]
+def start_loads(sems, sources, targets):
+    loads = [pltpu.make_async_copy(src, dst, sems.at[n]) for n, (src, dst) in enumerate(zip(sources, targets))]
     for load in loads:
         load.start()
-    for load in loads:
-        load.wait()
-    return refs[count:2 * count]
-
-
-def upper_kernel(hops, pos, dist, tab1, tab0, src, wo3, wi3, slope, near_in, *refs):
+    return loads
+
+
+def upper_kernel(hops, pos, factor, odd, dist, tab1, tab0, src_h, wo3_h, slope_h, wi3_h, x2_h, h2_h, near_in, *refs):
     far_in, refs = refs[:hops - 1], refs[hops - 1:]
     near, refs = refs[0], refs[1:]
     far, refs = refs[:hops - 1], refs[hops - 1:]
-    grad_h, gm_h, gh_h, grad, gm3, gh3, gm, join, sems = refs
-    unpack(src, dist, tab1, 1, far_in, near_in, gm, join, hops, pos)
+    keep, send, grad_h, src, grad, wo3, slope, wi3, x2, h2, gm3, gh3, gm, join, sems = refs
+    first, *loads = start_loads(sems, (src_h, wo3_h, slope_h, wi3_h, x2_h, h2_h), (src, wo3, slope, wi3, x2, h2))
+    unpack_far(dist, tab1, 1, far_in, gm, hops, pos)
+    first.wait()
+    unpack_near(src, dist, tab1, 1, near_in, gm, join, pos)
+    loads[0].wait()
+    loads[1].wait()
     hidden(pos, wo3, slope, gm, gm3, gh3)
-    stores = [
-        pltpu.make_async_copy(gm3.at[0:2 * D, :], gm_h, sems.at[0]),
-        pltpu.make_async_copy(gh3.at[0:2 * HID, :], gh_h, sems.at[1]),
-        pltpu.make_async_copy(grad, grad_h, sems.at[2]),
-    ]
+    loads[2].wait()
+    inward(pos, wi3, gm, gh3, grad)
+    store = pltpu.make_async_copy(grad, grad_h, sems.at[6])
+    store.start()
+    pack(grad, tab0, far, near, hops, pos)
+    loads[3].wait()
+    loads[4].wait()
+    weight_terms(factor, odd[0], x2, gh3, h2, gm3, keep, send)
+    store.wait()
+
+
+def lower_kernel(hops, pos, factor, odd, dist, tab0, src_h, wo3_h, slope_h, x2_h, h2_h, near_in, *refs):
+    far_in, refs = refs[:hops - 1], refs[hops - 1:]
+    keep, send, gm_h, gh_h, src, gm, gh3, wo3, slope, x2, h2, gm3, join, sems = refs
+    first, *loads = start_loads(sems, (src_h, wo3_h, slope_h, x2_h, h2_h), (src, wo3, slope, x2, h2))
+    unpack_far(dist, tab0, 0, far_in, gm, hops, pos)
+    first.wait()
+    unpack_near(src, dist, tab0, 0, near_in, gm, join, pos)
+    stores = [pltpu.make_async_copy(gm, gm_h, sems.at[5]), pltpu.make_async_copy(gh3, gh_h, sems.at[6])]
     stores[0].start()
-    stores[1].start()
-    inward(pos, wi3, gm, gh3, grad)
-    stores[2].start()
-    pack(grad, tab0, far, near, hops, pos)
-    for store in stores:
-        store.wait()
-
-
-def terms_kernel(factor, odd, x2_h, gh_h, h2_h, gm_h, keep, send, x2, gh, h2, gm, sems):
-    fetch(sems, (x2_h, gh_h, h2_h, gm_h, x2, gh, h2, gm), 4)
-    weight_terms(factor, odd[0], x2, gh, h2, gm, keep, send)
-
-
-def lower_kernel(hops, pos, factor, odd, dist, tab0, wo3_h, src, slope, x2, h2, near_in, *refs):
-    far_in, refs = refs[:hops - 1], refs[hops - 1:]
-    keep, send, gm_h, gh_h, gm, gh3, gm3, join, wo3, sems = refs
-    load = pltpu.make_async_copy(wo3_h, wo3, sems.at[2])
-    load.start()
-    unpack(src, dist, tab0, 0, far_in, near_in, gm, join, hops, pos)
-    stores = [pltpu.make_async_copy(gm, gm_h, sems.at[0]), pltpu.make_async_copy(gh3, gh_h, sems.at[1])]
-    stores[0].start()
-    load.wait()
+    loads[0].wait()
+    loads[1].wait()
     hidden(pos, wo3, slope, gm, gm3, gh3)
     stores[1].start()
+    loads[2].wait()
+    loads[3].wait()
     weight_terms(factor, odd[0], x2, gh3, h2, gm3, keep, send)
     for store in stores:
         store.wait()
 
 
 def input_kernel(pos, wi3_h, gm_h, gh_h, out, wi3, gm, gh3, sems):
-    fetch(sems, (wi3_h, gm_h, gh_h, wi3, gm, gh3), 3)
+    for load in start_loads(sems, (wi3_h, gm_h, gh_h), (wi3, gm, gh3)):
+        load.wait()
     inward(pos, wi3, gm, gh3, out)
 
 
@@ -335,7 +337,7 @@
 
     whole_s = pltpu.VMEM((D, pos), f32)
     gm3_s = pltpu.VMEM((3 * D, pos), bf16)
-    join_s = pltpu.VMEM((INNER, TW, 2 * pos + LANES), f32)
+    join_s = pltpu.VMEM((4, TW, 2 * pos + LANES), f32)
     distances, out_grad_h = [pltpu.with_memory_space_constraint(v, pltpu.HBM) for v in (distances, out_grad)]
     tab_1, near, *far = pl.pallas_call(
         lambda *refs: pack_kernel(hops, pos, *refs),
@@ -352,18 +354,16 @@
     act_ins = []
     for layer in range(2):
         act_ins += [saved[layer], weight_in[layer], bias_in[layer][:, None], w_out_t[layer]]
-    def act_shapes(of):
-        return [
-            stored(2 * D + 32, pos, dtype=bf16),
-            stored(2 * HID, pos, dtype=bf16),
-            of(HID, pos),
-            of(D, 3 * HID, dtype=bf16),
-            of(HID, 3 * D, dtype=bf16),
-        ]
-
+    act_shapes = [
+        stored(2 * D + 32, pos, dtype=bf16),
+        stored(2 * HID, pos, dtype=bf16),
+        stored(HID, pos),
+        stored(D, 3 * HID, dtype=bf16),
+        stored(HID, 3 * D, dtype=bf16),
+    ]
     tab_0, *acts = pl.pallas_call(
         lambda *refs: act_kernel(hops, pos, *refs),
-        out_shape=[shape(32, dtype=i32)] + act_shapes(stored) + act_shapes(held),
+        out_shape=[shape(32, dtype=i32)] + act_shapes * 2,
         in_specs=[SM] + [VM] * 8,
         out_specs=[SM] + [VM] * 10,
         scratch_shapes=[pltpu.VMEM((3 * D, 256), bf16)],
@@ -371,41 +371,37 @@
     )(distances, *act_ins)
     x2_0, h2_0, slope_0, wi3_0, wo3_0, x2_1, h2_1, slope_1, wi3_1, wo3_1 = acts
 
+    gh3_s = pltpu.VMEM((3 * HID, pos), bf16)
     x2_s = pltpu.VMEM((2 * D + 32, pos), bf16)
     h2_s = pltpu.VMEM((2 * HID, pos), bf16)
-    gm2_s = pltpu.VMEM((2 * D, pos), bf16)
-    gh3_s = pltpu.VMEM((3 * HID, pos), bf16)
-    sems_s = pltpu.SemaphoreType.DMA((4,))
+    slope_s = pltpu.VMEM((HID, pos), f32)
+    wi3_s = pltpu.VMEM((D, 3 * HID), bf16)
+    wo3_s = pltpu.VMEM((HID, 3 * D), bf16)
+    sems_s = pltpu.SemaphoreType.DMA((7,))
     near, *rest = pl.pallas_call(
-        lambda *refs: upper_kernel(hops, pos, *refs),
-        out_shape=[near_shape] + far_shapes + [stored(D, pos), stored(2 * D, pos, dtype=bf16), stored(2 * HID, pos, dtype=bf16)],
-        in_specs=[SM] * 3 + [VM] * (hops + 4),
-        out_specs=[VM] * hops + [HB] * 3,
-        scratch_shapes=[whole_s, gm3_s, gh3_s, whole_s, join_s, sems_s],
-        **kernel_options("upper", 14, 5),
-    )(distances, tab_1, tab_0, out_grad, *stay(wo3_1, wi3_1, slope_1), near, *far)
-    far, (grad_1, gm2_1, gh2_1) = rest[:hops - 1], rest[hops - 1:]
+        lambda *refs: upper_kernel(hops, pos, factor, *refs),
+        out_shape=[near_shape] + far_shapes + [shape(half, LANES)] * 2 + [stored(D, pos)],
+        in_specs=[SM] * 4 + [HB] * 6 + [VM] * hops,
+        out_specs=[VM] * (hops + 2) + [HB],
+        scratch_shapes=[whole_s, whole_s, wo3_s, slope_s, wi3_s, x2_s, h2_s, gm3_s, gh3_s, whole_s, join_s, sems_s],
+        **kernel_options("upper", 16, 6),
+    )(odd, distances, tab_1, tab_0, *stay(out_grad, wo3_1, slope_1, wi3_1, x2_1, h2_1, where=pltpu.HBM), near, *far)
+    far, (keep_1, send_1, grad_1) = rest[:hops - 1], rest[hops - 1:]
     near, far = travel(near, far)
 
-    keep_1, send_1 = pl.pallas_call(
-        lambda *refs: terms_kernel(factor, *refs),
-        out_shape=[shape(half, LANES)] * 2,
-        in_specs=[SM] + [HB] * 4,
-        out_specs=[VM] * 2,
-        scratch_shapes=[x2_s, h2_s, h2_s, gm2_s, sems_s],
-        **kernel_options("terms", 14, 0.001),
-    )(odd, *stay(x2_1, gh2_1, h2_1, gm2_1, where=pltpu.HBM))
-    send_1, near, far = lax.optimization_barrier((send_1, near, far))
     sum_1 = keep_1 + exchange(send_1, 1)
+    sum_1, near, far = lax.optimization_barrier((sum_1, near, far))
+    sum_1 = fold(sum_1, masks[0])
 
     keep, send, gm_0, gh3_0 = pl.pallas_call(
         lambda *refs: lower_kernel(hops, pos, factor, *refs),
         out_shape=[shape(half, LANES)] * 2 + [stored(D, pos), stored(3 * HID, pos, dtype=bf16)],
-        in_specs=[SM] * 3 + [HB] + [VM] * (hops + 4),
+        in_specs=[SM] * 3 + [HB] * 5 + [VM] * hops,
         out_specs=[VM] * 2 + [HB] * 2,
-        scratch_shapes=[whole_s, gh3_s, gm3_s, join_s, pltpu.VMEM((HID, 3 * D), bf16), sems_s],
+        scratch_shapes=[whole_s, whole_s, gh3_s, wo3_s, slope_s, x2_s, h2_s, gm3_s, join_s, sems_s],
         **kernel_options("lower", 16, 5),
-    )(odd, distances, tab_0, *stay(wo3_0, where=pltpu.HBM), grad_1, slope_0, x2_0, h2_0, near, *far)
+    )(odd, distances, tab_0, *stay(grad_1, wo3_0, slope_0, x2_0, h2_0, where=pltpu.HBM), near, *far)
+    sum_1, send = lax.optimization_barrier((sum_1, send))
     sum_0 = keep + exchange(send, 1)
     sum_0, gm_0 = lax.optimization_barrier((sum_0, gm_0))
 
@@ -418,10 +414,12 @@
         **kernel_options("inward", 12, 3),
     )(*stay(wi3_0, gm_0, gh3_0, where=pltpu.HBM))
     for number, mask in enumerate(masks):
-        sum_1 = fold(sum_1, mask)
         if number == 1:
             sum_0, input_grad = lax.optimization_barrier((sum_0, input_grad))
-        sum_0 = fold(sum_0, mask)
+        if number > 0:
+            sum_1 = fold(sum_1, mask)
+            sum_1, _ = lax.optimization_barrier((sum_1, early))
+        early, sum_0 = sum_0, fold(sum_0, mask)
     for mask in masks[::-1]:
         sum_1 = spread(sum_1, mask)
         sum_0 = spread(sum_0, mask)

time: 111 us -> 116 us (1.045)
  waiting for transfers between devices: 33.2 us -> 47.8 us
  starting transfers between devices: 39.9 us -> 33.8 us
  Pallas kernels: 32.7 us -> 30.7 us
    ppermute x16, waiting for transfers between devices: 12.3 us -> 23 us  [exchange(): return lax.ppermute(value, 'seq', [(s, s ^ mask) for s in range(count)])]
    ppermute x16, starting transfers between devices: 27.8 us -> 21.3 us  [exchange(): return lax.ppermute(value, 'seq', [(s, s ^ mask) for s in range(count)])]
    ppermute x8, waiting for transfers between devices: 20.9 us -> 24.8 us  [from_ahead(): lax.ppermute(value, 'seq', [(s, (s - steps) % count) for s in range(count)])]
    pallas_call x2 -> x1, Pallas kernels: 11 us -> 7.68 us  [body(): pl.pallas_call(lambda *refs: upper_kernel(hops, pos, factor, *refs), out_...]
  transfers between devices with their start and end apart: 24 -> 24, of which waited for: 16 -> 17; matrix products, arithmetic and copies ran while one was open for 3% -> 2% of each run, Pallas kernels for 20% -> 16%
where the time goes in v4:
time: 116 us
  waiting for transfers between devices  47.8 us (41%)
  starting transfers between devices  33.8 us (29%)
  Pallas kernels  30.7 us (26%)
  local copies, waits for them, and re-layouts  2.17 us (2%)
    ppermute x8, waiting for transfers between devices, from_ahead(): lax.ppermute(value, 'seq', [(s, (s - steps) % count) for s in range(count)])  24.8 us
    ppermute x16, waiting for transfers between devices, exchange(): return lax.ppermute(value, 'seq', [(s, s ^ mask) for s in range(count)])  23 us
    ppermute x16, starting transfers between devices, exchange(): return lax.ppermute(value, 'seq', [(s, s ^ mask) for s in range(count)])  21.3 us
    ppermute x8, starting transfers between devices, from_ahead(): lax.ppermute(value, 'seq', [(s, (s - steps) % count) for s in range(count)])  12.5 us
    pallas_call x1, Pallas kernels, body(): pl.pallas_call(lambda *refs: act_kernel(hops, pos, *refs), out_shape=[sha...  7.88 us
    pallas_call x1, Pallas kernels, body(): pl.pallas_call(lambda *refs: upper_kernel(hops, pos, factor, *refs), out_...  7.68 us
    pallas_call x1, Pallas kernels, body(): pl.pallas_call(lambda *refs: lower_kernel(hops, pos, factor, *refs), out_...  6.88 us
    pallas_call x1, Pallas kernels, body(): pl.pallas_call(lambda *refs: input_kernel(pos, *refs), out_shape=shape(D,...  4.24 us
  transfers between devices with their start and end apart: 24, of which 17 were waited for; matrix products, arithmetic and copies ran while one was open for 2% of the time, Pallas kernels for 16%

profile of v4, /device:TPU:0, one launch (start us, length us, event | category | flops | bytes accessed | tf_op | source)
XLA Modules:
  0.0 116.0 jit_solution(6992695344943910716)
XLA Ops:
  0.7 2.7 %pack.1 = (s32[32]{0:T(128)S(1)}, f32[16,6144]{1,0:T(8,128)S(1)}, f32[48,1024]{1,0:T(8,128)S(1)}, f32[48,1024]{1,0:T(8,128)S(1)}, f32[48,1024]{1,0:T(8,128)S(1)}) custom-call(s32[2,18]{1,0:T(2,128)} %refs_1_.7, f32[288,1024]{1,0:T(8,128)} %refs_4_.1), custom_call_target="tpu_custom_call" | custom-call | flops 2000000000 | bytes 6000000 | tf_op jit(solution)/shard_map/pack/pallas_call | solution.py:342
  3.4 5.5 %collective-permute-start = (f32[16,6144]{1,0:T(8,128)S(1)}, f32[16,6144]{1,0:T(8,128)S(1)}, u32[]{:S(2)}, u32[]{:S(2)}) collective-permute-start(f32[16,6144]{1,0:T(8,128)S(1)} %get-tuple-element.54), channel_id=1, source_target_pairs={{0,15},{1,0},{2,1},{3,2},{4,3},{5,4},{6,5},{7,6},{8,7},{9,8},{10,9... | collective-permute-start | bytes 1179656 | tf_op jit(solution)/shard_map/ppermute | solution.py:284
  8.8 0.6 collective-permute-start.1
  9.5 0.4 collective-permute-start.2
  9.9 0.1 copy.11.refs_3_
  10.1 0.1 copy.12.refs_7_
  10.3 1.4 %slice_bitcast_fusion = (f32[288,384]{1,0:T(8,128)S(1)}, f32[288,384]{1,0:T(8,128)S(1)}, f32[288,384]{1,0:T(8,128)S(1)}, f32[288,384]{1,0:T(8,128)S(1)}) fusion(f32[2,288,384]{2,1,0:T(8,128)S(1)} %bitcast.15, f32[2,288,384]{2,1,0:T(8,128)} %param.10), kind=kLoop, calls=%fused_computation.2 | loop fusion | bytes 3538944 | tf_op jit(solution)/shard_map/squeeze | solution.py:356
  11.7 0.1 copy-done
  11.8 0.4 copy-done.1
  12.1 7.9 %act.1 = (s32[32]{0:T(128)S(1)}, bf16[608,1024]{1,0:T(8,128)(2,1)}, bf16[768,1024]{1,0:T(8,128)(2,1)}, f32[384,1024]{1,0:T(8,128)}, bf16[288,1152]{1,0:T(8,128)(...) custom-call(s32[2,18]{1,0:T(2,128)} %refs_1_.7, ...), custom_call_target="tpu_custom_call" | custom-call | flops 5000000000 | bytes 15000000 | tf_op jit(solution)/shard_map/act/pallas_call | solution.py:364
  20.0 2.5 %collective-permute-done.1.refs_11_ = f32[48,1024]{1,0:T(8,128)S(1)} collective-permute-done((f32[48,1024]{1,0:T(8,128)S(1)}, f32[48,1024]{1,0:T(8,128)S(1)}, u32[]{:S(2)}, u32[]{:S(2)}) %collective-permute-start.1) | collective-permute-done | bytes 196640 | tf_op jit(solution)/shard_map/ppermute | solution.py:284
  22.5 2.2 %collective-permute-done.2.refs_12_ = f32[48,1024]{1,0:T(8,128)S(1)} collective-permute-done((f32[48,1024]{1,0:T(8,128)S(1)}, f32[48,1024]{1,0:T(8,128)S(1)}, u32[]{:S(2)}, u32[]{:S(2)}) %collective-permute-start.2) | collective-permute-done | bytes 196640 | tf_op jit(solution)/shard_map/ppermute | solution.py:284
  24.7 6.2 %collective-permute-done.3.refs_13_ = f32[48,1024]{1,0:T(8,128)S(1)} collective-permute-done((f32[48,1024]{1,0:T(8,128)S(1)}, f32[48,1024]{1,0:T(8,128)S(1)}, u32[]{:S(2)}, u32[]{:S(2)}) %collective-permute-start.3) | collective-permute-done | bytes 196640 | tf_op jit(solution)/shard_map/ppermute | solution.py:284
  30.9 7.7 %upper.1 = (f32[16,6144]{1,0:T(8,128)S(1)}, f32[48,1024]{1,0:T(8,128)S(1)}, f32[48,1024]{1,0:T(8,128)S(1)}, f32[48,1024]{1,0:T(8,128)S(1)}, f32[896,128]{1,0:T(8...) custom-call(s32[1]{0:T(128)} %bitcast.refs_0_.odd, s32[2,18]{1,0:T(2,128)} %refs_1_.7, ...), custom_call_target="tpu_custom_call" | custom-call | flops 6000000000 | bytes 18000000 | tf_op jit(solution)/shard_map/upper/pallas_call | solution.py:381
  38.6 0.1 collective-permute-start.4
  38.7 5.9 %collective-permute-start.6 = (f32[48,1024]{1,0:T(8,128)S(1)}, f32[48,1024]{1,0:T(8,128)S(1)}, u32[]{:S(2)}, u32[]{:S(2)}) collective-permute-start(f32[48,1024]{1,0:T(8,128)S(1)} %get-tuple-element.66), channel_id=1, source_target_pairs={{0,14},{1,15},{2,0},{3,1},{4,2},{5,3},{6,4},{7,5},{8,6},{9,7},{10,... | collective-permute-start | bytes 589832 | tf_op jit(solution)/shard_map/ppermute | solution.py:284
  44.7 7.6 %collective-permute-done.6.refs_9_ = f32[48,1024]{1,0:T(8,128)S(1)} collective-permute-done((f32[48,1024]{1,0:T(8,128)S(1)}, f32[48,1024]{1,0:T(8,128)S(1)}, u32[]{:S(2)}, u32[]{:S(2)}) %collective-permute-start.6) | collective-permute-done | bytes 196640 | tf_op jit(solution)/shard_map/ppermute | solution.py:284
  52.3 4.5 %collective-permute-done.7.refs_10_ = f32[48,1024]{1,0:T(8,128)S(1)} collective-permute-done((f32[48,1024]{1,0:T(8,128)S(1)}, f32[48,1024]{1,0:T(8,128)S(1)}, u32[]{:S(2)}, u32[]{:S(2)}) %collective-permute-start.7) | collective-permute-done | bytes 196640 | tf_op jit(solution)/shard_map/ppermute | solution.py:284
  56.8 1.8 %collective-permute-done.8.refs_11_ = f32[48,1024]{1,0:T(8,128)S(1)} collective-permute-done((f32[48,1024]{1,0:T(8,128)S(1)}, f32[48,1024]{1,0:T(8,128)S(1)}, u32[]{:S(2)}, u32[]{:S(2)}) %collective-permute-start.8) | collective-permute-done | bytes 196640 | tf_op jit(solution)/shard_map/ppermute | solution.py:284
  58.6 0.1 collective-permute-start.9
  58.7 6.9 %lower.1 = (f32[896,128]{1,0:T(8,128)S(1)}, f32[896,128]{1,0:T(8,128)S(1)}, f32[288,1024]{1,0:T(8,128)}, bf16[1152,1024]{1,0:T(8,128)(2,1)}) custom-call(s32[1]{0:T(128)} %bitcast.refs_0_.odd, s32[2,18]{1,0:T(2,128)} %refs_1_.7, s32[32]{0:T(128)S(1)} %get-tuple-element.47.refs_3_.refs_2_, f32[288,1024]{1,0:T(8,128)} %get-tuple-element.58.refs_3_, ...), custom_call_target="tpu_custom_call" | custom-call | flops 5000000000 | bytes 15000000 | tf_op jit(solution)/shard_map/lower/pallas_call | solution.py:396
  65.6 0.1 collective-permute-start.10
  65.7 4.2 %collective-permute-start.18 = (f32[224,128]{1,0:T(8,128)S(1)}, f32[224,128]{1,0:T(8,128)S(1)}, u32[]{:S(2)}, u32[]{:S(2)}) collective-permute-start(f32[224,128]{1,0:T(8,128)S(1)} %slice_select_fusion.2), channel_id=1, source_target_pairs={{0,4},{1,5},{2,6},{3,7},{4,0},{5,1},{6,2},{7,3},{8,12},{9,13},{10,... | collective-permute-start | bytes 344072 | tf_op jit(solution)/shard_map/ppermute | solution.py:289
  70.0 3.8 %collective-permute-done.18 = f32[224,128]{1,0:T(8,128)S(1)} collective-permute-done((f32[224,128]{1,0:T(8,128)S(1)}, f32[224,128]{1,0:T(8,128)S(1)}, u32[]{:S(2)}, u32[]{:S(2)}) %collective-permute-start.18) | collective-permute-done | bytes 114720 | tf_op jit(solution)/shard_map/ppermute | solution.py:289
  73.9 3.4 %collective-permute-start.19 = (f32[112,128]{1,0:T(8,128)S(1)}, f32[112,128]{1,0:T(8,128)S(1)}, u32[]{:S(2)}, u32[]{:S(2)}) collective-permute-start(f32[112,128]{1,0:T(8,128)S(1)} %slice_select_fusion.5), channel_id=1, source_target_pairs={{0,8},{1,9},{2,10},{3,11},{4,12},{5,13},{6,14},{7,15},{8,0},{9,1},... | collective-permute-start | bytes 172040 | tf_op jit(solution)/shard_map/ppermute | solution.py:289
  77.4 1.4 %collective-permute-start.11 = (f32[448,128]{1,0:T(8,128)S(1)}, f32[448,128]{1,0:T(8,128)S(1)}, u32[]{:S(2)}, u32[]{:S(2)}) collective-permute-start(f32[448,128]{1,0:T(8,128)S(1)} %slice_select_fusion), channel_id=1, source_target_pairs={{0,2},{1,3},{2,0},{3,1},{4,6},{5,7},{6,4},{7,5},{8,10},{9,11},{10,... | collective-permute-start | bytes 688136 | tf_op jit(solution)/shard_map/ppermute | solution.py:289
  78.8 4.2 %inward.1 = f32[288,1024]{1,0:T(8,128)} custom-call(bf16[288,1152]{1,0:T(8,128)(2,1)} %get-tuple-element.79.refs_0_, f32[288,1024]{1,0:T(8,128)} %get-tuple-element.80.refs_1_, bf16[1152,1024]{1,0:T(8,128)(2,1)} %get-tuple-element.81.refs_2_), custom_call_target="tpu_custom_call" | custom-call | flops 3000000000 | bytes 9000000 | tf_op jit(solution)/shard_map/inward/pallas_call | solution.py:408
  83.0 1.5 %collective-permute-done.11 = f32[448,128]{1,0:T(8,128)S(1)} collective-permute-done((f32[448,128]{1,0:T(8,128)S(1)}, f32[448,128]{1,0:T(8,128)S(1)}, u32[]{:S(2)}, u32[]{:S(2)}) %collective-permute-start.11) | collective-permute-done | bytes 229408 | tf_op jit(solution)/shard_map/ppermute | solution.py:289
  84.6 0.4 collective-permute-start.20
  85.0 1.6 %collective-permute-start.12 = (f32[224,128]{1,0:T(8,128)S(1)}, f32[224,128]{1,0:T(8,128)S(1)}, u32[]{:S(2)}, u32[]{:S(2)}) collective-permute-start(f32[224,128]{1,0:T(8,128)S(1)} %slice_select_fusion.3), channel_id=1, source_target_pairs={{0,4},{1,5},{2,6},{3,7},{4,0},{5,1},{6,2},{7,3},{8,12},{9,13},{10,... | collective-permute-start | bytes 344072 | tf_op jit(solution)/shard_map/ppermute | solution.py:289
  86.6 3.2 %collective-permute-done.20 = f32[112,128]{1,0:T(8,128)S(1)} collective-permute-done((f32[112,128]{1,0:T(8,128)S(1)}, f32[112,128]{1,0:T(8,128)S(1)}, u32[]{:S(2)}, u32[]{:S(2)}) %collective-permute-start.20) | collective-permute-done | bytes 57376 | tf_op jit(solution)/shard_map/ppermute | solution.py:289
  89.8 0.6 collective-permute-done.12
  90.5 2.1 %collective-permute-start.13 = (f32[112,128]{1,0:T(8,128)S(1)}, f32[112,128]{1,0:T(8,128)S(1)}, u32[]{:S(2)}, u32[]{:S(2)}) collective-permute-start(f32[112,128]{1,0:T(8,128)S(1)} %slice_select_fusion.4), channel_id=1, source_target_pairs={{0,8},{1,9},{2,10},{3,11},{4,12},{5,13},{6,14},{7,15},{8,0},{9,1},... | collective-permute-start | bytes 172040 | tf_op jit(solution)/shard_map/ppermute | solution.py:289
  92.6 1.6 %collective-permute-start.21 = (f32[224,128]{1,0:T(8,128)S(1)}, f32[224,128]{1,0:T(8,128)S(1)}, u32[]{:S(2)}, u32[]{:S(2)}) collective-permute-start(f32[224,128]{1,0:T(8,128)S(1)} %pad_maximum_fusion.5), channel_id=1, source_target_pairs={{0,4},{1,5},{2,6},{3,7},{4,0},{5,1},{6,2},{7,3},{8,12},{9,13},{10,... | collective-permute-start | bytes 344072 | tf_op jit(solution)/shard_map/ppermute | solution.py:289
  94.1 2.4 %collective-permute-done.13 = f32[112,128]{1,0:T(8,128)S(1)} collective-permute-done((f32[112,128]{1,0:T(8,128)S(1)}, f32[112,128]{1,0:T(8,128)S(1)}, u32[]{:S(2)}, u32[]{:S(2)}) %collective-permute-start.13) | collective-permute-done | bytes 57376 | tf_op jit(solution)/shard_map/ppermute | solution.py:289
  96.5 1.3 %collective-permute-start.14 = (f32[112,128]{1,0:T(8,128)S(1)}, f32[112,128]{1,0:T(8,128)S(1)}, u32[]{:S(2)}, u32[]{:S(2)}) collective-permute-start(f32[112,128]{1,0:T(8,128)S(1)} %select_add_fusion.5), channel_id=1, source_target_pairs={{0,8},{1,9},{2,10},{3,11},{4,12},{5,13},{6,14},{7,15},{8,0},{9,1},... | collective-permute-start | bytes 172040 | tf_op jit(solution)/shard_map/ppermute | solution.py:289
  97.8 0.3 collective-permute-done.21
  98.1 3.5 %collective-permute-done.14 = f32[112,128]{1,0:T(8,128)S(1)} collective-permute-done((f32[112,128]{1,0:T(8,128)S(1)}, f32[112,128]{1,0:T(8,128)S(1)}, u32[]{:S(2)}, u32[]{:S(2)}) %collective-permute-start.14) | collective-permute-done | bytes 57376 | tf_op jit(solution)/shard_map/ppermute | solution.py:289
  101.7 2.0 %collective-permute-start.15 = (f32[224,128]{1,0:T(8,128)S(1)}, f32[224,128]{1,0:T(8,128)S(1)}, u32[]{:S(2)}, u32[]{:S(2)}) collective-permute-start(f32[224,128]{1,0:T(8,128)S(1)} %pad_maximum_fusion.4), channel_id=1, source_target_pairs={{0,4},{1,5},{2,6},{3,7},{4,0},{5,1},{6,2},{7,3},{8,12},{9,13},{10,... | collective-permute-start | bytes 344072 | tf_op jit(solution)/shard_map/ppermute | solution.py:289
  103.7 1.5 %collective-permute-start.22 = (f32[448,128]{1,0:T(8,128)S(1)}, f32[448,128]{1,0:T(8,128)S(1)}, u32[]{:S(2)}, u32[]{:S(2)}) collective-permute-start(f32[448,128]{1,0:T(8,128)S(1)} %pad_maximum_fusion.3), channel_id=1, source_target_pairs={{0,2},{1,3},{2,0},{3,1},{4,6},{5,7},{6,4},{7,5},{8,10},{9,11},{10,... | collective-permute-start | bytes 688136 | tf_op jit(solution)/shard_map/ppermute | solution.py:289
  105.1 1.4 %collective-permute-done.15 = f32[224,128]{1,0:T(8,128)S(1)} collective-permute-done((f32[224,128]{1,0:T(8,128)S(1)}, f32[224,128]{1,0:T(8,128)S(1)}, u32[]{:S(2)}, u32[]{:S(2)}) %collective-permute-start.15) | collective-permute-done | bytes 114720 | tf_op jit(solution)/shard_map/ppermute | solution.py:289
  106.6 1.5 %collective-permute-start.16 = (f32[448,128]{1,0:T(8,128)S(1)}, f32[448,128]{1,0:T(8,128)S(1)}, u32[]{:S(2)}, u32[]{:S(2)}) collective-permute-start(f32[448,128]{1,0:T(8,128)S(1)} %pad_maximum_fusion.2), channel_id=1, source_target_pairs={{0,2},{1,3},{2,0},{3,1},{4,6},{5,7},{6,4},{7,5},{8,10},{9,11},{10,... | collective-permute-start | bytes 688136 | tf_op jit(solution)/shard_map/ppermute | solution.py:289
  108.0 1.7 %collective-permute-done.22 = f32[448,128]{1,0:T(8,128)S(1)} collective-permute-done((f32[448,128]{1,0:T(8,128)S(1)}, f32[448,128]{1,0:T(8,128)S(1)}, u32[]{:S(2)}, u32[]{:S(2)}) %collective-permute-start.22) | collective-permute-done | bytes 229408 | tf_op jit(solution)/shard_map/ppermute | solution.py:289
  109.9 0.1 collective-permute-start.23
  109.9 2.7 %collective-permute-done.16 = f32[448,128]{1,0:T(8,128)S(1)} collective-permute-done((f32[448,128]{1,0:T(8,128)S(1)}, f32[448,128]{1,0:T(8,128)S(1)}, u32[]{:S(2)}, u32[]{:S(2)}) %collective-permute-start.16) | collective-permute-done | bytes 229408 | tf_op jit(solution)/shard_map/ppermute | solution.py:289
  112.8 0.1 collective-permute-start.17
  112.8 1.8 %collective-permute-done.17.refs_1_ = f32[896,128]{1,0:T(8,128)S(1)} collective-permute-done((f32[896,128]{1,0:T(8,128)S(1)}, f32[896,128]{1,0:T(8,128)S(1)}, u32[]{:S(2)}, u32[]{:S(2)}) %collective-permute-start.17) | collective-permute-done | bytes 458784 | tf_op jit(solution)/shard_map/ppermute | solution.py:289
  114.6 1.3 %finish.1 = (f32[2,288,384]{2,1,0:T(8,128)}, f32[2,384]{1,0:T(2,128)}, f32[2,288,384]{2,1,0:T(8,128)}) custom-call(s32[1]{0:T(128)} %bitcast.refs_0_.odd, f32[896,128]{1,0:T(8,128)S(1)} %pad_maximum_fusion.refs_0_, f32[896,128]{1,0:T(8,128)S(1)} %collective-permute-done.17.refs_1_, f32[896,128]{1,0:T(8,128)S(1)} %pad_maximum_fusion.1.refs_2_, ...), custom_call_target="tpu_custom_call" | custom-call | flops 1000000000 | bytes 3000000 | tf_op jit(solution)/shard_map/finish/pallas_call | solution.py:429
  (44 shorter events, 0.7 us)
Async XLA Ops:
  0.6 9.3 %copy-start.3 = (f32[2,384]{1,0:T(2,128)S(1)}, f32[2,384]{1,0:T(2,128)}, u32[]{:S(2)}) copy-start(f32[2,384]{1,0:T(2,128)} %param.11) | copy-start | bytes 9220
  0.6 9.6 %copy-start.2 = (f32[2,384,288]{1,2,0:T(8,128)S(1)}, f32[2,384,288]{1,2,0:T(8,128)}, u32[]{:S(2)}) copy-start(f32[2,384,288]{1,2,0:T(8,128)} %param.12) | copy-start | bytes 2654212
  3.4 27.5 %collective-permute-start = (f32[16,6144]{1,0:T(8,128)S(1)}, f32[16,6144]{1,0:T(8,128)S(1)}, u32[]{:S(2)}, u32[]{:S(2)}) collective-permute-start(f32[16,6144]{1,0:T(8,128)S(1)} %get-tuple-element.54), channel_id=1, source_target_pairs={{0,15},{1,0},{2,1},{3,2},{4,3},{5,4},{6,5},{7,6},{8,7},{9,8},{10,9... | collective-permute-start | bytes 1179656 | tf_op jit(solution)/shard_map/ppermute | solution.py:284
  8.8 13.7 %collective-permute-start.1 = (f32[48,1024]{1,0:T(8,128)S(1)}, f32[48,1024]{1,0:T(8,128)S(1)}, u32[]{:S(2)}, u32[]{:S(2)}) collective-permute-start(f32[48,1024]{1,0:T(8,128)S(1)} %get-tuple-element.55), channel_id=1, source_target_pairs={{0,14},{1,15},{2,0},{3,1},{4,2},{5,3},{6,4},{7,5},{8,6},{9,7},{10,... | collective-permute-start | bytes 589832 | tf_op jit(solution)/shard_map/ppermute | solution.py:284
  9.5 15.2 %collective-permute-start.2 = (f32[48,1024]{1,0:T(8,128)S(1)}, f32[48,1024]{1,0:T(8,128)S(1)}, u32[]{:S(2)}, u32[]{:S(2)}) collective-permute-start(f32[48,1024]{1,0:T(8,128)S(1)} %get-tuple-element.56), channel_id=1, source_target_pairs={{0,12},{1,13},{2,14},{3,15},{4,0},{5,1},{6,2},{7,3},{8,4},{9,5},{1... | collective-permute-start | bytes 589832 | tf_op jit(solution)/shard_map/ppermute | solution.py:284
  9.9 21.0 %collective-permute-start.3 = (f32[48,1024]{1,0:T(8,128)S(1)}, f32[48,1024]{1,0:T(8,128)S(1)}, u32[]{:S(2)}, u32[]{:S(2)}) collective-permute-start(f32[48,1024]{1,0:T(8,128)S(1)} %get-tuple-element.57), channel_id=1, source_target_pairs={{0,8},{1,9},{2,10},{3,11},{4,12},{5,13},{6,14},{7,15},{8,0},{9,1},... | collective-permute-start | bytes 589832 | tf_op jit(solution)/shard_map/ppermute | solution.py:284
  10.2 1.5 %copy-start = (f32[288,1024]{1,0:T(8,128)S(1)}, f32[288,1024]{1,0:T(8,128)}, u32[]{:S(2)}) copy-start(f32[288,1024]{1,0:T(8,128)} %refs_1_.4) | copy-start | bytes 3538948
  10.3 1.9 %copy-start.1 = (f32[288,1024]{1,0:T(8,128)S(1)}, f32[288,1024]{1,0:T(8,128)}, u32[]{:S(2)}) copy-start(f32[288,1024]{1,0:T(8,128)} %refs_5_.1) | copy-start | bytes 3538948
  38.6 6.0 %collective-permute-start.4 = (f32[896,128]{1,0:T(8,128)S(1)}, f32[896,128]{1,0:T(8,128)S(1)}, u32[]{:S(2)}, u32[]{:S(2)}) collective-permute-start(f32[896,128]{1,0:T(8,128)S(1)} %get-tuple-element.64), channel_id=1, source_target_pairs={{0,1},{1,0},{2,3},{3,2},{4,5},{5,4},{6,7},{7,6},{8,9},{9,8},{10,11... | collective-permute-start | bytes 1376264 | tf_op jit(solution)/shard_map/ppermute | solution.py:289
  38.7 19.9 %collective-permute-start.5 = (f32[16,6144]{1,0:T(8,128)S(1)}, f32[16,6144]{1,0:T(8,128)S(1)}, u32[]{:S(2)}, u32[]{:S(2)}) collective-permute-start(f32[16,6144]{1,0:T(8,128)S(1)} %get-tuple-element.65), channel_id=1, source_target_pairs={{0,15},{1,0},{2,1},{3,2},{4,3},{5,4},{6,5},{7,6},{8,7},{9,8},{10,9... | collective-permute-start | bytes 1179656 | tf_op jit(solution)/shard_map/ppermute | solution.py:284
  38.7 13.6 %collective-permute-start.6 = (f32[48,1024]{1,0:T(8,128)S(1)}, f32[48,1024]{1,0:T(8,128)S(1)}, u32[]{:S(2)}, u32[]{:S(2)}) collective-permute-start(f32[48,1024]{1,0:T(8,128)S(1)} %get-tuple-element.66), channel_id=1, source_target_pairs={{0,14},{1,15},{2,0},{3,1},{4,2},{5,3},{6,4},{7,5},{8,6},{9,7},{10,... | collective-permute-start | bytes 589832 | tf_op jit(solution)/shard_map/ppermute | solution.py:284
  44.6 12.2 %collective-permute-start.7 = (f32[48,1024]{1,0:T(8,128)S(1)}, f32[48,1024]{1,0:T(8,128)S(1)}, u32[]{:S(2)}, u32[]{:S(2)}) collective-permute-start(f32[48,1024]{1,0:T(8,128)S(1)} %get-tuple-element.67), channel_id=1, source_target_pairs={{0,12},{1,13},{2,14},{3,15},{4,0},{5,1},{6,2},{7,3},{8,4},{9,5},{1... | collective-permute-start | bytes 589832 | tf_op jit(solution)/shard_map/ppermute | solution.py:284
  44.6 14.0 %collective-permute-start.8 = (f32[48,1024]{1,0:T(8,128)S(1)}, f32[48,1024]{1,0:T(8,128)S(1)}, u32[]{:S(2)}, u32[]{:S(2)}) collective-permute-start(f32[48,1024]{1,0:T(8,128)S(1)} %get-tuple-element.68), channel_id=1, source_target_pairs={{0,8},{1,9},{2,10},{3,11},{4,12},{5,13},{6,14},{7,15},{8,0},{9,1},... | collective-permute-start | bytes 589832 | tf_op jit(solution)/shard_map/ppermute | solution.py:284
  58.6 7.0 %collective-permute-start.9 = (f32[448,128]{1,0:T(8,128)S(1)}, f32[448,128]{1,0:T(8,128)S(1)}, u32[]{:S(2)}, u32[]{:S(2)}) collective-permute-start(f32[448,128]{1,0:T(8,128)S(1)} %slice_select_fusion.1), channel_id=1, source_target_pairs={{0,2},{1,3},{2,0},{3,1},{4,6},{5,7},{6,4},{7,5},{8,10},{9,11},{10,... | collective-permute-start | bytes 688136 | tf_op jit(solution)/shard_map/ppermute | solution.py:289
  65.6 8.2 %collective-permute-start.10 = (f32[896,128]{1,0:T(8,128)S(1)}, f32[896,128]{1,0:T(8,128)S(1)}, u32[]{:S(2)}, u32[]{:S(2)}) collective-permute-start(f32[896,128]{1,0:T(8,128)S(1)} %get-tuple-element.76), channel_id=1, source_target_pairs={{0,1},{1,0},{2,3},{3,2},{4,5},{5,4},{6,7},{7,6},{8,9},{9,8},{10,11... | collective-permute-start | bytes 1376264 | tf_op jit(solution)/shard_map/ppermute | solution.py:289
  65.7 8.1 %collective-permute-start.18 = (f32[224,128]{1,0:T(8,128)S(1)}, f32[224,128]{1,0:T(8,128)S(1)}, u32[]{:S(2)}, u32[]{:S(2)}) collective-permute-start(f32[224,128]{1,0:T(8,128)S(1)} %slice_select_fusion.2), channel_id=1, source_target_pairs={{0,4},{1,5},{2,6},{3,7},{4,0},{5,1},{6,2},{7,3},{8,12},{9,13},{10,... | collective-permute-start | bytes 344072 | tf_op jit(solution)/shard_map/ppermute | solution.py:289
  73.9 9.1 %collective-permute-start.19 = (f32[112,128]{1,0:T(8,128)S(1)}, f32[112,128]{1,0:T(8,128)S(1)}, u32[]{:S(2)}, u32[]{:S(2)}) collective-permute-start(f32[112,128]{1,0:T(8,128)S(1)} %slice_select_fusion.5), channel_id=1, source_target_pairs={{0,8},{1,9},{2,10},{3,11},{4,12},{5,13},{6,14},{7,15},{8,0},{9,1},... | collective-permute-start | bytes 172040 | tf_op jit(solution)/shard_map/ppermute | solution.py:289
  77.4 7.1 %collective-permute-start.11 = (f32[448,128]{1,0:T(8,128)S(1)}, f32[448,128]{1,0:T(8,128)S(1)}, u32[]{:S(2)}, u32[]{:S(2)}) collective-permute-start(f32[448,128]{1,0:T(8,128)S(1)} %slice_select_fusion), channel_id=1, source_target_pairs={{0,2},{1,3},{2,0},{3,1},{4,6},{5,7},{6,4},{7,5},{8,10},{9,11},{10,... | collective-permute-start | bytes 688136 | tf_op jit(solution)/shard_map/ppermute | solution.py:289
  84.6 5.2 %collective-permute-start.20 = (f32[112,128]{1,0:T(8,128)S(1)}, f32[112,128]{1,0:T(8,128)S(1)}, u32[]{:S(2)}, u32[]{:S(2)}) collective-permute-start(f32[112,128]{1,0:T(8,128)S(1)} %select_add_fusion.4), channel_id=1, source_target_pairs={{0,8},{1,9},{2,10},{3,11},{4,12},{5,13},{6,14},{7,15},{8,0},{9,1},... | collective-permute-start | bytes 172040 | tf_op jit(solution)/shard_map/ppermute | solution.py:289
  85.0 5.5 %collective-permute-start.12 = (f32[224,128]{1,0:T(8,128)S(1)}, f32[224,128]{1,0:T(8,128)S(1)}, u32[]{:S(2)}, u32[]{:S(2)}) collective-permute-start(f32[224,128]{1,0:T(8,128)S(1)} %slice_select_fusion.3), channel_id=1, source_target_pairs={{0,4},{1,5},{2,6},{3,7},{4,0},{5,1},{6,2},{7,3},{8,12},{9,13},{10,... | collective-permute-start | bytes 344072 | tf_op jit(solution)/shard_map/ppermute | solution.py:289
  90.5 6.0 %collective-permute-start.13 = (f32[112,128]{1,0:T(8,128)S(1)}, f32[112,128]{1,0:T(8,128)S(1)}, u32[]{:S(2)}, u32[]{:S(2)}) collective-permute-start(f32[112,128]{1,0:T(8,128)S(1)} %slice_select_fusion.4), channel_id=1, source_target_pairs={{0,8},{1,9},{2,10},{3,11},{4,12},{5,13},{6,14},{7,15},{8,0},{9,1},... | collective-permute-start | bytes 172040 | tf_op jit(solution)/shard_map/ppermute | solution.py:289
  92.6 5.5 %collective-permute-start.21 = (f32[224,128]{1,0:T(8,128)S(1)}, f32[224,128]{1,0:T(8,128)S(1)}, u32[]{:S(2)}, u32[]{:S(2)}) collective-permute-start(f32[224,128]{1,0:T(8,128)S(1)} %pad_maximum_fusion.5), channel_id=1, source_target_pairs={{0,4},{1,5},{2,6},{3,7},{4,0},{5,1},{6,2},{7,3},{8,12},{9,13},{10,... | collective-permute-start | bytes 344072 | tf_op jit(solution)/shard_map/ppermute | solution.py:289
  96.5 5.1 %collective-permute-start.14 = (f32[112,128]{1,0:T(8,128)S(1)}, f32[112,128]{1,0:T(8,128)S(1)}, u32[]{:S(2)}, u32[]{:S(2)}) collective-permute-start(f32[112,128]{1,0:T(8,128)S(1)} %select_add_fusion.5), channel_id=1, source_target_pairs={{0,8},{1,9},{2,10},{3,11},{4,12},{5,13},{6,14},{7,15},{8,0},{9,1},... | collective-permute-start | bytes 172040 | tf_op jit(solution)/shard_map/ppermute | solution.py:289
  101.7 4.9 %collective-permute-start.15 = (f32[224,128]{1,0:T(8,128)S(1)}, f32[224,128]{1,0:T(8,128)S(1)}, u32[]{:S(2)}, u32[]{:S(2)}) collective-permute-start(f32[224,128]{1,0:T(8,128)S(1)} %pad_maximum_fusion.4), channel_id=1, source_target_pairs={{0,4},{1,5},{2,6},{3,7},{4,0},{5,1},{6,2},{7,3},{8,12},{9,13},{10,... | collective-permute-start | bytes 344072 | tf_op jit(solution)/shard_map/ppermute | solution.py:289
  103.7 6.1 %collective-permute-start.22 = (f32[448,128]{1,0:T(8,128)S(1)}, f32[448,128]{1,0:T(8,128)S(1)}, u32[]{:S(2)}, u32[]{:S(2)}) collective-permute-start(f32[448,128]{1,0:T(8,128)S(1)} %pad_maximum_fusion.3), channel_id=1, source_target_pairs={{0,2},{1,3},{2,0},{3,1},{4,6},{5,7},{6,4},{7,5},{8,10},{9,11},{10,... | collective-permute-start | bytes 688136 | tf_op jit(solution)/shard_map/ppermute | solution.py:289
  106.6 6.1 %collective-permute-start.16 = (f32[448,128]{1,0:T(8,128)S(1)}, f32[448,128]{1,0:T(8,128)S(1)}, u32[]{:S(2)}, u32[]{:S(2)}) collective-permute-start(f32[448,128]{1,0:T(8,128)S(1)} %pad_maximum_fusion.2), channel_id=1, source_target_pairs={{0,2},{1,3},{2,0},{3,1},{4,6},{5,7},{6,4},{7,5},{8,10},{9,11},{10,... | collective-permute-start | bytes 688136 | tf_op jit(solution)/shard_map/ppermute | solution.py:289
  109.9 3.0 %collective-permute-start.23 = (f32[896,128]{1,0:T(8,128)S(1)}, f32[896,128]{1,0:T(8,128)S(1)}, u32[]{:S(2)}, u32[]{:S(2)}) collective-permute-start(f32[896,128]{1,0:T(8,128)S(1)} %pad_maximum_fusion.1.refs_2_), channel_id=1, source_target_pairs={{0,1},{1,0},{2,3},{3,2},{4,5},{5,4},{6,7},{7,6},{8,9},{9,8},{10,11... | collective-permute-start | bytes 1376264 | tf_op jit(solution)/shard_map/ppermute | solution.py:289
  112.8 1.9 %collective-permute-start.17 = (f32[896,128]{1,0:T(8,128)S(1)}, f32[896,128]{1,0:T(8,128)S(1)}, u32[]{:S(2)}, u32[]{:S(2)}) collective-permute-start(f32[896,128]{1,0:T(8,128)S(1)} %pad_maximum_fusion.refs_0_), channel_id=1, source_target_pairs={{0,1},{1,0},{2,3},{3,2},{4,5},{5,4},{6,7},{7,6},{8,9},{9,8},{10,11... | collective-permute-start | bytes 1376264 | tf_op jit(solution)/shard_map/ppermute | solution.py:289

commit v5 on v4

--- a/solution.py
+++ b/solution.py
@@ -90,14 +90,16 @@
         near[:, offset:offset + width] = src[rows_of(t), 0:width]
 
 
-def unpack_far(dist, tab, layer, far, out, hops, pos):
+def unpack_far(where, dist, tab, layer, far, out, hops, pos):
     for k in range(1, hops):
         for slot in range(MOST):
             place, t = track_at(tab, k, slot)
-
-            @pl.when((place < TRACKS) & (dist[layer, t] == (pos << k)))
-            def _(k=k, slot=slot, t=t):
-                out[rows_of(t), :] = far[k - 1][slot * TW:(slot + 1) * TW, :]
+            mine = (place < TRACKS) & (dist[layer, t] == (pos << k))
+            sources = [(far[0], where[1] == 0), (far[1], where[1] == 1)] if k == 1 else [(far[k], True)]
+            for source, here in sources:
+                @pl.when(mine & here)
+                def _(source=source, slot=slot, t=t):
+                    out[rows_of(t), :] = source[slot * TW:(slot + 1) * TW, :]
 
 
 def unpack_near(src, dist, tab, layer, near, out, join, pos):
@@ -207,13 +209,13 @@
     return loads
 
 
-def upper_kernel(hops, pos, factor, odd, dist, tab1, tab0, src_h, wo3_h, slope_h, wi3_h, x2_h, h2_h, near_in, *refs):
-    far_in, refs = refs[:hops - 1], refs[hops - 1:]
+def upper_kernel(hops, pos, factor, where, dist, tab1, tab0, src_h, wo3_h, slope_h, wi3_h, x2_h, h2_h, near_in, *refs):
+    far_in, refs = refs[:hops], refs[hops:]
     near, refs = refs[0], refs[1:]
     far, refs = refs[:hops - 1], refs[hops - 1:]
     keep, send, grad_h, src, grad, wo3, slope, wi3, x2, h2, gm3, gh3, gm, join, sems = refs
     first, *loads = start_loads(sems, (src_h, wo3_h, slope_h, wi3_h, x2_h, h2_h), (src, wo3, slope, wi3, x2, h2))
-    unpack_far(dist, tab1, 1, far_in, gm, hops, pos)
+    unpack_far(where, dist, tab1, 1, far_in, gm, hops, pos)
     first.wait()
     unpack_near(src, dist, tab1, 1, near_in, gm, join, pos)
     loads[0].wait()
@@ -226,15 +228,15 @@
     pack(grad, tab0, far, near, hops, pos)
     loads[3].wait()
     loads[4].wait()
-    weight_terms(factor, odd[0], x2, gh3, h2, gm3, keep, send)
+    weight_terms(factor, where[0], x2, gh3, h2, gm3, keep, send)
     store.wait()
 
 
-def lower_kernel(hops, pos, factor, odd, dist, tab0, src_h, wo3_h, slope_h, x2_h, h2_h, near_in, *refs):
-    far_in, refs = refs[:hops - 1], refs[hops - 1:]
+def lower_kernel(hops, pos, factor, where, dist, tab0, src_h, wo3_h, slope_h, x2_h, h2_h, near_in, *refs):
+    far_in, refs = refs[:hops], refs[hops:]
     keep, send, gm_h, gh_h, src, gm, gh3, wo3, slope, x2, h2, gm3, join, sems = refs
     first, *loads = start_loads(sems, (src_h, wo3_h, slope_h, x2_h, h2_h), (src, wo3, slope, x2, h2))
-    unpack_far(dist, tab0, 0, far_in, gm, hops, pos)
+    unpack_far(where, dist, tab0, 0, far_in, gm, hops, pos)
     first.wait()
     unpack_near(src, dist, tab0, 0, near_in, gm, join, pos)
     stores = [pltpu.make_async_copy(gm, gm_h, sems.at[5]), pltpu.make_async_copy(gh3, gh_h, sems.at[6])]
@@ -245,7 +247,7 @@
     stores[1].start()
     loads[2].wait()
     loads[3].wait()
-    weight_terms(factor, odd[0], x2, gh3, h2, gm3, keep, send)
+    weight_terms(factor, where[0], x2, gh3, h2, gm3, keep, send)
     for store in stores:
         store.wait()
 
@@ -329,11 +331,15 @@
     half = -(-3 * (D + 8) // (8 * count)) * 8 * count
     masks = [1 << b for b in range(1, hops)]
     far_hops = [1 << k for k in range(1, hops)]
-    odd = (lax.axis_index("seq") & 1).astype(i32).reshape(1)
+    index = lax.axis_index("seq")
+    where = jnp.stack([index & 1, (index >> 1) & 1]).astype(i32)
 
     def travel(near, far):
-        moved = [from_ahead(f, h) for f, h in zip(far[::-1], far_hops[::-1])][::-1]
-        return from_ahead(near, 1), moved
+        paired = exchange(far[0], 2)
+        moved = [from_ahead(f, h) for f, h in zip(far[:0:-1], far_hops[:0:-1])][::-1]
+        near = from_ahead(near, 1)
+        passed = lax.ppermute(paired, "seq", [(s, (s - 4) % count) for s in range(count) if s & 2])
+        return near, [paired, passed] + moved
 
     whole_s = pltpu.VMEM((D, pos), f32)
     gm3_s = pltpu.VMEM((3 * D, pos), bf16)
@@ -381,11 +387,11 @@
     near, *rest = pl.pallas_call(
         lambda *refs: upper_kernel(hops, pos, factor, *refs),
         out_shape=[near_shape] + far_shapes + [shape(half, LANES)] * 2 + [stored(D, pos)],
-        in_specs=[SM] * 4 + [HB] * 6 + [VM] * hops,
+        in_specs=[SM] * 4 + [HB] * 6 + [VM] * (hops + 1),
         out_specs=[VM] * (hops + 2) + [HB],
         scratch_shapes=[whole_s, whole_s, wo3_s, slope_s, wi3_s, x2_s, h2_s, gm3_s, gh3_s, whole_s, join_s, sems_s],
         **kernel_options("upper", 16, 6),
-    )(odd, distances, tab_1, tab_0, *stay(out_grad, wo3_1, slope_1, wi3_1, x2_1, h2_1, where=pltpu.HBM), near, *far)
+    )(where, distances, tab_1, tab_0, *stay(out_grad, wo3_1, slope_1, wi3_1, x2_1, h2_1, where=pltpu.HBM), near, *far)
     far, (keep_1, send_1, grad_1) = rest[:hops - 1], rest[hops - 1:]
     near, far = travel(near, far)
 
@@ -396,12 +402,11 @@
     keep, send, gm_0, gh3_0 = pl.pallas_call(
         lambda *refs: lower_kernel(hops, pos, factor, *refs),
         out_shape=[shape(half, LANES)] * 2 + [stored(D, pos), stored(3 * HID, pos, dtype=bf16)],
-        in_specs=[SM] * 3 + [HB] * 5 + [VM] * hops,
+        in_specs=[SM] * 3 + [HB] * 5 + [VM] * (hops + 1),
         out_specs=[VM] * 2 + [HB] * 2,
         scratch_shapes=[whole_s, whole_s, gh3_s, wo3_s, slope_s, x2_s, h2_s, gm3_s, join_s, sems_s],
         **kernel_options("lower", 16, 5),
-    )(odd, distances, tab_0, *stay(grad_1, wo3_0, slope_0, x2_0, h2_0, where=pltpu.HBM), near, *far)
-    sum_1, send = lax.optimization_barrier((sum_1, send))
+    )(where, distances, tab_0, *stay(grad_1, wo3_0, slope_0, x2_0, h2_0, where=pltpu.HBM), near, *far)
     sum_0 = keep + exchange(send, 1)
     sum_0, gm_0 = lax.optimization_barrier((sum_0, gm_0))
 
@@ -413,13 +418,13 @@
         scratch_shapes=[pltpu.VMEM((D, 3 * HID), bf16), whole_s, gh3_s, sems_s],
         **kernel_options("inward", 12, 3),
     )(*stay(wi3_0, gm_0, gh3_0, where=pltpu.HBM))
+    sum_1, _ = lax.optimization_barrier((sum_1, sum_0))
     for number, mask in enumerate(masks):
+        if number > 0:
+            sum_1 = fold(sum_1, mask)
         if number == 1:
             sum_0, input_grad = lax.optimization_barrier((sum_0, input_grad))
-        if number > 0:
-            sum_1 = fold(sum_1, mask)
-            sum_1, _ = lax.optimization_barrier((sum_1, early))
-        early, sum_0 = sum_0, fold(sum_0, mask)
+        sum_0 = fold(sum_0, mask)
     for mask in masks[::-1]:
         sum_1 = spread(sum_1, mask)
         sum_0 = spread(sum_0, mask)
@@ -432,7 +437,7 @@
         in_specs=[SM] + [VM] * 4,
         out_specs=[VM] * 3,
         **kernel_options("finish", 4, 1),
-    )(odd, sum_0, other_0, sum_1, other_1)
+    )(where, sum_0, other_0, sum_1, other_1)
     return input_grad, w_in_grad, bias_grad, jnp.transpose(w_out_t_grad, (0, 2, 1))
 
 

time: 116 us -> 109 us (0.940)
  waiting for transfers between devices: 47.8 us -> 40.7 us
  starting transfers between devices: 33.8 us -> 31.7 us
    ppermute x8 -> x6, waiting for transfers between devices: 24.8 us -> 15.4 us  [from_ahead(): lax.ppermute(value, 'seq', [(s, (s - steps) % count) for s in range(count)])]
    ppermute x8 -> x6, starting transfers between devices: 12.5 us -> 9.04 us  [from_ahead(): lax.ppermute(value, 'seq', [(s, (s - steps) % count) for s in range(count)])]
    ppermute x16 -> x18, waiting for transfers between devices: 23 us -> 25.4 us  [exchange(): return lax.ppermute(value, 'seq', [(s, s ^ mask) for s in range(count)])]
    ppermute x0 -> x2, starting transfers between devices: none -> 1.32 us  [travel(): lax.ppermute(paired, 'seq', [(s, (s - 4) % count) for s in range(count) i...]
    ppermute x16 -> x18, starting transfers between devices: 21.3 us -> 21.3 us  [exchange(): return lax.ppermute(value, 'seq', [(s, s ^ mask) for s in range(count)])]
  transfers between devices with their start and end apart: 24 -> 26, of which waited for: 17 -> 14; matrix products, arithmetic and copies ran while one was open for 2% -> 3% of each run, Pallas kernels for 16% -> 17%
where the time goes in v5:
time: 109 us
  waiting for transfers between devices  40.7 us (37%)
  starting transfers between devices  31.7 us (29%)
  Pallas kernels  31 us (28%)
  local copies, waits for them, and re-layouts  2.48 us (2%)
  other arithmetic  1.7 us (2%)
    ppermute x18, waiting for transfers between devices, exchange(): return lax.ppermute(value, 'seq', [(s, s ^ mask) for s in range(count)])  25.4 us
    ppermute x18, starting transfers between devices, exchange(): return lax.ppermute(value, 'seq', [(s, s ^ mask) for s in range(count)])  21.3 us
    ppermute x6, waiting for transfers between devices, from_ahead(): lax.ppermute(value, 'seq', [(s, (s - steps) % count) for s in range(count)])  15.4 us
    ppermute x6, starting transfers between devices, from_ahead(): lax.ppermute(value, 'seq', [(s, (s - steps) % count) for s in range(count)])  9.04 us
    pallas_call x1, Pallas kernels, body(): pl.pallas_call(lambda *refs: act_kernel(hops, pos, *refs), out_shape=[sha...  7.89 us
    pallas_call x1, Pallas kernels, body(): pl.pallas_call(lambda *refs: upper_kernel(hops, pos, factor, *refs), out_...  7.58 us
    pallas_call x1, Pallas kernels, body(): pl.pallas_call(lambda *refs: lower_kernel(hops, pos, factor, *refs), out_...  6.69 us
    pallas_call x1, Pallas kernels, body(): pl.pallas_call(lambda *refs: input_kernel(pos, *refs), out_shape=shape(D,...  4.24 us
  transfers between devices with their start and end apart: 26, of which 14 were waited for; matrix products, arithmetic and copies ran while one was open for 3% of the time, Pallas kernels for 17%

profile of v5, /device:TPU:0, one launch (start us, length us, event | category | flops | bytes accessed | tf_op | source)
XLA Modules:
  0.0 108.6 jit_solution(4682141202869314935)
XLA Ops:
  0.7 2.7 %pack.1 = (s32[32]{0:T(128)S(1)}, f32[16,6144]{1,0:T(8,128)S(1)}, f32[48,1024]{1,0:T(8,128)S(1)}, f32[48,1024]{1,0:T(8,128)S(1)}, f32[48,1024]{1,0:T(8,128)S(1)}) custom-call(s32[2,18]{1,0:T(2,128)} %refs_1_.7, f32[288,1024]{1,0:T(8,128)} %refs_4_.1), custom_call_target="tpu_custom_call" | custom-call | flops 2000000000 | bytes 6000000 | tf_op jit(solution)/shard_map/pack/pallas_call | solution.py:348
  3.4 3.0 %collective-permute-start.1 = (f32[48,1024]{1,0:T(8,128)S(1)}, f32[48,1024]{1,0:T(8,128)S(1)}, u32[]{:S(2)}, u32[]{:S(2)}) collective-permute-start(f32[48,1024]{1,0:T(8,128)S(1)} %get-tuple-element.53), channel_id=1, source_target_pairs={{0,2},{1,3},{2,0},{3,1},{4,6},{5,7},{6,4},{7,5},{8,10},{9,11},{10,... | collective-permute-start | bytes 589832 | tf_op jit(solution)/shard_map/ppermute | solution.py:291
  6.4 2.7 %collective-permute-start = (f32[16,6144]{1,0:T(8,128)S(1)}, f32[16,6144]{1,0:T(8,128)S(1)}, u32[]{:S(2)}, u32[]{:S(2)}) collective-permute-start(f32[16,6144]{1,0:T(8,128)S(1)} %get-tuple-element.52), channel_id=1, source_target_pairs={{0,15},{1,0},{2,1},{3,2},{4,3},{5,4},{6,5},{7,6},{8,7},{9,8},{10,9... | collective-permute-start | bytes 1179656 | tf_op jit(solution)/shard_map/ppermute | solution.py:286
  9.1 0.9 collective-permute-start.3
  10.0 0.1 copy.11.refs_3_
  10.1 0.1 copy.12.refs_7_
  10.3 1.4 %slice_bitcast_fusion = (f32[288,384]{1,0:T(8,128)S(1)}, f32[288,384]{1,0:T(8,128)S(1)}, f32[288,384]{1,0:T(8,128)S(1)}, f32[288,384]{1,0:T(8,128)S(1)}) fusion(f32[2,288,384]{2,1,0:T(8,128)S(1)} %bitcast.16, f32[2,288,384]{2,1,0:T(8,128)} %param.10), kind=kLoop, calls=%fused_computation.2 | loop fusion | bytes 3538944 | tf_op jit(solution)/shard_map/squeeze | solution.py:362
  11.8 0.7 collective-permute-done.1.refs_11_
  12.5 0.7 collective-permute-start.2
  13.1 7.9 %act.1 = (s32[32]{0:T(128)S(1)}, bf16[608,1024]{1,0:T(8,128)(2,1)}, bf16[768,1024]{1,0:T(8,128)(2,1)}, f32[384,1024]{1,0:T(8,128)}, bf16[288,1152]{1,0:T(8,128)(...) custom-call(s32[2,18]{1,0:T(2,128)} %refs_1_.7, ...), custom_call_target="tpu_custom_call" | custom-call | flops 5000000000 | bytes 15000000 | tf_op jit(solution)/shard_map/act/pallas_call | solution.py:370
  21.1 0.1 pad_add_fusion.refs_0_.odd
  21.1 6.2 %collective-permute-done.4.refs_14_ = f32[48,1024]{1,0:T(8,128)S(1)} collective-permute-done((f32[48,1024]{1,0:T(8,128)S(1)}, f32[48,1024]{1,0:T(8,128)S(1)}, u32[]{:S(2)}, u32[]{:S(2)}) %collective-permute-start.4) | collective-permute-done | bytes 196640 | tf_op jit(solution)/shard_map/ppermute | solution.py:286
  27.4 7.6 %upper.1 = (f32[16,6144]{1,0:T(8,128)S(1)}, f32[48,1024]{1,0:T(8,128)S(1)}, f32[48,1024]{1,0:T(8,128)S(1)}, f32[48,1024]{1,0:T(8,128)S(1)}, f32[896,128]{1,0:T(8...) custom-call(s32[2]{0:T(128)S(1)} %pad_add_fusion.refs_0_.odd, s32[2,18]{1,0:T(2,128)} %refs_1_.7, ...), custom_call_target="tpu_custom_call" | custom-call | flops 6000000000 | bytes 18000000 | tf_op jit(solution)/shard_map/upper/pallas_call | solution.py:387
  35.0 0.1 collective-permute-start.5
  35.0 0.3 collective-permute-start.7
  35.3 4.7 %collective-permute-start.6 = (f32[16,6144]{1,0:T(8,128)S(1)}, f32[16,6144]{1,0:T(8,128)S(1)}, u32[]{:S(2)}, u32[]{:S(2)}) collective-permute-start(f32[16,6144]{1,0:T(8,128)S(1)} %get-tuple-element.63), channel_id=1, source_target_pairs={{0,15},{1,0},{2,1},{3,2},{4,3},{5,4},{6,5},{7,6},{8,7},{9,8},{10,9... | collective-permute-start | bytes 1179656 | tf_op jit(solution)/shard_map/ppermute | solution.py:286
  40.0 0.7 collective-permute-start.9
  40.7 1.6 %collective-permute-done.7.refs_9_ = f32[48,1024]{1,0:T(8,128)S(1)} collective-permute-done((f32[48,1024]{1,0:T(8,128)S(1)}, f32[48,1024]{1,0:T(8,128)S(1)}, u32[]{:S(2)}, u32[]{:S(2)}) %collective-permute-start.7) | collective-permute-done | bytes 196640 | tf_op jit(solution)/shard_map/ppermute | solution.py:291
  42.3 0.7 collective-permute-start.8
  43.0 0.8 copy-done.3
  43.8 1.1 %add.24 = f32[896,128]{1,0:T(8,128)S(1)} add(f32[896,128]{1,0:T(8,128)S(1)} %get-tuple-element.61, f32[896,128]{1,0:T(8,128)} %copy-done.3) | non-fusion elementwise | flops 114688 | bytes 1376256 | tf_op jit(solution)/shard_map/add | solution.py:398
  44.9 9.1 %collective-permute-done.10.refs_12_ = f32[48,1024]{1,0:T(8,128)S(1)} collective-permute-done((f32[48,1024]{1,0:T(8,128)S(1)}, f32[48,1024]{1,0:T(8,128)S(1)}, u32[]{:S(2)}, u32[]{:S(2)}) %collective-permute-start.10) | collective-permute-done | bytes 196640 | tf_op jit(solution)/shard_map/ppermute | solution.py:286
  54.2 6.7 %lower.1 = (f32[896,128]{1,0:T(8,128)S(1)}, f32[896,128]{1,0:T(8,128)S(1)}, f32[288,1024]{1,0:T(8,128)}, bf16[1152,1024]{1,0:T(8,128)(2,1)}) custom-call(s32[2]{0:T(128)S(1)} %pad_add_fusion.refs_0_.odd, s32[2,18]{1,0:T(2,128)} %refs_1_.7, s32[32]{0:T(128)S(1)} %get-tuple-element.45.refs_3_.refs_2_, f32[288,1024]{1,0:T(8,128)} %get-tuple-element.56.refs_3_, ...), custom_call_target="tpu_custom_call" | custom-call | flops 5000000000 | bytes 15000000 | tf_op jit(solution)/shard_map/lower/pallas_call | solution.py:402
  60.9 0.1 collective-permute-start.11
  61.0 1.7 %collective-permute-done.11 = f32[896,128]{1,0:T(8,128)S(1)} collective-permute-done((f32[896,128]{1,0:T(8,128)S(1)}, f32[896,128]{1,0:T(8,128)S(1)}, u32[]{:S(2)}, u32[]{:S(2)}) %collective-permute-start.11) | collective-permute-done | bytes 458784 | tf_op jit(solution)/shard_map/ppermute | solution.py:291
  62.8 4.6 %collective-permute-start.20 = (f32[224,128]{1,0:T(8,128)S(1)}, f32[224,128]{1,0:T(8,128)S(1)}, u32[]{:S(2)}, u32[]{:S(2)}) collective-permute-start(f32[224,128]{1,0:T(8,128)S(1)} %slice_select_fusion.2), channel_id=1, source_target_pairs={{0,4},{1,5},{2,6},{3,7},{4,0},{5,1},{6,2},{7,3},{8,12},{9,13},{10,... | collective-permute-start | bytes 344072 | tf_op jit(solution)/shard_map/ppermute | solution.py:291
  67.4 0.2 collective-permute-start.12
  67.7 3.2 %collective-permute-done.20 = f32[224,128]{1,0:T(8,128)S(1)} collective-permute-done((f32[224,128]{1,0:T(8,128)S(1)}, f32[224,128]{1,0:T(8,128)S(1)}, u32[]{:S(2)}, u32[]{:S(2)}) %collective-permute-start.20) | collective-permute-done | bytes 114720 | tf_op jit(solution)/shard_map/ppermute | solution.py:291
  70.9 1.2 %collective-permute-start.21 = (f32[112,128]{1,0:T(8,128)S(1)}, f32[112,128]{1,0:T(8,128)S(1)}, u32[]{:S(2)}, u32[]{:S(2)}) collective-permute-start(f32[112,128]{1,0:T(8,128)S(1)} %slice_select_fusion.4), channel_id=1, source_target_pairs={{0,8},{1,9},{2,10},{3,11},{4,12},{5,13},{6,14},{7,15},{8,0},{9,1},... | collective-permute-start | bytes 172040 | tf_op jit(solution)/shard_map/ppermute | solution.py:291
  72.1 4.2 %inward.1 = f32[288,1024]{1,0:T(8,128)} custom-call(bf16[288,1152]{1,0:T(8,128)(2,1)} %get-tuple-element.76.refs_0_, f32[288,1024]{1,0:T(8,128)} %get-tuple-element.77.refs_1_, bf16[1152,1024]{1,0:T(8,128)(2,1)} %get-tuple-element.78.refs_2_), custom_call_target="tpu_custom_call" | custom-call | flops 3000000000 | bytes 9000000 | tf_op jit(solution)/shard_map/inward/pallas_call | solution.py:413
  76.4 1.8 %collective-permute-start.22 = (f32[112,128]{1,0:T(8,128)S(1)}, f32[112,128]{1,0:T(8,128)S(1)}, u32[]{:S(2)}, u32[]{:S(2)}) collective-permute-start(f32[112,128]{1,0:T(8,128)S(1)} %select_add_fusion.4), channel_id=1, source_target_pairs={{0,8},{1,9},{2,10},{3,11},{4,12},{5,13},{6,14},{7,15},{8,0},{9,1},... | collective-permute-start | bytes 172040 | tf_op jit(solution)/shard_map/ppermute | solution.py:291
  78.3 1.8 %collective-permute-start.13 = (f32[224,128]{1,0:T(8,128)S(1)}, f32[224,128]{1,0:T(8,128)S(1)}, u32[]{:S(2)}, u32[]{:S(2)}) collective-permute-start(f32[224,128]{1,0:T(8,128)S(1)} %slice_select_fusion.3), channel_id=1, source_target_pairs={{0,4},{1,5},{2,6},{3,7},{4,0},{5,1},{6,2},{7,3},{8,12},{9,13},{10,... | collective-permute-start | bytes 344072 | tf_op jit(solution)/shard_map/ppermute | solution.py:291
  80.1 1.5 %collective-permute-done.22 = f32[112,128]{1,0:T(8,128)S(1)} collective-permute-done((f32[112,128]{1,0:T(8,128)S(1)}, f32[112,128]{1,0:T(8,128)S(1)}, u32[]{:S(2)}, u32[]{:S(2)}) %collective-permute-start.22) | collective-permute-done | bytes 57376 | tf_op jit(solution)/shard_map/ppermute | solution.py:291
  81.7 1.5 %collective-permute-done.13 = f32[224,128]{1,0:T(8,128)S(1)} collective-permute-done((f32[224,128]{1,0:T(8,128)S(1)}, f32[224,128]{1,0:T(8,128)S(1)}, u32[]{:S(2)}, u32[]{:S(2)}) %collective-permute-start.13) | collective-permute-done | bytes 114720 | tf_op jit(solution)/shard_map/ppermute | solution.py:291
  83.2 1.4 %collective-permute-start.14 = (f32[112,128]{1,0:T(8,128)S(1)}, f32[112,128]{1,0:T(8,128)S(1)}, u32[]{:S(2)}, u32[]{:S(2)}) collective-permute-start(f32[112,128]{1,0:T(8,128)S(1)} %slice_select_fusion.5), channel_id=1, source_target_pairs={{0,8},{1,9},{2,10},{3,11},{4,12},{5,13},{6,14},{7,15},{8,0},{9,1},... | collective-permute-start | bytes 172040 | tf_op jit(solution)/shard_map/ppermute | solution.py:291
  84.6 2.0 %collective-permute-start.23 = (f32[224,128]{1,0:T(8,128)S(1)}, f32[224,128]{1,0:T(8,128)S(1)}, u32[]{:S(2)}, u32[]{:S(2)}) collective-permute-start(f32[224,128]{1,0:T(8,128)S(1)} %pad_maximum_fusion.5), channel_id=1, source_target_pairs={{0,4},{1,5},{2,6},{3,7},{4,0},{5,1},{6,2},{7,3},{8,12},{9,13},{10,... | collective-permute-start | bytes 344072 | tf_op jit(solution)/shard_map/ppermute | solution.py:291
  86.7 1.7 %collective-permute-done.14 = f32[112,128]{1,0:T(8,128)S(1)} collective-permute-done((f32[112,128]{1,0:T(8,128)S(1)}, f32[112,128]{1,0:T(8,128)S(1)}, u32[]{:S(2)}, u32[]{:S(2)}) %collective-permute-start.14) | collective-permute-done | bytes 57376 | tf_op jit(solution)/shard_map/ppermute | solution.py:291
  88.4 1.4 %collective-permute-start.15 = (f32[112,128]{1,0:T(8,128)S(1)}, f32[112,128]{1,0:T(8,128)S(1)}, u32[]{:S(2)}, u32[]{:S(2)}) collective-permute-start(f32[112,128]{1,0:T(8,128)S(1)} %select_add_fusion.5), channel_id=1, source_target_pairs={{0,8},{1,9},{2,10},{3,11},{4,12},{5,13},{6,14},{7,15},{8,0},{9,1},... | collective-permute-start | bytes 172040 | tf_op jit(solution)/shard_map/ppermute | solution.py:291
  89.8 3.8 %collective-permute-done.15 = f32[112,128]{1,0:T(8,128)S(1)} collective-permute-done((f32[112,128]{1,0:T(8,128)S(1)}, f32[112,128]{1,0:T(8,128)S(1)}, u32[]{:S(2)}, u32[]{:S(2)}) %collective-permute-start.15) | collective-permute-done | bytes 57376 | tf_op jit(solution)/shard_map/ppermute | solution.py:291
  93.6 2.2 %collective-permute-start.16 = (f32[224,128]{1,0:T(8,128)S(1)}, f32[224,128]{1,0:T(8,128)S(1)}, u32[]{:S(2)}, u32[]{:S(2)}) collective-permute-start(f32[224,128]{1,0:T(8,128)S(1)} %pad_maximum_fusion.4), channel_id=1, source_target_pairs={{0,4},{1,5},{2,6},{3,7},{4,0},{5,1},{6,2},{7,3},{8,12},{9,13},{10,... | collective-permute-start | bytes 344072 | tf_op jit(solution)/shard_map/ppermute | solution.py:291
  95.8 0.4 collective-permute-start.24
  96.2 2.4 %collective-permute-done.16 = f32[224,128]{1,0:T(8,128)S(1)} collective-permute-done((f32[224,128]{1,0:T(8,128)S(1)}, f32[224,128]{1,0:T(8,128)S(1)}, u32[]{:S(2)}, u32[]{:S(2)}) %collective-permute-start.16) | collective-permute-done | bytes 114720 | tf_op jit(solution)/shard_map/ppermute | solution.py:291
  98.6 0.6 collective-permute-start.17
  99.2 2.8 %collective-permute-done.24 = f32[448,128]{1,0:T(8,128)S(1)} collective-permute-done((f32[448,128]{1,0:T(8,128)S(1)}, f32[448,128]{1,0:T(8,128)S(1)}, u32[]{:S(2)}, u32[]{:S(2)}) %collective-permute-start.24) | collective-permute-done | bytes 229408 | tf_op jit(solution)/shard_map/ppermute | solution.py:291
  102.1 0.1 collective-permute-start.25
  102.1 2.6 %collective-permute-done.17 = f32[448,128]{1,0:T(8,128)S(1)} collective-permute-done((f32[448,128]{1,0:T(8,128)S(1)}, f32[448,128]{1,0:T(8,128)S(1)}, u32[]{:S(2)}, u32[]{:S(2)}) %collective-permute-start.17) | collective-permute-done | bytes 229408 | tf_op jit(solution)/shard_map/ppermute | solution.py:291
  104.9 1.8 %collective-permute-done.18.refs_1_ = f32[896,128]{1,0:T(8,128)S(1)} collective-permute-done((f32[896,128]{1,0:T(8,128)S(1)}, f32[896,128]{1,0:T(8,128)S(1)}, u32[]{:S(2)}, u32[]{:S(2)}) %collective-permute-start.18) | collective-permute-done | bytes 458784 | tf_op jit(solution)/shard_map/ppermute | solution.py:291
  106.7 1.9 %finish.1 = (f32[2,288,384]{2,1,0:T(8,128)}, f32[2,384]{1,0:T(2,128)}, f32[2,288,384]{2,1,0:T(8,128)}) custom-call(s32[2]{0:T(128)S(1)} %pad_add_fusion.refs_0_.odd, f32[896,128]{1,0:T(8,128)S(1)} %pad_maximum_fusion.refs_0_, f32[896,128]{1,0:T(8,128)S(1)} %collective-permute-done.18.refs_1_, f32[896,128]{1,0:T(8,128)S(1)} %pad_maximum_fusion.1.refs_2_, ...), custom_call_target="tpu_custom_call" | custom-call | flops 1000000000 | bytes 3000000 | tf_op jit(solution)/shard_map/finish/pallas_call | solution.py:434
  (51 shorter events, 0.8 us)
Async XLA Ops:
  0.6 9.4 %copy-start.4 = (f32[2,384]{1,0:T(2,128)S(1)}, f32[2,384]{1,0:T(2,128)}, u32[]{:S(2)}) copy-start(f32[2,384]{1,0:T(2,128)} %param.11) | copy-start | bytes 9220
  0.6 9.7 %copy-start.2 = (f32[2,384,288]{1,2,0:T(8,128)S(1)}, f32[2,384,288]{1,2,0:T(8,128)}, u32[]{:S(2)}) copy-start(f32[2,384,288]{1,2,0:T(8,128)} %param.12) | copy-start | bytes 2654212
  3.4 9.1 %collective-permute-start.1 = (f32[48,1024]{1,0:T(8,128)S(1)}, f32[48,1024]{1,0:T(8,128)S(1)}, u32[]{:S(2)}, u32[]{:S(2)}) collective-permute-start(f32[48,1024]{1,0:T(8,128)S(1)} %get-tuple-element.53), channel_id=1, source_target_pairs={{0,2},{1,3},{2,0},{3,1},{4,6},{5,7},{6,4},{7,5},{8,10},{9,11},{10,... | collective-permute-start | bytes 589832 | tf_op jit(solution)/shard_map/ppermute | solution.py:291
  6.4 21.0 %collective-permute-start = (f32[16,6144]{1,0:T(8,128)S(1)}, f32[16,6144]{1,0:T(8,128)S(1)}, u32[]{:S(2)}, u32[]{:S(2)}) collective-permute-start(f32[16,6144]{1,0:T(8,128)S(1)} %get-tuple-element.52), channel_id=1, source_target_pairs={{0,15},{1,0},{2,1},{3,2},{4,3},{5,4},{6,5},{7,6},{8,7},{9,8},{10,9... | collective-permute-start | bytes 1179656 | tf_op jit(solution)/shard_map/ppermute | solution.py:286
  9.1 12.0 %collective-permute-start.3 = (f32[48,1024]{1,0:T(8,128)S(1)}, f32[48,1024]{1,0:T(8,128)S(1)}, u32[]{:S(2)}, u32[]{:S(2)}) collective-permute-start(f32[48,1024]{1,0:T(8,128)S(1)} %get-tuple-element.54), channel_id=1, source_target_pairs={{0,12},{1,13},{2,14},{3,15},{4,0},{5,1},{6,2},{7,3},{8,4},{9,5},{1... | collective-permute-start | bytes 589832 | tf_op jit(solution)/shard_map/ppermute | solution.py:286
  10.0 17.4 %collective-permute-start.4 = (f32[48,1024]{1,0:T(8,128)S(1)}, f32[48,1024]{1,0:T(8,128)S(1)}, u32[]{:S(2)}, u32[]{:S(2)}) collective-permute-start(f32[48,1024]{1,0:T(8,128)S(1)} %get-tuple-element.55), channel_id=1, source_target_pairs={{0,8},{1,9},{2,10},{3,11},{4,12},{5,13},{6,14},{7,15},{8,0},{9,1},... | collective-permute-start | bytes 589832 | tf_op jit(solution)/shard_map/ppermute | solution.py:286
  10.3 2.8 %copy-start = (f32[288,1024]{1,0:T(8,128)S(1)}, f32[288,1024]{1,0:T(8,128)}, u32[]{:S(2)}) copy-start(f32[288,1024]{1,0:T(8,128)} %refs_1_.4) | copy-start | bytes 3538948
  10.3 2.8 %copy-start.1 = (f32[288,1024]{1,0:T(8,128)S(1)}, f32[288,1024]{1,0:T(8,128)}, u32[]{:S(2)}) copy-start(f32[288,1024]{1,0:T(8,128)} %refs_5_.1) | copy-start | bytes 3538948
  12.5 14.9 %collective-permute-start.2 = (f32[48,1024]{1,0:T(8,128)S(1)}, f32[48,1024]{1,0:T(8,128)S(1)}, u32[]{:S(2)}, u32[]{:S(2)}) collective-permute-start(f32[48,1024]{1,0:T(8,128)S(1)} %collective-permute-done.1.refs_11_), channel_id=1, source_target_pairs={{2,14},{3,15},{6,2},{7,3},{10,6},{11,7},{14,10},{15,11},{18,30},{1... | collective-permute-start | bytes 589832 | tf_op jit(solution)/shard_map/ppermute | solution.py:341
  35.0 8.1 %collective-permute-start.5 = (f32[896,128]{1,0:T(8,128)S(1)}, f32[896,128]{1,0:T(8,128)S(1)}, u32[]{:S(2)}, u32[]{:S(2)}) collective-permute-start(f32[896,128]{1,0:T(8,128)S(1)} %get-tuple-element.62), channel_id=1, source_target_pairs={{0,1},{1,0},{2,3},{3,2},{4,5},{5,4},{6,7},{7,6},{8,9},{9,8},{10,11... | collective-permute-start | bytes 1376264 | tf_op jit(solution)/shard_map/ppermute | solution.py:291
  35.0 7.3 %collective-permute-start.7 = (f32[48,1024]{1,0:T(8,128)S(1)}, f32[48,1024]{1,0:T(8,128)S(1)}, u32[]{:S(2)}, u32[]{:S(2)}) collective-permute-start(f32[48,1024]{1,0:T(8,128)S(1)} %get-tuple-element.64), channel_id=1, source_target_pairs={{0,2},{1,3},{2,0},{3,1},{4,6},{5,7},{6,4},{7,5},{8,10},{9,11},{10,... | collective-permute-start | bytes 589832 | tf_op jit(solution)/shard_map/ppermute | solution.py:291
  35.3 18.8 %collective-permute-start.6 = (f32[16,6144]{1,0:T(8,128)S(1)}, f32[16,6144]{1,0:T(8,128)S(1)}, u32[]{:S(2)}, u32[]{:S(2)}) collective-permute-start(f32[16,6144]{1,0:T(8,128)S(1)} %get-tuple-element.63), channel_id=1, source_target_pairs={{0,15},{1,0},{2,1},{3,2},{4,3},{5,4},{6,5},{7,6},{8,7},{9,8},{10,9... | collective-permute-start | bytes 1179656 | tf_op jit(solution)/shard_map/ppermute | solution.py:286
  40.0 14.1 %collective-permute-start.10 = (f32[48,1024]{1,0:T(8,128)S(1)}, f32[48,1024]{1,0:T(8,128)S(1)}, u32[]{:S(2)}, u32[]{:S(2)}) collective-permute-start(f32[48,1024]{1,0:T(8,128)S(1)} %get-tuple-element.66), channel_id=1, source_target_pairs={{0,8},{1,9},{2,10},{3,11},{4,12},{5,13},{6,14},{7,15},{8,0},{9,1},... | collective-permute-start | bytes 589832 | tf_op jit(solution)/shard_map/ppermute | solution.py:286
  40.0 14.1 %collective-permute-start.9 = (f32[48,1024]{1,0:T(8,128)S(1)}, f32[48,1024]{1,0:T(8,128)S(1)}, u32[]{:S(2)}, u32[]{:S(2)}) collective-permute-start(f32[48,1024]{1,0:T(8,128)S(1)} %get-tuple-element.65), channel_id=1, source_target_pairs={{0,12},{1,13},{2,14},{3,15},{4,0},{5,1},{6,2},{7,3},{8,4},{9,5},{1... | collective-permute-start | bytes 589832 | tf_op jit(solution)/shard_map/ppermute | solution.py:286
  42.3 11.7 %collective-permute-start.8 = (f32[48,1024]{1,0:T(8,128)S(1)}, f32[48,1024]{1,0:T(8,128)S(1)}, u32[]{:S(2)}, u32[]{:S(2)}) collective-permute-start(f32[48,1024]{1,0:T(8,128)S(1)} %collective-permute-done.7.refs_9_), channel_id=1, source_target_pairs={{2,14},{3,15},{6,2},{7,3},{10,6},{11,7},{14,10},{15,11},{18,30},{1... | collective-permute-start | bytes 589832 | tf_op jit(solution)/shard_map/ppermute | solution.py:341
  43.0 0.8 copy-start.3
  54.1 6.9 %collective-permute-start.19 = (f32[448,128]{1,0:T(8,128)S(1)}, f32[448,128]{1,0:T(8,128)S(1)}, u32[]{:S(2)}, u32[]{:S(2)}) collective-permute-start(f32[448,128]{1,0:T(8,128)S(1)} %slice_select_fusion), channel_id=1, source_target_pairs={{0,2},{1,3},{2,0},{3,1},{4,6},{5,7},{6,4},{7,5},{8,10},{9,11},{10,... | collective-permute-start | bytes 688136 | tf_op jit(solution)/shard_map/ppermute | solution.py:291
  60.9 1.9 %collective-permute-start.11 = (f32[896,128]{1,0:T(8,128)S(1)}, f32[896,128]{1,0:T(8,128)S(1)}, u32[]{:S(2)}, u32[]{:S(2)}) collective-permute-start(f32[896,128]{1,0:T(8,128)S(1)} %get-tuple-element.73), channel_id=1, source_target_pairs={{0,1},{1,0},{2,3},{3,2},{4,5},{5,4},{6,7},{7,6},{8,9},{9,8},{10,11... | collective-permute-start | bytes 1376264 | tf_op jit(solution)/shard_map/ppermute | solution.py:291
  62.8 8.0 %collective-permute-start.20 = (f32[224,128]{1,0:T(8,128)S(1)}, f32[224,128]{1,0:T(8,128)S(1)}, u32[]{:S(2)}, u32[]{:S(2)}) collective-permute-start(f32[224,128]{1,0:T(8,128)S(1)} %slice_select_fusion.2), channel_id=1, source_target_pairs={{0,4},{1,5},{2,6},{3,7},{4,0},{5,1},{6,2},{7,3},{8,12},{9,13},{10,... | collective-permute-start | bytes 344072 | tf_op jit(solution)/shard_map/ppermute | solution.py:291
  67.4 10.8 %collective-permute-start.12 = (f32[448,128]{1,0:T(8,128)S(1)}, f32[448,128]{1,0:T(8,128)S(1)}, u32[]{:S(2)}, u32[]{:S(2)}) collective-permute-start(f32[448,128]{1,0:T(8,128)S(1)} %slice_select_fusion.1), channel_id=1, source_target_pairs={{0,2},{1,3},{2,0},{3,1},{4,6},{5,7},{6,4},{7,5},{8,10},{9,11},{10,... | collective-permute-start | bytes 688136 | tf_op jit(solution)/shard_map/ppermute | solution.py:291
  70.9 5.5 %collective-permute-start.21 = (f32[112,128]{1,0:T(8,128)S(1)}, f32[112,128]{1,0:T(8,128)S(1)}, u32[]{:S(2)}, u32[]{:S(2)}) collective-permute-start(f32[112,128]{1,0:T(8,128)S(1)} %slice_select_fusion.4), channel_id=1, source_target_pairs={{0,8},{1,9},{2,10},{3,11},{4,12},{5,13},{6,14},{7,15},{8,0},{9,1},... | collective-permute-start | bytes 172040 | tf_op jit(solution)/shard_map/ppermute | solution.py:291
  76.4 5.2 %collective-permute-start.22 = (f32[112,128]{1,0:T(8,128)S(1)}, f32[112,128]{1,0:T(8,128)S(1)}, u32[]{:S(2)}, u32[]{:S(2)}) collective-permute-start(f32[112,128]{1,0:T(8,128)S(1)} %select_add_fusion.4), channel_id=1, source_target_pairs={{0,8},{1,9},{2,10},{3,11},{4,12},{5,13},{6,14},{7,15},{8,0},{9,1},... | collective-permute-start | bytes 172040 | tf_op jit(solution)/shard_map/ppermute | solution.py:291
  78.3 4.9 %collective-permute-start.13 = (f32[224,128]{1,0:T(8,128)S(1)}, f32[224,128]{1,0:T(8,128)S(1)}, u32[]{:S(2)}, u32[]{:S(2)}) collective-permute-start(f32[224,128]{1,0:T(8,128)S(1)} %slice_select_fusion.3), channel_id=1, source_target_pairs={{0,4},{1,5},{2,6},{3,7},{4,0},{5,1},{6,2},{7,3},{8,12},{9,13},{10,... | collective-permute-start | bytes 344072 | tf_op jit(solution)/shard_map/ppermute | solution.py:291
  83.2 5.1 %collective-permute-start.14 = (f32[112,128]{1,0:T(8,128)S(1)}, f32[112,128]{1,0:T(8,128)S(1)}, u32[]{:S(2)}, u32[]{:S(2)}) collective-permute-start(f32[112,128]{1,0:T(8,128)S(1)} %slice_select_fusion.5), channel_id=1, source_target_pairs={{0,8},{1,9},{2,10},{3,11},{4,12},{5,13},{6,14},{7,15},{8,0},{9,1},... | collective-permute-start | bytes 172040 | tf_op jit(solution)/shard_map/ppermute | solution.py:291
  84.6 5.2 %collective-permute-start.23 = (f32[224,128]{1,0:T(8,128)S(1)}, f32[224,128]{1,0:T(8,128)S(1)}, u32[]{:S(2)}, u32[]{:S(2)}) collective-permute-start(f32[224,128]{1,0:T(8,128)S(1)} %pad_maximum_fusion.5), channel_id=1, source_target_pairs={{0,4},{1,5},{2,6},{3,7},{4,0},{5,1},{6,2},{7,3},{8,12},{9,13},{10,... | collective-permute-start | bytes 344072 | tf_op jit(solution)/shard_map/ppermute | solution.py:291
  88.4 5.2 %collective-permute-start.15 = (f32[112,128]{1,0:T(8,128)S(1)}, f32[112,128]{1,0:T(8,128)S(1)}, u32[]{:S(2)}, u32[]{:S(2)}) collective-permute-start(f32[112,128]{1,0:T(8,128)S(1)} %select_add_fusion.5), channel_id=1, source_target_pairs={{0,8},{1,9},{2,10},{3,11},{4,12},{5,13},{6,14},{7,15},{8,0},{9,1},... | collective-permute-start | bytes 172040 | tf_op jit(solution)/shard_map/ppermute | solution.py:291
  93.6 5.0 %collective-permute-start.16 = (f32[224,128]{1,0:T(8,128)S(1)}, f32[224,128]{1,0:T(8,128)S(1)}, u32[]{:S(2)}, u32[]{:S(2)}) collective-permute-start(f32[224,128]{1,0:T(8,128)S(1)} %pad_maximum_fusion.4), channel_id=1, source_target_pairs={{0,4},{1,5},{2,6},{3,7},{4,0},{5,1},{6,2},{7,3},{8,12},{9,13},{10,... | collective-permute-start | bytes 344072 | tf_op jit(solution)/shard_map/ppermute | solution.py:291
  95.8 6.1 %collective-permute-start.24 = (f32[448,128]{1,0:T(8,128)S(1)}, f32[448,128]{1,0:T(8,128)S(1)}, u32[]{:S(2)}, u32[]{:S(2)}) collective-permute-start(f32[448,128]{1,0:T(8,128)S(1)} %pad_maximum_fusion.3), channel_id=1, source_target_pairs={{0,2},{1,3},{2,0},{3,1},{4,6},{5,7},{6,4},{7,5},{8,10},{9,11},{10,... | collective-permute-start | bytes 688136 | tf_op jit(solution)/shard_map/ppermute | solution.py:291
  98.6 6.1 %collective-permute-start.17 = (f32[448,128]{1,0:T(8,128)S(1)}, f32[448,128]{1,0:T(8,128)S(1)}, u32[]{:S(2)}, u32[]{:S(2)}) collective-permute-start(f32[448,128]{1,0:T(8,128)S(1)} %pad_maximum_fusion.2), channel_id=1, source_target_pairs={{0,2},{1,3},{2,0},{3,1},{4,6},{5,7},{6,4},{7,5},{8,10},{9,11},{10,... | collective-permute-start | bytes 688136 | tf_op jit(solution)/shard_map/ppermute | solution.py:291
  102.1 2.8 %collective-permute-start.25 = (f32[896,128]{1,0:T(8,128)S(1)}, f32[896,128]{1,0:T(8,128)S(1)}, u32[]{:S(2)}, u32[]{:S(2)}) collective-permute-start(f32[896,128]{1,0:T(8,128)S(1)} %pad_maximum_fusion.1.refs_2_), channel_id=1, source_target_pairs={{0,1},{1,0},{2,3},{3,2},{4,5},{5,4},{6,7},{7,6},{8,9},{9,8},{10,11... | collective-permute-start | bytes 1376264 | tf_op jit(solution)/shard_map/ppermute | solution.py:291
  104.8 1.9 %collective-permute-start.18 = (f32[896,128]{1,0:T(8,128)S(1)}, f32[896,128]{1,0:T(8,128)S(1)}, u32[]{:S(2)}, u32[]{:S(2)}) collective-permute-start(f32[896,128]{1,0:T(8,128)S(1)} %pad_maximum_fusion.refs_0_), channel_id=1, source_target_pairs={{0,1},{1,0},{2,3},{3,2},{4,5},{5,4},{6,7},{7,6},{8,9},{9,8},{10,11... | collective-permute-start | bytes 1376264 | tf_op jit(solution)/shard_map/ppermute | solution.py:291

commit v6 on v5

--- a/solution.py
+++ b/solution.py
@@ -396,7 +396,6 @@
     near, far = travel(near, far)
 
     sum_1 = keep_1 + exchange(send_1, 1)
-    sum_1, near, far = lax.optimization_barrier((sum_1, near, far))
     sum_1 = fold(sum_1, masks[0])
 
     keep, send, gm_0, gh3_0 = pl.pallas_call(
@@ -408,6 +407,11 @@
         **kernel_options("lower", 16, 5),
     )(where, distances, tab_0, *stay(grad_1, wo3_0, slope_0, x2_0, h2_0, where=pltpu.HBM), near, *far)
     sum_0 = keep + exchange(send, 1)
+    steps = [(fold, mask) for mask in masks] + [(spread, mask) for mask in masks[::-1]]
+    for (step, mask), (ahead, mask_1) in zip(steps[:-1], steps[1:]):
+        sum_1, _ = lax.optimization_barrier((sum_1, sum_0))
+        sum_1 = ahead(sum_1, mask_1)
+        sum_0 = step(sum_0, mask)
     sum_0, gm_0 = lax.optimization_barrier((sum_0, gm_0))
 
     input_grad = pl.pallas_call(
@@ -419,16 +423,9 @@
         **kernel_options("inward", 12, 3),
     )(*stay(wi3_0, gm_0, gh3_0, where=pltpu.HBM))
     sum_1, _ = lax.optimization_barrier((sum_1, sum_0))
-    for number, mask in enumerate(masks):
-        if number > 0:
-            sum_1 = fold(sum_1, mask)
-        if number == 1:
-            sum_0, input_grad = lax.optimization_barrier((sum_0, input_grad))
-        sum_0 = fold(sum_0, mask)
-    for mask in masks[::-1]:
-        sum_1 = spread(sum_1, mask)
-        sum_0 = spread(sum_0, mask)
     other_1 = exchange(sum_1, 1)
+    sum_0 = spread(sum_0, masks[0])
+    sum_0, input_grad = lax.optimization_barrier((sum_0, input_grad))
     other_0 = exchange(sum_0, 1)
 
     w_in_grad, bias_grad, w_out_t_grad = pl.pallas_call(

time: 109 us -> 107 us (0.982)
  waiting for transfers between devices: 40.7 us -> 37.1 us
  starting transfers between devices: 31.7 us -> 34.4 us
    ppermute x18, starting transfers between devices: 21.3 us -> 24.8 us  [exchange(): return lax.ppermute(value, 'seq', [(s, s ^ mask) for s in range(count)])]
    ppermute x6, waiting for transfers between devices: 15.4 us -> 12.5 us  [from_ahead(): lax.ppermute(value, 'seq', [(s, (s - steps) % count) for s in range(count)])]
  transfers between devices with their start and end apart: 26 -> 26, of which waited for: 14 -> 16; matrix products, arithmetic and copies ran while one was open for 3% -> 3% of each run, Pallas kernels for 17% -> 18%
where the time goes in v6:
time: 107 us
  waiting for transfers between devices  37.1 us (35%)
  starting transfers between devices  34.4 us (32%)
  Pallas kernels  31.2 us (29%)
  local copies, waits for them, and re-layouts  1.72 us (2%)
  other arithmetic  1.7 us (2%)
    ppermute x18, starting transfers between devices, exchange(): return lax.ppermute(value, 'seq', [(s, s ^ mask) for s in range(count)])  24.8 us
    ppermute x18, waiting for transfers between devices, exchange(): return lax.ppermute(value, 'seq', [(s, s ^ mask) for s in range(count)])  24.6 us
    ppermute x6, waiting for transfers between devices, from_ahead(): lax.ppermute(value, 'seq', [(s, (s - steps) % count) for s in range(count)])  12.5 us
    ppermute x6, starting transfers between devices, from_ahead(): lax.ppermute(value, 'seq', [(s, (s - steps) % count) for s in range(count)])  8.32 us
    pallas_call x1, Pallas kernels, body(): pl.pallas_call(lambda *refs: act_kernel(hops, pos, *refs), out_shape=[sha...  7.89 us
    pallas_call x1, Pallas kernels, body(): pl.pallas_call(lambda *refs: upper_kernel(hops, pos, factor, *refs), out_...  7.79 us
    pallas_call x1, Pallas kernels, body(): pl.pallas_call(lambda *refs: lower_kernel(hops, pos, factor, *refs), out_...  6.69 us
    pallas_call x1, Pallas kernels, body(): pl.pallas_call(lambda *refs: input_kernel(pos, *refs), out_shape=shape(D,...  4.24 us
  transfers between devices with their start and end apart: 26, of which 16 were waited for; matrix products, arithmetic and copies ran while one was open for 3% of the time, Pallas kernels for 18%

profile of v6, /device:TPU:0, one launch (start us, length us, event | category | flops | bytes accessed | tf_op | source)
XLA Modules:
  0.0 107.1 jit_solution(6858840621273924742)
XLA Ops:
  0.7 2.7 %pack.1 = (s32[32]{0:T(128)S(1)}, f32[16,6144]{1,0:T(8,128)S(1)}, f32[48,1024]{1,0:T(8,128)S(1)}, f32[48,1024]{1,0:T(8,128)S(1)}, f32[48,1024]{1,0:T(8,128)S(1)}) custom-call(s32[2,18]{1,0:T(2,128)} %refs_1_.7, f32[288,1024]{1,0:T(8,128)} %refs_4_.1), custom_call_target="tpu_custom_call" | custom-call | flops 2000000000 | bytes 6000000 | tf_op jit(solution)/shard_map/pack/pallas_call | solution.py:348
  3.4 3.0 %collective-permute-start.1 = (f32[48,1024]{1,0:T(8,128)S(1)}, f32[48,1024]{1,0:T(8,128)S(1)}, u32[]{:S(2)}, u32[]{:S(2)}) collective-permute-start(f32[48,1024]{1,0:T(8,128)S(1)} %get-tuple-element.52), channel_id=1, source_target_pairs={{0,2},{1,3},{2,0},{3,1},{4,6},{5,7},{6,4},{7,5},{8,10},{9,11},{10,... | collective-permute-start | bytes 589832 | tf_op jit(solution)/shard_map/ppermute | solution.py:291
  6.4 2.7 %collective-permute-start = (f32[16,6144]{1,0:T(8,128)S(1)}, f32[16,6144]{1,0:T(8,128)S(1)}, u32[]{:S(2)}, u32[]{:S(2)}) collective-permute-start(f32[16,6144]{1,0:T(8,128)S(1)} %get-tuple-element.51), channel_id=1, source_target_pairs={{0,15},{1,0},{2,1},{3,2},{4,3},{5,4},{6,5},{7,6},{8,7},{9,8},{10,9... | collective-permute-start | bytes 1179656 | tf_op jit(solution)/shard_map/ppermute | solution.py:286
  9.1 0.9 collective-permute-start.3
  10.0 0.1 copy.11.refs_3_
  10.1 0.1 copy.12.refs_7_
  10.3 1.4 %slice_bitcast_fusion = (f32[288,384]{1,0:T(8,128)S(1)}, f32[288,384]{1,0:T(8,128)S(1)}, f32[288,384]{1,0:T(8,128)S(1)}, f32[288,384]{1,0:T(8,128)S(1)}) fusion(f32[2,288,384]{2,1,0:T(8,128)S(1)} %bitcast.16, f32[2,288,384]{2,1,0:T(8,128)} %param.10), kind=kLoop, calls=%fused_computation.2 | loop fusion | bytes 3538944 | tf_op jit(solution)/shard_map/squeeze | solution.py:362
  11.8 0.7 collective-permute-done.1.refs_11_
  12.5 0.7 collective-permute-start.2
  13.1 7.9 %act.1 = (s32[32]{0:T(128)S(1)}, bf16[608,1024]{1,0:T(8,128)(2,1)}, bf16[768,1024]{1,0:T(8,128)(2,1)}, f32[384,1024]{1,0:T(8,128)}, bf16[288,1152]{1,0:T(8,128)(...) custom-call(s32[2,18]{1,0:T(2,128)} %refs_1_.7, ...), custom_call_target="tpu_custom_call" | custom-call | flops 5000000000 | bytes 15000000 | tf_op jit(solution)/shard_map/act/pallas_call | solution.py:370
  21.1 0.1 pad_add_fusion.refs_0_.odd
  21.1 6.2 %collective-permute-done.4.refs_14_ = f32[48,1024]{1,0:T(8,128)S(1)} collective-permute-done((f32[48,1024]{1,0:T(8,128)S(1)}, f32[48,1024]{1,0:T(8,128)S(1)}, u32[]{:S(2)}, u32[]{:S(2)}) %collective-permute-start.4) | collective-permute-done | bytes 196640 | tf_op jit(solution)/shard_map/ppermute | solution.py:286
  27.4 7.8 %upper.1 = (f32[16,6144]{1,0:T(8,128)S(1)}, f32[48,1024]{1,0:T(8,128)S(1)}, f32[48,1024]{1,0:T(8,128)S(1)}, f32[48,1024]{1,0:T(8,128)S(1)}, f32[896,128]{1,0:T(8...) custom-call(s32[2]{0:T(128)S(1)} %pad_add_fusion.refs_0_.odd, s32[2,18]{1,0:T(2,128)} %refs_1_.7, ...), custom_call_target="tpu_custom_call" | custom-call | flops 6000000000 | bytes 18000000 | tf_op jit(solution)/shard_map/upper/pallas_call | solution.py:387
  35.2 0.1 collective-permute-start.18
  35.2 0.3 collective-permute-start.6
  35.5 4.7 %collective-permute-start.5 = (f32[16,6144]{1,0:T(8,128)S(1)}, f32[16,6144]{1,0:T(8,128)S(1)}, u32[]{:S(2)}, u32[]{:S(2)}) collective-permute-start(f32[16,6144]{1,0:T(8,128)S(1)} %get-tuple-element.60), channel_id=1, source_target_pairs={{0,15},{1,0},{2,1},{3,2},{4,3},{5,4},{6,5},{7,6},{8,7},{9,8},{10,9... | collective-permute-start | bytes 1179656 | tf_op jit(solution)/shard_map/ppermute | solution.py:286
  40.2 3.1 %collective-permute-done.6.refs_9_ = f32[48,1024]{1,0:T(8,128)S(1)} collective-permute-done((f32[48,1024]{1,0:T(8,128)S(1)}, f32[48,1024]{1,0:T(8,128)S(1)}, u32[]{:S(2)}, u32[]{:S(2)}) %collective-permute-start.6) | collective-permute-done | bytes 196640 | tf_op jit(solution)/shard_map/ppermute | solution.py:291
  43.3 0.7 collective-permute-start.7
  44.0 1.1 %add.28 = f32[896,128]{1,0:T(8,128)S(1)} add(f32[896,128]{1,0:T(8,128)S(1)} %get-tuple-element.73, f32[896,128]{1,0:T(8,128)} %collective-permute-done.18) | non-fusion elementwise | flops 114688 | bytes 1376256 | tf_op jit(solution)/shard_map/add | solution.py:398
  45.1 4.7 %collective-permute-start.19 = (f32[448,128]{1,0:T(8,128)S(1)}, f32[448,128]{1,0:T(8,128)S(1)}, u32[]{:S(2)}, u32[]{:S(2)}) collective-permute-start(f32[448,128]{1,0:T(8,128)S(1)} %slice_select_fusion), channel_id=1, source_target_pairs={{0,2},{1,3},{2,0},{3,1},{4,6},{5,7},{6,4},{7,5},{8,10},{9,11},{10,... | collective-permute-start | bytes 688136 | tf_op jit(solution)/shard_map/ppermute | solution.py:291
  49.8 0.8 collective-permute-done.8.refs_11_
  50.7 5.4 %collective-permute-done.9.refs_12_ = f32[48,1024]{1,0:T(8,128)S(1)} collective-permute-done((f32[48,1024]{1,0:T(8,128)S(1)}, f32[48,1024]{1,0:T(8,128)S(1)}, u32[]{:S(2)}, u32[]{:S(2)}) %collective-permute-start.9) | collective-permute-done | bytes 196640 | tf_op jit(solution)/shard_map/ppermute | solution.py:286
  56.1 6.7 %lower.1 = (f32[896,128]{1,0:T(8,128)S(1)}, f32[896,128]{1,0:T(8,128)S(1)}, f32[288,1024]{1,0:T(8,128)}, bf16[1152,1024]{1,0:T(8,128)(2,1)}) custom-call(s32[2]{0:T(128)S(1)} %pad_add_fusion.refs_0_.odd, s32[2,18]{1,0:T(2,128)} %refs_1_.7, s32[32]{0:T(128)S(1)} %get-tuple-element.44.refs_3_.refs_2_, f32[288,1024]{1,0:T(8,128)} %get-tuple-element.55.refs_3_, ...), custom_call_target="tpu_custom_call" | custom-call | flops 5000000000 | bytes 15000000 | tf_op jit(solution)/shard_map/lower/pallas_call | solution.py:401
  62.9 1.7 %collective-permute-done.10 = f32[896,128]{1,0:T(8,128)S(1)} collective-permute-done((f32[896,128]{1,0:T(8,128)S(1)}, f32[896,128]{1,0:T(8,128)S(1)}, u32[]{:S(2)}, u32[]{:S(2)}) %collective-permute-start.10) | collective-permute-done | bytes 458784 | tf_op jit(solution)/shard_map/ppermute | solution.py:291
  64.8 1.5 %collective-permute-start.20 = (f32[224,128]{1,0:T(8,128)S(1)}, f32[224,128]{1,0:T(8,128)S(1)}, u32[]{:S(2)}, u32[]{:S(2)}) collective-permute-start(f32[224,128]{1,0:T(8,128)S(1)} %slice_select_fusion.3), channel_id=1, source_target_pairs={{0,4},{1,5},{2,6},{3,7},{4,0},{5,1},{6,2},{7,3},{8,12},{9,13},{10,... | collective-permute-start | bytes 344072 | tf_op jit(solution)/shard_map/ppermute | solution.py:291
  66.3 1.6 %collective-permute-start.11 = (f32[448,128]{1,0:T(8,128)S(1)}, f32[448,128]{1,0:T(8,128)S(1)}, u32[]{:S(2)}, u32[]{:S(2)}) collective-permute-start(f32[448,128]{1,0:T(8,128)S(1)} %slice_select_fusion.1), channel_id=1, source_target_pairs={{0,2},{1,3},{2,0},{3,1},{4,6},{5,7},{6,4},{7,5},{8,10},{9,11},{10,... | collective-permute-start | bytes 688136 | tf_op jit(solution)/shard_map/ppermute | solution.py:291
  67.9 2.2 %collective-permute-done.20 = f32[224,128]{1,0:T(8,128)S(1)} collective-permute-done((f32[224,128]{1,0:T(8,128)S(1)}, f32[224,128]{1,0:T(8,128)S(1)}, u32[]{:S(2)}, u32[]{:S(2)}) %collective-permute-start.20) | collective-permute-done | bytes 114720 | tf_op jit(solution)/shard_map/ppermute | solution.py:291
  70.0 3.7 %collective-permute-done.11 = f32[448,128]{1,0:T(8,128)S(1)} collective-permute-done((f32[448,128]{1,0:T(8,128)S(1)}, f32[448,128]{1,0:T(8,128)S(1)}, u32[]{:S(2)}, u32[]{:S(2)}) %collective-permute-start.11) | collective-permute-done | bytes 229408 | tf_op jit(solution)/shard_map/ppermute | solution.py:291
  73.8 0.7 collective-permute-start.12
  74.5 3.1 %collective-permute-start.21 = (f32[112,128]{1,0:T(8,128)S(1)}, f32[112,128]{1,0:T(8,128)S(1)}, u32[]{:S(2)}, u32[]{:S(2)}) collective-permute-start(f32[112,128]{1,0:T(8,128)S(1)} %slice_select_fusion.5), channel_id=1, source_target_pairs={{0,8},{1,9},{2,10},{3,11},{4,12},{5,13},{6,14},{7,15},{8,0},{9,1},... | collective-permute-start | bytes 172040 | tf_op jit(solution)/shard_map/ppermute | solution.py:291
  77.6 2.1 %collective-permute-done.12 = f32[224,128]{1,0:T(8,128)S(1)} collective-permute-done((f32[224,128]{1,0:T(8,128)S(1)}, f32[224,128]{1,0:T(8,128)S(1)}, u32[]{:S(2)}, u32[]{:S(2)}) %collective-permute-start.12) | collective-permute-done | bytes 114720 | tf_op jit(solution)/shard_map/ppermute | solution.py:291
  79.7 3.0 %collective-permute-start.13 = (f32[112,128]{1,0:T(8,128)S(1)}, f32[112,128]{1,0:T(8,128)S(1)}, u32[]{:S(2)}, u32[]{:S(2)}) collective-permute-start(f32[112,128]{1,0:T(8,128)S(1)} %slice_select_fusion.4), channel_id=1, source_target_pairs={{0,8},{1,9},{2,10},{3,11},{4,12},{5,13},{6,14},{7,15},{8,0},{9,1},... | collective-permute-start | bytes 172040 | tf_op jit(solution)/shard_map/ppermute | solution.py:291
  82.7 0.1 collective-permute-start.22
  82.8 3.2 %collective-permute-done.13 = f32[112,128]{1,0:T(8,128)S(1)} collective-permute-done((f32[112,128]{1,0:T(8,128)S(1)}, f32[112,128]{1,0:T(8,128)S(1)}, u32[]{:S(2)}, u32[]{:S(2)}) %collective-permute-start.13) | collective-permute-done | bytes 57376 | tf_op jit(solution)/shard_map/ppermute | solution.py:291
  86.0 2.2 %collective-permute-start.14 = (f32[112,128]{1,0:T(8,128)S(1)}, f32[112,128]{1,0:T(8,128)S(1)}, u32[]{:S(2)}, u32[]{:S(2)}) collective-permute-start(f32[112,128]{1,0:T(8,128)S(1)} %select_add_fusion.5), channel_id=1, source_target_pairs={{0,8},{1,9},{2,10},{3,11},{4,12},{5,13},{6,14},{7,15},{8,0},{9,1},... | collective-permute-start | bytes 172040 | tf_op jit(solution)/shard_map/ppermute | solution.py:291
  88.2 0.8 collective-permute-done.22
  89.0 0.4 collective-permute-start.23
  89.4 2.3 %collective-permute-done.14 = f32[112,128]{1,0:T(8,128)S(1)} collective-permute-done((f32[112,128]{1,0:T(8,128)S(1)}, f32[112,128]{1,0:T(8,128)S(1)}, u32[]{:S(2)}, u32[]{:S(2)}) %collective-permute-start.14) | collective-permute-done | bytes 57376 | tf_op jit(solution)/shard_map/ppermute | solution.py:291
  91.8 0.2 collective-permute-start.15
  92.0 1.9 %collective-permute-done.23 = f32[224,128]{1,0:T(8,128)S(1)} collective-permute-done((f32[224,128]{1,0:T(8,128)S(1)}, f32[224,128]{1,0:T(8,128)S(1)}, u32[]{:S(2)}, u32[]{:S(2)}) %collective-permute-start.23) | collective-permute-done | bytes 114720 | tf_op jit(solution)/shard_map/ppermute | solution.py:291
  93.9 1.6 %collective-permute-start.24 = (f32[448,128]{1,0:T(8,128)S(1)}, f32[448,128]{1,0:T(8,128)S(1)}, u32[]{:S(2)}, u32[]{:S(2)}) collective-permute-start(f32[448,128]{1,0:T(8,128)S(1)} %pad_maximum_fusion.3), channel_id=1, source_target_pairs={{0,2},{1,3},{2,0},{3,1},{4,6},{5,7},{6,4},{7,5},{8,10},{9,11},{10,... | collective-permute-start | bytes 688136 | tf_op jit(solution)/shard_map/ppermute | solution.py:291
  95.5 1.1 %collective-permute-done.15 = f32[224,128]{1,0:T(8,128)S(1)} collective-permute-done((f32[224,128]{1,0:T(8,128)S(1)}, f32[224,128]{1,0:T(8,128)S(1)}, u32[]{:S(2)}, u32[]{:S(2)}) %collective-permute-start.15) | collective-permute-done | bytes 114720 | tf_op jit(solution)/shard_map/ppermute | solution.py:291
  96.7 1.7 %collective-permute-start.16 = (f32[448,128]{1,0:T(8,128)S(1)}, f32[448,128]{1,0:T(8,128)S(1)}, u32[]{:S(2)}, u32[]{:S(2)}) collective-permute-start(f32[448,128]{1,0:T(8,128)S(1)} %pad_maximum_fusion.2), channel_id=1, source_target_pairs={{0,2},{1,3},{2,0},{3,1},{4,6},{5,7},{6,4},{7,5},{8,10},{9,11},{10,... | collective-permute-start | bytes 688136 | tf_op jit(solution)/shard_map/ppermute | solution.py:291
  98.3 4.2 %inward.1 = f32[288,1024]{1,0:T(8,128)} custom-call(bf16[288,1152]{1,0:T(8,128)(2,1)} %get-tuple-element.68.refs_0_, f32[288,1024]{1,0:T(8,128)} %get-tuple-element.69.refs_1_, bf16[1152,1024]{1,0:T(8,128)(2,1)} %get-tuple-element.70.refs_2_), custom_call_target="tpu_custom_call" | custom-call | flops 3000000000 | bytes 9000000 | tf_op jit(solution)/shard_map/inward/pallas_call | solution.py:417
  102.9 0.5 collective-permute-start.17
  103.4 1.2 %collective-permute-done.25.refs_3_ = f32[896,128]{1,0:T(8,128)S(1)} collective-permute-done((f32[896,128]{1,0:T(8,128)S(1)}, f32[896,128]{1,0:T(8,128)S(1)}, u32[]{:S(2)}, u32[]{:S(2)}) %collective-permute-start.25) | collective-permute-done | bytes 458784 | tf_op jit(solution)/shard_map/ppermute | solution.py:291
  104.6 0.7 collective-permute-done.17.refs_1_
  105.2 1.9 %finish.1 = (f32[2,288,384]{2,1,0:T(8,128)}, f32[2,384]{1,0:T(2,128)}, f32[2,288,384]{2,1,0:T(8,128)}) custom-call(s32[2]{0:T(128)S(1)} %pad_add_fusion.refs_0_.odd, f32[896,128]{1,0:T(8,128)S(1)} %pad_maximum_fusion.refs_0_, f32[896,128]{1,0:T(8,128)S(1)} %collective-permute-done.17.refs_1_, f32[896,128]{1,0:T(8,128)S(1)} %pad_maximum_fusion.1.refs_2_, ...), custom_call_target="tpu_custom_call" | custom-call | flops 1000000000 | bytes 3000000 | tf_op jit(solution)/shard_map/finish/pallas_call | solution.py:431
  (49 shorter events, 0.7 us)
Async XLA Ops:
  0.6 9.4 %copy-start.3 = (f32[2,384]{1,0:T(2,128)S(1)}, f32[2,384]{1,0:T(2,128)}, u32[]{:S(2)}) copy-start(f32[2,384]{1,0:T(2,128)} %param.11) | copy-start | bytes 9220
  0.6 9.7 %copy-start.2 = (f32[2,384,288]{1,2,0:T(8,128)S(1)}, f32[2,384,288]{1,2,0:T(8,128)}, u32[]{:S(2)}) copy-start(f32[2,384,288]{1,2,0:T(8,128)} %param.12) | copy-start | bytes 2654212
  3.4 9.1 %collective-permute-start.1 = (f32[48,1024]{1,0:T(8,128)S(1)}, f32[48,1024]{1,0:T(8,128)S(1)}, u32[]{:S(2)}, u32[]{:S(2)}) collective-permute-start(f32[48,1024]{1,0:T(8,128)S(1)} %get-tuple-element.52), channel_id=1, source_target_pairs={{0,2},{1,3},{2,0},{3,1},{4,6},{5,7},{6,4},{7,5},{8,10},{9,11},{10,... | collective-permute-start | bytes 589832 | tf_op jit(solution)/shard_map/ppermute | solution.py:291
  6.4 21.0 %collective-permute-start = (f32[16,6144]{1,0:T(8,128)S(1)}, f32[16,6144]{1,0:T(8,128)S(1)}, u32[]{:S(2)}, u32[]{:S(2)}) collective-permute-start(f32[16,6144]{1,0:T(8,128)S(1)} %get-tuple-element.51), channel_id=1, source_target_pairs={{0,15},{1,0},{2,1},{3,2},{4,3},{5,4},{6,5},{7,6},{8,7},{9,8},{10,9... | collective-permute-start | bytes 1179656 | tf_op jit(solution)/shard_map/ppermute | solution.py:286
  9.1 12.0 %collective-permute-start.3 = (f32[48,1024]{1,0:T(8,128)S(1)}, f32[48,1024]{1,0:T(8,128)S(1)}, u32[]{:S(2)}, u32[]{:S(2)}) collective-permute-start(f32[48,1024]{1,0:T(8,128)S(1)} %get-tuple-element.53), channel_id=1, source_target_pairs={{0,12},{1,13},{2,14},{3,15},{4,0},{5,1},{6,2},{7,3},{8,4},{9,5},{1... | collective-permute-start | bytes 589832 | tf_op jit(solution)/shard_map/ppermute | solution.py:286
  10.0 17.4 %collective-permute-start.4 = (f32[48,1024]{1,0:T(8,128)S(1)}, f32[48,1024]{1,0:T(8,128)S(1)}, u32[]{:S(2)}, u32[]{:S(2)}) collective-permute-start(f32[48,1024]{1,0:T(8,128)S(1)} %get-tuple-element.54), channel_id=1, source_target_pairs={{0,8},{1,9},{2,10},{3,11},{4,12},{5,13},{6,14},{7,15},{8,0},{9,1},... | collective-permute-start | bytes 589832 | tf_op jit(solution)/shard_map/ppermute | solution.py:286
  10.3 2.8 %copy-start = (f32[288,1024]{1,0:T(8,128)S(1)}, f32[288,1024]{1,0:T(8,128)}, u32[]{:S(2)}) copy-start(f32[288,1024]{1,0:T(8,128)} %refs_1_.4) | copy-start | bytes 3538948
  10.3 2.8 %copy-start.1 = (f32[288,1024]{1,0:T(8,128)S(1)}, f32[288,1024]{1,0:T(8,128)}, u32[]{:S(2)}) copy-start(f32[288,1024]{1,0:T(8,128)} %refs_5_.1) | copy-start | bytes 3538948
  12.5 14.9 %collective-permute-start.2 = (f32[48,1024]{1,0:T(8,128)S(1)}, f32[48,1024]{1,0:T(8,128)S(1)}, u32[]{:S(2)}, u32[]{:S(2)}) collective-permute-start(f32[48,1024]{1,0:T(8,128)S(1)} %collective-permute-done.1.refs_11_), channel_id=1, source_target_pairs={{2,14},{3,15},{6,2},{7,3},{10,6},{11,7},{14,10},{15,11},{18,30},{1... | collective-permute-start | bytes 589832 | tf_op jit(solution)/shard_map/ppermute | solution.py:341
  35.2 8.8 %collective-permute-start.18 = (f32[896,128]{1,0:T(8,128)S(1)}, f32[896,128]{1,0:T(8,128)}, u32[]{:S(2)}, u32[]{:S(2)}) collective-permute-start(f32[896,128]{1,0:T(8,128)S(1)} %get-tuple-element.74), channel_id=1, source_target_pairs={{0,1},{1,0},{2,3},{3,2},{4,5},{5,4},{6,7},{7,6},{8,9},{9,8},{10,11... | collective-permute-start | bytes 1376264 | tf_op jit(solution)/shard_map/ppermute | solution.py:291
  35.2 8.1 %collective-permute-start.6 = (f32[48,1024]{1,0:T(8,128)S(1)}, f32[48,1024]{1,0:T(8,128)S(1)}, u32[]{:S(2)}, u32[]{:S(2)}) collective-permute-start(f32[48,1024]{1,0:T(8,128)S(1)} %get-tuple-element.61), channel_id=1, source_target_pairs={{0,2},{1,3},{2,0},{3,1},{4,6},{5,7},{6,4},{7,5},{8,10},{9,11},{10,... | collective-permute-start | bytes 589832 | tf_op jit(solution)/shard_map/ppermute | solution.py:291
  35.5 20.6 %collective-permute-start.5 = (f32[16,6144]{1,0:T(8,128)S(1)}, f32[16,6144]{1,0:T(8,128)S(1)}, u32[]{:S(2)}, u32[]{:S(2)}) collective-permute-start(f32[16,6144]{1,0:T(8,128)S(1)} %get-tuple-element.60), channel_id=1, source_target_pairs={{0,15},{1,0},{2,1},{3,2},{4,3},{5,4},{6,5},{7,6},{8,7},{9,8},{10,9... | collective-permute-start | bytes 1179656 | tf_op jit(solution)/shard_map/ppermute | solution.py:286
  40.2 10.5 %collective-permute-start.8 = (f32[48,1024]{1,0:T(8,128)S(1)}, f32[48,1024]{1,0:T(8,128)S(1)}, u32[]{:S(2)}, u32[]{:S(2)}) collective-permute-start(f32[48,1024]{1,0:T(8,128)S(1)} %get-tuple-element.62), channel_id=1, source_target_pairs={{0,12},{1,13},{2,14},{3,15},{4,0},{5,1},{6,2},{7,3},{8,4},{9,5},{1... | collective-permute-start | bytes 589832 | tf_op jit(solution)/shard_map/ppermute | solution.py:286
  40.2 15.9 %collective-permute-start.9 = (f32[48,1024]{1,0:T(8,128)S(1)}, f32[48,1024]{1,0:T(8,128)S(1)}, u32[]{:S(2)}, u32[]{:S(2)}) collective-permute-start(f32[48,1024]{1,0:T(8,128)S(1)} %get-tuple-element.63), channel_id=1, source_target_pairs={{0,8},{1,9},{2,10},{3,11},{4,12},{5,13},{6,14},{7,15},{8,0},{9,1},... | collective-permute-start | bytes 589832 | tf_op jit(solution)/shard_map/ppermute | solution.py:286
  43.3 12.8 %collective-permute-start.7 = (f32[48,1024]{1,0:T(8,128)S(1)}, f32[48,1024]{1,0:T(8,128)S(1)}, u32[]{:S(2)}, u32[]{:S(2)}) collective-permute-start(f32[48,1024]{1,0:T(8,128)S(1)} %collective-permute-done.6.refs_9_), channel_id=1, source_target_pairs={{2,14},{3,15},{6,2},{7,3},{10,6},{11,7},{14,10},{15,11},{18,30},{1... | collective-permute-start | bytes 589832 | tf_op jit(solution)/shard_map/ppermute | solution.py:341
  45.1 17.8 %collective-permute-start.19 = (f32[448,128]{1,0:T(8,128)S(1)}, f32[448,128]{1,0:T(8,128)S(1)}, u32[]{:S(2)}, u32[]{:S(2)}) collective-permute-start(f32[448,128]{1,0:T(8,128)S(1)} %slice_select_fusion), channel_id=1, source_target_pairs={{0,2},{1,3},{2,0},{3,1},{4,6},{5,7},{6,4},{7,5},{8,10},{9,11},{10,... | collective-permute-start | bytes 688136 | tf_op jit(solution)/shard_map/ppermute | solution.py:291
  62.8 1.9 %collective-permute-start.10 = (f32[896,128]{1,0:T(8,128)S(1)}, f32[896,128]{1,0:T(8,128)S(1)}, u32[]{:S(2)}, u32[]{:S(2)}) collective-permute-start(f32[896,128]{1,0:T(8,128)S(1)} %get-tuple-element.65), channel_id=1, source_target_pairs={{0,1},{1,0},{2,3},{3,2},{4,5},{5,4},{6,7},{7,6},{8,9},{9,8},{10,11... | collective-permute-start | bytes 1376264 | tf_op jit(solution)/shard_map/ppermute | solution.py:291
  64.8 5.3 %collective-permute-start.20 = (f32[224,128]{1,0:T(8,128)S(1)}, f32[224,128]{1,0:T(8,128)S(1)}, u32[]{:S(2)}, u32[]{:S(2)}) collective-permute-start(f32[224,128]{1,0:T(8,128)S(1)} %slice_select_fusion.3), channel_id=1, source_target_pairs={{0,4},{1,5},{2,6},{3,7},{4,0},{5,1},{6,2},{7,3},{8,12},{9,13},{10,... | collective-permute-start | bytes 344072 | tf_op jit(solution)/shard_map/ppermute | solution.py:291
  66.3 7.4 %collective-permute-start.11 = (f32[448,128]{1,0:T(8,128)S(1)}, f32[448,128]{1,0:T(8,128)S(1)}, u32[]{:S(2)}, u32[]{:S(2)}) collective-permute-start(f32[448,128]{1,0:T(8,128)S(1)} %slice_select_fusion.1), channel_id=1, source_target_pairs={{0,2},{1,3},{2,0},{3,1},{4,6},{5,7},{6,4},{7,5},{8,10},{9,11},{10,... | collective-permute-start | bytes 688136 | tf_op jit(solution)/shard_map/ppermute | solution.py:291
  73.8 5.9 %collective-permute-start.12 = (f32[224,128]{1,0:T(8,128)S(1)}, f32[224,128]{1,0:T(8,128)S(1)}, u32[]{:S(2)}, u32[]{:S(2)}) collective-permute-start(f32[224,128]{1,0:T(8,128)S(1)} %slice_select_fusion.2), channel_id=1, source_target_pairs={{0,4},{1,5},{2,6},{3,7},{4,0},{5,1},{6,2},{7,3},{8,12},{9,13},{10,... | collective-permute-start | bytes 344072 | tf_op jit(solution)/shard_map/ppermute | solution.py:291
  74.5 8.3 %collective-permute-start.21 = (f32[112,128]{1,0:T(8,128)S(1)}, f32[112,128]{1,0:T(8,128)S(1)}, u32[]{:S(2)}, u32[]{:S(2)}) collective-permute-start(f32[112,128]{1,0:T(8,128)S(1)} %slice_select_fusion.5), channel_id=1, source_target_pairs={{0,8},{1,9},{2,10},{3,11},{4,12},{5,13},{6,14},{7,15},{8,0},{9,1},... | collective-permute-start | bytes 172040 | tf_op jit(solution)/shard_map/ppermute | solution.py:291
  79.7 6.3 %collective-permute-start.13 = (f32[112,128]{1,0:T(8,128)S(1)}, f32[112,128]{1,0:T(8,128)S(1)}, u32[]{:S(2)}, u32[]{:S(2)}) collective-permute-start(f32[112,128]{1,0:T(8,128)S(1)} %slice_select_fusion.4), channel_id=1, source_target_pairs={{0,8},{1,9},{2,10},{3,11},{4,12},{5,13},{6,14},{7,15},{8,0},{9,1},... | collective-permute-start | bytes 172040 | tf_op jit(solution)/shard_map/ppermute | solution.py:291
  82.7 6.2 %collective-permute-start.22 = (f32[112,128]{1,0:T(8,128)S(1)}, f32[112,128]{1,0:T(8,128)S(1)}, u32[]{:S(2)}, u32[]{:S(2)}) collective-permute-start(f32[112,128]{1,0:T(8,128)S(1)} %select_add_fusion.4), channel_id=1, source_target_pairs={{0,8},{1,9},{2,10},{3,11},{4,12},{5,13},{6,14},{7,15},{8,0},{9,1},... | collective-permute-start | bytes 172040 | tf_op jit(solution)/shard_map/ppermute | solution.py:291
  86.0 5.8 %collective-permute-start.14 = (f32[112,128]{1,0:T(8,128)S(1)}, f32[112,128]{1,0:T(8,128)S(1)}, u32[]{:S(2)}, u32[]{:S(2)}) collective-permute-start(f32[112,128]{1,0:T(8,128)S(1)} %select_add_fusion.5), channel_id=1, source_target_pairs={{0,8},{1,9},{2,10},{3,11},{4,12},{5,13},{6,14},{7,15},{8,0},{9,1},... | collective-permute-start | bytes 172040 | tf_op jit(solution)/shard_map/ppermute | solution.py:291
  89.0 4.9 %collective-permute-start.23 = (f32[224,128]{1,0:T(8,128)S(1)}, f32[224,128]{1,0:T(8,128)S(1)}, u32[]{:S(2)}, u32[]{:S(2)}) collective-permute-start(f32[224,128]{1,0:T(8,128)S(1)} %pad_maximum_fusion.5), channel_id=1, source_target_pairs={{0,4},{1,5},{2,6},{3,7},{4,0},{5,1},{6,2},{7,3},{8,12},{9,13},{10,... | collective-permute-start | bytes 344072 | tf_op jit(solution)/shard_map/ppermute | solution.py:291
  91.8 4.9 %collective-permute-start.15 = (f32[224,128]{1,0:T(8,128)S(1)}, f32[224,128]{1,0:T(8,128)S(1)}, u32[]{:S(2)}, u32[]{:S(2)}) collective-permute-start(f32[224,128]{1,0:T(8,128)S(1)} %pad_maximum_fusion.4), channel_id=1, source_target_pairs={{0,4},{1,5},{2,6},{3,7},{4,0},{5,1},{6,2},{7,3},{8,12},{9,13},{10,... | collective-permute-start | bytes 344072 | tf_op jit(solution)/shard_map/ppermute | solution.py:291
  93.9 8.7 %collective-permute-start.24 = (f32[448,128]{1,0:T(8,128)S(1)}, f32[448,128]{1,0:T(8,128)S(1)}, u32[]{:S(2)}, u32[]{:S(2)}) collective-permute-start(f32[448,128]{1,0:T(8,128)S(1)} %pad_maximum_fusion.3), channel_id=1, source_target_pairs={{0,2},{1,3},{2,0},{3,1},{4,6},{5,7},{6,4},{7,5},{8,10},{9,11},{10,... | collective-permute-start | bytes 688136 | tf_op jit(solution)/shard_map/ppermute | solution.py:291
  96.7 6.1 %collective-permute-start.16 = (f32[448,128]{1,0:T(8,128)S(1)}, f32[448,128]{1,0:T(8,128)S(1)}, u32[]{:S(2)}, u32[]{:S(2)}) collective-permute-start(f32[448,128]{1,0:T(8,128)S(1)} %pad_maximum_fusion.2), channel_id=1, source_target_pairs={{0,2},{1,3},{2,0},{3,1},{4,6},{5,7},{6,4},{7,5},{8,10},{9,11},{10,... | collective-permute-start | bytes 688136 | tf_op jit(solution)/shard_map/ppermute | solution.py:291
  102.7 1.9 %collective-permute-start.25 = (f32[896,128]{1,0:T(8,128)S(1)}, f32[896,128]{1,0:T(8,128)S(1)}, u32[]{:S(2)}, u32[]{:S(2)}) collective-permute-start(f32[896,128]{1,0:T(8,128)S(1)} %pad_maximum_fusion.1.refs_2_), channel_id=1, source_target_pairs={{0,1},{1,0},{2,3},{3,2},{4,5},{5,4},{6,7},{7,6},{8,9},{9,8},{10,11... | collective-permute-start | bytes 1376264 | tf_op jit(solution)/shard_map/ppermute | solution.py:291
  102.9 2.4 %collective-permute-start.17 = (f32[896,128]{1,0:T(8,128)S(1)}, f32[896,128]{1,0:T(8,128)S(1)}, u32[]{:S(2)}, u32[]{:S(2)}) collective-permute-start(f32[896,128]{1,0:T(8,128)S(1)} %pad_maximum_fusion.refs_0_), channel_id=1, source_target_pairs={{0,1},{1,0},{2,3},{3,2},{4,5},{5,4},{6,7},{7,6},{8,9},{9,8},{10,11... | collective-permute-start | bytes 1376264 | tf_op jit(solution)/shard_map/ppermute | solution.py:291

commit v7 on v6

--- a/solution.py
+++ b/solution.py
@@ -291,7 +291,7 @@
     return lax.ppermute(value, "seq", [(s, s ^ mask) for s in range(count)])
 
 
-def fold(x, mask, send=None):
+def fold(x, mask):
     half = x.shape[0] // 2
     bit = (lax.axis_index("seq") & mask) != 0
     low, high = x[:half], x[half:]
@@ -302,6 +302,32 @@
     bit = (lax.axis_index("seq") & mask) != 0
     other = exchange(x, mask)
     return jnp.concatenate([jnp.where(bit, other, x), jnp.where(bit, x, other)], 0)
+
+
+def groups_of_four(offset):
+    count = lax.axis_size("seq")
+    return [(s, (s + 4 * offset) % count) for s in range(count)]
+
+
+def fold_far(x):
+    number = lax.axis_size("seq") // 4
+    mine = lax.axis_index("seq") >> 2
+    rows = x.shape[0] // number
+
+    def part(group):
+        return lax.dynamic_slice_in_dim(x, (group % number) * rows, rows, 0)
+
+    arrived = [lax.ppermute(part(mine + o), "seq", groups_of_four(o)) for o in range(1, number)]
+    return sum(arrived, part(mine))
+
+
+def spread_far(x):
+    number = lax.axis_size("seq") // 4
+    mine = lax.axis_index("seq") >> 2
+    rows = x.shape[0]
+    arrived = [lax.ppermute(x, "seq", groups_of_four(o)) for o in range(1, number)]
+    turned = jnp.concatenate([x] + arrived[::-1], 0)
+    return lax.dynamic_slice_in_dim(jnp.concatenate([turned, turned], 0), ((number - mine) % number) * rows, number * rows, 0)
 
 
 def shape(*dims, dtype=f32):
@@ -329,7 +355,6 @@
     far_shapes = [shape(MOST * TW, pos)] * (hops - 1)
     near_shape = shape(TW, near_width)
     half = -(-3 * (D + 8) // (8 * count)) * 8 * count
-    masks = [1 << b for b in range(1, hops)]
     far_hops = [1 << k for k in range(1, hops)]
     index = lax.axis_index("seq")
     where = jnp.stack([index & 1, (index >> 1) & 1]).astype(i32)
@@ -396,7 +421,7 @@
     near, far = travel(near, far)
 
     sum_1 = keep_1 + exchange(send_1, 1)
-    sum_1 = fold(sum_1, masks[0])
+    sum_1 = fold(sum_1, 2)
 
     keep, send, gm_0, gh3_0 = pl.pallas_call(
         lambda *refs: lower_kernel(hops, pos, factor, *refs),
@@ -407,11 +432,11 @@
         **kernel_options("lower", 16, 5),
     )(where, distances, tab_0, *stay(grad_1, wo3_0, slope_0, x2_0, h2_0, where=pltpu.HBM), near, *far)
     sum_0 = keep + exchange(send, 1)
-    steps = [(fold, mask) for mask in masks] + [(spread, mask) for mask in masks[::-1]]
-    for (step, mask), (ahead, mask_1) in zip(steps[:-1], steps[1:]):
+    steps = [lambda x: fold(x, 2), fold_far, spread_far, lambda x: spread(x, 2)]
+    for step, ahead in zip(steps[:-1], steps[1:]):
         sum_1, _ = lax.optimization_barrier((sum_1, sum_0))
-        sum_1 = ahead(sum_1, mask_1)
-        sum_0 = step(sum_0, mask)
+        sum_1 = ahead(sum_1)
+        sum_0 = step(sum_0)
     sum_0, gm_0 = lax.optimization_barrier((sum_0, gm_0))
 
     input_grad = pl.pallas_call(
@@ -424,7 +449,7 @@
     )(*stay(wi3_0, gm_0, gh3_0, where=pltpu.HBM))
     sum_1, _ = lax.optimization_barrier((sum_1, sum_0))
     other_1 = exchange(sum_1, 1)
-    sum_0 = spread(sum_0, masks[0])
+    sum_0 = spread(sum_0, 2)
     sum_0, input_grad = lax.optimization_barrier((sum_0, input_grad))
     other_0 = exchange(sum_0, 1)
 

time: 107 us -> 108 us (level)
  waiting for transfers between devices: 37.1 us -> 32.4 us
  starting transfers between devices: 34.4 us -> 38.6 us
    ppermute x0 -> x12, starting transfers between devices: none -> 15.6 us  [the longest x6 9.01 us: fold_far(): lax.ppermute(part(mine + o), 'seq', groups_of_four(o))]
    ppermute x18 -> x10, waiting for transfers between devices: 24.6 us -> 9.84 us  [exchange(): return lax.ppermute(value, 'seq', [(s, s ^ mask) for s in range(count)])]
    ppermute x18 -> x10, starting transfers between devices: 24.8 us -> 13.5 us  [exchange(): return lax.ppermute(value, 'seq', [(s, s ^ mask) for s in range(count)])]
    ppermute x0 -> x12, waiting for transfers between devices: none -> 10.9 us  [the longest x6 6.89 us: fold_far(): lax.ppermute(part(mine + o), 'seq', groups_of_four(o))]
  transfers between devices with their start and end apart: 26 -> 30, of which waited for: 16 -> 18; matrix products, arithmetic and copies ran while one was open for 3% -> 3% of each run, Pallas kernels for 18% -> 18%
where the time goes in v7:
time: 108 us
  starting transfers between devices  38.6 us (36%)
  waiting for transfers between devices  32.4 us (30%)
  Pallas kernels  31.5 us (29%)
  local copies, waits for them, and re-layouts  2.71 us (3%)
  other arithmetic  1.49 us (1%)
  between operations  1.08 us (1%)
    ppermute x10, starting transfers between devices, exchange(): return lax.ppermute(value, 'seq', [(s, s ^ mask) for s in range(count)])  13.5 us
    ppermute x6, waiting for transfers between devices, from_ahead(): lax.ppermute(value, 'seq', [(s, (s - steps) % count) for s in range(count)])  11.7 us
    ppermute x10, waiting for transfers between devices, exchange(): return lax.ppermute(value, 'seq', [(s, s ^ mask) for s in range(count)])  9.84 us
    ppermute x6, starting transfers between devices, fold_far(): lax.ppermute(part(mine + o), 'seq', groups_of_four(o))  9.01 us
    ppermute x6, starting transfers between devices, from_ahead(): lax.ppermute(value, 'seq', [(s, (s - steps) % count) for s in range(count)])  8.24 us
    pallas_call x1, Pallas kernels, body(): pl.pallas_call(lambda *refs: act_kernel(hops, pos, *refs), out_shape=[sha...  7.97 us
    pallas_call x1, Pallas kernels, body(): pl.pallas_call(lambda *refs: upper_kernel(hops, pos, factor, *refs), out_...  7.69 us
    pallas_call x1, Pallas kernels, body(): pl.pallas_call(lambda *refs: lower_kernel(hops, pos, factor, *refs), out_...  7 us
  transfers between devices with their start and end apart: 30, of which 18 were waited for; matrix products, arithmetic and copies ran while one was open for 3% of the time, Pallas kernels for 18%

profile of v7, /device:TPU:0, one launch (start us, length us, event | category | flops | bytes accessed | tf_op | source)
XLA Modules:
  0.0 107.7 jit_solution(180637386766746043)
XLA Ops:
  0.7 2.7 %pack.1 = (s32[32]{0:T(128)S(1)}, f32[16,6144]{1,0:T(8,128)S(1)}, f32[48,1024]{1,0:T(8,128)S(1)}, f32[48,1024]{1,0:T(8,128)S(1)}, f32[48,1024]{1,0:T(8,128)S(1)}) custom-call(s32[2,18]{1,0:T(2,128)} %refs_1_.7, f32[288,1024]{1,0:T(8,128)} %refs_4_.1), custom_call_target="tpu_custom_call" | custom-call | flops 2000000000 | bytes 6000000 | tf_op jit(solution)/shard_map/pack/pallas_call | solution.py:373
  3.4 3.0 %collective-permute-start.1 = (f32[48,1024]{1,0:T(8,128)S(1)}, f32[48,1024]{1,0:T(8,128)S(1)}, u32[]{:S(2)}, u32[]{:S(2)}) collective-permute-start(f32[48,1024]{1,0:T(8,128)S(1)} %get-tuple-element.50), channel_id=1, source_target_pairs={{0,2},{1,3},{2,0},{3,1},{4,6},{5,7},{6,4},{7,5},{8,10},{9,11},{10,... | collective-permute-start | bytes 589832 | tf_op jit(solution)/shard_map/ppermute | solution.py:291
  6.4 2.7 %collective-permute-start = (f32[16,6144]{1,0:T(8,128)S(1)}, f32[16,6144]{1,0:T(8,128)S(1)}, u32[]{:S(2)}, u32[]{:S(2)}) collective-permute-start(f32[16,6144]{1,0:T(8,128)S(1)} %get-tuple-element.49), channel_id=1, source_target_pairs={{0,15},{1,0},{2,1},{3,2},{4,3},{5,4},{6,5},{7,6},{8,7},{9,8},{10,9... | collective-permute-start | bytes 1179656 | tf_op jit(solution)/shard_map/ppermute | solution.py:286
  9.1 0.9 collective-permute-start.3
  10.3 1.5 %slice_bitcast_fusion = (f32[288,384]{1,0:T(8,128)S(1)}, f32[288,384]{1,0:T(8,128)S(1)}, f32[288,384]{1,0:T(8,128)S(1)}, f32[288,384]{1,0:T(8,128)S(1)}) fusion(f32[2,288,384]{2,1,0:T(8,128)S(1)} %bitcast.16, f32[2,288,384]{2,1,0:T(8,128)} %param.10), kind=kLoop, calls=%fused_computation.2 | loop fusion | bytes 3538944 | tf_op jit(solution)/shard_map/squeeze | solution.py:387
  11.8 0.7 collective-permute-done.1.refs_11_
  12.5 0.7 collective-permute-start.2
  13.1 8.0 %act.1 = (s32[32]{0:T(128)S(1)}, bf16[608,1024]{1,0:T(8,128)(2,1)}, bf16[768,1024]{1,0:T(8,128)(2,1)}, f32[384,1024]{1,0:T(8,128)}, bf16[288,1152]{1,0:T(8,128)(...) custom-call(s32[2,18]{1,0:T(2,128)} %refs_1_.7, ...), custom_call_target="tpu_custom_call" | custom-call | flops 5000000000 | bytes 15000000 | tf_op jit(solution)/shard_map/act/pallas_call | solution.py:395
  21.2 6.1 %collective-permute-done.4.refs_14_ = f32[48,1024]{1,0:T(8,128)S(1)} collective-permute-done((f32[48,1024]{1,0:T(8,128)S(1)}, f32[48,1024]{1,0:T(8,128)S(1)}, u32[]{:S(2)}, u32[]{:S(2)}) %collective-permute-start.4) | collective-permute-done | bytes 196640 | tf_op jit(solution)/shard_map/ppermute | solution.py:286
  27.4 7.7 %upper.1 = (f32[16,6144]{1,0:T(8,128)S(1)}, f32[48,1024]{1,0:T(8,128)S(1)}, f32[48,1024]{1,0:T(8,128)S(1)}, f32[48,1024]{1,0:T(8,128)S(1)}, f32[896,128]{1,0:T(8...) custom-call(s32[2]{0:T(128)S(1)} %pad_add_fusion.refs_0_.odd, s32[2,18]{1,0:T(2,128)} %refs_1_.7, ...), custom_call_target="tpu_custom_call" | custom-call | flops 6000000000 | bytes 18000000 | tf_op jit(solution)/shard_map/upper/pallas_call | solution.py:412
  35.1 0.3 collective-permute-start.6
  35.5 4.6 %collective-permute-start.5 = (f32[16,6144]{1,0:T(8,128)S(1)}, f32[16,6144]{1,0:T(8,128)S(1)}, u32[]{:S(2)}, u32[]{:S(2)}) collective-permute-start(f32[16,6144]{1,0:T(8,128)S(1)} %get-tuple-element.58), channel_id=1, source_target_pairs={{0,15},{1,0},{2,1},{3,2},{4,3},{5,4},{6,5},{7,6},{8,7},{9,8},{10,9... | collective-permute-start | bytes 1179656 | tf_op jit(solution)/shard_map/ppermute | solution.py:286
  40.1 3.0 %collective-permute-done.6.refs_9_ = f32[48,1024]{1,0:T(8,128)S(1)} collective-permute-done((f32[48,1024]{1,0:T(8,128)S(1)}, f32[48,1024]{1,0:T(8,128)S(1)}, u32[]{:S(2)}, u32[]{:S(2)}) %collective-permute-start.6) | collective-permute-done | bytes 196640 | tf_op jit(solution)/shard_map/ppermute | solution.py:291
  43.1 0.7 collective-permute-start.7
  43.8 0.8 copy-done.3
  44.5 1.1 add.101
  45.6 4.8 %collective-permute-start.21 = (f32[448,128]{1,0:T(8,128)S(1)}, f32[448,128]{1,0:T(8,128)S(1)}, u32[]{:S(2)}, u32[]{:S(2)}) collective-permute-start(f32[448,128]{1,0:T(8,128)S(1)} %slice_select_fusion), channel_id=1, source_target_pairs={{0,2},{1,3},{2,0},{3,1},{4,6},{5,7},{6,4},{7,5},{8,10},{9,11},{10,... | collective-permute-start | bytes 688136 | tf_op jit(solution)/shard_map/ppermute | solution.py:291
  50.6 5.4 %collective-permute-done.9.refs_12_ = f32[48,1024]{1,0:T(8,128)S(1)} collective-permute-done((f32[48,1024]{1,0:T(8,128)S(1)}, f32[48,1024]{1,0:T(8,128)S(1)}, u32[]{:S(2)}, u32[]{:S(2)}) %collective-permute-start.9) | collective-permute-done | bytes 196640 | tf_op jit(solution)/shard_map/ppermute | solution.py:286
  56.0 7.0 %lower.1 = (f32[896,128]{1,0:T(8,128)S(1)}, f32[896,128]{1,0:T(8,128)S(1)}, f32[288,1024]{1,0:T(8,128)}, bf16[1152,1024]{1,0:T(8,128)(2,1)}) custom-call(s32[2]{0:T(128)S(1)} %pad_add_fusion.refs_0_.odd, s32[2,18]{1,0:T(2,128)} %refs_1_.7, s32[32]{0:T(128)S(1)} %get-tuple-element.42.refs_3_.refs_2_, f32[288,1024]{1,0:T(8,128)} %get-tuple-element.53.refs_3_, ...), custom_call_target="tpu_custom_call" | custom-call | flops 5000000000 | bytes 15000000 | tf_op jit(solution)/shard_map/lower/pallas_call | solution.py:426
  63.2 1.7 %collective-permute-done.10 = f32[896,128]{1,0:T(8,128)S(1)} collective-permute-done((f32[896,128]{1,0:T(8,128)S(1)}, f32[896,128]{1,0:T(8,128)S(1)}, u32[]{:S(2)}, u32[]{:S(2)}) %collective-permute-start.10) | collective-permute-done | bytes 458784 | tf_op jit(solution)/shard_map/ppermute | solution.py:291
  65.0 1.5 %collective-permute-start.22 = (f32[112,128]{1,0:T(8,128)S(1)}, f32[112,128]{1,0:T(8,128)S(1)}, u32[]{:S(2)}, u32[]{:S(2)}) collective-permute-start(f32[112,128]{1,0:T(8,128)S(1)} %get-tuple-element.90), channel_id=1, source_target_pairs={{0,4},{1,5},{2,6},{3,7},{4,8},{5,9},{6,10},{7,11},{8,12},{9,13},{1... | collective-permute-start | bytes 172040 | tf_op jit(solution)/shard_map/ppermute | solution.py:320
  66.4 3.4 %collective-permute-start.23 = (f32[112,128]{1,0:T(8,128)S(1)}, f32[112,128]{1,0:T(8,128)S(1)}, u32[]{:S(2)}, u32[]{:S(2)}) collective-permute-start(f32[112,128]{1,0:T(8,128)S(1)} %get-tuple-element.92), channel_id=1, source_target_pairs={{0,8},{1,9},{2,10},{3,11},{4,12},{5,13},{6,14},{7,15},{8,0},{9,1},... | collective-permute-start | bytes 172040 | tf_op jit(solution)/shard_map/ppermute | solution.py:320
  69.9 1.6 %collective-permute-start.11 = (f32[448,128]{1,0:T(8,128)S(1)}, f32[448,128]{1,0:T(8,128)S(1)}, u32[]{:S(2)}, u32[]{:S(2)}) collective-permute-start(f32[448,128]{1,0:T(8,128)S(1)} %slice_select_fusion.1), channel_id=1, source_target_pairs={{0,2},{1,3},{2,0},{3,1},{4,6},{5,7},{6,4},{7,5},{8,10},{9,11},{10,... | collective-permute-start | bytes 688136 | tf_op jit(solution)/shard_map/ppermute | solution.py:291
  71.4 0.6 collective-permute-done.22
  72.1 2.0 %collective-permute-done.23 = f32[112,128]{1,0:T(8,128)S(1)} collective-permute-done((f32[112,128]{1,0:T(8,128)S(1)}, f32[112,128]{1,0:T(8,128)S(1)}, u32[]{:S(2)}, u32[]{:S(2)}) %collective-permute-start.23) | collective-permute-done | bytes 57376 | tf_op jit(solution)/shard_map/ppermute | solution.py:320
  74.0 0.5 collective-permute-done.24
  74.6 2.4 %collective-permute-done.11 = f32[448,128]{1,0:T(8,128)S(1)} collective-permute-done((f32[448,128]{1,0:T(8,128)S(1)}, f32[448,128]{1,0:T(8,128)S(1)}, u32[]{:S(2)}, u32[]{:S(2)}) %collective-permute-start.11) | collective-permute-done | bytes 229408 | tf_op jit(solution)/shard_map/ppermute | solution.py:291
  77.0 1.5 %collective-permute-start.25 = (f32[112,128]{1,0:T(8,128)S(1)}, f32[112,128]{1,0:T(8,128)S(1)}, u32[]{:S(2)}, u32[]{:S(2)}) collective-permute-start(f32[112,128]{1,0:T(8,128)S(1)} %add_add_fusion), channel_id=1, source_target_pairs={{0,12},{1,13},{2,14},{3,15},{4,0},{5,1},{6,2},{7,3},{8,4},{9,5},{1... | collective-permute-start | bytes 172040 | tf_op jit(solution)/shard_map/ppermute | solution.py:328
  78.6 1.7 %collective-permute-start.26 = (f32[112,128]{1,0:T(8,128)S(1)}, f32[112,128]{1,0:T(8,128)S(1)}, u32[]{:S(2)}, u32[]{:S(2)}) collective-permute-start(f32[112,128]{1,0:T(8,128)S(1)} %add_add_fusion), channel_id=1, source_target_pairs={{0,8},{1,9},{2,10},{3,11},{4,12},{5,13},{6,14},{7,15},{8,0},{9,1},... | collective-permute-start | bytes 172040 | tf_op jit(solution)/shard_map/ppermute | solution.py:328
  80.3 0.4 collective-permute-start.12
  80.7 1.4 %collective-permute-start.13 = (f32[112,128]{1,0:T(8,128)S(1)}, f32[112,128]{1,0:T(8,128)S(1)}, u32[]{:S(2)}, u32[]{:S(2)}) collective-permute-start(f32[112,128]{1,0:T(8,128)S(1)} %get-tuple-element.95), channel_id=1, source_target_pairs={{0,8},{1,9},{2,10},{3,11},{4,12},{5,13},{6,14},{7,15},{8,0},{9,1},... | collective-permute-start | bytes 172040 | tf_op jit(solution)/shard_map/ppermute | solution.py:320
  82.1 2.4 %collective-permute-start.14 = (f32[112,128]{1,0:T(8,128)S(1)}, f32[112,128]{1,0:T(8,128)S(1)}, u32[]{:S(2)}, u32[]{:S(2)}) collective-permute-start(f32[112,128]{1,0:T(8,128)S(1)} %get-tuple-element.94), channel_id=1, source_target_pairs={{0,12},{1,13},{2,14},{3,15},{4,0},{5,1},{6,2},{7,3},{8,4},{9,5},{1... | collective-permute-start | bytes 172040 | tf_op jit(solution)/shard_map/ppermute | solution.py:320
  84.5 2.0 %collective-permute-done.12 = f32[112,128]{1,0:T(8,128)S(1)} collective-permute-done((f32[112,128]{1,0:T(8,128)S(1)}, f32[112,128]{1,0:T(8,128)S(1)}, u32[]{:S(2)}, u32[]{:S(2)}) %collective-permute-start.12) | collective-permute-done | bytes 57376 | tf_op jit(solution)/shard_map/ppermute | solution.py:320
  86.5 0.3 collective-permute-start.27
  86.8 1.8 %collective-permute-done.13 = f32[112,128]{1,0:T(8,128)S(1)} collective-permute-done((f32[112,128]{1,0:T(8,128)S(1)}, f32[112,128]{1,0:T(8,128)S(1)}, u32[]{:S(2)}, u32[]{:S(2)}) %collective-permute-start.13) | collective-permute-done | bytes 57376 | tf_op jit(solution)/shard_map/ppermute | solution.py:320
  88.6 2.3 %collective-permute-start.15 = (f32[112,128]{1,0:T(8,128)S(1)}, f32[112,128]{1,0:T(8,128)S(1)}, u32[]{:S(2)}, u32[]{:S(2)}) collective-permute-start(f32[112,128]{1,0:T(8,128)S(1)} %get-tuple-element.81), channel_id=1, source_target_pairs={{0,12},{1,13},{2,14},{3,15},{4,0},{5,1},{6,2},{7,3},{8,4},{9,5},{1... | collective-permute-start | bytes 172040 | tf_op jit(solution)/shard_map/ppermute | solution.py:328
  91.0 0.4 collective-permute-start.16
  91.3 0.3 collective-permute-start.17
  91.6 0.9 collective-permute-done.27
  92.7 1.6 %collective-permute-start.28 = (f32[448,128]{1,0:T(8,128)S(1)}, f32[448,128]{1,0:T(8,128)S(1)}, u32[]{:S(2)}, u32[]{:S(2)}) collective-permute-start(f32[448,128]{1,0:T(8,128)S(1)} %constant_dynamic-slice_fusion), channel_id=1, source_target_pairs={{0,2},{1,3},{2,0},{3,1},{4,6},{5,7},{6,4},{7,5},{8,10},{9,11},{10,... | collective-permute-start | bytes 688136 | tf_op jit(solution)/shard_map/ppermute | solution.py:291
  94.3 1.8 %collective-permute-done.16 = f32[112,128]{1,0:T(8,128)S(1)} collective-permute-done((f32[112,128]{1,0:T(8,128)S(1)}, f32[112,128]{1,0:T(8,128)S(1)}, u32[]{:S(2)}, u32[]{:S(2)}) %collective-permute-start.16) | collective-permute-done | bytes 57376 | tf_op jit(solution)/shard_map/ppermute | solution.py:328
  96.0 1.3 %collective-permute-done.17 = f32[112,128]{1,0:T(8,128)S(1)} collective-permute-done((f32[112,128]{1,0:T(8,128)S(1)}, f32[112,128]{1,0:T(8,128)S(1)}, u32[]{:S(2)}, u32[]{:S(2)}) %collective-permute-start.17) | collective-permute-done | bytes 57376 | tf_op jit(solution)/shard_map/ppermute | solution.py:328
  97.4 1.6 %collective-permute-start.18 = (f32[448,128]{1,0:T(8,128)S(1)}, f32[448,128]{1,0:T(8,128)S(1)}, u32[]{:S(2)}, u32[]{:S(2)}) collective-permute-start(f32[448,128]{1,0:T(8,128)S(1)} %constant_dynamic-slice_fusion.4), channel_id=1, source_target_pairs={{0,2},{1,3},{2,0},{3,1},{4,6},{5,7},{6,4},{7,5},{8,10},{9,11},{10,... | collective-permute-start | bytes 688136 | tf_op jit(solution)/shard_map/ppermute | solution.py:291
  99.0 4.2 %inward.1 = f32[288,1024]{1,0:T(8,128)} custom-call(bf16[288,1152]{1,0:T(8,128)(2,1)} %get-tuple-element.66.refs_0_, f32[288,1024]{1,0:T(8,128)} %get-tuple-element.67.refs_1_, bf16[1152,1024]{1,0:T(8,128)(2,1)} %get-tuple-element.68.refs_2_), custom_call_target="tpu_custom_call" | custom-call | flops 3000000000 | bytes 9000000 | tf_op jit(solution)/shard_map/inward/pallas_call | solution.py:442
  103.7 0.3 collective-permute-start.19
  104.0 1.2 %collective-permute-done.29.refs_3_ = f32[896,128]{1,0:T(8,128)S(1)} collective-permute-done((f32[896,128]{1,0:T(8,128)S(1)}, f32[896,128]{1,0:T(8,128)S(1)}, u32[]{:S(2)}, u32[]{:S(2)}) %collective-permute-start.29) | collective-permute-done | bytes 458784 | tf_op jit(solution)/shard_map/ppermute | solution.py:291
  105.2 0.7 collective-permute-done.19.refs_1_
  105.8 1.9 %finish.1 = (f32[2,288,384]{2,1,0:T(8,128)}, f32[2,384]{1,0:T(2,128)}, f32[2,288,384]{2,1,0:T(8,128)}) custom-call(s32[2]{0:T(128)S(1)} %pad_add_fusion.refs_0_.odd, f32[896,128]{1,0:T(8,128)S(1)} %pad_maximum_fusion.refs_0_, f32[896,128]{1,0:T(8,128)S(1)} %collective-permute-done.19.refs_1_, f32[896,128]{1,0:T(8,128)S(1)} %pad_maximum_fusion.1.refs_2_, ...), custom_call_target="tpu_custom_call" | custom-call | flops 1000000000 | bytes 3000000 | tf_op jit(solution)/shard_map/finish/pallas_call | solution.py:456
  (64 shorter events, 1.5 us)
Async XLA Ops:
  0.6 9.4 %copy-start.4 = (f32[2,384]{1,0:T(2,128)S(1)}, f32[2,384]{1,0:T(2,128)}, u32[]{:S(2)}) copy-start(f32[2,384]{1,0:T(2,128)} %param.11) | copy-start | bytes 9220
  0.6 9.7 %copy-start.2 = (f32[2,384,288]{1,2,0:T(8,128)S(1)}, f32[2,384,288]{1,2,0:T(8,128)}, u32[]{:S(2)}) copy-start(f32[2,384,288]{1,2,0:T(8,128)} %param.12) | copy-start | bytes 2654212
  3.4 9.1 %collective-permute-start.1 = (f32[48,1024]{1,0:T(8,128)S(1)}, f32[48,1024]{1,0:T(8,128)S(1)}, u32[]{:S(2)}, u32[]{:S(2)}) collective-permute-start(f32[48,1024]{1,0:T(8,128)S(1)} %get-tuple-element.50), channel_id=1, source_target_pairs={{0,2},{1,3},{2,0},{3,1},{4,6},{5,7},{6,4},{7,5},{8,10},{9,11},{10,... | collective-permute-start | bytes 589832 | tf_op jit(solution)/shard_map/ppermute | solution.py:291
  6.4 21.0 %collective-permute-start = (f32[16,6144]{1,0:T(8,128)S(1)}, f32[16,6144]{1,0:T(8,128)S(1)}, u32[]{:S(2)}, u32[]{:S(2)}) collective-permute-start(f32[16,6144]{1,0:T(8,128)S(1)} %get-tuple-element.49), channel_id=1, source_target_pairs={{0,15},{1,0},{2,1},{3,2},{4,3},{5,4},{6,5},{7,6},{8,7},{9,8},{10,9... | collective-permute-start | bytes 1179656 | tf_op jit(solution)/shard_map/ppermute | solution.py:286
  9.1 12.1 %collective-permute-start.3 = (f32[48,1024]{1,0:T(8,128)S(1)}, f32[48,1024]{1,0:T(8,128)S(1)}, u32[]{:S(2)}, u32[]{:S(2)}) collective-permute-start(f32[48,1024]{1,0:T(8,128)S(1)} %get-tuple-element.51), channel_id=1, source_target_pairs={{0,12},{1,13},{2,14},{3,15},{4,0},{5,1},{6,2},{7,3},{8,4},{9,5},{1... | collective-permute-start | bytes 589832 | tf_op jit(solution)/shard_map/ppermute | solution.py:286
  10.0 17.4 %collective-permute-start.4 = (f32[48,1024]{1,0:T(8,128)S(1)}, f32[48,1024]{1,0:T(8,128)S(1)}, u32[]{:S(2)}, u32[]{:S(2)}) collective-permute-start(f32[48,1024]{1,0:T(8,128)S(1)} %get-tuple-element.52), channel_id=1, source_target_pairs={{0,8},{1,9},{2,10},{3,11},{4,12},{5,13},{6,14},{7,15},{8,0},{9,1},... | collective-permute-start | bytes 589832 | tf_op jit(solution)/shard_map/ppermute | solution.py:286
  10.3 2.8 %copy-start = (f32[288,1024]{1,0:T(8,128)S(1)}, f32[288,1024]{1,0:T(8,128)}, u32[]{:S(2)}) copy-start(f32[288,1024]{1,0:T(8,128)} %refs_1_.4) | copy-start | bytes 3538948
  10.3 2.8 %copy-start.1 = (f32[288,1024]{1,0:T(8,128)S(1)}, f32[288,1024]{1,0:T(8,128)}, u32[]{:S(2)}) copy-start(f32[288,1024]{1,0:T(8,128)} %refs_5_.1) | copy-start | bytes 3538948
  12.5 14.9 %collective-permute-start.2 = (f32[48,1024]{1,0:T(8,128)S(1)}, f32[48,1024]{1,0:T(8,128)S(1)}, u32[]{:S(2)}, u32[]{:S(2)}) collective-permute-start(f32[48,1024]{1,0:T(8,128)S(1)} %collective-permute-done.1.refs_11_), channel_id=1, source_target_pairs={{2,14},{3,15},{6,2},{7,3},{10,6},{11,7},{14,10},{15,11},{18,30},{1... | collective-permute-start | bytes 589832 | tf_op jit(solution)/shard_map/ppermute | solution.py:366
  35.1 8.7 %collective-permute-start.20 = (f32[896,128]{1,0:T(8,128)S(1)}, f32[896,128]{1,0:T(8,128)S(1)}, u32[]{:S(2)}, u32[]{:S(2)}) collective-permute-start(f32[896,128]{1,0:T(8,128)S(1)} %get-tuple-element.72), channel_id=1, source_target_pairs={{0,1},{1,0},{2,3},{3,2},{4,5},{5,4},{6,7},{7,6},{8,9},{9,8},{10,11... | collective-permute-start | bytes 1376264 | tf_op jit(solution)/shard_map/ppermute | solution.py:291
  35.1 7.9 %collective-permute-start.6 = (f32[48,1024]{1,0:T(8,128)S(1)}, f32[48,1024]{1,0:T(8,128)S(1)}, u32[]{:S(2)}, u32[]{:S(2)}) collective-permute-start(f32[48,1024]{1,0:T(8,128)S(1)} %get-tuple-element.59), channel_id=1, source_target_pairs={{0,2},{1,3},{2,0},{3,1},{4,6},{5,7},{6,4},{7,5},{8,10},{9,11},{10,... | collective-permute-start | bytes 589832 | tf_op jit(solution)/shard_map/ppermute | solution.py:291
  35.5 20.5 %collective-permute-start.5 = (f32[16,6144]{1,0:T(8,128)S(1)}, f32[16,6144]{1,0:T(8,128)S(1)}, u32[]{:S(2)}, u32[]{:S(2)}) collective-permute-start(f32[16,6144]{1,0:T(8,128)S(1)} %get-tuple-element.58), channel_id=1, source_target_pairs={{0,15},{1,0},{2,1},{3,2},{4,3},{5,4},{6,5},{7,6},{8,7},{9,8},{10,9... | collective-permute-start | bytes 1179656 | tf_op jit(solution)/shard_map/ppermute | solution.py:286
  40.1 10.5 %collective-permute-start.8 = (f32[48,1024]{1,0:T(8,128)S(1)}, f32[48,1024]{1,0:T(8,128)S(1)}, u32[]{:S(2)}, u32[]{:S(2)}) collective-permute-start(f32[48,1024]{1,0:T(8,128)S(1)} %get-tuple-element.60), channel_id=1, source_target_pairs={{0,12},{1,13},{2,14},{3,15},{4,0},{5,1},{6,2},{7,3},{8,4},{9,5},{1... | collective-permute-start | bytes 589832 | tf_op jit(solution)/shard_map/ppermute | solution.py:286
  40.1 15.9 %collective-permute-start.9 = (f32[48,1024]{1,0:T(8,128)S(1)}, f32[48,1024]{1,0:T(8,128)S(1)}, u32[]{:S(2)}, u32[]{:S(2)}) collective-permute-start(f32[48,1024]{1,0:T(8,128)S(1)} %get-tuple-element.61), channel_id=1, source_target_pairs={{0,8},{1,9},{2,10},{3,11},{4,12},{5,13},{6,14},{7,15},{8,0},{9,1},... | collective-permute-start | bytes 589832 | tf_op jit(solution)/shard_map/ppermute | solution.py:286
  43.1 12.9 %collective-permute-start.7 = (f32[48,1024]{1,0:T(8,128)S(1)}, f32[48,1024]{1,0:T(8,128)S(1)}, u32[]{:S(2)}, u32[]{:S(2)}) collective-permute-start(f32[48,1024]{1,0:T(8,128)S(1)} %collective-permute-done.6.refs_9_), channel_id=1, source_target_pairs={{2,14},{3,15},{6,2},{7,3},{10,6},{11,7},{14,10},{15,11},{18,30},{1... | collective-permute-start | bytes 589832 | tf_op jit(solution)/shard_map/ppermute | solution.py:366
  43.8 0.8 copy-start.3
  45.6 17.5 %collective-permute-start.21 = (f32[448,128]{1,0:T(8,128)S(1)}, f32[448,128]{1,0:T(8,128)S(1)}, u32[]{:S(2)}, u32[]{:S(2)}) collective-permute-start(f32[448,128]{1,0:T(8,128)S(1)} %slice_select_fusion), channel_id=1, source_target_pairs={{0,2},{1,3},{2,0},{3,1},{4,6},{5,7},{6,4},{7,5},{8,10},{9,11},{10,... | collective-permute-start | bytes 688136 | tf_op jit(solution)/shard_map/ppermute | solution.py:291
  63.0 1.9 %collective-permute-start.10 = (f32[896,128]{1,0:T(8,128)S(1)}, f32[896,128]{1,0:T(8,128)S(1)}, u32[]{:S(2)}, u32[]{:S(2)}) collective-permute-start(f32[896,128]{1,0:T(8,128)S(1)} %get-tuple-element.63), channel_id=1, source_target_pairs={{0,1},{1,0},{2,3},{3,2},{4,5},{5,4},{6,7},{7,6},{8,9},{9,8},{10,11... | collective-permute-start | bytes 1376264 | tf_op jit(solution)/shard_map/ppermute | solution.py:291
  65.0 7.1 %collective-permute-start.22 = (f32[112,128]{1,0:T(8,128)S(1)}, f32[112,128]{1,0:T(8,128)S(1)}, u32[]{:S(2)}, u32[]{:S(2)}) collective-permute-start(f32[112,128]{1,0:T(8,128)S(1)} %get-tuple-element.90), channel_id=1, source_target_pairs={{0,4},{1,5},{2,6},{3,7},{4,8},{5,9},{6,10},{7,11},{8,12},{9,13},{1... | collective-permute-start | bytes 172040 | tf_op jit(solution)/shard_map/ppermute | solution.py:320
  66.4 7.6 %collective-permute-start.23 = (f32[112,128]{1,0:T(8,128)S(1)}, f32[112,128]{1,0:T(8,128)S(1)}, u32[]{:S(2)}, u32[]{:S(2)}) collective-permute-start(f32[112,128]{1,0:T(8,128)S(1)} %get-tuple-element.92), channel_id=1, source_target_pairs={{0,8},{1,9},{2,10},{3,11},{4,12},{5,13},{6,14},{7,15},{8,0},{9,1},... | collective-permute-start | bytes 172040 | tf_op jit(solution)/shard_map/ppermute | solution.py:320
  69.8 4.7 %collective-permute-start.24 = (f32[112,128]{1,0:T(8,128)S(1)}, f32[112,128]{1,0:T(8,128)S(1)}, u32[]{:S(2)}, u32[]{:S(2)}) collective-permute-start(f32[112,128]{1,0:T(8,128)S(1)} %get-tuple-element.91), channel_id=1, source_target_pairs={{0,12},{1,13},{2,14},{3,15},{4,0},{5,1},{6,2},{7,3},{8,4},{9,5},{1... | collective-permute-start | bytes 172040 | tf_op jit(solution)/shard_map/ppermute | solution.py:320
  69.9 7.2 %collective-permute-start.11 = (f32[448,128]{1,0:T(8,128)S(1)}, f32[448,128]{1,0:T(8,128)S(1)}, u32[]{:S(2)}, u32[]{:S(2)}) collective-permute-start(f32[448,128]{1,0:T(8,128)S(1)} %slice_select_fusion.1), channel_id=1, source_target_pairs={{0,2},{1,3},{2,0},{3,1},{4,6},{5,7},{6,4},{7,5},{8,10},{9,11},{10,... | collective-permute-start | bytes 688136 | tf_op jit(solution)/shard_map/ppermute | solution.py:291
  77.0 14.3 %collective-permute-start.25 = (f32[112,128]{1,0:T(8,128)S(1)}, f32[112,128]{1,0:T(8,128)S(1)}, u32[]{:S(2)}, u32[]{:S(2)}) collective-permute-start(f32[112,128]{1,0:T(8,128)S(1)} %add_add_fusion), channel_id=1, source_target_pairs={{0,12},{1,13},{2,14},{3,15},{4,0},{5,1},{6,2},{7,3},{8,4},{9,5},{1... | collective-permute-start | bytes 172040 | tf_op jit(solution)/shard_map/ppermute | solution.py:328
  78.6 13.1 %collective-permute-start.26 = (f32[112,128]{1,0:T(8,128)S(1)}, f32[112,128]{1,0:T(8,128)S(1)}, u32[]{:S(2)}, u32[]{:S(2)}) collective-permute-start(f32[112,128]{1,0:T(8,128)S(1)} %add_add_fusion), channel_id=1, source_target_pairs={{0,8},{1,9},{2,10},{3,11},{4,12},{5,13},{6,14},{7,15},{8,0},{9,1},... | collective-permute-start | bytes 172040 | tf_op jit(solution)/shard_map/ppermute | solution.py:328
  80.3 6.1 %collective-permute-start.12 = (f32[112,128]{1,0:T(8,128)S(1)}, f32[112,128]{1,0:T(8,128)S(1)}, u32[]{:S(2)}, u32[]{:S(2)}) collective-permute-start(f32[112,128]{1,0:T(8,128)S(1)} %get-tuple-element.93), channel_id=1, source_target_pairs={{0,4},{1,5},{2,6},{3,7},{4,8},{5,9},{6,10},{7,11},{8,12},{9,13},{1... | collective-permute-start | bytes 172040 | tf_op jit(solution)/shard_map/ppermute | solution.py:320
  80.7 7.9 %collective-permute-start.13 = (f32[112,128]{1,0:T(8,128)S(1)}, f32[112,128]{1,0:T(8,128)S(1)}, u32[]{:S(2)}, u32[]{:S(2)}) collective-permute-start(f32[112,128]{1,0:T(8,128)S(1)} %get-tuple-element.95), channel_id=1, source_target_pairs={{0,8},{1,9},{2,10},{3,11},{4,12},{5,13},{6,14},{7,15},{8,0},{9,1},... | collective-permute-start | bytes 172040 | tf_op jit(solution)/shard_map/ppermute | solution.py:320
  82.1 6.5 %collective-permute-start.14 = (f32[112,128]{1,0:T(8,128)S(1)}, f32[112,128]{1,0:T(8,128)S(1)}, u32[]{:S(2)}, u32[]{:S(2)}) collective-permute-start(f32[112,128]{1,0:T(8,128)S(1)} %get-tuple-element.94), channel_id=1, source_target_pairs={{0,12},{1,13},{2,14},{3,15},{4,0},{5,1},{6,2},{7,3},{8,4},{9,5},{1... | collective-permute-start | bytes 172040 | tf_op jit(solution)/shard_map/ppermute | solution.py:320
  86.5 6.1 %collective-permute-start.27 = (f32[112,128]{1,0:T(8,128)S(1)}, f32[112,128]{1,0:T(8,128)S(1)}, u32[]{:S(2)}, u32[]{:S(2)}) collective-permute-start(f32[112,128]{1,0:T(8,128)S(1)} %add_add_fusion), channel_id=1, source_target_pairs={{0,4},{1,5},{2,6},{3,7},{4,8},{5,9},{6,10},{7,11},{8,12},{9,13},{1... | collective-permute-start | bytes 172040 | tf_op jit(solution)/shard_map/ppermute | solution.py:328
  88.6 5.6 %collective-permute-start.15 = (f32[112,128]{1,0:T(8,128)S(1)}, f32[112,128]{1,0:T(8,128)S(1)}, u32[]{:S(2)}, u32[]{:S(2)}) collective-permute-start(f32[112,128]{1,0:T(8,128)S(1)} %get-tuple-element.81), channel_id=1, source_target_pairs={{0,12},{1,13},{2,14},{3,15},{4,0},{5,1},{6,2},{7,3},{8,4},{9,5},{1... | collective-permute-start | bytes 172040 | tf_op jit(solution)/shard_map/ppermute | solution.py:328
  91.0 5.1 %collective-permute-start.16 = (f32[112,128]{1,0:T(8,128)S(1)}, f32[112,128]{1,0:T(8,128)S(1)}, u32[]{:S(2)}, u32[]{:S(2)}) collective-permute-start(f32[112,128]{1,0:T(8,128)S(1)} %get-tuple-element.81), channel_id=1, source_target_pairs={{0,8},{1,9},{2,10},{3,11},{4,12},{5,13},{6,14},{7,15},{8,0},{9,1},... | collective-permute-start | bytes 172040 | tf_op jit(solution)/shard_map/ppermute | solution.py:328
  91.3 6.0 %collective-permute-start.17 = (f32[112,128]{1,0:T(8,128)S(1)}, f32[112,128]{1,0:T(8,128)S(1)}, u32[]{:S(2)}, u32[]{:S(2)}) collective-permute-start(f32[112,128]{1,0:T(8,128)S(1)} %get-tuple-element.81), channel_id=1, source_target_pairs={{0,4},{1,5},{2,6},{3,7},{4,8},{5,9},{6,10},{7,11},{8,12},{9,13},{1... | collective-permute-start | bytes 172040 | tf_op jit(solution)/shard_map/ppermute | solution.py:328
  92.7 10.6 %collective-permute-start.28 = (f32[448,128]{1,0:T(8,128)S(1)}, f32[448,128]{1,0:T(8,128)S(1)}, u32[]{:S(2)}, u32[]{:S(2)}) collective-permute-start(f32[448,128]{1,0:T(8,128)S(1)} %constant_dynamic-slice_fusion), channel_id=1, source_target_pairs={{0,2},{1,3},{2,0},{3,1},{4,6},{5,7},{6,4},{7,5},{8,10},{9,11},{10,... | collective-permute-start | bytes 688136 | tf_op jit(solution)/shard_map/ppermute | solution.py:291
  97.4 6.3 %collective-permute-start.18 = (f32[448,128]{1,0:T(8,128)S(1)}, f32[448,128]{1,0:T(8,128)S(1)}, u32[]{:S(2)}, u32[]{:S(2)}) collective-permute-start(f32[448,128]{1,0:T(8,128)S(1)} %constant_dynamic-slice_fusion.4), channel_id=1, source_target_pairs={{0,2},{1,3},{2,0},{3,1},{4,6},{5,7},{6,4},{7,5},{8,10},{9,11},{10,... | collective-permute-start | bytes 688136 | tf_op jit(solution)/shard_map/ppermute | solution.py:291
  103.3 1.9 %collective-permute-start.29 = (f32[896,128]{1,0:T(8,128)S(1)}, f32[896,128]{1,0:T(8,128)S(1)}, u32[]{:S(2)}, u32[]{:S(2)}) collective-permute-start(f32[896,128]{1,0:T(8,128)S(1)} %pad_maximum_fusion.1.refs_2_), channel_id=1, source_target_pairs={{0,1},{1,0},{2,3},{3,2},{4,5},{5,4},{6,7},{7,6},{8,9},{9,8},{10,11... | collective-permute-start | bytes 1376264 | tf_op jit(solution)/shard_map/ppermute | solution.py:291
  103.7 2.1 %collective-permute-start.19 = (f32[896,128]{1,0:T(8,128)S(1)}, f32[896,128]{1,0:T(8,128)S(1)}, u32[]{:S(2)}, u32[]{:S(2)}) collective-permute-start(f32[896,128]{1,0:T(8,128)S(1)} %pad_maximum_fusion.refs_0_), channel_id=1, source_target_pairs={{0,1},{1,0},{2,3},{3,2},{4,5},{5,4},{6,7},{7,6},{8,9},{9,8},{10,11... | collective-permute-start | bytes 1376264 | tf_op jit(solution)/shard_map/ppermute | solution.py:291

commit v8 on v7

--- a/solution.py
+++ b/solution.py
@@ -69,6 +69,8 @@
         for t in range(TRACKS):
             first = first + (d[t] > (pos << k)).astype(i32)
         tab[TRACKS + k] = first
+    for t in range(TRACKS):
+        tab[32 + t] = d[t]
 
 
 def track_at(tab, k, slot):
@@ -90,11 +92,16 @@
         near[:, offset:offset + width] = src[rows_of(t), 0:width]
 
 
-def unpack_far(where, dist, tab, layer, far, out, hops, pos):
+def place_bits():
+    index = lax.axis_index("seq")
+    return index & 1, (index >> 1) & 1
+
+
+def unpack_far(where, tab, far, out, hops, pos):
     for k in range(1, hops):
         for slot in range(MOST):
             place, t = track_at(tab, k, slot)
-            mine = (place < TRACKS) & (dist[layer, t] == (pos << k))
+            mine = (place < TRACKS) & (tab[32 + t] == (pos << k))
             sources = [(far[0], where[1] == 0), (far[1], where[1] == 1)] if k == 1 else [(far[k], True)]
             for source, here in sources:
                 @pl.when(mine & here)
@@ -102,13 +109,13 @@
                     out[rows_of(t), :] = source[slot * TW:(slot + 1) * TW, :]
 
 
-def unpack_near(src, dist, tab, layer, near, out, join, pos):
+def unpack_near(src, tab, near, out, join, pos):
     for slot, (offset, width) in enumerate(near_slots(pos)[0]):
         place, t = track_at(tab, 0, slot)
 
         @pl.when(place < TRACKS)
         def _(slot=slot, t=t, offset=offset, width=width):
-            shift = dist[layer, t]
+            shift = tab[32 + t]
             join[slot % 4, :, :pos] = src[rows_of(t), :]
             join[slot % 4, :, pos:pos + width] = near[:, offset:offset + width]
             base = pl.multiple_of(shift // LANES * LANES, LANES)
@@ -202,22 +209,23 @@
         put(first, send)
 
 
-def start_loads(sems, sources, targets):
-    loads = [pltpu.make_async_copy(src, dst, sems.at[n]) for n, (src, dst) in enumerate(zip(sources, targets))]
-    for load in loads:
-        load.start()
-    return loads
-
-
-def upper_kernel(hops, pos, factor, where, dist, tab1, tab0, src_h, wo3_h, slope_h, wi3_h, x2_h, h2_h, near_in, *refs):
+def plan_loads(sems, sources, targets):
+    return [pltpu.make_async_copy(src, dst, sems.at[n]) for n, (src, dst) in enumerate(zip(sources, targets))]
+
+
+def upper_kernel(hops, pos, factor, tab1, tab0, src_h, wo3_h, slope_h, wi3_h, x2_h, h2_h, near_in, *refs):
     far_in, refs = refs[:hops], refs[hops:]
     near, refs = refs[0], refs[1:]
     far, refs = refs[:hops - 1], refs[hops - 1:]
     keep, send, grad_h, src, grad, wo3, slope, wi3, x2, h2, gm3, gh3, gm, join, sems = refs
-    first, *loads = start_loads(sems, (src_h, wo3_h, slope_h, wi3_h, x2_h, h2_h), (src, wo3, slope, wi3, x2, h2))
-    unpack_far(where, dist, tab1, 1, far_in, gm, hops, pos)
+    where = place_bits()
+    first, *loads = plan_loads(sems, (src_h, wo3_h, slope_h, wi3_h, x2_h, h2_h), (src, wo3, slope, wi3, x2, h2))
+    first.start()
+    unpack_far(where, tab1, far_in, gm, hops, pos)
     first.wait()
-    unpack_near(src, dist, tab1, 1, near_in, gm, join, pos)
+    for load in loads:
+        load.start()
+    unpack_near(src, tab1, near_in, gm, join, pos)
     loads[0].wait()
     loads[1].wait()
     hidden(pos, wo3, slope, gm, gm3, gh3)
@@ -232,13 +240,17 @@
     store.wait()
 
 
-def lower_kernel(hops, pos, factor, where, dist, tab0, src_h, wo3_h, slope_h, x2_h, h2_h, near_in, *refs):
+def lower_kernel(hops, pos, factor, tab0, src_h, wo3_h, slope_h, x2_h, h2_h, near_in, *refs):
     far_in, refs = refs[:hops], refs[hops:]
     keep, send, gm_h, gh_h, src, gm, gh3, wo3, slope, x2, h2, gm3, join, sems = refs
-    first, *loads = start_loads(sems, (src_h, wo3_h, slope_h, x2_h, h2_h), (src, wo3, slope, x2, h2))
-    unpack_far(where, dist, tab0, 0, far_in, gm, hops, pos)
+    where = place_bits()
+    first, *loads = plan_loads(sems, (src_h, wo3_h, slope_h, x2_h, h2_h), (src, wo3, slope, x2, h2))
+    first.start()
+    unpack_far(where, tab0, far_in, gm, hops, pos)
     first.wait()
-    unpack_near(src, dist, tab0, 0, near_in, gm, join, pos)
+    for load in loads:
+        load.start()
+    unpack_near(src, tab0, near_in, gm, join, pos)
     stores = [pltpu.make_async_copy(gm, gm_h, sems.at[5]), pltpu.make_async_copy(gh3, gh_h, sems.at[6])]
     stores[0].start()
     loads[0].wait()
@@ -253,14 +265,18 @@
 
 
 def input_kernel(pos, wi3_h, gm_h, gh_h, out, wi3, gm, gh3, sems):
-    for load in start_loads(sems, (wi3_h, gm_h, gh_h), (wi3, gm, gh3)):
+    loads = plan_loads(sems, (wi3_h, gm_h, gh_h), (wi3, gm, gh3))
+    for load in loads:
+        load.start()
+    for load in loads:
         load.wait()
     inward(pos, wi3, gm, gh3, out)
 
 
-def finish_kernel(odd, *refs):
+def finish_kernel(*refs):
     sums, (w_in_grad, bias_grad, w_out_t_grad) = refs[:4], refs[4:]
     rows = D + 8
+    odd, _ = place_bits()
 
     def put(layer, first, second):
         for j in range(HID // LANES):
@@ -272,11 +288,11 @@
     for layer in range(2):
         mine, other = sums[2 * layer], sums[2 * layer + 1]
 
-        @pl.when(odd[0] == 0)
+        @pl.when(odd == 0)
         def _(layer=layer, mine=mine, other=other):
             put(layer, mine, other)
 
-        @pl.when(odd[0] == 1)
+        @pl.when(odd == 1)
         def _(layer=layer, mine=mine, other=other):
             put(layer, other, mine)
 
@@ -356,8 +372,6 @@
     near_shape = shape(TW, near_width)
     half = -(-3 * (D + 8) // (8 * count)) * 8 * count
     far_hops = [1 << k for k in range(1, hops)]
-    index = lax.axis_index("seq")
-    where = jnp.stack([index & 1, (index >> 1) & 1]).astype(i32)
 
     def travel(near, far):
         paired = exchange(far[0], 2)
@@ -372,7 +386,7 @@
     distances, out_grad_h = [pltpu.with_memory_space_constraint(v, pltpu.HBM) for v in (distances, out_grad)]
     tab_1, near, *far = pl.pallas_call(
         lambda *refs: pack_kernel(hops, pos, *refs),
-        out_shape=[shape(32, dtype=i32), near_shape] + far_shapes,
+        out_shape=[shape(64, dtype=i32), near_shape] + far_shapes,
         in_specs=[SM, HB],
         out_specs=[SM] + [VM] * hops,
         scratch_shapes=[whole_s, pltpu.SemaphoreType.DMA],
@@ -394,7 +408,7 @@
     ]
     tab_0, *acts = pl.pallas_call(
         lambda *refs: act_kernel(hops, pos, *refs),
-        out_shape=[shape(32, dtype=i32)] + act_shapes * 2,
+        out_shape=[shape(64, dtype=i32)] + act_shapes * 2,
         in_specs=[SM] + [VM] * 8,
         out_specs=[SM] + [VM] * 10,
         scratch_shapes=[pltpu.VMEM((3 * D, 256), bf16)],
@@ -412,11 +426,11 @@
     near, *rest = pl.pallas_call(
         lambda *refs: upper_kernel(hops, pos, factor, *refs),
         out_shape=[near_shape] + far_shapes + [shape(half, LANES)] * 2 + [stored(D, pos)],
-        in_specs=[SM] * 4 + [HB] * 6 + [VM] * (hops + 1),
+        in_specs=[SM] * 2 + [HB] * 6 + [VM] * (hops + 1),
         out_specs=[VM] * (hops + 2) + [HB],
         scratch_shapes=[whole_s, whole_s, wo3_s, slope_s, wi3_s, x2_s, h2_s, gm3_s, gh3_s, whole_s, join_s, sems_s],
         **kernel_options("upper", 16, 6),
-    )(where, distances, tab_1, tab_0, *stay(out_grad, wo3_1, slope_1, wi3_1, x2_1, h2_1, where=pltpu.HBM), near, *far)
+    )(tab_1, tab_0, *stay(out_grad, wo3_1, slope_1, wi3_1, x2_1, h2_1, where=pltpu.HBM), near, *far)
     far, (keep_1, send_1, grad_1) = rest[:hops - 1], rest[hops - 1:]
     near, far = travel(near, far)
 
@@ -426,11 +440,11 @@
     keep, send, gm_0, gh3_0 = pl.pallas_call(
         lambda *refs: lower_kernel(hops, pos, factor, *refs),
         out_shape=[shape(half, LANES)] * 2 + [stored(D, pos), stored(3 * HID, pos, dtype=bf16)],
-        in_specs=[SM] * 3 + [HB] * 5 + [VM] * (hops + 1),
+        in_specs=[SM] + [HB] * 5 + [VM] * (hops + 1),
         out_specs=[VM] * 2 + [HB] * 2,
         scratch_shapes=[whole_s, whole_s, gh3_s, wo3_s, slope_s, x2_s, h2_s, gm3_s, join_s, sems_s],
         **kernel_options("lower", 16, 5),
-    )(where, distances, tab_0, *stay(grad_1, wo3_0, slope_0, x2_0, h2_0, where=pltpu.HBM), near, *far)
+    )(tab_0, *stay(grad_1, wo3_0, slope_0, x2_0, h2_0, where=pltpu.HBM), near, *far)
     sum_0 = keep + exchange(send, 1)
     steps = [lambda x: fold(x, 2), fold_far, spread_far, lambda x: spread(x, 2)]
     for step, ahead in zip(steps[:-1], steps[1:]):
@@ -456,10 +470,10 @@
     w_in_grad, bias_grad, w_out_t_grad = pl.pallas_call(
         finish_kernel,
         out_shape=[shape(2, D, HID), shape(2, HID), shape(2, D, HID)],
-        in_specs=[SM] + [VM] * 4,
+        in_specs=[VM] * 4,
         out_specs=[VM] * 3,
         **kernel_options("finish", 4, 1),
-    )(where, sum_0, other_0, sum_1, other_1)
+    )(sum_0, other_0, sum_1, other_1)
     return input_grad, w_in_grad, bias_grad, jnp.transpose(w_out_t_grad, (0, 2, 1))
 
 

time: 108 us -> 107 us (level)
  no operation moved by 1% of the time
where the time goes in v8:
time: 107 us
  starting transfers between devices  38.3 us (36%)
  waiting for transfers between devices  32.8 us (31%)
  Pallas kernels  30.5 us (29%)
  local copies, waits for them, and re-layouts  2.71 us (3%)
  other arithmetic  1.41 us (1%)
  between operations  1.08 us (1%)
    ppermute x10, starting transfers between devices, exchange(): return lax.ppermute(value, 'seq', [(s, s ^ mask) for s in range(count)])  13 us
    ppermute x6, waiting for transfers between devices, from_ahead(): lax.ppermute(value, 'seq', [(s, (s - steps) % count) for s in range(count)])  11.8 us
    ppermute x10, waiting for transfers between devices, exchange(): return lax.ppermute(value, 'seq', [(s, s ^ mask) for s in range(count)])  10.1 us
    ppermute x6, starting transfers between devices, fold_far(): lax.ppermute(part(mine + o), 'seq', groups_of_four(o))  9.02 us
    ppermute x6, starting transfers between devices, from_ahead(): lax.ppermute(value, 'seq', [(s, (s - steps) % count) for s in range(count)])  8.38 us
    pallas_call x1, Pallas kernels, body(): pl.pallas_call(lambda *refs: act_kernel(hops, pos, *refs), out_shape=[sha...  7.89 us
    pallas_call x1, Pallas kernels, body(): pl.pallas_call(lambda *refs: upper_kernel(hops, pos, factor, *refs), out_...  7.62 us
    ppermute x6, waiting for transfers between devices, fold_far(): lax.ppermute(part(mine + o), 'seq', groups_of_four(o))  6.89 us
  transfers between devices with their start and end apart: 30, of which 18 were waited for; matrix products, arithmetic and copies ran while one was open for 3% of the time, Pallas kernels for 18%

profile of v8, /device:TPU:0, one launch (start us, length us, event | category | flops | bytes accessed | tf_op | source)
XLA Modules:
  0.0 106.8 jit_solution(934805615401631877)
XLA Ops:
  0.7 2.7 %pack.1 = (s32[64]{0:T(128)S(1)}, f32[16,6144]{1,0:T(8,128)S(1)}, f32[48,1024]{1,0:T(8,128)S(1)}, f32[48,1024]{1,0:T(8,128)S(1)}, f32[48,1024]{1,0:T(8,128)S(1)}) custom-call(s32[2,18]{1,0:T(2,128)} %refs_0_.3, f32[288,1024]{1,0:T(8,128)} %refs_2_.1), custom_call_target="tpu_custom_call" | custom-call | flops 2000000000 | bytes 6000000 | tf_op jit(solution)/shard_map/pack/pallas_call | solution.py:387
  3.4 3.0 %collective-permute-start.1 = (f32[48,1024]{1,0:T(8,128)S(1)}, f32[48,1024]{1,0:T(8,128)S(1)}, u32[]{:S(2)}, u32[]{:S(2)}) collective-permute-start(f32[48,1024]{1,0:T(8,128)S(1)} %get-tuple-element.50), channel_id=1, source_target_pairs={{0,2},{1,3},{2,0},{3,1},{4,6},{5,7},{6,4},{7,5},{8,10},{9,11},{10,... | collective-permute-start | bytes 589832 | tf_op jit(solution)/shard_map/ppermute | solution.py:307
  6.4 2.7 %collective-permute-start = (f32[16,6144]{1,0:T(8,128)S(1)}, f32[16,6144]{1,0:T(8,128)S(1)}, u32[]{:S(2)}, u32[]{:S(2)}) collective-permute-start(f32[16,6144]{1,0:T(8,128)S(1)} %get-tuple-element.49), channel_id=1, source_target_pairs={{0,15},{1,0},{2,1},{3,2},{4,3},{5,4},{6,5},{7,6},{8,7},{9,8},{10,9... | collective-permute-start | bytes 1179656 | tf_op jit(solution)/shard_map/ppermute | solution.py:302
  9.1 0.9 collective-permute-start.3
  10.3 1.5 %slice_bitcast_fusion = (f32[288,384]{1,0:T(8,128)S(1)}, f32[288,384]{1,0:T(8,128)S(1)}, f32[288,384]{1,0:T(8,128)S(1)}, f32[288,384]{1,0:T(8,128)S(1)}) fusion(f32[2,288,384]{2,1,0:T(8,128)S(1)} %bitcast.14, f32[2,288,384]{2,1,0:T(8,128)} %param.10), kind=kLoop, calls=%fused_computation.2 | loop fusion | bytes 3538944 | tf_op jit(solution)/shard_map/squeeze | solution.py:401
  11.8 0.7 collective-permute-done.1.refs_9_
  12.5 0.7 collective-permute-start.2
  13.1 7.9 %act.1 = (s32[64]{0:T(128)S(1)}, bf16[608,1024]{1,0:T(8,128)(2,1)}, bf16[768,1024]{1,0:T(8,128)(2,1)}, f32[384,1024]{1,0:T(8,128)}, bf16[288,1152]{1,0:T(8,128)(...) custom-call(s32[2,18]{1,0:T(2,128)} %refs_0_.3, ...), custom_call_target="tpu_custom_call" | custom-call | flops 5000000000 | bytes 15000000 | tf_op jit(solution)/shard_map/act/pallas_call | solution.py:409
  21.1 6.3 %collective-permute-done.4.refs_12_ = f32[48,1024]{1,0:T(8,128)S(1)} collective-permute-done((f32[48,1024]{1,0:T(8,128)S(1)}, f32[48,1024]{1,0:T(8,128)S(1)}, u32[]{:S(2)}, u32[]{:S(2)}) %collective-permute-start.4) | collective-permute-done | bytes 196640 | tf_op jit(solution)/shard_map/ppermute | solution.py:302
  27.4 7.6 %upper.1 = (f32[16,6144]{1,0:T(8,128)S(1)}, f32[48,1024]{1,0:T(8,128)S(1)}, f32[48,1024]{1,0:T(8,128)S(1)}, f32[48,1024]{1,0:T(8,128)S(1)}, f32[896,128]{1,0:T(8...) custom-call(s32[64]{0:T(128)S(1)} %get-tuple-element.43.refs_0_, s32[64]{0:T(128)S(1)} %get-tuple-element.42.refs_1_.refs_0_, ...), custom_call_target="tpu_custom_call" | custom-call | flops 6000000000 | bytes 18000000 | tf_op jit(solution)/shard_map/upper/pallas_call | solution.py:426
  35.3 4.8 %collective-permute-start.5 = (f32[16,6144]{1,0:T(8,128)S(1)}, f32[16,6144]{1,0:T(8,128)S(1)}, u32[]{:S(2)}, u32[]{:S(2)}) collective-permute-start(f32[16,6144]{1,0:T(8,128)S(1)} %get-tuple-element.58), channel_id=1, source_target_pairs={{0,15},{1,0},{2,1},{3,2},{4,3},{5,4},{6,5},{7,6},{8,7},{9,8},{10,9... | collective-permute-start | bytes 1179656 | tf_op jit(solution)/shard_map/ppermute | solution.py:302
  40.0 3.3 %collective-permute-done.6.refs_7_ = f32[48,1024]{1,0:T(8,128)S(1)} collective-permute-done((f32[48,1024]{1,0:T(8,128)S(1)}, f32[48,1024]{1,0:T(8,128)S(1)}, u32[]{:S(2)}, u32[]{:S(2)}) %collective-permute-start.6) | collective-permute-done | bytes 196640 | tf_op jit(solution)/shard_map/ppermute | solution.py:307
  43.3 0.7 collective-permute-start.7
  44.0 0.8 copy-done.3
  44.8 1.1 add.101
  45.9 4.5 %collective-permute-start.21 = (f32[448,128]{1,0:T(8,128)S(1)}, f32[448,128]{1,0:T(8,128)S(1)}, u32[]{:S(2)}, u32[]{:S(2)}) collective-permute-start(f32[448,128]{1,0:T(8,128)S(1)} %slice_select_fusion), channel_id=1, source_target_pairs={{0,2},{1,3},{2,0},{3,1},{4,6},{5,7},{6,4},{7,5},{8,10},{9,11},{10,... | collective-permute-start | bytes 688136 | tf_op jit(solution)/shard_map/ppermute | solution.py:307
  50.5 5.4 %collective-permute-done.9.refs_10_ = f32[48,1024]{1,0:T(8,128)S(1)} collective-permute-done((f32[48,1024]{1,0:T(8,128)S(1)}, f32[48,1024]{1,0:T(8,128)S(1)}, u32[]{:S(2)}, u32[]{:S(2)}) %collective-permute-start.9) | collective-permute-done | bytes 196640 | tf_op jit(solution)/shard_map/ppermute | solution.py:302
  55.9 6.7 %lower.1 = (f32[896,128]{1,0:T(8,128)S(1)}, f32[896,128]{1,0:T(8,128)S(1)}, f32[288,1024]{1,0:T(8,128)}, bf16[1152,1024]{1,0:T(8,128)(2,1)}) custom-call(s32[64]{0:T(128)S(1)} %get-tuple-element.42.refs_1_.refs_0_, f32[288,1024]{1,0:T(8,128)} %get-tuple-element.53.refs_1_, bf16[384,864]{1,0:T(8,128)(2,1)} %get-tuple-element.54.refs_2_, ...), custom_call_target="tpu_custom_call" | custom-call | flops 5000000000 | bytes 15000000 | tf_op jit(solution)/shard_map/lower/pallas_call | solution.py:440
  62.8 1.7 %collective-permute-done.10 = f32[896,128]{1,0:T(8,128)S(1)} collective-permute-done((f32[896,128]{1,0:T(8,128)S(1)}, f32[896,128]{1,0:T(8,128)S(1)}, u32[]{:S(2)}, u32[]{:S(2)}) %collective-permute-start.10) | collective-permute-done | bytes 458784 | tf_op jit(solution)/shard_map/ppermute | solution.py:307
  64.6 1.5 %collective-permute-start.22 = (f32[112,128]{1,0:T(8,128)S(1)}, f32[112,128]{1,0:T(8,128)S(1)}, u32[]{:S(2)}, u32[]{:S(2)}) collective-permute-start(f32[112,128]{1,0:T(8,128)S(1)} %get-tuple-element.90), channel_id=1, source_target_pairs={{0,4},{1,5},{2,6},{3,7},{4,8},{5,9},{6,10},{7,11},{8,12},{9,13},{1... | collective-permute-start | bytes 172040 | tf_op jit(solution)/shard_map/ppermute | solution.py:336
  66.1 3.4 %collective-permute-start.23 = (f32[112,128]{1,0:T(8,128)S(1)}, f32[112,128]{1,0:T(8,128)S(1)}, u32[]{:S(2)}, u32[]{:S(2)}) collective-permute-start(f32[112,128]{1,0:T(8,128)S(1)} %get-tuple-element.92), channel_id=1, source_target_pairs={{0,8},{1,9},{2,10},{3,11},{4,12},{5,13},{6,14},{7,15},{8,0},{9,1},... | collective-permute-start | bytes 172040 | tf_op jit(solution)/shard_map/ppermute | solution.py:336
  69.5 1.6 %collective-permute-start.11 = (f32[448,128]{1,0:T(8,128)S(1)}, f32[448,128]{1,0:T(8,128)S(1)}, u32[]{:S(2)}, u32[]{:S(2)}) collective-permute-start(f32[448,128]{1,0:T(8,128)S(1)} %slice_select_fusion.1), channel_id=1, source_target_pairs={{0,2},{1,3},{2,0},{3,1},{4,6},{5,7},{6,4},{7,5},{8,10},{9,11},{10,... | collective-permute-start | bytes 688136 | tf_op jit(solution)/shard_map/ppermute | solution.py:307
  71.1 0.6 collective-permute-done.22
  71.7 2.0 %collective-permute-done.23 = f32[112,128]{1,0:T(8,128)S(1)} collective-permute-done((f32[112,128]{1,0:T(8,128)S(1)}, f32[112,128]{1,0:T(8,128)S(1)}, u32[]{:S(2)}, u32[]{:S(2)}) %collective-permute-start.23) | collective-permute-done | bytes 57376 | tf_op jit(solution)/shard_map/ppermute | solution.py:336
  73.6 0.5 collective-permute-done.24
  74.2 2.4 %collective-permute-done.11 = f32[448,128]{1,0:T(8,128)S(1)} collective-permute-done((f32[448,128]{1,0:T(8,128)S(1)}, f32[448,128]{1,0:T(8,128)S(1)}, u32[]{:S(2)}, u32[]{:S(2)}) %collective-permute-start.11) | collective-permute-done | bytes 229408 | tf_op jit(solution)/shard_map/ppermute | solution.py:307
  76.7 1.5 %collective-permute-start.25 = (f32[112,128]{1,0:T(8,128)S(1)}, f32[112,128]{1,0:T(8,128)S(1)}, u32[]{:S(2)}, u32[]{:S(2)}) collective-permute-start(f32[112,128]{1,0:T(8,128)S(1)} %add_add_fusion), channel_id=1, source_target_pairs={{0,12},{1,13},{2,14},{3,15},{4,0},{5,1},{6,2},{7,3},{8,4},{9,5},{1... | collective-permute-start | bytes 172040 | tf_op jit(solution)/shard_map/ppermute | solution.py:344
  78.2 1.7 %collective-permute-start.26 = (f32[112,128]{1,0:T(8,128)S(1)}, f32[112,128]{1,0:T(8,128)S(1)}, u32[]{:S(2)}, u32[]{:S(2)}) collective-permute-start(f32[112,128]{1,0:T(8,128)S(1)} %add_add_fusion), channel_id=1, source_target_pairs={{0,8},{1,9},{2,10},{3,11},{4,12},{5,13},{6,14},{7,15},{8,0},{9,1},... | collective-permute-start | bytes 172040 | tf_op jit(solution)/shard_map/ppermute | solution.py:344
  79.9 0.4 collective-permute-start.12
  80.3 1.4 %collective-permute-start.13 = (f32[112,128]{1,0:T(8,128)S(1)}, f32[112,128]{1,0:T(8,128)S(1)}, u32[]{:S(2)}, u32[]{:S(2)}) collective-permute-start(f32[112,128]{1,0:T(8,128)S(1)} %get-tuple-element.95), channel_id=1, source_target_pairs={{0,8},{1,9},{2,10},{3,11},{4,12},{5,13},{6,14},{7,15},{8,0},{9,1},... | collective-permute-start | bytes 172040 | tf_op jit(solution)/shard_map/ppermute | solution.py:336
  81.7 2.4 %collective-permute-start.14 = (f32[112,128]{1,0:T(8,128)S(1)}, f32[112,128]{1,0:T(8,128)S(1)}, u32[]{:S(2)}, u32[]{:S(2)}) collective-permute-start(f32[112,128]{1,0:T(8,128)S(1)} %get-tuple-element.94), channel_id=1, source_target_pairs={{0,12},{1,13},{2,14},{3,15},{4,0},{5,1},{6,2},{7,3},{8,4},{9,5},{1... | collective-permute-start | bytes 172040 | tf_op jit(solution)/shard_map/ppermute | solution.py:336
  84.1 2.0 %collective-permute-done.12 = f32[112,128]{1,0:T(8,128)S(1)} collective-permute-done((f32[112,128]{1,0:T(8,128)S(1)}, f32[112,128]{1,0:T(8,128)S(1)}, u32[]{:S(2)}, u32[]{:S(2)}) %collective-permute-start.12) | collective-permute-done | bytes 57376 | tf_op jit(solution)/shard_map/ppermute | solution.py:336
  86.1 0.3 collective-permute-start.27
  86.4 1.8 %collective-permute-done.13 = f32[112,128]{1,0:T(8,128)S(1)} collective-permute-done((f32[112,128]{1,0:T(8,128)S(1)}, f32[112,128]{1,0:T(8,128)S(1)}, u32[]{:S(2)}, u32[]{:S(2)}) %collective-permute-start.13) | collective-permute-done | bytes 57376 | tf_op jit(solution)/shard_map/ppermute | solution.py:336
  88.2 2.3 %collective-permute-start.15 = (f32[112,128]{1,0:T(8,128)S(1)}, f32[112,128]{1,0:T(8,128)S(1)}, u32[]{:S(2)}, u32[]{:S(2)}) collective-permute-start(f32[112,128]{1,0:T(8,128)S(1)} %get-tuple-element.81), channel_id=1, source_target_pairs={{0,12},{1,13},{2,14},{3,15},{4,0},{5,1},{6,2},{7,3},{8,4},{9,5},{1... | collective-permute-start | bytes 172040 | tf_op jit(solution)/shard_map/ppermute | solution.py:344
  90.6 0.4 collective-permute-start.16
  90.9 0.3 collective-permute-start.17
  91.2 0.9 collective-permute-done.27
  92.3 1.6 %collective-permute-start.28 = (f32[448,128]{1,0:T(8,128)S(1)}, f32[448,128]{1,0:T(8,128)S(1)}, u32[]{:S(2)}, u32[]{:S(2)}) collective-permute-start(f32[448,128]{1,0:T(8,128)S(1)} %constant_dynamic-slice_fusion), channel_id=1, source_target_pairs={{0,2},{1,3},{2,0},{3,1},{4,6},{5,7},{6,4},{7,5},{8,10},{9,11},{10,... | collective-permute-start | bytes 688136 | tf_op jit(solution)/shard_map/ppermute | solution.py:307
  93.9 1.8 %collective-permute-done.16 = f32[112,128]{1,0:T(8,128)S(1)} collective-permute-done((f32[112,128]{1,0:T(8,128)S(1)}, f32[112,128]{1,0:T(8,128)S(1)}, u32[]{:S(2)}, u32[]{:S(2)}) %collective-permute-start.16) | collective-permute-done | bytes 57376 | tf_op jit(solution)/shard_map/ppermute | solution.py:344
  95.7 1.3 %collective-permute-done.17 = f32[112,128]{1,0:T(8,128)S(1)} collective-permute-done((f32[112,128]{1,0:T(8,128)S(1)}, f32[112,128]{1,0:T(8,128)S(1)}, u32[]{:S(2)}, u32[]{:S(2)}) %collective-permute-start.17) | collective-permute-done | bytes 57376 | tf_op jit(solution)/shard_map/ppermute | solution.py:344
  97.0 1.6 %collective-permute-start.18 = (f32[448,128]{1,0:T(8,128)S(1)}, f32[448,128]{1,0:T(8,128)S(1)}, u32[]{:S(2)}, u32[]{:S(2)}) collective-permute-start(f32[448,128]{1,0:T(8,128)S(1)} %constant_dynamic-slice_fusion.4), channel_id=1, source_target_pairs={{0,2},{1,3},{2,0},{3,1},{4,6},{5,7},{6,4},{7,5},{8,10},{9,11},{10,... | collective-permute-start | bytes 688136 | tf_op jit(solution)/shard_map/ppermute | solution.py:307
  98.6 4.2 %inward.1 = f32[288,1024]{1,0:T(8,128)} custom-call(bf16[288,1152]{1,0:T(8,128)(2,1)} %get-tuple-element.66.refs_0_, f32[288,1024]{1,0:T(8,128)} %get-tuple-element.67.refs_1_, bf16[1152,1024]{1,0:T(8,128)(2,1)} %get-tuple-element.68.refs_2_), custom_call_target="tpu_custom_call" | custom-call | flops 3000000000 | bytes 9000000 | tf_op jit(solution)/shard_map/inward/pallas_call | solution.py:456
  103.0 0.3 collective-permute-done.18
  103.4 0.3 collective-permute-start.19
  103.7 1.2 %collective-permute-done.29.refs_3_ = f32[896,128]{1,0:T(8,128)S(1)} collective-permute-done((f32[896,128]{1,0:T(8,128)S(1)}, f32[896,128]{1,0:T(8,128)S(1)}, u32[]{:S(2)}, u32[]{:S(2)}) %collective-permute-start.29) | collective-permute-done | bytes 458784 | tf_op jit(solution)/shard_map/ppermute | solution.py:307
  104.8 0.7 collective-permute-done.19.refs_1_
  105.5 1.3 %finish.1 = (f32[2,288,384]{2,1,0:T(8,128)}, f32[2,384]{1,0:T(2,128)}, f32[2,288,384]{2,1,0:T(8,128)}) custom-call(f32[896,128]{1,0:T(8,128)S(1)} %pad_maximum_fusion.refs_0_, f32[896,128]{1,0:T(8,128)S(1)} %collective-permute-done.19.refs_1_, f32[896,128]{1,0:T(8,128)S(1)} %pad_maximum_fusion.1.refs_2_, f32[896,128]{1,0:T(8,128)S(1)} %collective-permute-done.29.refs_3_), custom_call_target="tpu_custom_call" | custom-call | flops 1000000000 | bytes 3000000 | tf_op jit(solution)/shard_map/finish/pallas_call | solution.py:470
  (63 shorter events, 1.4 us)
Async XLA Ops:
  0.6 9.4 %copy-start.4 = (f32[2,384]{1,0:T(2,128)S(1)}, f32[2,384]{1,0:T(2,128)}, u32[]{:S(2)}) copy-start(f32[2,384]{1,0:T(2,128)} %param.11) | copy-start | bytes 9220
  0.6 9.7 %copy-start.2 = (f32[2,384,288]{1,2,0:T(8,128)S(1)}, f32[2,384,288]{1,2,0:T(8,128)}, u32[]{:S(2)}) copy-start(f32[2,384,288]{1,2,0:T(8,128)} %param.12) | copy-start | bytes 2654212
  3.4 9.1 %collective-permute-start.1 = (f32[48,1024]{1,0:T(8,128)S(1)}, f32[48,1024]{1,0:T(8,128)S(1)}, u32[]{:S(2)}, u32[]{:S(2)}) collective-permute-start(f32[48,1024]{1,0:T(8,128)S(1)} %get-tuple-element.50), channel_id=1, source_target_pairs={{0,2},{1,3},{2,0},{3,1},{4,6},{5,7},{6,4},{7,5},{8,10},{9,11},{10,... | collective-permute-start | bytes 589832 | tf_op jit(solution)/shard_map/ppermute | solution.py:307
  6.4 21.0 %collective-permute-start = (f32[16,6144]{1,0:T(8,128)S(1)}, f32[16,6144]{1,0:T(8,128)S(1)}, u32[]{:S(2)}, u32[]{:S(2)}) collective-permute-start(f32[16,6144]{1,0:T(8,128)S(1)} %get-tuple-element.49), channel_id=1, source_target_pairs={{0,15},{1,0},{2,1},{3,2},{4,3},{5,4},{6,5},{7,6},{8,7},{9,8},{10,9... | collective-permute-start | bytes 1179656 | tf_op jit(solution)/shard_map/ppermute | solution.py:302
  9.1 12.0 %collective-permute-start.3 = (f32[48,1024]{1,0:T(8,128)S(1)}, f32[48,1024]{1,0:T(8,128)S(1)}, u32[]{:S(2)}, u32[]{:S(2)}) collective-permute-start(f32[48,1024]{1,0:T(8,128)S(1)} %get-tuple-element.51), channel_id=1, source_target_pairs={{0,12},{1,13},{2,14},{3,15},{4,0},{5,1},{6,2},{7,3},{8,4},{9,5},{1... | collective-permute-start | bytes 589832 | tf_op jit(solution)/shard_map/ppermute | solution.py:302
  10.0 17.4 %collective-permute-start.4 = (f32[48,1024]{1,0:T(8,128)S(1)}, f32[48,1024]{1,0:T(8,128)S(1)}, u32[]{:S(2)}, u32[]{:S(2)}) collective-permute-start(f32[48,1024]{1,0:T(8,128)S(1)} %get-tuple-element.52), channel_id=1, source_target_pairs={{0,8},{1,9},{2,10},{3,11},{4,12},{5,13},{6,14},{7,15},{8,0},{9,1},... | collective-permute-start | bytes 589832 | tf_op jit(solution)/shard_map/ppermute | solution.py:302
  10.3 2.8 %copy-start = (f32[288,1024]{1,0:T(8,128)S(1)}, f32[288,1024]{1,0:T(8,128)}, u32[]{:S(2)}) copy-start(f32[288,1024]{1,0:T(8,128)} %refs_1_.2) | copy-start | bytes 3538948
  10.3 2.8 %copy-start.1 = (f32[288,1024]{1,0:T(8,128)S(1)}, f32[288,1024]{1,0:T(8,128)}, u32[]{:S(2)}) copy-start(f32[288,1024]{1,0:T(8,128)} %refs_5_.1) | copy-start | bytes 3538948
  12.5 14.9 %collective-permute-start.2 = (f32[48,1024]{1,0:T(8,128)S(1)}, f32[48,1024]{1,0:T(8,128)S(1)}, u32[]{:S(2)}, u32[]{:S(2)}) collective-permute-start(f32[48,1024]{1,0:T(8,128)S(1)} %collective-permute-done.1.refs_9_), channel_id=1, source_target_pairs={{2,14},{3,15},{6,2},{7,3},{10,6},{11,7},{14,10},{15,11},{18,30},{1... | collective-permute-start | bytes 589832 | tf_op jit(solution)/shard_map/ppermute | solution.py:380
  35.0 9.0 %collective-permute-start.20 = (f32[896,128]{1,0:T(8,128)S(1)}, f32[896,128]{1,0:T(8,128)S(1)}, u32[]{:S(2)}, u32[]{:S(2)}) collective-permute-start(f32[896,128]{1,0:T(8,128)S(1)} %get-tuple-element.72), channel_id=1, source_target_pairs={{0,1},{1,0},{2,3},{3,2},{4,5},{5,4},{6,7},{7,6},{8,9},{9,8},{10,11... | collective-permute-start | bytes 1376264 | tf_op jit(solution)/shard_map/ppermute | solution.py:307
  35.1 8.2 %collective-permute-start.6 = (f32[48,1024]{1,0:T(8,128)S(1)}, f32[48,1024]{1,0:T(8,128)S(1)}, u32[]{:S(2)}, u32[]{:S(2)}) collective-permute-start(f32[48,1024]{1,0:T(8,128)S(1)} %get-tuple-element.59), channel_id=1, source_target_pairs={{0,2},{1,3},{2,0},{3,1},{4,6},{5,7},{6,4},{7,5},{8,10},{9,11},{10,... | collective-permute-start | bytes 589832 | tf_op jit(solution)/shard_map/ppermute | solution.py:307
  35.3 20.7 %collective-permute-start.5 = (f32[16,6144]{1,0:T(8,128)S(1)}, f32[16,6144]{1,0:T(8,128)S(1)}, u32[]{:S(2)}, u32[]{:S(2)}) collective-permute-start(f32[16,6144]{1,0:T(8,128)S(1)} %get-tuple-element.58), channel_id=1, source_target_pairs={{0,15},{1,0},{2,1},{3,2},{4,3},{5,4},{6,5},{7,6},{8,7},{9,8},{10,9... | collective-permute-start | bytes 1179656 | tf_op jit(solution)/shard_map/ppermute | solution.py:302
  40.0 10.5 %collective-permute-start.8 = (f32[48,1024]{1,0:T(8,128)S(1)}, f32[48,1024]{1,0:T(8,128)S(1)}, u32[]{:S(2)}, u32[]{:S(2)}) collective-permute-start(f32[48,1024]{1,0:T(8,128)S(1)} %get-tuple-element.60), channel_id=1, source_target_pairs={{0,12},{1,13},{2,14},{3,15},{4,0},{5,1},{6,2},{7,3},{8,4},{9,5},{1... | collective-permute-start | bytes 589832 | tf_op jit(solution)/shard_map/ppermute | solution.py:302
  40.0 15.9 %collective-permute-start.9 = (f32[48,1024]{1,0:T(8,128)S(1)}, f32[48,1024]{1,0:T(8,128)S(1)}, u32[]{:S(2)}, u32[]{:S(2)}) collective-permute-start(f32[48,1024]{1,0:T(8,128)S(1)} %get-tuple-element.61), channel_id=1, source_target_pairs={{0,8},{1,9},{2,10},{3,11},{4,12},{5,13},{6,14},{7,15},{8,0},{9,1},... | collective-permute-start | bytes 589832 | tf_op jit(solution)/shard_map/ppermute | solution.py:302
  43.3 12.6 %collective-permute-start.7 = (f32[48,1024]{1,0:T(8,128)S(1)}, f32[48,1024]{1,0:T(8,128)S(1)}, u32[]{:S(2)}, u32[]{:S(2)}) collective-permute-start(f32[48,1024]{1,0:T(8,128)S(1)} %collective-permute-done.6.refs_7_), channel_id=1, source_target_pairs={{2,14},{3,15},{6,2},{7,3},{10,6},{11,7},{14,10},{15,11},{18,30},{1... | collective-permute-start | bytes 589832 | tf_op jit(solution)/shard_map/ppermute | solution.py:380
  44.0 0.8 copy-start.3
  45.9 16.9 %collective-permute-start.21 = (f32[448,128]{1,0:T(8,128)S(1)}, f32[448,128]{1,0:T(8,128)S(1)}, u32[]{:S(2)}, u32[]{:S(2)}) collective-permute-start(f32[448,128]{1,0:T(8,128)S(1)} %slice_select_fusion), channel_id=1, source_target_pairs={{0,2},{1,3},{2,0},{3,1},{4,6},{5,7},{6,4},{7,5},{8,10},{9,11},{10,... | collective-permute-start | bytes 688136 | tf_op jit(solution)/shard_map/ppermute | solution.py:307
  62.6 1.9 %collective-permute-start.10 = (f32[896,128]{1,0:T(8,128)S(1)}, f32[896,128]{1,0:T(8,128)S(1)}, u32[]{:S(2)}, u32[]{:S(2)}) collective-permute-start(f32[896,128]{1,0:T(8,128)S(1)} %get-tuple-element.63), channel_id=1, source_target_pairs={{0,1},{1,0},{2,3},{3,2},{4,5},{5,4},{6,7},{7,6},{8,9},{9,8},{10,11... | collective-permute-start | bytes 1376264 | tf_op jit(solution)/shard_map/ppermute | solution.py:307
  64.6 7.1 %collective-permute-start.22 = (f32[112,128]{1,0:T(8,128)S(1)}, f32[112,128]{1,0:T(8,128)S(1)}, u32[]{:S(2)}, u32[]{:S(2)}) collective-permute-start(f32[112,128]{1,0:T(8,128)S(1)} %get-tuple-element.90), channel_id=1, source_target_pairs={{0,4},{1,5},{2,6},{3,7},{4,8},{5,9},{6,10},{7,11},{8,12},{9,13},{1... | collective-permute-start | bytes 172040 | tf_op jit(solution)/shard_map/ppermute | solution.py:336
  66.1 7.6 %collective-permute-start.23 = (f32[112,128]{1,0:T(8,128)S(1)}, f32[112,128]{1,0:T(8,128)S(1)}, u32[]{:S(2)}, u32[]{:S(2)}) collective-permute-start(f32[112,128]{1,0:T(8,128)S(1)} %get-tuple-element.92), channel_id=1, source_target_pairs={{0,8},{1,9},{2,10},{3,11},{4,12},{5,13},{6,14},{7,15},{8,0},{9,1},... | collective-permute-start | bytes 172040 | tf_op jit(solution)/shard_map/ppermute | solution.py:336
  69.4 4.7 %collective-permute-start.24 = (f32[112,128]{1,0:T(8,128)S(1)}, f32[112,128]{1,0:T(8,128)S(1)}, u32[]{:S(2)}, u32[]{:S(2)}) collective-permute-start(f32[112,128]{1,0:T(8,128)S(1)} %get-tuple-element.91), channel_id=1, source_target_pairs={{0,12},{1,13},{2,14},{3,15},{4,0},{5,1},{6,2},{7,3},{8,4},{9,5},{1... | collective-permute-start | bytes 172040 | tf_op jit(solution)/shard_map/ppermute | solution.py:336
  69.5 7.2 %collective-permute-start.11 = (f32[448,128]{1,0:T(8,128)S(1)}, f32[448,128]{1,0:T(8,128)S(1)}, u32[]{:S(2)}, u32[]{:S(2)}) collective-permute-start(f32[448,128]{1,0:T(8,128)S(1)} %slice_select_fusion.1), channel_id=1, source_target_pairs={{0,2},{1,3},{2,0},{3,1},{4,6},{5,7},{6,4},{7,5},{8,10},{9,11},{10,... | collective-permute-start | bytes 688136 | tf_op jit(solution)/shard_map/ppermute | solution.py:307
  76.7 14.3 %collective-permute-start.25 = (f32[112,128]{1,0:T(8,128)S(1)}, f32[112,128]{1,0:T(8,128)S(1)}, u32[]{:S(2)}, u32[]{:S(2)}) collective-permute-start(f32[112,128]{1,0:T(8,128)S(1)} %add_add_fusion), channel_id=1, source_target_pairs={{0,12},{1,13},{2,14},{3,15},{4,0},{5,1},{6,2},{7,3},{8,4},{9,5},{1... | collective-permute-start | bytes 172040 | tf_op jit(solution)/shard_map/ppermute | solution.py:344
  78.2 13.1 %collective-permute-start.26 = (f32[112,128]{1,0:T(8,128)S(1)}, f32[112,128]{1,0:T(8,128)S(1)}, u32[]{:S(2)}, u32[]{:S(2)}) collective-permute-start(f32[112,128]{1,0:T(8,128)S(1)} %add_add_fusion), channel_id=1, source_target_pairs={{0,8},{1,9},{2,10},{3,11},{4,12},{5,13},{6,14},{7,15},{8,0},{9,1},... | collective-permute-start | bytes 172040 | tf_op jit(solution)/shard_map/ppermute | solution.py:344
  79.9 6.1 %collective-permute-start.12 = (f32[112,128]{1,0:T(8,128)S(1)}, f32[112,128]{1,0:T(8,128)S(1)}, u32[]{:S(2)}, u32[]{:S(2)}) collective-permute-start(f32[112,128]{1,0:T(8,128)S(1)} %get-tuple-element.93), channel_id=1, source_target_pairs={{0,4},{1,5},{2,6},{3,7},{4,8},{5,9},{6,10},{7,11},{8,12},{9,13},{1... | collective-permute-start | bytes 172040 | tf_op jit(solution)/shard_map/ppermute | solution.py:336
  80.3 7.9 %collective-permute-start.13 = (f32[112,128]{1,0:T(8,128)S(1)}, f32[112,128]{1,0:T(8,128)S(1)}, u32[]{:S(2)}, u32[]{:S(2)}) collective-permute-start(f32[112,128]{1,0:T(8,128)S(1)} %get-tuple-element.95), channel_id=1, source_target_pairs={{0,8},{1,9},{2,10},{3,11},{4,12},{5,13},{6,14},{7,15},{8,0},{9,1},... | collective-permute-start | bytes 172040 | tf_op jit(solution)/shard_map/ppermute | solution.py:336
  81.7 6.5 %collective-permute-start.14 = (f32[112,128]{1,0:T(8,128)S(1)}, f32[112,128]{1,0:T(8,128)S(1)}, u32[]{:S(2)}, u32[]{:S(2)}) collective-permute-start(f32[112,128]{1,0:T(8,128)S(1)} %get-tuple-element.94), channel_id=1, source_target_pairs={{0,12},{1,13},{2,14},{3,15},{4,0},{5,1},{6,2},{7,3},{8,4},{9,5},{1... | collective-permute-start | bytes 172040 | tf_op jit(solution)/shard_map/ppermute | solution.py:336
  86.1 6.1 %collective-permute-start.27 = (f32[112,128]{1,0:T(8,128)S(1)}, f32[112,128]{1,0:T(8,128)S(1)}, u32[]{:S(2)}, u32[]{:S(2)}) collective-permute-start(f32[112,128]{1,0:T(8,128)S(1)} %add_add_fusion), channel_id=1, source_target_pairs={{0,4},{1,5},{2,6},{3,7},{4,8},{5,9},{6,10},{7,11},{8,12},{9,13},{1... | collective-permute-start | bytes 172040 | tf_op jit(solution)/shard_map/ppermute | solution.py:344
  88.2 5.6 %collective-permute-start.15 = (f32[112,128]{1,0:T(8,128)S(1)}, f32[112,128]{1,0:T(8,128)S(1)}, u32[]{:S(2)}, u32[]{:S(2)}) collective-permute-start(f32[112,128]{1,0:T(8,128)S(1)} %get-tuple-element.81), channel_id=1, source_target_pairs={{0,12},{1,13},{2,14},{3,15},{4,0},{5,1},{6,2},{7,3},{8,4},{9,5},{1... | collective-permute-start | bytes 172040 | tf_op jit(solution)/shard_map/ppermute | solution.py:344
  90.6 5.1 %collective-permute-start.16 = (f32[112,128]{1,0:T(8,128)S(1)}, f32[112,128]{1,0:T(8,128)S(1)}, u32[]{:S(2)}, u32[]{:S(2)}) collective-permute-start(f32[112,128]{1,0:T(8,128)S(1)} %get-tuple-element.81), channel_id=1, source_target_pairs={{0,8},{1,9},{2,10},{3,11},{4,12},{5,13},{6,14},{7,15},{8,0},{9,1},... | collective-permute-start | bytes 172040 | tf_op jit(solution)/shard_map/ppermute | solution.py:344
  90.9 6.0 %collective-permute-start.17 = (f32[112,128]{1,0:T(8,128)S(1)}, f32[112,128]{1,0:T(8,128)S(1)}, u32[]{:S(2)}, u32[]{:S(2)}) collective-permute-start(f32[112,128]{1,0:T(8,128)S(1)} %get-tuple-element.81), channel_id=1, source_target_pairs={{0,4},{1,5},{2,6},{3,7},{4,8},{5,9},{6,10},{7,11},{8,12},{9,13},{1... | collective-permute-start | bytes 172040 | tf_op jit(solution)/shard_map/ppermute | solution.py:344
  92.3 10.6 %collective-permute-start.28 = (f32[448,128]{1,0:T(8,128)S(1)}, f32[448,128]{1,0:T(8,128)S(1)}, u32[]{:S(2)}, u32[]{:S(2)}) collective-permute-start(f32[448,128]{1,0:T(8,128)S(1)} %constant_dynamic-slice_fusion), channel_id=1, source_target_pairs={{0,2},{1,3},{2,0},{3,1},{4,6},{5,7},{6,4},{7,5},{8,10},{9,11},{10,... | collective-permute-start | bytes 688136 | tf_op jit(solution)/shard_map/ppermute | solution.py:307
  97.0 6.3 %collective-permute-start.18 = (f32[448,128]{1,0:T(8,128)S(1)}, f32[448,128]{1,0:T(8,128)S(1)}, u32[]{:S(2)}, u32[]{:S(2)}) collective-permute-start(f32[448,128]{1,0:T(8,128)S(1)} %constant_dynamic-slice_fusion.4), channel_id=1, source_target_pairs={{0,2},{1,3},{2,0},{3,1},{4,6},{5,7},{6,4},{7,5},{8,10},{9,11},{10,... | collective-permute-start | bytes 688136 | tf_op jit(solution)/shard_map/ppermute | solution.py:307
  102.9 1.9 %collective-permute-start.29 = (f32[896,128]{1,0:T(8,128)S(1)}, f32[896,128]{1,0:T(8,128)S(1)}, u32[]{:S(2)}, u32[]{:S(2)}) collective-permute-start(f32[896,128]{1,0:T(8,128)S(1)} %pad_maximum_fusion.1.refs_2_), channel_id=1, source_target_pairs={{0,1},{1,0},{2,3},{3,2},{4,5},{5,4},{6,7},{7,6},{8,9},{9,8},{10,11... | collective-permute-start | bytes 1376264 | tf_op jit(solution)/shard_map/ppermute | solution.py:307
  103.4 2.1 %collective-permute-start.19 = (f32[896,128]{1,0:T(8,128)S(1)}, f32[896,128]{1,0:T(8,128)S(1)}, u32[]{:S(2)}, u32[]{:S(2)}) collective-permute-start(f32[896,128]{1,0:T(8,128)S(1)} %pad_maximum_fusion.refs_0_), channel_id=1, source_target_pairs={{0,1},{1,0},{2,3},{3,2},{4,5},{5,4},{6,7},{7,6},{8,9},{9,8},{10,11... | collective-permute-start | bytes 1376264 | tf_op jit(solution)/shard_map/ppermute | solution.py:307

commit v9 on v8

--- a/solution.py
+++ b/solution.py
@@ -447,8 +447,9 @@
     )(tab_0, *stay(grad_1, wo3_0, slope_0, x2_0, h2_0, where=pltpu.HBM), near, *far)
     sum_0 = keep + exchange(send, 1)
     steps = [lambda x: fold(x, 2), fold_far, spread_far, lambda x: spread(x, 2)]
-    for step, ahead in zip(steps[:-1], steps[1:]):
-        sum_1, _ = lax.optimization_barrier((sum_1, sum_0))
+    for number, (step, ahead) in enumerate(zip(steps[:-1], steps[1:])):
+        if number > 0:
+            sum_1, _ = lax.optimization_barrier((sum_1, sum_0))
         sum_1 = ahead(sum_1)
         sum_0 = step(sum_0)
     sum_0, gm_0 = lax.optimization_barrier((sum_0, gm_0))

time: 107 us -> 106 us (level)
  waiting for transfers between devices: 32.8 us -> 30.8 us
    ppermute x10, waiting for transfers between devices: 10.1 us -> 8.43 us  [exchange(): return lax.ppermute(value, 'seq', [(s, s ^ mask) for s in range(count)])]
  transfers between devices with their start and end apart: 30 -> 30, of which waited for: 18 -> 17; matrix products, arithmetic and copies ran while one was open for 3% -> 3% of each run, Pallas kernels for 18% -> 18%
where the time goes in v9:
time: 106 us
  starting transfers between devices  39.2 us (37%)
  waiting for transfers between devices  30.8 us (29%)
  Pallas kernels  30.6 us (29%)
  local copies, waits for them, and re-layouts  2.71 us (3%)
  other arithmetic  1.41 us (1%)
  between operations  1.09 us (1%)
    ppermute x10, starting transfers between devices, exchange(): return lax.ppermute(value, 'seq', [(s, s ^ mask) for s in range(count)])  13.2 us
    ppermute x6, waiting for transfers between devices, from_ahead(): lax.ppermute(value, 'seq', [(s, (s - steps) % count) for s in range(count)])  11.8 us
    ppermute x6, starting transfers between devices, fold_far(): lax.ppermute(part(mine + o), 'seq', groups_of_four(o))  9.01 us
    ppermute x10, waiting for transfers between devices, exchange(): return lax.ppermute(value, 'seq', [(s, s ^ mask) for s in range(count)])  8.43 us
    ppermute x6, starting transfers between devices, from_ahead(): lax.ppermute(value, 'seq', [(s, (s - steps) % count) for s in range(count)])  8.38 us
    pallas_call x1, Pallas kernels, body(): pl.pallas_call(lambda *refs: act_kernel(hops, pos, *refs), out_shape=[sha...  7.89 us
    pallas_call x1, Pallas kernels, body(): pl.pallas_call(lambda *refs: upper_kernel(hops, pos, factor, *refs), out_...  7.62 us
    ppermute x6, starting transfers between devices, spread_far(): lax.ppermute(x, 'seq', groups_of_four(o))  7.29 us
  transfers between devices with their start and end apart: 30, of which 17 were waited for; matrix products, arithmetic and copies ran while one was open for 3% of the time, Pallas kernels for 18%

profile of v9, /device:TPU:0, one launch (start us, length us, event | category | flops | bytes accessed | tf_op | source)
XLA Modules:
  0.0 105.8 jit_solution(2524330037963534672)
XLA Ops:
  0.7 2.7 %pack.1 = (s32[64]{0:T(128)S(1)}, f32[16,6144]{1,0:T(8,128)S(1)}, f32[48,1024]{1,0:T(8,128)S(1)}, f32[48,1024]{1,0:T(8,128)S(1)}, f32[48,1024]{1,0:T(8,128)S(1)}) custom-call(s32[2,18]{1,0:T(2,128)} %refs_0_.3, f32[288,1024]{1,0:T(8,128)} %refs_2_.1), custom_call_target="tpu_custom_call" | custom-call | flops 2000000000 | bytes 6000000 | tf_op jit(solution)/shard_map/pack/pallas_call | solution.py:387
  3.4 3.0 %collective-permute-start.1 = (f32[48,1024]{1,0:T(8,128)S(1)}, f32[48,1024]{1,0:T(8,128)S(1)}, u32[]{:S(2)}, u32[]{:S(2)}) collective-permute-start(f32[48,1024]{1,0:T(8,128)S(1)} %get-tuple-element.49), channel_id=1, source_target_pairs={{0,2},{1,3},{2,0},{3,1},{4,6},{5,7},{6,4},{7,5},{8,10},{9,11},{10,... | collective-permute-start | bytes 589832 | tf_op jit(solution)/shard_map/ppermute | solution.py:307
  6.4 2.7 %collective-permute-start = (f32[16,6144]{1,0:T(8,128)S(1)}, f32[16,6144]{1,0:T(8,128)S(1)}, u32[]{:S(2)}, u32[]{:S(2)}) collective-permute-start(f32[16,6144]{1,0:T(8,128)S(1)} %get-tuple-element.48), channel_id=1, source_target_pairs={{0,15},{1,0},{2,1},{3,2},{4,3},{5,4},{6,5},{7,6},{8,7},{9,8},{10,9... | collective-permute-start | bytes 1179656 | tf_op jit(solution)/shard_map/ppermute | solution.py:302
  9.1 0.9 collective-permute-start.3
  10.3 1.5 %slice_bitcast_fusion = (f32[288,384]{1,0:T(8,128)S(1)}, f32[288,384]{1,0:T(8,128)S(1)}, f32[288,384]{1,0:T(8,128)S(1)}, f32[288,384]{1,0:T(8,128)S(1)}) fusion(f32[2,288,384]{2,1,0:T(8,128)S(1)} %bitcast.14, f32[2,288,384]{2,1,0:T(8,128)} %param.10), kind=kLoop, calls=%fused_computation.2 | loop fusion | bytes 3538944 | tf_op jit(solution)/shard_map/squeeze | solution.py:401
  11.8 0.7 collective-permute-done.1.refs_9_
  12.5 0.7 collective-permute-start.2
  13.1 7.9 %act.1 = (s32[64]{0:T(128)S(1)}, bf16[608,1024]{1,0:T(8,128)(2,1)}, bf16[768,1024]{1,0:T(8,128)(2,1)}, f32[384,1024]{1,0:T(8,128)}, bf16[288,1152]{1,0:T(8,128)(...) custom-call(s32[2,18]{1,0:T(2,128)} %refs_0_.3, ...), custom_call_target="tpu_custom_call" | custom-call | flops 5000000000 | bytes 15000000 | tf_op jit(solution)/shard_map/act/pallas_call | solution.py:409
  21.1 6.3 %collective-permute-done.4.refs_12_ = f32[48,1024]{1,0:T(8,128)S(1)} collective-permute-done((f32[48,1024]{1,0:T(8,128)S(1)}, f32[48,1024]{1,0:T(8,128)S(1)}, u32[]{:S(2)}, u32[]{:S(2)}) %collective-permute-start.4) | collective-permute-done | bytes 196640 | tf_op jit(solution)/shard_map/ppermute | solution.py:302
  27.4 7.6 %upper.1 = (f32[16,6144]{1,0:T(8,128)S(1)}, f32[48,1024]{1,0:T(8,128)S(1)}, f32[48,1024]{1,0:T(8,128)S(1)}, f32[48,1024]{1,0:T(8,128)S(1)}, f32[896,128]{1,0:T(8...) custom-call(s32[64]{0:T(128)S(1)} %get-tuple-element.42.refs_0_, s32[64]{0:T(128)S(1)} %get-tuple-element.41.refs_1_.refs_0_, ...), custom_call_target="tpu_custom_call" | custom-call | flops 6000000000 | bytes 18000000 | tf_op jit(solution)/shard_map/upper/pallas_call | solution.py:426
  35.1 0.2 collective-permute-start.6
  35.3 4.8 %collective-permute-start.5 = (f32[16,6144]{1,0:T(8,128)S(1)}, f32[16,6144]{1,0:T(8,128)S(1)}, u32[]{:S(2)}, u32[]{:S(2)}) collective-permute-start(f32[16,6144]{1,0:T(8,128)S(1)} %get-tuple-element.57), channel_id=1, source_target_pairs={{0,15},{1,0},{2,1},{3,2},{4,3},{5,4},{6,5},{7,6},{8,7},{9,8},{10,9... | collective-permute-start | bytes 1179656 | tf_op jit(solution)/shard_map/ppermute | solution.py:302
  40.0 3.3 %collective-permute-done.6.refs_7_ = f32[48,1024]{1,0:T(8,128)S(1)} collective-permute-done((f32[48,1024]{1,0:T(8,128)S(1)}, f32[48,1024]{1,0:T(8,128)S(1)}, u32[]{:S(2)}, u32[]{:S(2)}) %collective-permute-start.6) | collective-permute-done | bytes 196640 | tf_op jit(solution)/shard_map/ppermute | solution.py:307
  43.3 0.7 collective-permute-start.7
  44.0 0.8 copy-done.3
  44.8 1.1 %add.101 = f32[896,128]{1,0:T(8,128)S(1)} add(f32[896,128]{1,0:T(8,128)S(1)} %get-tuple-element.70, f32[896,128]{1,0:T(8,128)} %copy-done.3) | non-fusion elementwise | flops 114688 | bytes 1376256 | tf_op jit(solution)/shard_map/add | solution.py:437
  45.9 4.5 %collective-permute-start.21 = (f32[448,128]{1,0:T(8,128)S(1)}, f32[448,128]{1,0:T(8,128)S(1)}, u32[]{:S(2)}, u32[]{:S(2)}) collective-permute-start(f32[448,128]{1,0:T(8,128)S(1)} %slice_select_fusion), channel_id=1, source_target_pairs={{0,2},{1,3},{2,0},{3,1},{4,6},{5,7},{6,4},{7,5},{8,10},{9,11},{10,... | collective-permute-start | bytes 688136 | tf_op jit(solution)/shard_map/ppermute | solution.py:307
  50.5 5.4 %collective-permute-done.9.refs_10_ = f32[48,1024]{1,0:T(8,128)S(1)} collective-permute-done((f32[48,1024]{1,0:T(8,128)S(1)}, f32[48,1024]{1,0:T(8,128)S(1)}, u32[]{:S(2)}, u32[]{:S(2)}) %collective-permute-start.9) | collective-permute-done | bytes 196640 | tf_op jit(solution)/shard_map/ppermute | solution.py:302
  55.9 6.8 %lower.1 = (f32[896,128]{1,0:T(8,128)S(1)}, f32[896,128]{1,0:T(8,128)S(1)}, f32[288,1024]{1,0:T(8,128)}, bf16[1152,1024]{1,0:T(8,128)(2,1)}) custom-call(s32[64]{0:T(128)S(1)} %get-tuple-element.41.refs_1_.refs_0_, f32[288,1024]{1,0:T(8,128)} %get-tuple-element.52.refs_1_, bf16[384,864]{1,0:T(8,128)(2,1)} %get-tuple-element.53.refs_2_, ...), custom_call_target="tpu_custom_call" | custom-call | flops 5000000000 | bytes 15000000 | tf_op jit(solution)/shard_map/lower/pallas_call | solution.py:440
  63.0 1.5 %collective-permute-start.22 = (f32[112,128]{1,0:T(8,128)S(1)}, f32[112,128]{1,0:T(8,128)S(1)}, u32[]{:S(2)}, u32[]{:S(2)}) collective-permute-start(f32[112,128]{1,0:T(8,128)S(1)} %get-tuple-element.88), channel_id=1, source_target_pairs={{0,4},{1,5},{2,6},{3,7},{4,8},{5,9},{6,10},{7,11},{8,12},{9,13},{1... | collective-permute-start | bytes 172040 | tf_op jit(solution)/shard_map/ppermute | solution.py:336
  64.5 3.4 %collective-permute-start.23 = (f32[112,128]{1,0:T(8,128)S(1)}, f32[112,128]{1,0:T(8,128)S(1)}, u32[]{:S(2)}, u32[]{:S(2)}) collective-permute-start(f32[112,128]{1,0:T(8,128)S(1)} %get-tuple-element.90), channel_id=1, source_target_pairs={{0,8},{1,9},{2,10},{3,11},{4,12},{5,13},{6,14},{7,15},{8,0},{9,1},... | collective-permute-start | bytes 172040 | tf_op jit(solution)/shard_map/ppermute | solution.py:336
  68.0 1.6 %collective-permute-start.11 = (f32[448,128]{1,0:T(8,128)S(1)}, f32[448,128]{1,0:T(8,128)S(1)}, u32[]{:S(2)}, u32[]{:S(2)}) collective-permute-start(f32[448,128]{1,0:T(8,128)S(1)} %slice_select_fusion.1), channel_id=1, source_target_pairs={{0,2},{1,3},{2,0},{3,1},{4,6},{5,7},{6,4},{7,5},{8,10},{9,11},{10,... | collective-permute-start | bytes 688136 | tf_op jit(solution)/shard_map/ppermute | solution.py:307
  69.6 0.6 collective-permute-done.22
  70.2 2.2 %collective-permute-done.23 = f32[112,128]{1,0:T(8,128)S(1)} collective-permute-done((f32[112,128]{1,0:T(8,128)S(1)}, f32[112,128]{1,0:T(8,128)S(1)}, u32[]{:S(2)}, u32[]{:S(2)}) %collective-permute-start.23) | collective-permute-done | bytes 57376 | tf_op jit(solution)/shard_map/ppermute | solution.py:336
  72.4 0.5 collective-permute-done.24
  72.9 2.5 %collective-permute-done.11 = f32[448,128]{1,0:T(8,128)S(1)} collective-permute-done((f32[448,128]{1,0:T(8,128)S(1)}, f32[448,128]{1,0:T(8,128)S(1)}, u32[]{:S(2)}, u32[]{:S(2)}) %collective-permute-start.11) | collective-permute-done | bytes 229408 | tf_op jit(solution)/shard_map/ppermute | solution.py:307
  75.5 1.5 %collective-permute-start.25 = (f32[112,128]{1,0:T(8,128)S(1)}, f32[112,128]{1,0:T(8,128)S(1)}, u32[]{:S(2)}, u32[]{:S(2)}) collective-permute-start(f32[112,128]{1,0:T(8,128)S(1)} %add_add_fusion), channel_id=1, source_target_pairs={{0,12},{1,13},{2,14},{3,15},{4,0},{5,1},{6,2},{7,3},{8,4},{9,5},{1... | collective-permute-start | bytes 172040 | tf_op jit(solution)/shard_map/ppermute | solution.py:344
  77.0 1.7 %collective-permute-start.26 = (f32[112,128]{1,0:T(8,128)S(1)}, f32[112,128]{1,0:T(8,128)S(1)}, u32[]{:S(2)}, u32[]{:S(2)}) collective-permute-start(f32[112,128]{1,0:T(8,128)S(1)} %add_add_fusion), channel_id=1, source_target_pairs={{0,8},{1,9},{2,10},{3,11},{4,12},{5,13},{6,14},{7,15},{8,0},{9,1},... | collective-permute-start | bytes 172040 | tf_op jit(solution)/shard_map/ppermute | solution.py:344
  78.7 0.4 collective-permute-start.12
  79.1 1.4 %collective-permute-start.13 = (f32[112,128]{1,0:T(8,128)S(1)}, f32[112,128]{1,0:T(8,128)S(1)}, u32[]{:S(2)}, u32[]{:S(2)}) collective-permute-start(f32[112,128]{1,0:T(8,128)S(1)} %get-tuple-element.93), channel_id=1, source_target_pairs={{0,8},{1,9},{2,10},{3,11},{4,12},{5,13},{6,14},{7,15},{8,0},{9,1},... | collective-permute-start | bytes 172040 | tf_op jit(solution)/shard_map/ppermute | solution.py:336
  80.5 2.4 %collective-permute-start.14 = (f32[112,128]{1,0:T(8,128)S(1)}, f32[112,128]{1,0:T(8,128)S(1)}, u32[]{:S(2)}, u32[]{:S(2)}) collective-permute-start(f32[112,128]{1,0:T(8,128)S(1)} %get-tuple-element.92), channel_id=1, source_target_pairs={{0,12},{1,13},{2,14},{3,15},{4,0},{5,1},{6,2},{7,3},{8,4},{9,5},{1... | collective-permute-start | bytes 172040 | tf_op jit(solution)/shard_map/ppermute | solution.py:336
  82.9 2.0 %collective-permute-done.12 = f32[112,128]{1,0:T(8,128)S(1)} collective-permute-done((f32[112,128]{1,0:T(8,128)S(1)}, f32[112,128]{1,0:T(8,128)S(1)}, u32[]{:S(2)}, u32[]{:S(2)}) %collective-permute-start.12) | collective-permute-done | bytes 57376 | tf_op jit(solution)/shard_map/ppermute | solution.py:336
  84.9 0.3 collective-permute-start.27
  85.2 1.4 %collective-permute-done.13 = f32[112,128]{1,0:T(8,128)S(1)} collective-permute-done((f32[112,128]{1,0:T(8,128)S(1)}, f32[112,128]{1,0:T(8,128)S(1)}, u32[]{:S(2)}, u32[]{:S(2)}) %collective-permute-start.13) | collective-permute-done | bytes 57376 | tf_op jit(solution)/shard_map/ppermute | solution.py:336
  86.6 3.1 %collective-permute-start.15 = (f32[112,128]{1,0:T(8,128)S(1)}, f32[112,128]{1,0:T(8,128)S(1)}, u32[]{:S(2)}, u32[]{:S(2)}) collective-permute-start(f32[112,128]{1,0:T(8,128)S(1)} %get-tuple-element.79), channel_id=1, source_target_pairs={{0,12},{1,13},{2,14},{3,15},{4,0},{5,1},{6,2},{7,3},{8,4},{9,5},{1... | collective-permute-start | bytes 172040 | tf_op jit(solution)/shard_map/ppermute | solution.py:344
  89.7 0.2 collective-permute-start.16
  89.9 0.4 collective-permute-start.17
  90.3 0.7 collective-permute-done.27
  91.1 1.6 %collective-permute-start.28 = (f32[448,128]{1,0:T(8,128)S(1)}, f32[448,128]{1,0:T(8,128)S(1)}, u32[]{:S(2)}, u32[]{:S(2)}) collective-permute-start(f32[448,128]{1,0:T(8,128)S(1)} %constant_dynamic-slice_fusion), channel_id=1, source_target_pairs={{0,2},{1,3},{2,0},{3,1},{4,6},{5,7},{6,4},{7,5},{8,10},{9,11},{10,... | collective-permute-start | bytes 688136 | tf_op jit(solution)/shard_map/ppermute | solution.py:307
  92.7 2.0 %collective-permute-done.16 = f32[112,128]{1,0:T(8,128)S(1)} collective-permute-done((f32[112,128]{1,0:T(8,128)S(1)}, f32[112,128]{1,0:T(8,128)S(1)}, u32[]{:S(2)}, u32[]{:S(2)}) %collective-permute-start.16) | collective-permute-done | bytes 57376 | tf_op jit(solution)/shard_map/ppermute | solution.py:344
  94.7 1.1 %collective-permute-done.17 = f32[112,128]{1,0:T(8,128)S(1)} collective-permute-done((f32[112,128]{1,0:T(8,128)S(1)}, f32[112,128]{1,0:T(8,128)S(1)}, u32[]{:S(2)}, u32[]{:S(2)}) %collective-permute-start.17) | collective-permute-done | bytes 57376 | tf_op jit(solution)/shard_map/ppermute | solution.py:344
  96.0 1.6 %collective-permute-start.18 = (f32[448,128]{1,0:T(8,128)S(1)}, f32[448,128]{1,0:T(8,128)S(1)}, u32[]{:S(2)}, u32[]{:S(2)}) collective-permute-start(f32[448,128]{1,0:T(8,128)S(1)} %constant_dynamic-slice_fusion.4), channel_id=1, source_target_pairs={{0,2},{1,3},{2,0},{3,1},{4,6},{5,7},{6,4},{7,5},{8,10},{9,11},{10,... | collective-permute-start | bytes 688136 | tf_op jit(solution)/shard_map/ppermute | solution.py:307
  97.5 4.2 %inward.1 = f32[288,1024]{1,0:T(8,128)} custom-call(bf16[288,1152]{1,0:T(8,128)(2,1)} %get-tuple-element.65.refs_0_, f32[288,1024]{1,0:T(8,128)} %get-tuple-element.66.refs_1_, bf16[1152,1024]{1,0:T(8,128)(2,1)} %get-tuple-element.67.refs_2_), custom_call_target="tpu_custom_call" | custom-call | flops 3000000000 | bytes 9000000 | tf_op jit(solution)/shard_map/inward/pallas_call | solution.py:457
  102.0 0.2 collective-permute-done.18
  102.2 0.4 collective-permute-start.19
  102.6 1.2 %collective-permute-done.29.refs_3_ = f32[896,128]{1,0:T(8,128)S(1)} collective-permute-done((f32[896,128]{1,0:T(8,128)S(1)}, f32[896,128]{1,0:T(8,128)S(1)}, u32[]{:S(2)}, u32[]{:S(2)}) %collective-permute-start.29) | collective-permute-done | bytes 458784 | tf_op jit(solution)/shard_map/ppermute | solution.py:307
  103.8 0.7 collective-permute-done.19.refs_1_
  104.4 1.3 %finish.1 = (f32[2,288,384]{2,1,0:T(8,128)}, f32[2,384]{1,0:T(2,128)}, f32[2,288,384]{2,1,0:T(8,128)}) custom-call(f32[896,128]{1,0:T(8,128)S(1)} %pad_maximum_fusion.refs_0_, f32[896,128]{1,0:T(8,128)S(1)} %collective-permute-done.19.refs_1_, f32[896,128]{1,0:T(8,128)S(1)} %pad_maximum_fusion.1.refs_2_, f32[896,128]{1,0:T(8,128)S(1)} %collective-permute-done.29.refs_3_), custom_call_target="tpu_custom_call" | custom-call | flops 1000000000 | bytes 3000000 | tf_op jit(solution)/shard_map/finish/pallas_call | solution.py:471
  (63 shorter events, 1.2 us)
Async XLA Ops:
  0.6 9.4 %copy-start.4 = (f32[2,384]{1,0:T(2,128)S(1)}, f32[2,384]{1,0:T(2,128)}, u32[]{:S(2)}) copy-start(f32[2,384]{1,0:T(2,128)} %param.11) | copy-start | bytes 9220
  0.6 9.7 %copy-start.2 = (f32[2,384,288]{1,2,0:T(8,128)S(1)}, f32[2,384,288]{1,2,0:T(8,128)}, u32[]{:S(2)}) copy-start(f32[2,384,288]{1,2,0:T(8,128)} %param.12) | copy-start | bytes 2654212
  3.4 9.1 %collective-permute-start.1 = (f32[48,1024]{1,0:T(8,128)S(1)}, f32[48,1024]{1,0:T(8,128)S(1)}, u32[]{:S(2)}, u32[]{:S(2)}) collective-permute-start(f32[48,1024]{1,0:T(8,128)S(1)} %get-tuple-element.49), channel_id=1, source_target_pairs={{0,2},{1,3},{2,0},{3,1},{4,6},{5,7},{6,4},{7,5},{8,10},{9,11},{10,... | collective-permute-start | bytes 589832 | tf_op jit(solution)/shard_map/ppermute | solution.py:307
  6.4 21.0 %collective-permute-start = (f32[16,6144]{1,0:T(8,128)S(1)}, f32[16,6144]{1,0:T(8,128)S(1)}, u32[]{:S(2)}, u32[]{:S(2)}) collective-permute-start(f32[16,6144]{1,0:T(8,128)S(1)} %get-tuple-element.48), channel_id=1, source_target_pairs={{0,15},{1,0},{2,1},{3,2},{4,3},{5,4},{6,5},{7,6},{8,7},{9,8},{10,9... | collective-permute-start | bytes 1179656 | tf_op jit(solution)/shard_map/ppermute | solution.py:302
  9.1 12.0 %collective-permute-start.3 = (f32[48,1024]{1,0:T(8,128)S(1)}, f32[48,1024]{1,0:T(8,128)S(1)}, u32[]{:S(2)}, u32[]{:S(2)}) collective-permute-start(f32[48,1024]{1,0:T(8,128)S(1)} %get-tuple-element.50), channel_id=1, source_target_pairs={{0,12},{1,13},{2,14},{3,15},{4,0},{5,1},{6,2},{7,3},{8,4},{9,5},{1... | collective-permute-start | bytes 589832 | tf_op jit(solution)/shard_map/ppermute | solution.py:302
  10.0 17.4 %collective-permute-start.4 = (f32[48,1024]{1,0:T(8,128)S(1)}, f32[48,1024]{1,0:T(8,128)S(1)}, u32[]{:S(2)}, u32[]{:S(2)}) collective-permute-start(f32[48,1024]{1,0:T(8,128)S(1)} %get-tuple-element.51), channel_id=1, source_target_pairs={{0,8},{1,9},{2,10},{3,11},{4,12},{5,13},{6,14},{7,15},{8,0},{9,1},... | collective-permute-start | bytes 589832 | tf_op jit(solution)/shard_map/ppermute | solution.py:302
  10.3 2.8 %copy-start = (f32[288,1024]{1,0:T(8,128)S(1)}, f32[288,1024]{1,0:T(8,128)}, u32[]{:S(2)}) copy-start(f32[288,1024]{1,0:T(8,128)} %refs_1_.2) | copy-start | bytes 3538948
  10.3 2.8 %copy-start.1 = (f32[288,1024]{1,0:T(8,128)S(1)}, f32[288,1024]{1,0:T(8,128)}, u32[]{:S(2)}) copy-start(f32[288,1024]{1,0:T(8,128)} %refs_5_.1) | copy-start | bytes 3538948
  12.5 14.9 %collective-permute-start.2 = (f32[48,1024]{1,0:T(8,128)S(1)}, f32[48,1024]{1,0:T(8,128)S(1)}, u32[]{:S(2)}, u32[]{:S(2)}) collective-permute-start(f32[48,1024]{1,0:T(8,128)S(1)} %collective-permute-done.1.refs_9_), channel_id=1, source_target_pairs={{2,14},{3,15},{6,2},{7,3},{10,6},{11,7},{14,10},{15,11},{18,30},{1... | collective-permute-start | bytes 589832 | tf_op jit(solution)/shard_map/ppermute | solution.py:380
  35.0 9.0 %collective-permute-start.20 = (f32[896,128]{1,0:T(8,128)S(1)}, f32[896,128]{1,0:T(8,128)S(1)}, u32[]{:S(2)}, u32[]{:S(2)}) collective-permute-start(f32[896,128]{1,0:T(8,128)S(1)} %get-tuple-element.71), channel_id=1, source_target_pairs={{0,1},{1,0},{2,3},{3,2},{4,5},{5,4},{6,7},{7,6},{8,9},{9,8},{10,11... | collective-permute-start | bytes 1376264 | tf_op jit(solution)/shard_map/ppermute | solution.py:307
  35.1 8.2 %collective-permute-start.6 = (f32[48,1024]{1,0:T(8,128)S(1)}, f32[48,1024]{1,0:T(8,128)S(1)}, u32[]{:S(2)}, u32[]{:S(2)}) collective-permute-start(f32[48,1024]{1,0:T(8,128)S(1)} %get-tuple-element.58), channel_id=1, source_target_pairs={{0,2},{1,3},{2,0},{3,1},{4,6},{5,7},{6,4},{7,5},{8,10},{9,11},{10,... | collective-permute-start | bytes 589832 | tf_op jit(solution)/shard_map/ppermute | solution.py:307
  35.3 20.7 %collective-permute-start.5 = (f32[16,6144]{1,0:T(8,128)S(1)}, f32[16,6144]{1,0:T(8,128)S(1)}, u32[]{:S(2)}, u32[]{:S(2)}) collective-permute-start(f32[16,6144]{1,0:T(8,128)S(1)} %get-tuple-element.57), channel_id=1, source_target_pairs={{0,15},{1,0},{2,1},{3,2},{4,3},{5,4},{6,5},{7,6},{8,7},{9,8},{10,9... | collective-permute-start | bytes 1179656 | tf_op jit(solution)/shard_map/ppermute | solution.py:302
  40.0 10.5 %collective-permute-start.8 = (f32[48,1024]{1,0:T(8,128)S(1)}, f32[48,1024]{1,0:T(8,128)S(1)}, u32[]{:S(2)}, u32[]{:S(2)}) collective-permute-start(f32[48,1024]{1,0:T(8,128)S(1)} %get-tuple-element.59), channel_id=1, source_target_pairs={{0,12},{1,13},{2,14},{3,15},{4,0},{5,1},{6,2},{7,3},{8,4},{9,5},{1... | collective-permute-start | bytes 589832 | tf_op jit(solution)/shard_map/ppermute | solution.py:302
  40.0 15.9 %collective-permute-start.9 = (f32[48,1024]{1,0:T(8,128)S(1)}, f32[48,1024]{1,0:T(8,128)S(1)}, u32[]{:S(2)}, u32[]{:S(2)}) collective-permute-start(f32[48,1024]{1,0:T(8,128)S(1)} %get-tuple-element.60), channel_id=1, source_target_pairs={{0,8},{1,9},{2,10},{3,11},{4,12},{5,13},{6,14},{7,15},{8,0},{9,1},... | collective-permute-start | bytes 589832 | tf_op jit(solution)/shard_map/ppermute | solution.py:302
  43.3 12.6 %collective-permute-start.7 = (f32[48,1024]{1,0:T(8,128)S(1)}, f32[48,1024]{1,0:T(8,128)S(1)}, u32[]{:S(2)}, u32[]{:S(2)}) collective-permute-start(f32[48,1024]{1,0:T(8,128)S(1)} %collective-permute-done.6.refs_7_), channel_id=1, source_target_pairs={{2,14},{3,15},{6,2},{7,3},{10,6},{11,7},{14,10},{15,11},{18,30},{1... | collective-permute-start | bytes 589832 | tf_op jit(solution)/shard_map/ppermute | solution.py:380
  44.0 0.8 copy-start.3
  45.9 17.1 %collective-permute-start.21 = (f32[448,128]{1,0:T(8,128)S(1)}, f32[448,128]{1,0:T(8,128)S(1)}, u32[]{:S(2)}, u32[]{:S(2)}) collective-permute-start(f32[448,128]{1,0:T(8,128)S(1)} %slice_select_fusion), channel_id=1, source_target_pairs={{0,2},{1,3},{2,0},{3,1},{4,6},{5,7},{6,4},{7,5},{8,10},{9,11},{10,... | collective-permute-start | bytes 688136 | tf_op jit(solution)/shard_map/ppermute | solution.py:307
  62.8 5.1 %collective-permute-start.10 = (f32[896,128]{1,0:T(8,128)S(1)}, f32[896,128]{1,0:T(8,128)S(1)}, u32[]{:S(2)}, u32[]{:S(2)}) collective-permute-start(f32[896,128]{1,0:T(8,128)S(1)} %get-tuple-element.62), channel_id=1, source_target_pairs={{0,1},{1,0},{2,3},{3,2},{4,5},{5,4},{6,7},{7,6},{8,9},{9,8},{10,11... | collective-permute-start | bytes 1376264 | tf_op jit(solution)/shard_map/ppermute | solution.py:307
  63.0 7.2 %collective-permute-start.22 = (f32[112,128]{1,0:T(8,128)S(1)}, f32[112,128]{1,0:T(8,128)S(1)}, u32[]{:S(2)}, u32[]{:S(2)}) collective-permute-start(f32[112,128]{1,0:T(8,128)S(1)} %get-tuple-element.88), channel_id=1, source_target_pairs={{0,4},{1,5},{2,6},{3,7},{4,8},{5,9},{6,10},{7,11},{8,12},{9,13},{1... | collective-permute-start | bytes 172040 | tf_op jit(solution)/shard_map/ppermute | solution.py:336
  64.5 7.8 %collective-permute-start.23 = (f32[112,128]{1,0:T(8,128)S(1)}, f32[112,128]{1,0:T(8,128)S(1)}, u32[]{:S(2)}, u32[]{:S(2)}) collective-permute-start(f32[112,128]{1,0:T(8,128)S(1)} %get-tuple-element.90), channel_id=1, source_target_pairs={{0,8},{1,9},{2,10},{3,11},{4,12},{5,13},{6,14},{7,15},{8,0},{9,1},... | collective-permute-start | bytes 172040 | tf_op jit(solution)/shard_map/ppermute | solution.py:336
  67.9 5.0 %collective-permute-start.24 = (f32[112,128]{1,0:T(8,128)S(1)}, f32[112,128]{1,0:T(8,128)S(1)}, u32[]{:S(2)}, u32[]{:S(2)}) collective-permute-start(f32[112,128]{1,0:T(8,128)S(1)} %get-tuple-element.89), channel_id=1, source_target_pairs={{0,12},{1,13},{2,14},{3,15},{4,0},{5,1},{6,2},{7,3},{8,4},{9,5},{1... | collective-permute-start | bytes 172040 | tf_op jit(solution)/shard_map/ppermute | solution.py:336
  68.0 7.4 %collective-permute-start.11 = (f32[448,128]{1,0:T(8,128)S(1)}, f32[448,128]{1,0:T(8,128)S(1)}, u32[]{:S(2)}, u32[]{:S(2)}) collective-permute-start(f32[448,128]{1,0:T(8,128)S(1)} %slice_select_fusion.1), channel_id=1, source_target_pairs={{0,2},{1,3},{2,0},{3,1},{4,6},{5,7},{6,4},{7,5},{8,10},{9,11},{10,... | collective-permute-start | bytes 688136 | tf_op jit(solution)/shard_map/ppermute | solution.py:307
  75.5 14.4 %collective-permute-start.25 = (f32[112,128]{1,0:T(8,128)S(1)}, f32[112,128]{1,0:T(8,128)S(1)}, u32[]{:S(2)}, u32[]{:S(2)}) collective-permute-start(f32[112,128]{1,0:T(8,128)S(1)} %add_add_fusion), channel_id=1, source_target_pairs={{0,12},{1,13},{2,14},{3,15},{4,0},{5,1},{6,2},{7,3},{8,4},{9,5},{1... | collective-permute-start | bytes 172040 | tf_op jit(solution)/shard_map/ppermute | solution.py:344
  77.0 13.3 %collective-permute-start.26 = (f32[112,128]{1,0:T(8,128)S(1)}, f32[112,128]{1,0:T(8,128)S(1)}, u32[]{:S(2)}, u32[]{:S(2)}) collective-permute-start(f32[112,128]{1,0:T(8,128)S(1)} %add_add_fusion), channel_id=1, source_target_pairs={{0,8},{1,9},{2,10},{3,11},{4,12},{5,13},{6,14},{7,15},{8,0},{9,1},... | collective-permute-start | bytes 172040 | tf_op jit(solution)/shard_map/ppermute | solution.py:344
  78.7 6.1 %collective-permute-start.12 = (f32[112,128]{1,0:T(8,128)S(1)}, f32[112,128]{1,0:T(8,128)S(1)}, u32[]{:S(2)}, u32[]{:S(2)}) collective-permute-start(f32[112,128]{1,0:T(8,128)S(1)} %get-tuple-element.91), channel_id=1, source_target_pairs={{0,4},{1,5},{2,6},{3,7},{4,8},{5,9},{6,10},{7,11},{8,12},{9,13},{1... | collective-permute-start | bytes 172040 | tf_op jit(solution)/shard_map/ppermute | solution.py:336
  79.1 7.4 %collective-permute-start.13 = (f32[112,128]{1,0:T(8,128)S(1)}, f32[112,128]{1,0:T(8,128)S(1)}, u32[]{:S(2)}, u32[]{:S(2)}) collective-permute-start(f32[112,128]{1,0:T(8,128)S(1)} %get-tuple-element.93), channel_id=1, source_target_pairs={{0,8},{1,9},{2,10},{3,11},{4,12},{5,13},{6,14},{7,15},{8,0},{9,1},... | collective-permute-start | bytes 172040 | tf_op jit(solution)/shard_map/ppermute | solution.py:336
  80.5 6.0 %collective-permute-start.14 = (f32[112,128]{1,0:T(8,128)S(1)}, f32[112,128]{1,0:T(8,128)S(1)}, u32[]{:S(2)}, u32[]{:S(2)}) collective-permute-start(f32[112,128]{1,0:T(8,128)S(1)} %get-tuple-element.92), channel_id=1, source_target_pairs={{0,12},{1,13},{2,14},{3,15},{4,0},{5,1},{6,2},{7,3},{8,4},{9,5},{1... | collective-permute-start | bytes 172040 | tf_op jit(solution)/shard_map/ppermute | solution.py:336
  84.9 6.2 %collective-permute-start.27 = (f32[112,128]{1,0:T(8,128)S(1)}, f32[112,128]{1,0:T(8,128)S(1)}, u32[]{:S(2)}, u32[]{:S(2)}) collective-permute-start(f32[112,128]{1,0:T(8,128)S(1)} %add_add_fusion), channel_id=1, source_target_pairs={{0,4},{1,5},{2,6},{3,7},{4,8},{5,9},{6,10},{7,11},{8,12},{9,13},{1... | collective-permute-start | bytes 172040 | tf_op jit(solution)/shard_map/ppermute | solution.py:344
  86.6 6.1 %collective-permute-start.15 = (f32[112,128]{1,0:T(8,128)S(1)}, f32[112,128]{1,0:T(8,128)S(1)}, u32[]{:S(2)}, u32[]{:S(2)}) collective-permute-start(f32[112,128]{1,0:T(8,128)S(1)} %get-tuple-element.79), channel_id=1, source_target_pairs={{0,12},{1,13},{2,14},{3,15},{4,0},{5,1},{6,2},{7,3},{8,4},{9,5},{1... | collective-permute-start | bytes 172040 | tf_op jit(solution)/shard_map/ppermute | solution.py:344
  89.7 5.1 %collective-permute-start.16 = (f32[112,128]{1,0:T(8,128)S(1)}, f32[112,128]{1,0:T(8,128)S(1)}, u32[]{:S(2)}, u32[]{:S(2)}) collective-permute-start(f32[112,128]{1,0:T(8,128)S(1)} %get-tuple-element.79), channel_id=1, source_target_pairs={{0,8},{1,9},{2,10},{3,11},{4,12},{5,13},{6,14},{7,15},{8,0},{9,1},... | collective-permute-start | bytes 172040 | tf_op jit(solution)/shard_map/ppermute | solution.py:344
  89.9 6.0 %collective-permute-start.17 = (f32[112,128]{1,0:T(8,128)S(1)}, f32[112,128]{1,0:T(8,128)S(1)}, u32[]{:S(2)}, u32[]{:S(2)}) collective-permute-start(f32[112,128]{1,0:T(8,128)S(1)} %get-tuple-element.79), channel_id=1, source_target_pairs={{0,4},{1,5},{2,6},{3,7},{4,8},{5,9},{6,10},{7,11},{8,12},{9,13},{1... | collective-permute-start | bytes 172040 | tf_op jit(solution)/shard_map/ppermute | solution.py:344
  91.1 10.7 %collective-permute-start.28 = (f32[448,128]{1,0:T(8,128)S(1)}, f32[448,128]{1,0:T(8,128)S(1)}, u32[]{:S(2)}, u32[]{:S(2)}) collective-permute-start(f32[448,128]{1,0:T(8,128)S(1)} %constant_dynamic-slice_fusion), channel_id=1, source_target_pairs={{0,2},{1,3},{2,0},{3,1},{4,6},{5,7},{6,4},{7,5},{8,10},{9,11},{10,... | collective-permute-start | bytes 688136 | tf_op jit(solution)/shard_map/ppermute | solution.py:307
  96.0 6.2 %collective-permute-start.18 = (f32[448,128]{1,0:T(8,128)S(1)}, f32[448,128]{1,0:T(8,128)S(1)}, u32[]{:S(2)}, u32[]{:S(2)}) collective-permute-start(f32[448,128]{1,0:T(8,128)S(1)} %constant_dynamic-slice_fusion.4), channel_id=1, source_target_pairs={{0,2},{1,3},{2,0},{3,1},{4,6},{5,7},{6,4},{7,5},{8,10},{9,11},{10,... | collective-permute-start | bytes 688136 | tf_op jit(solution)/shard_map/ppermute | solution.py:307
  101.9 1.9 %collective-permute-start.29 = (f32[896,128]{1,0:T(8,128)S(1)}, f32[896,128]{1,0:T(8,128)S(1)}, u32[]{:S(2)}, u32[]{:S(2)}) collective-permute-start(f32[896,128]{1,0:T(8,128)S(1)} %pad_maximum_fusion.1.refs_2_), channel_id=1, source_target_pairs={{0,1},{1,0},{2,3},{3,2},{4,5},{5,4},{6,7},{7,6},{8,9},{9,8},{10,11... | collective-permute-start | bytes 1376264 | tf_op jit(solution)/shard_map/ppermute | solution.py:307
  102.2 2.2 %collective-permute-start.19 = (f32[896,128]{1,0:T(8,128)S(1)}, f32[896,128]{1,0:T(8,128)S(1)}, u32[]{:S(2)}, u32[]{:S(2)}) collective-permute-start(f32[896,128]{1,0:T(8,128)S(1)} %pad_maximum_fusion.refs_0_), channel_id=1, source_target_pairs={{0,1},{1,0},{2,3},{3,2},{4,5},{5,4},{6,7},{7,6},{8,9},{9,8},{10,11... | collective-permute-start | bytes 1376264 | tf_op jit(solution)/shard_map/ppermute | solution.py:307

commit v10 on v9

--- a/solution.py
+++ b/solution.py
@@ -448,7 +448,7 @@
     sum_0 = keep + exchange(send, 1)
     steps = [lambda x: fold(x, 2), fold_far, spread_far, lambda x: spread(x, 2)]
     for number, (step, ahead) in enumerate(zip(steps[:-1], steps[1:])):
-        if number > 0:
+        if number > 1:
             sum_1, _ = lax.optimization_barrier((sum_1, sum_0))
         sum_1 = ahead(sum_1)
         sum_0 = step(sum_0)

time: 106 us -> 115 us (1.085)
  waiting for transfers between devices: 30.8 us -> 42 us
    ppermute x10, waiting for transfers between devices: 8.43 us -> 17.2 us  [exchange(): return lax.ppermute(value, 'seq', [(s, s ^ mask) for s in range(count)])]
    ppermute x6, waiting for transfers between devices: 3.84 us -> 9.46 us  [spread_far(): lax.ppermute(x, 'seq', groups_of_four(o))]
    ppermute x6, waiting for transfers between devices: 6.66 us -> 1.97 us  [fold_far(): lax.ppermute(part(mine + o), 'seq', groups_of_four(o))]
    ppermute x6, starting transfers between devices: 9.01 us -> 12.2 us  [fold_far(): lax.ppermute(part(mine + o), 'seq', groups_of_four(o))]
    ppermute x10, starting transfers between devices: 13.2 us -> 11.2 us  [exchange(): return lax.ppermute(value, 'seq', [(s, s ^ mask) for s in range(count)])]
    ppermute x6, waiting for transfers between devices: 11.8 us -> 13.4 us  [from_ahead(): lax.ppermute(value, 'seq', [(s, (s - steps) % count) for s in range(count)])]
  transfers between devices with their start and end apart: 30 -> 30, of which waited for: 17 -> 16; matrix products, arithmetic and copies ran while one was open for 3% -> 2% of each run, Pallas kernels for 18% -> 16%
where the time goes in v10:
time: 115 us
  waiting for transfers between devices  42 us (37%)
  starting transfers between devices  38.7 us (34%)
  Pallas kernels  30.5 us (27%)
  local copies, waits for them, and re-layouts  1.94 us (2%)
    ppermute x10, waiting for transfers between devices, exchange(): return lax.ppermute(value, 'seq', [(s, s ^ mask) for s in range(count)])  17.2 us
    ppermute x6, waiting for transfers between devices, from_ahead(): lax.ppermute(value, 'seq', [(s, (s - steps) % count) for s in range(count)])  13.4 us
    ppermute x6, starting transfers between devices, fold_far(): lax.ppermute(part(mine + o), 'seq', groups_of_four(o))  12.2 us
    ppermute x10, starting transfers between devices, exchange(): return lax.ppermute(value, 'seq', [(s, s ^ mask) for s in range(count)])  11.2 us
    ppermute x6, waiting for transfers between devices, spread_far(): lax.ppermute(x, 'seq', groups_of_four(o))  9.46 us
    pallas_call x1, Pallas kernels, body(): pl.pallas_call(lambda *refs: act_kernel(hops, pos, *refs), out_shape=[sha...  7.89 us
    pallas_call x1, Pallas kernels, body(): pl.pallas_call(lambda *refs: upper_kernel(hops, pos, factor, *refs), out_...  7.62 us
    ppermute x6, starting transfers between devices, from_ahead(): lax.ppermute(value, 'seq', [(s, (s - steps) % count) for s in range(count)])  7.28 us
  transfers between devices with their start and end apart: 30, of which 16 were waited for; matrix products, arithmetic and copies ran while one was open for 2% of the time, Pallas kernels for 16%

profile of v10, /device:TPU:0, one launch (start us, length us, event | category | flops | bytes accessed | tf_op | source)
XLA Modules:
  0.0 114.6 jit_solution(9641009736689288487)
XLA Ops:
  0.7 2.7 %pack.1 = (s32[64]{0:T(128)S(1)}, f32[16,6144]{1,0:T(8,128)S(1)}, f32[48,1024]{1,0:T(8,128)S(1)}, f32[48,1024]{1,0:T(8,128)S(1)}, f32[48,1024]{1,0:T(8,128)S(1)}) custom-call(s32[2,18]{1,0:T(2,128)} %refs_0_.3, f32[288,1024]{1,0:T(8,128)} %refs_2_.1), custom_call_target="tpu_custom_call" | custom-call | flops 2000000000 | bytes 6000000 | tf_op jit(solution)/shard_map/pack/pallas_call | solution.py:387
  3.4 3.0 %collective-permute-start.1 = (f32[48,1024]{1,0:T(8,128)S(1)}, f32[48,1024]{1,0:T(8,128)S(1)}, u32[]{:S(2)}, u32[]{:S(2)}) collective-permute-start(f32[48,1024]{1,0:T(8,128)S(1)} %get-tuple-element.48), channel_id=1, source_target_pairs={{0,2},{1,3},{2,0},{3,1},{4,6},{5,7},{6,4},{7,5},{8,10},{9,11},{10,... | collective-permute-start | bytes 589832 | tf_op jit(solution)/shard_map/ppermute | solution.py:307
  6.4 2.7 %collective-permute-start = (f32[16,6144]{1,0:T(8,128)S(1)}, f32[16,6144]{1,0:T(8,128)S(1)}, u32[]{:S(2)}, u32[]{:S(2)}) collective-permute-start(f32[16,6144]{1,0:T(8,128)S(1)} %get-tuple-element.47), channel_id=1, source_target_pairs={{0,15},{1,0},{2,1},{3,2},{4,3},{5,4},{6,5},{7,6},{8,7},{9,8},{10,9... | collective-permute-start | bytes 1179656 | tf_op jit(solution)/shard_map/ppermute | solution.py:302
  9.1 0.9 collective-permute-start.3
  10.0 0.1 copy.11.refs_3_
  10.1 0.1 copy.12.refs_7_
  10.3 1.5 %slice_bitcast_fusion = (f32[288,384]{1,0:T(8,128)S(1)}, f32[288,384]{1,0:T(8,128)S(1)}, f32[288,384]{1,0:T(8,128)S(1)}, f32[288,384]{1,0:T(8,128)S(1)}) fusion(f32[2,288,384]{2,1,0:T(8,128)S(1)} %bitcast.14, f32[2,288,384]{2,1,0:T(8,128)} %param.10), kind=kLoop, calls=%fused_computation.2 | loop fusion | bytes 3538944 | tf_op jit(solution)/shard_map/squeeze | solution.py:401
  11.8 0.7 collective-permute-done.1.refs_9_
  12.5 0.7 collective-permute-start.2
  13.1 7.9 %act.1 = (s32[64]{0:T(128)S(1)}, bf16[608,1024]{1,0:T(8,128)(2,1)}, bf16[768,1024]{1,0:T(8,128)(2,1)}, f32[384,1024]{1,0:T(8,128)}, bf16[288,1152]{1,0:T(8,128)(...) custom-call(s32[2,18]{1,0:T(2,128)} %refs_0_.3, ...), custom_call_target="tpu_custom_call" | custom-call | flops 5000000000 | bytes 15000000 | tf_op jit(solution)/shard_map/act/pallas_call | solution.py:409
  21.1 6.3 %collective-permute-done.4.refs_12_ = f32[48,1024]{1,0:T(8,128)S(1)} collective-permute-done((f32[48,1024]{1,0:T(8,128)S(1)}, f32[48,1024]{1,0:T(8,128)S(1)}, u32[]{:S(2)}, u32[]{:S(2)}) %collective-permute-start.4) | collective-permute-done | bytes 196640 | tf_op jit(solution)/shard_map/ppermute | solution.py:302
  27.4 7.6 %upper.1 = (f32[16,6144]{1,0:T(8,128)S(1)}, f32[48,1024]{1,0:T(8,128)S(1)}, f32[48,1024]{1,0:T(8,128)S(1)}, f32[48,1024]{1,0:T(8,128)S(1)}, f32[896,128]{1,0:T(8...) custom-call(s32[64]{0:T(128)S(1)} %get-tuple-element.41.refs_0_, s32[64]{0:T(128)S(1)} %get-tuple-element.40.refs_1_.refs_0_, ...), custom_call_target="tpu_custom_call" | custom-call | flops 6000000000 | bytes 18000000 | tf_op jit(solution)/shard_map/upper/pallas_call | solution.py:426
  35.0 0.1 collective-permute-start.20
  35.1 1.8 %collective-permute-done.20 = f32[896,128]{1,0:T(8,128)S(1)} collective-permute-done((f32[896,128]{1,0:T(8,128)S(1)}, f32[896,128]{1,0:T(8,128)S(1)}, u32[]{:S(2)}, u32[]{:S(2)}) %collective-permute-start.20) | collective-permute-done | bytes 458784 | tf_op jit(solution)/shard_map/ppermute | solution.py:307
  37.0 0.2 collective-permute-start.21
  37.1 1.9 %collective-permute-start.6 = (f32[48,1024]{1,0:T(8,128)S(1)}, f32[48,1024]{1,0:T(8,128)S(1)}, u32[]{:S(2)}, u32[]{:S(2)}) collective-permute-start(f32[48,1024]{1,0:T(8,128)S(1)} %get-tuple-element.57), channel_id=1, source_target_pairs={{0,2},{1,3},{2,0},{3,1},{4,6},{5,7},{6,4},{7,5},{8,10},{9,11},{10,... | collective-permute-start | bytes 589832 | tf_op jit(solution)/shard_map/ppermute | solution.py:307
  39.1 2.8 %collective-permute-start.5 = (f32[16,6144]{1,0:T(8,128)S(1)}, f32[16,6144]{1,0:T(8,128)S(1)}, u32[]{:S(2)}, u32[]{:S(2)}) collective-permute-start(f32[16,6144]{1,0:T(8,128)S(1)} %get-tuple-element.56), channel_id=1, source_target_pairs={{0,15},{1,0},{2,1},{3,2},{4,3},{5,4},{6,5},{7,6},{8,7},{9,8},{10,9... | collective-permute-start | bytes 1179656 | tf_op jit(solution)/shard_map/ppermute | solution.py:302
  41.8 0.9 collective-permute-start.8
  42.7 8.2 %collective-permute-done.6.refs_7_ = f32[48,1024]{1,0:T(8,128)S(1)} collective-permute-done((f32[48,1024]{1,0:T(8,128)S(1)}, f32[48,1024]{1,0:T(8,128)S(1)}, u32[]{:S(2)}, u32[]{:S(2)}) %collective-permute-start.6) | collective-permute-done | bytes 196640 | tf_op jit(solution)/shard_map/ppermute | solution.py:307
  50.9 0.7 collective-permute-start.7
  51.7 1.1 collective-permute-start.22
  52.8 1.3 %collective-permute-done.8.refs_9_ = f32[48,1024]{1,0:T(8,128)S(1)} collective-permute-done((f32[48,1024]{1,0:T(8,128)S(1)}, f32[48,1024]{1,0:T(8,128)S(1)}, u32[]{:S(2)}, u32[]{:S(2)}) %collective-permute-start.8) | collective-permute-done | bytes 196640 | tf_op jit(solution)/shard_map/ppermute | solution.py:302
  54.1 2.1 %collective-permute-start.23 = (f32[112,128]{1,0:T(8,128)S(1)}, f32[112,128]{1,0:T(8,128)S(1)}, u32[]{:S(2)}, u32[]{:S(2)}) collective-permute-start(f32[112,128]{1,0:T(8,128)S(1)} %get-tuple-element.90), channel_id=1, source_target_pairs={{0,8},{1,9},{2,10},{3,11},{4,12},{5,13},{6,14},{7,15},{8,0},{9,1},... | collective-permute-start | bytes 172040 | tf_op jit(solution)/shard_map/ppermute | solution.py:336
  56.2 5.8 %collective-permute-done.9.refs_10_ = f32[48,1024]{1,0:T(8,128)S(1)} collective-permute-done((f32[48,1024]{1,0:T(8,128)S(1)}, f32[48,1024]{1,0:T(8,128)S(1)}, u32[]{:S(2)}, u32[]{:S(2)}) %collective-permute-start.9) | collective-permute-done | bytes 196640 | tf_op jit(solution)/shard_map/ppermute | solution.py:302
  61.9 3.5 %collective-permute-start.24 = (f32[112,128]{1,0:T(8,128)S(1)}, f32[112,128]{1,0:T(8,128)S(1)}, u32[]{:S(2)}, u32[]{:S(2)}) collective-permute-start(f32[112,128]{1,0:T(8,128)S(1)} %get-tuple-element.89), channel_id=1, source_target_pairs={{0,12},{1,13},{2,14},{3,15},{4,0},{5,1},{6,2},{7,3},{8,4},{9,5},{1... | collective-permute-start | bytes 172040 | tf_op jit(solution)/shard_map/ppermute | solution.py:336
  65.4 6.7 %lower.1 = (f32[896,128]{1,0:T(8,128)S(1)}, f32[896,128]{1,0:T(8,128)S(1)}, f32[288,1024]{1,0:T(8,128)}, bf16[1152,1024]{1,0:T(8,128)(2,1)}) custom-call(s32[64]{0:T(128)S(1)} %get-tuple-element.40.refs_1_.refs_0_, f32[288,1024]{1,0:T(8,128)} %get-tuple-element.51.refs_1_, bf16[384,864]{1,0:T(8,128)(2,1)} %get-tuple-element.52.refs_2_, ...), custom_call_target="tpu_custom_call" | custom-call | flops 5000000000 | bytes 15000000 | tf_op jit(solution)/shard_map/lower/pallas_call | solution.py:440
  72.5 1.9 %collective-permute-start.27 = (f32[112,128]{1,0:T(8,128)S(1)}, f32[112,128]{1,0:T(8,128)S(1)}, u32[]{:S(2)}, u32[]{:S(2)}) collective-permute-start(f32[112,128]{1,0:T(8,128)S(1)} %get-tuple-element.77), channel_id=1, source_target_pairs={{0,4},{1,5},{2,6},{3,7},{4,8},{5,9},{6,10},{7,11},{8,12},{9,13},{1... | collective-permute-start | bytes 172040 | tf_op jit(solution)/shard_map/ppermute | solution.py:344
  74.4 3.4 %collective-permute-done.25 = f32[112,128]{1,0:T(8,128)S(1)} collective-permute-done((f32[112,128]{1,0:T(8,128)S(1)}, f32[112,128]{1,0:T(8,128)S(1)}, u32[]{:S(2)}, u32[]{:S(2)}) %collective-permute-start.25) | collective-permute-done | bytes 57376 | tf_op jit(solution)/shard_map/ppermute | solution.py:344
  77.8 2.4 %collective-permute-done.26 = f32[112,128]{1,0:T(8,128)S(1)} collective-permute-done((f32[112,128]{1,0:T(8,128)S(1)}, f32[112,128]{1,0:T(8,128)S(1)}, u32[]{:S(2)}, u32[]{:S(2)}) %collective-permute-start.26) | collective-permute-done | bytes 57376 | tf_op jit(solution)/shard_map/ppermute | solution.py:344
  80.3 1.7 %collective-permute-start.11 = (f32[448,128]{1,0:T(8,128)S(1)}, f32[448,128]{1,0:T(8,128)S(1)}, u32[]{:S(2)}, u32[]{:S(2)}) collective-permute-start(f32[448,128]{1,0:T(8,128)S(1)} %slice_select_fusion.1), channel_id=1, source_target_pairs={{0,2},{1,3},{2,0},{3,1},{4,6},{5,7},{6,4},{7,5},{8,10},{9,11},{10,... | collective-permute-start | bytes 688136 | tf_op jit(solution)/shard_map/ppermute | solution.py:307
  82.0 4.8 %collective-permute-done.11 = f32[448,128]{1,0:T(8,128)S(1)} collective-permute-done((f32[448,128]{1,0:T(8,128)S(1)}, f32[448,128]{1,0:T(8,128)S(1)}, u32[]{:S(2)}, u32[]{:S(2)}) %collective-permute-start.11) | collective-permute-done | bytes 229408 | tf_op jit(solution)/shard_map/ppermute | solution.py:307
  86.9 1.2 %collective-permute-start.12 = (f32[112,128]{1,0:T(8,128)S(1)}, f32[112,128]{1,0:T(8,128)S(1)}, u32[]{:S(2)}, u32[]{:S(2)}) collective-permute-start(f32[112,128]{1,0:T(8,128)S(1)} %get-tuple-element.91), channel_id=1, source_target_pairs={{0,4},{1,5},{2,6},{3,7},{4,8},{5,9},{6,10},{7,11},{8,12},{9,13},{1... | collective-permute-start | bytes 172040 | tf_op jit(solution)/shard_map/ppermute | solution.py:336
  88.1 1.6 %collective-permute-start.13 = (f32[112,128]{1,0:T(8,128)S(1)}, f32[112,128]{1,0:T(8,128)S(1)}, u32[]{:S(2)}, u32[]{:S(2)}) collective-permute-start(f32[112,128]{1,0:T(8,128)S(1)} %get-tuple-element.93), channel_id=1, source_target_pairs={{0,8},{1,9},{2,10},{3,11},{4,12},{5,13},{6,14},{7,15},{8,0},{9,1},... | collective-permute-start | bytes 172040 | tf_op jit(solution)/shard_map/ppermute | solution.py:336
  89.7 2.7 %collective-permute-start.14 = (f32[112,128]{1,0:T(8,128)S(1)}, f32[112,128]{1,0:T(8,128)S(1)}, u32[]{:S(2)}, u32[]{:S(2)}) collective-permute-start(f32[112,128]{1,0:T(8,128)S(1)} %get-tuple-element.92), channel_id=1, source_target_pairs={{0,12},{1,13},{2,14},{3,15},{4,0},{5,1},{6,2},{7,3},{8,4},{9,5},{1... | collective-permute-start | bytes 172040 | tf_op jit(solution)/shard_map/ppermute | solution.py:336
  92.4 1.1 collective-permute-done.12
  93.5 0.3 collective-permute-done.13
  93.8 0.6 collective-permute-done.14
  94.4 4.1 %collective-permute-start.15 = (f32[112,128]{1,0:T(8,128)S(1)}, f32[112,128]{1,0:T(8,128)S(1)}, u32[]{:S(2)}, u32[]{:S(2)}) collective-permute-start(f32[112,128]{1,0:T(8,128)S(1)} %get-tuple-element.79), channel_id=1, source_target_pairs={{0,12},{1,13},{2,14},{3,15},{4,0},{5,1},{6,2},{7,3},{8,4},{9,5},{1... | collective-permute-start | bytes 172040 | tf_op jit(solution)/shard_map/ppermute | solution.py:344
  98.5 0.6 collective-permute-start.17
  99.1 1.7 %collective-permute-start.28 = (f32[448,128]{1,0:T(8,128)S(1)}, f32[448,128]{1,0:T(8,128)S(1)}, u32[]{:S(2)}, u32[]{:S(2)}) collective-permute-start(f32[448,128]{1,0:T(8,128)S(1)} %constant_dynamic-slice_fusion), channel_id=1, source_target_pairs={{0,2},{1,3},{2,0},{3,1},{4,6},{5,7},{6,4},{7,5},{8,10},{9,11},{10,... | collective-permute-start | bytes 688136 | tf_op jit(solution)/shard_map/ppermute | solution.py:307
  100.8 2.7 %collective-permute-done.16 = f32[112,128]{1,0:T(8,128)S(1)} collective-permute-done((f32[112,128]{1,0:T(8,128)S(1)}, f32[112,128]{1,0:T(8,128)S(1)}, u32[]{:S(2)}, u32[]{:S(2)}) %collective-permute-start.16) | collective-permute-done | bytes 57376 | tf_op jit(solution)/shard_map/ppermute | solution.py:344
  103.6 1.0 collective-permute-done.17
  104.6 1.8 %collective-permute-start.18 = (f32[448,128]{1,0:T(8,128)S(1)}, f32[448,128]{1,0:T(8,128)S(1)}, u32[]{:S(2)}, u32[]{:S(2)}) collective-permute-start(f32[448,128]{1,0:T(8,128)S(1)} %constant_dynamic-slice_fusion.4), channel_id=1, source_target_pairs={{0,2},{1,3},{2,0},{3,1},{4,6},{5,7},{6,4},{7,5},{8,10},{9,11},{10,... | collective-permute-start | bytes 688136 | tf_op jit(solution)/shard_map/ppermute | solution.py:307
  106.4 4.2 %inward.1 = f32[288,1024]{1,0:T(8,128)} custom-call(bf16[288,1152]{1,0:T(8,128)(2,1)} %get-tuple-element.64.refs_0_, f32[288,1024]{1,0:T(8,128)} %get-tuple-element.65.refs_1_, bf16[1152,1024]{1,0:T(8,128)(2,1)} %get-tuple-element.66.refs_2_), custom_call_target="tpu_custom_call" | custom-call | flops 3000000000 | bytes 9000000 | tf_op jit(solution)/shard_map/inward/pallas_call | solution.py:457
  110.9 0.5 collective-permute-start.19
  111.5 1.2 %collective-permute-done.29.refs_3_ = f32[896,128]{1,0:T(8,128)S(1)} collective-permute-done((f32[896,128]{1,0:T(8,128)S(1)}, f32[896,128]{1,0:T(8,128)S(1)}, u32[]{:S(2)}, u32[]{:S(2)}) %collective-permute-start.29) | collective-permute-done | bytes 458784 | tf_op jit(solution)/shard_map/ppermute | solution.py:307
  112.7 0.7 collective-permute-done.19.refs_1_
  113.3 1.3 %finish.1 = (f32[2,288,384]{2,1,0:T(8,128)}, f32[2,384]{1,0:T(2,128)}, f32[2,288,384]{2,1,0:T(8,128)}) custom-call(f32[896,128]{1,0:T(8,128)S(1)} %pad_maximum_fusion.refs_0_, f32[896,128]{1,0:T(8,128)S(1)} %collective-permute-done.19.refs_1_, f32[896,128]{1,0:T(8,128)S(1)} %pad_maximum_fusion.1.refs_2_, f32[896,128]{1,0:T(8,128)S(1)} %collective-permute-done.29.refs_3_), custom_call_target="tpu_custom_call" | custom-call | flops 1000000000 | bytes 3000000 | tf_op jit(solution)/shard_map/finish/pallas_call | solution.py:471
  (60 shorter events, 1.0 us)
Async XLA Ops:
  0.6 9.4 %copy-start.3 = (f32[2,384]{1,0:T(2,128)S(1)}, f32[2,384]{1,0:T(2,128)}, u32[]{:S(2)}) copy-start(f32[2,384]{1,0:T(2,128)} %param.11) | copy-start | bytes 9220
  0.6 9.7 %copy-start.2 = (f32[2,384,288]{1,2,0:T(8,128)S(1)}, f32[2,384,288]{1,2,0:T(8,128)}, u32[]{:S(2)}) copy-start(f32[2,384,288]{1,2,0:T(8,128)} %param.12) | copy-start | bytes 2654212
  3.4 9.1 %collective-permute-start.1 = (f32[48,1024]{1,0:T(8,128)S(1)}, f32[48,1024]{1,0:T(8,128)S(1)}, u32[]{:S(2)}, u32[]{:S(2)}) collective-permute-start(f32[48,1024]{1,0:T(8,128)S(1)} %get-tuple-element.48), channel_id=1, source_target_pairs={{0,2},{1,3},{2,0},{3,1},{4,6},{5,7},{6,4},{7,5},{8,10},{9,11},{10,... | collective-permute-start | bytes 589832 | tf_op jit(solution)/shard_map/ppermute | solution.py:307
  6.4 21.0 %collective-permute-start = (f32[16,6144]{1,0:T(8,128)S(1)}, f32[16,6144]{1,0:T(8,128)S(1)}, u32[]{:S(2)}, u32[]{:S(2)}) collective-permute-start(f32[16,6144]{1,0:T(8,128)S(1)} %get-tuple-element.47), channel_id=1, source_target_pairs={{0,15},{1,0},{2,1},{3,2},{4,3},{5,4},{6,5},{7,6},{8,7},{9,8},{10,9... | collective-permute-start | bytes 1179656 | tf_op jit(solution)/shard_map/ppermute | solution.py:302
  9.1 12.0 %collective-permute-start.3 = (f32[48,1024]{1,0:T(8,128)S(1)}, f32[48,1024]{1,0:T(8,128)S(1)}, u32[]{:S(2)}, u32[]{:S(2)}) collective-permute-start(f32[48,1024]{1,0:T(8,128)S(1)} %get-tuple-element.49), channel_id=1, source_target_pairs={{0,12},{1,13},{2,14},{3,15},{4,0},{5,1},{6,2},{7,3},{8,4},{9,5},{1... | collective-permute-start | bytes 589832 | tf_op jit(solution)/shard_map/ppermute | solution.py:302
  10.0 17.4 %collective-permute-start.4 = (f32[48,1024]{1,0:T(8,128)S(1)}, f32[48,1024]{1,0:T(8,128)S(1)}, u32[]{:S(2)}, u32[]{:S(2)}) collective-permute-start(f32[48,1024]{1,0:T(8,128)S(1)} %get-tuple-element.50), channel_id=1, source_target_pairs={{0,8},{1,9},{2,10},{3,11},{4,12},{5,13},{6,14},{7,15},{8,0},{9,1},... | collective-permute-start | bytes 589832 | tf_op jit(solution)/shard_map/ppermute | solution.py:302
  10.3 2.8 %copy-start = (f32[288,1024]{1,0:T(8,128)S(1)}, f32[288,1024]{1,0:T(8,128)}, u32[]{:S(2)}) copy-start(f32[288,1024]{1,0:T(8,128)} %refs_1_.2) | copy-start | bytes 3538948
  10.3 2.8 %copy-start.1 = (f32[288,1024]{1,0:T(8,128)S(1)}, f32[288,1024]{1,0:T(8,128)}, u32[]{:S(2)}) copy-start(f32[288,1024]{1,0:T(8,128)} %refs_5_.1) | copy-start | bytes 3538948
  12.5 14.9 %collective-permute-start.2 = (f32[48,1024]{1,0:T(8,128)S(1)}, f32[48,1024]{1,0:T(8,128)S(1)}, u32[]{:S(2)}, u32[]{:S(2)}) collective-permute-start(f32[48,1024]{1,0:T(8,128)S(1)} %collective-permute-done.1.refs_9_), channel_id=1, source_target_pairs={{2,14},{3,15},{6,2},{7,3},{10,6},{11,7},{14,10},{15,11},{18,30},{1... | collective-permute-start | bytes 589832 | tf_op jit(solution)/shard_map/ppermute | solution.py:380
  35.0 1.9 %collective-permute-start.20 = (f32[896,128]{1,0:T(8,128)S(1)}, f32[896,128]{1,0:T(8,128)S(1)}, u32[]{:S(2)}, u32[]{:S(2)}) collective-permute-start(f32[896,128]{1,0:T(8,128)S(1)} %get-tuple-element.70), channel_id=1, source_target_pairs={{0,1},{1,0},{2,3},{3,2},{4,5},{5,4},{6,7},{7,6},{8,9},{9,8},{10,11... | collective-permute-start | bytes 1376264 | tf_op jit(solution)/shard_map/ppermute | solution.py:307
  37.0 14.6 %collective-permute-start.21 = (f32[448,128]{1,0:T(8,128)S(1)}, f32[448,128]{1,0:T(8,128)S(1)}, u32[]{:S(2)}, u32[]{:S(2)}) collective-permute-start(f32[448,128]{1,0:T(8,128)S(1)} %slice_select_fusion), channel_id=1, source_target_pairs={{0,2},{1,3},{2,0},{3,1},{4,6},{5,7},{6,4},{7,5},{8,10},{9,11},{10,... | collective-permute-start | bytes 688136 | tf_op jit(solution)/shard_map/ppermute | solution.py:307
  37.1 13.8 %collective-permute-start.6 = (f32[48,1024]{1,0:T(8,128)S(1)}, f32[48,1024]{1,0:T(8,128)S(1)}, u32[]{:S(2)}, u32[]{:S(2)}) collective-permute-start(f32[48,1024]{1,0:T(8,128)S(1)} %get-tuple-element.57), channel_id=1, source_target_pairs={{0,2},{1,3},{2,0},{3,1},{4,6},{5,7},{6,4},{7,5},{8,10},{9,11},{10,... | collective-permute-start | bytes 589832 | tf_op jit(solution)/shard_map/ppermute | solution.py:307
  39.1 26.4 %collective-permute-start.5 = (f32[16,6144]{1,0:T(8,128)S(1)}, f32[16,6144]{1,0:T(8,128)S(1)}, u32[]{:S(2)}, u32[]{:S(2)}) collective-permute-start(f32[16,6144]{1,0:T(8,128)S(1)} %get-tuple-element.56), channel_id=1, source_target_pairs={{0,15},{1,0},{2,1},{3,2},{4,3},{5,4},{6,5},{7,6},{8,7},{9,8},{10,9... | collective-permute-start | bytes 1179656 | tf_op jit(solution)/shard_map/ppermute | solution.py:302
  41.8 12.3 %collective-permute-start.8 = (f32[48,1024]{1,0:T(8,128)S(1)}, f32[48,1024]{1,0:T(8,128)S(1)}, u32[]{:S(2)}, u32[]{:S(2)}) collective-permute-start(f32[48,1024]{1,0:T(8,128)S(1)} %get-tuple-element.58), channel_id=1, source_target_pairs={{0,12},{1,13},{2,14},{3,15},{4,0},{5,1},{6,2},{7,3},{8,4},{9,5},{1... | collective-permute-start | bytes 589832 | tf_op jit(solution)/shard_map/ppermute | solution.py:302
  42.7 19.2 %collective-permute-start.9 = (f32[48,1024]{1,0:T(8,128)S(1)}, f32[48,1024]{1,0:T(8,128)S(1)}, u32[]{:S(2)}, u32[]{:S(2)}) collective-permute-start(f32[48,1024]{1,0:T(8,128)S(1)} %get-tuple-element.59), channel_id=1, source_target_pairs={{0,8},{1,9},{2,10},{3,11},{4,12},{5,13},{6,14},{7,15},{8,0},{9,1},... | collective-permute-start | bytes 589832 | tf_op jit(solution)/shard_map/ppermute | solution.py:302
  50.9 14.5 %collective-permute-start.7 = (f32[48,1024]{1,0:T(8,128)S(1)}, f32[48,1024]{1,0:T(8,128)S(1)}, u32[]{:S(2)}, u32[]{:S(2)}) collective-permute-start(f32[48,1024]{1,0:T(8,128)S(1)} %collective-permute-done.6.refs_7_), channel_id=1, source_target_pairs={{2,14},{3,15},{6,2},{7,3},{10,6},{11,7},{14,10},{15,11},{18,30},{1... | collective-permute-start | bytes 589832 | tf_op jit(solution)/shard_map/ppermute | solution.py:380
  51.7 20.6 %collective-permute-start.22 = (f32[112,128]{1,0:T(8,128)S(1)}, f32[112,128]{1,0:T(8,128)S(1)}, u32[]{:S(2)}, u32[]{:S(2)}) collective-permute-start(f32[112,128]{1,0:T(8,128)S(1)} %get-tuple-element.88), channel_id=1, source_target_pairs={{0,4},{1,5},{2,6},{3,7},{4,8},{5,9},{6,10},{7,11},{8,12},{9,13},{1... | collective-permute-start | bytes 172040 | tf_op jit(solution)/shard_map/ppermute | solution.py:336
  54.1 18.1 %collective-permute-start.23 = (f32[112,128]{1,0:T(8,128)S(1)}, f32[112,128]{1,0:T(8,128)S(1)}, u32[]{:S(2)}, u32[]{:S(2)}) collective-permute-start(f32[112,128]{1,0:T(8,128)S(1)} %get-tuple-element.90), channel_id=1, source_target_pairs={{0,8},{1,9},{2,10},{3,11},{4,12},{5,13},{6,14},{7,15},{8,0},{9,1},... | collective-permute-start | bytes 172040 | tf_op jit(solution)/shard_map/ppermute | solution.py:336
  61.9 10.3 %collective-permute-start.24 = (f32[112,128]{1,0:T(8,128)S(1)}, f32[112,128]{1,0:T(8,128)S(1)}, u32[]{:S(2)}, u32[]{:S(2)}) collective-permute-start(f32[112,128]{1,0:T(8,128)S(1)} %get-tuple-element.89), channel_id=1, source_target_pairs={{0,12},{1,13},{2,14},{3,15},{4,0},{5,1},{6,2},{7,3},{8,4},{9,5},{1... | collective-permute-start | bytes 172040 | tf_op jit(solution)/shard_map/ppermute | solution.py:336
  72.2 8.0 %collective-permute-start.10 = (f32[896,128]{1,0:T(8,128)S(1)}, f32[896,128]{1,0:T(8,128)S(1)}, u32[]{:S(2)}, u32[]{:S(2)}) collective-permute-start(f32[896,128]{1,0:T(8,128)S(1)} %get-tuple-element.61), channel_id=1, source_target_pairs={{0,1},{1,0},{2,3},{3,2},{4,5},{5,4},{6,7},{7,6},{8,9},{9,8},{10,11... | collective-permute-start | bytes 1376264 | tf_op jit(solution)/shard_map/ppermute | solution.py:307
  72.3 5.5 %collective-permute-start.25 = (f32[112,128]{1,0:T(8,128)S(1)}, f32[112,128]{1,0:T(8,128)S(1)}, u32[]{:S(2)}, u32[]{:S(2)}) collective-permute-start(f32[112,128]{1,0:T(8,128)S(1)} %get-tuple-element.77), channel_id=1, source_target_pairs={{0,12},{1,13},{2,14},{3,15},{4,0},{5,1},{6,2},{7,3},{8,4},{9,5},{1... | collective-permute-start | bytes 172040 | tf_op jit(solution)/shard_map/ppermute | solution.py:344
  72.4 7.8 %collective-permute-start.26 = (f32[112,128]{1,0:T(8,128)S(1)}, f32[112,128]{1,0:T(8,128)S(1)}, u32[]{:S(2)}, u32[]{:S(2)}) collective-permute-start(f32[112,128]{1,0:T(8,128)S(1)} %get-tuple-element.77), channel_id=1, source_target_pairs={{0,8},{1,9},{2,10},{3,11},{4,12},{5,13},{6,14},{7,15},{8,0},{9,1},... | collective-permute-start | bytes 172040 | tf_op jit(solution)/shard_map/ppermute | solution.py:344
  72.5 7.7 %collective-permute-start.27 = (f32[112,128]{1,0:T(8,128)S(1)}, f32[112,128]{1,0:T(8,128)S(1)}, u32[]{:S(2)}, u32[]{:S(2)}) collective-permute-start(f32[112,128]{1,0:T(8,128)S(1)} %get-tuple-element.77), channel_id=1, source_target_pairs={{0,4},{1,5},{2,6},{3,7},{4,8},{5,9},{6,10},{7,11},{8,12},{9,13},{1... | collective-permute-start | bytes 172040 | tf_op jit(solution)/shard_map/ppermute | solution.py:344
  80.3 6.5 %collective-permute-start.11 = (f32[448,128]{1,0:T(8,128)S(1)}, f32[448,128]{1,0:T(8,128)S(1)}, u32[]{:S(2)}, u32[]{:S(2)}) collective-permute-start(f32[448,128]{1,0:T(8,128)S(1)} %slice_select_fusion.1), channel_id=1, source_target_pairs={{0,2},{1,3},{2,0},{3,1},{4,6},{5,7},{6,4},{7,5},{8,10},{9,11},{10,... | collective-permute-start | bytes 688136 | tf_op jit(solution)/shard_map/ppermute | solution.py:307
  86.9 6.6 %collective-permute-start.12 = (f32[112,128]{1,0:T(8,128)S(1)}, f32[112,128]{1,0:T(8,128)S(1)}, u32[]{:S(2)}, u32[]{:S(2)}) collective-permute-start(f32[112,128]{1,0:T(8,128)S(1)} %get-tuple-element.91), channel_id=1, source_target_pairs={{0,4},{1,5},{2,6},{3,7},{4,8},{5,9},{6,10},{7,11},{8,12},{9,13},{1... | collective-permute-start | bytes 172040 | tf_op jit(solution)/shard_map/ppermute | solution.py:336
  88.1 5.7 %collective-permute-start.13 = (f32[112,128]{1,0:T(8,128)S(1)}, f32[112,128]{1,0:T(8,128)S(1)}, u32[]{:S(2)}, u32[]{:S(2)}) collective-permute-start(f32[112,128]{1,0:T(8,128)S(1)} %get-tuple-element.93), channel_id=1, source_target_pairs={{0,8},{1,9},{2,10},{3,11},{4,12},{5,13},{6,14},{7,15},{8,0},{9,1},... | collective-permute-start | bytes 172040 | tf_op jit(solution)/shard_map/ppermute | solution.py:336
  89.7 4.6 %collective-permute-start.14 = (f32[112,128]{1,0:T(8,128)S(1)}, f32[112,128]{1,0:T(8,128)S(1)}, u32[]{:S(2)}, u32[]{:S(2)}) collective-permute-start(f32[112,128]{1,0:T(8,128)S(1)} %get-tuple-element.92), channel_id=1, source_target_pairs={{0,12},{1,13},{2,14},{3,15},{4,0},{5,1},{6,2},{7,3},{8,4},{9,5},{1... | collective-permute-start | bytes 172040 | tf_op jit(solution)/shard_map/ppermute | solution.py:336
  94.4 6.5 %collective-permute-start.15 = (f32[112,128]{1,0:T(8,128)S(1)}, f32[112,128]{1,0:T(8,128)S(1)}, u32[]{:S(2)}, u32[]{:S(2)}) collective-permute-start(f32[112,128]{1,0:T(8,128)S(1)} %get-tuple-element.79), channel_id=1, source_target_pairs={{0,12},{1,13},{2,14},{3,15},{4,0},{5,1},{6,2},{7,3},{8,4},{9,5},{1... | collective-permute-start | bytes 172040 | tf_op jit(solution)/shard_map/ppermute | solution.py:344
  98.4 5.1 %collective-permute-start.16 = (f32[112,128]{1,0:T(8,128)S(1)}, f32[112,128]{1,0:T(8,128)S(1)}, u32[]{:S(2)}, u32[]{:S(2)}) collective-permute-start(f32[112,128]{1,0:T(8,128)S(1)} %get-tuple-element.79), channel_id=1, source_target_pairs={{0,8},{1,9},{2,10},{3,11},{4,12},{5,13},{6,14},{7,15},{8,0},{9,1},... | collective-permute-start | bytes 172040 | tf_op jit(solution)/shard_map/ppermute | solution.py:344
  98.5 6.0 %collective-permute-start.17 = (f32[112,128]{1,0:T(8,128)S(1)}, f32[112,128]{1,0:T(8,128)S(1)}, u32[]{:S(2)}, u32[]{:S(2)}) collective-permute-start(f32[112,128]{1,0:T(8,128)S(1)} %get-tuple-element.79), channel_id=1, source_target_pairs={{0,4},{1,5},{2,6},{3,7},{4,8},{5,9},{6,10},{7,11},{8,12},{9,13},{1... | collective-permute-start | bytes 172040 | tf_op jit(solution)/shard_map/ppermute | solution.py:344
  99.1 11.6 %collective-permute-start.28 = (f32[448,128]{1,0:T(8,128)S(1)}, f32[448,128]{1,0:T(8,128)S(1)}, u32[]{:S(2)}, u32[]{:S(2)}) collective-permute-start(f32[448,128]{1,0:T(8,128)S(1)} %constant_dynamic-slice_fusion), channel_id=1, source_target_pairs={{0,2},{1,3},{2,0},{3,1},{4,6},{5,7},{6,4},{7,5},{8,10},{9,11},{10,... | collective-permute-start | bytes 688136 | tf_op jit(solution)/shard_map/ppermute | solution.py:307
  104.6 6.2 %collective-permute-start.18 = (f32[448,128]{1,0:T(8,128)S(1)}, f32[448,128]{1,0:T(8,128)S(1)}, u32[]{:S(2)}, u32[]{:S(2)}) collective-permute-start(f32[448,128]{1,0:T(8,128)S(1)} %constant_dynamic-slice_fusion.4), channel_id=1, source_target_pairs={{0,2},{1,3},{2,0},{3,1},{4,6},{5,7},{6,4},{7,5},{8,10},{9,11},{10,... | collective-permute-start | bytes 688136 | tf_op jit(solution)/shard_map/ppermute | solution.py:307
  110.8 1.9 %collective-permute-start.29 = (f32[896,128]{1,0:T(8,128)S(1)}, f32[896,128]{1,0:T(8,128)S(1)}, u32[]{:S(2)}, u32[]{:S(2)}) collective-permute-start(f32[896,128]{1,0:T(8,128)S(1)} %pad_maximum_fusion.1.refs_2_), channel_id=1, source_target_pairs={{0,1},{1,0},{2,3},{3,2},{4,5},{5,4},{6,7},{7,6},{8,9},{9,8},{10,11... | collective-permute-start | bytes 1376264 | tf_op jit(solution)/shard_map/ppermute | solution.py:307
  110.9 2.4 %collective-permute-start.19 = (f32[896,128]{1,0:T(8,128)S(1)}, f32[896,128]{1,0:T(8,128)S(1)}, u32[]{:S(2)}, u32[]{:S(2)}) collective-permute-start(f32[896,128]{1,0:T(8,128)S(1)} %pad_maximum_fusion.refs_0_), channel_id=1, source_target_pairs={{0,1},{1,0},{2,3},{3,2},{4,5},{5,4},{6,7},{7,6},{8,9},{9,8},{10,11... | collective-permute-start | bytes 1376264 | tf_op jit(solution)/shard_map/ppermute | solution.py:307
